TPU v7x, 32 devices: a whole 2x2x4 slice. The times are simulated.
32 devices in a mesh: blk: 16 (over z, x, core), tensor: 2 (over y).
Axes of the slice: x: 2, y: 2, z: 4, core: 2. Of those that a mesh axis runs over, the one named last changes fastest.
Arguments:
- tokens: bfloat16 [2048, 1024], P('blk'), may hold values from -6 to 6
- query_vecs: bfloat16 [4096, 128], replicated, may hold values from -6 to 6
- out_cotangent: bfloat16 [2048, 1024], P('blk'), may hold values from -6 to 6
- doc_lengths: int32 [4], replicated, may hold values from 1 to 2045, as said below
- live_mask: int32 [2048], P('blk'), may hold values from 0 to 1, as said below
- positives: int32 [128], replicated, may hold values from 0 to 3
- triple_weight: float32 [1024, 3, 1024], P('blk', None, 'tensor'), may hold values from -0.1875 to 0.1875
- triple_bias: float32 [3, 1024], P(None, 'tensor'), may hold values from -1.75 to 1.75
- output_weight: float32 [1024, 1024], P('tensor', 'blk'), may hold values from -2 to 2
- output_bias: float32 [1024], replicated, may hold values from -1.75 to 1.75
- first_gain: float32 [1024], replicated, may hold values from 0.5 to 1.5
- first_shift: float32 [1024], replicated, may hold values from -1.75 to 1.75
- expand_weight: float32 [1024, 4096], P('blk', 'tensor'), may hold values from -0.1875 to 0.1875
- expand_bias: float32 [4096], P('tensor'), may hold values from -1.75 to 1.75
- contract_weight: float32 [4096, 1024], P('tensor', 'blk'), may hold values from -0.09375 to 0.09375
- contract_bias: float32 [1024], replicated, may hold values from -1.75 to 1.75
- second_gain: float32 [1024], replicated, may hold values from 0.5 to 1.5
- second_shift: float32 [1024], replicated, may hold values from -1.75 to 1.75
- head_weight: float32 [1024, 128], replicated, may hold values from -0.1875 to 0.1875
Outputs:
- mixed: bfloat16 [2048, 1024], P('blk')
- loss: float32 [], replicated
- tokens_grad: float32 [2048, 1024], P('blk')
- queries_grad: float32 [4096, 128], replicated
- triple_grad: float32 [1024, 3, 1024], P('blk', None, 'tensor')
- triplebias_grad: float32 [3, 1024], P(None, 'tensor')
- output_grad: float32 [1024, 1024], P('tensor', 'blk')
- outputbias_grad: float32 [1024], replicated
- firstgain_grad: float32 [1024], replicated
- firstshift_grad: float32 [1024], replicated
- expand_grad: float32 [1024, 4096], P('blk', 'tensor')
- expandbias_grad: float32 [4096], P('tensor')
- contract_grad: float32 [4096, 1024], P('tensor', 'blk')
- contractbias_grad: float32 [1024], replicated
- secondgain_grad: float32 [1024], replicated
- secondshift_grad: float32 [1024], replicated
- head_grad: float32 [1024, 128], replicated
Inputs may be any that keep to these rules, and one draw needn't show every extreme that they name: `doc_lengths`: every aligned run of 2048 packed positions holds whole documents, 4 of them; in each run the longest is exactly 2045 tokens. `live_mask`: the first token of every document is live.
All inputs are finite; a program needn't handle non-finite values.
Results may differ from a plain program's by a relative error of at most 0.014.
The roundings to bfloat16 on the way count: a program that leaves them out, or rounds other values in their place, can miss the bound.
Values may be sent and summed in bfloat16 or wider, within the bound.
No kernel may reach another device: no remote copies, remote signals or barrier semaphores. Data moves between devices by JAX's collectives and lax.ppermute only.
A program may use at most 192 MiB of HBM per device.

v0:
```python
from functools import partial
import math

import jax
import jax.numpy as jnp
import numpy as np
from jax import lax
from jax.experimental import pallas as pl
from jax.experimental.pallas import tpu as pltpu
from jax.sharding import Mesh, PartitionSpec as P

HEAD_DIM = 64
PAIR = 2 * HEAD_DIM

SOFTMAX_TEMPER = 0.05
FLOOR_SCORE = -1e30
NORM_EPSILON = 1e-05
UNIT_EPSILON = 1e-06
PRECISE = lax.Precision.HIGHEST
LOW = jnp.bfloat16
WIDE = jnp.float32

BLK = ("o", "z", "x", "c")
NZ = 4
FOUR = [0, 1, 2, 3]

VMEM_BYTES = 56 * 1024 * 1024
LANES = (0, 64, 192)
QUAD = 4 * HEAD_DIM


def xor_z(value, mask):
    return lax.ppermute(value, "z", [(i, i ^ mask) for i in FOUR])


def xor_s(value, mask):
    return lax.ppermute(value, ("x", "c"), [(i, i ^ mask) for i in FOUR])


def flip(value, axis):
    return lax.ppermute(value, axis, [(0, 1), (1, 0)])


def pick(value, index, axis=0):
    return lax.dynamic_index_in_dim(value, index, axis, keepdims=False)


def after(value, *others):
    return lax.optimization_barrier((value,) + others)[0]


def place(pieces):
    first = pieces[0][1]
    whole = jnp.zeros((len(pieces),) + first.shape, first.dtype)
    for index, piece in pieces:
        whole = lax.dynamic_update_slice_in_dim(whole, piece[None], index, 0)
    return whole


def both(mine, other, where):
    return place([(where, mine), (1 - where, other)])


def doc_layout(doc_lengths, places):
    ends = jnp.cumsum(doc_lengths)
    starts = ends - doc_lengths
    passed = starts <= places[..., None]
    doc_index = jnp.sum(passed.astype(jnp.int32), axis=-1) - 1
    begin = jnp.max(jnp.where(passed, starts, 0), axis=-1)
    return (doc_index, places - begin)


def dot_nn(a, b, precision=None):
    return lax.dot_general(
        a, b, (((1,), (0,)), ((), ())), precision=precision, preferred_element_type=WIDE
    )


def dot_nt(a, b, precision=None):
    return lax.dot_general(
        a, b, (((1,), (1,)), ((), ())), precision=precision, preferred_element_type=WIDE
    )


def dot_tn(a, b, precision=None):
    return lax.dot_general(
        a, b, (((0,), (0,)), ((), ())), precision=precision, preferred_element_type=WIDE
    )


def shape(dims, dtype):
    return jax.ShapeDtypeStruct(dims, dtype)


PARAMS = pltpu.CompilerParams(vmem_limit_bytes=VMEM_BYTES)

TAKES = dict(
    prep=2.5, heads=2.0, project=3.8, attend=7.5, branch=3.5, forward=7.7, second=3.6, middle=12.0, first_back=3.8, attend_back=9.8, triple=2.9, triple_weight=3.8, tokens=3.9,
    tokens_sum=2.1, weights=5.2, output=2.3, core_sum=3.9, line_sum=2.7, columns=2.2, pair_sum=1.8,
    triple_out=1.9, query_units=2.8, query_sum=1.9, query_c=2.5, query_back=1.6, spread=3.5,
)


SCALE = 1.0


def cost(name):
    took = TAKES[name] * SCALE
    return pl.CostEstimate(
        flops=int(took * 1.15e9), bytes_accessed=int(took * 3.7e6), transcendentals=0
    )


def whole(kernel, name, index, inputs, outputs, scratch=(), slabs=()):
    return pl.pallas_call(
        kernel,
        in_specs=[pl.BlockSpec(memory_space=pltpu.SMEM)]
        + [pl.BlockSpec(memory_space=pltpu.VMEM)] * len(inputs)
        + [pl.BlockSpec(memory_space=pl.ANY)] * len(slabs),
        out_specs=[pl.BlockSpec(memory_space=pltpu.VMEM)] * len(outputs),
        out_shape=list(outputs),
        scratch_shapes=list(scratch),
        compiler_params=PARAMS,
        cost_estimate=cost(name),
        name=name,
    )(index, *inputs, *slabs)


def slab_copy(slabs, at, weight, sems):
    there = slabs.at[:, pl.ds(at, weight.shape[1])]
    return pltpu.make_async_copy(there, weight, sems.at[0])


def slab_scratch(rows, cols):
    return [pltpu.VMEM((rows, cols), LOW), pltpu.SemaphoreType.DMA((1,))]


def finish(copy, weight):
    copy.wait()
    return weight[...]


def prep_kernel(idx, tw, ow, ew, cw, live, heads, low, tri):
    slab, span = ew.shape
    alive = jnp.broadcast_to(live[...], (16, live.shape[1])).astype(WIDE).astype(LOW)
    for spot in range(NZ * 2):
        at = spot * HEAD_DIM
        for part, lane in enumerate(LANES):
            heads[spot, :slab, lane : lane + HEAD_DIM] = tw[part, :, at : at + HEAD_DIM].astype(LOW)
        heads[spot, :slab, PAIR : PAIR + HEAD_DIM] = jnp.zeros((slab, HEAD_DIM), LOW)
        heads[spot, slab:, : live.shape[1]] = alive
        heads[spot, slab:, PAIR:] = jnp.zeros((16, PAIR), LOW)
    low[:, :span] = ew[...].astype(LOW)
    low[:, span : 2 * span] = cw[...].astype(LOW)
    low[:, 2 * span :] = ow[...].astype(LOW)
    for part in range(3):
        tri[:, part * 2 * QUAD : (part + 1) * 2 * QUAD] = tw[part].astype(LOW)


def heads_kernel(idx, own, other, weight, live0, live1):
    slab, mc = own.shape[1] - 16, idx[3]
    for spot in range(NZ * 2):
        for source, c, live in ((own, mc, live0), (other, 1 - mc, live1)):
            rows = pl.ds(pl.multiple_of((spot * 2 + c) * slab, slab), slab)
            weight[rows, :] = source[spot, :slab, :]
            live[spot : spot + 1, :] = source[spot, slab : slab + 16, :PAIR].astype(WIDE)[:1]


def swap_halves(value):
    lane = lax.broadcasted_iota(jnp.int32, value.shape, 1)
    half = HEAD_DIM // 2
    return jnp.where(
        (lane & half) == 0,
        pltpu.roll(value, PAIR - half, 1),
        pltpu.roll(value, half, 1),
    )


def turn(value, cosine, sine):
    return value * cosine + swap_halves(value) * sine


def project_kernel(idx, *refs):
    sheets, (weight, cosine, sine, bias, query, kv) = refs[:8], refs[8:]
    rows = sheets[0].shape[0]
    mz, mx = idx[1], idx[2]
    mine = mz * 2 + mx
    parts = []
    for part in range(3):
        total = jnp.zeros((1, HEAD_DIM), WIDE)
        for h in range(NZ * 2):
            here = bias[part : part + 1, h * HEAD_DIM : (h + 1) * HEAD_DIM]
            total = jnp.where(mine == h, here, total)
        parts.append(total)
    empty = jnp.zeros((1, HEAD_DIM), WIDE)
    offset = jnp.concatenate([parts[0], parts[1], empty, parts[2]], axis=1)
    weights = weight[...]
    low_lanes = lax.broadcasted_iota(jnp.int32, (rows, PAIR), 1) < HEAD_DIM
    for z in range(NZ):
        for x in range(2):
            spot = (mz ^ z) * 2 + (mx ^ x)
            at = pl.ds(pl.multiple_of(spot * rows, rows), rows)
            triple = dot_nn(sheets[z * 2 + x][...], weights) + offset
            turned = turn(triple[:, :PAIR], cosine[at, :], sine[at, :])
            query[at, :] = jnp.where(low_lanes, turned, 0.0).astype(LOW)
            kv[at, :] = jnp.where(
                low_lanes, pltpu.roll(turned, HEAD_DIM, 1), triple[:, PAIR:]
            ).astype(LOW)


def key_row(ref):
    rows = ref[...]
    return jnp.concatenate([rows[i : i + 1] for i in range(rows.shape[0])], axis=1)


def attend_kernel(q_ref, kv0_ref, kv1_ref, qdoc_ref, kdoc0_ref, kdoc1_ref, out_ref, log_ref, pack_ref):
    scale = HEAD_DIM ** (-0.5)
    rows = q_ref.shape[3]
    queries = q_ref[0].reshape(4 * rows, PAIR)
    kv = (kv0_ref[...], kv1_ref[...])
    doc = qdoc_ref[0].reshape(4 * rows, 1)
    allowed = [doc == key_row(ref) for ref in (kdoc0_ref, kdoc1_ref)]
    scores = [
        jnp.where(ok, dot_nt(queries, keys) * scale, FLOOR_SCORE) for ok, keys in zip(allowed, kv)
    ]
    peak = jnp.maximum(*[jnp.max(s, axis=-1, keepdims=True) for s in scores])
    weights = [jnp.where(ok, jnp.exp(s - peak), 0.0) for ok, s in zip(allowed, scores)]
    total = sum(jnp.sum(w, axis=-1, keepdims=True) for w in weights)
    mixed = sum(dot_nn(w.astype(LOW), keys) for w, keys in zip(weights, kv)) / total
    out_ref[0] = mixed.reshape(2, 2, rows, PAIR)
    log_ref[0] = (peak + jnp.log(total)).reshape(2, 2, rows, 1)
    low_lanes = lax.broadcasted_iota(jnp.int32, (rows, PAIR), 1) < HEAD_DIM
    for x in range(2):
        upper = mixed[2 * x * rows : (2 * x + 1) * rows]
        lower = mixed[(2 * x + 1) * rows : (2 * x + 2) * rows]
        pack_ref[0, x] = jnp.where(low_lanes, pltpu.roll(upper, HEAD_DIM, 1), lower).astype(LOW)


def attend_specs(rows, keys, key_rows):
    half = rows // 2
    size = max(16, min(half, half * 2048 // (2 * keys)))
    full = lambda n, m: pl.BlockSpec((n, m), lambda i, j: (0, 0))
    part = lambda m: pl.BlockSpec((1, 2, 2, size, m), lambda i, j: (i, 0, 0, j, 0))
    pack = pl.BlockSpec((1, 2, size, PAIR), lambda i, j: (i, 0, j, 0))
    kv, docs = full(keys, PAIR), full(key_rows, rows)
    return (NZ, half // size), part, pack, kv, docs


def attend(queries, kv0, kv1, qdoc, kdoc0, kdoc1):
    rows = kdoc0.shape[1]
    half = rows // 2
    grid, part, pack, kv, docs = attend_specs(rows, kv0.shape[0], kdoc0.shape[0])
    return pl.pallas_call(
        attend_kernel,
        grid=grid,
        in_specs=[part(PAIR), kv, kv, part(1), docs, docs],
        out_specs=[part(PAIR), part(1), pack],
        out_shape=[
            shape((NZ, 2, 2, half, PAIR), WIDE),
            shape((NZ, 2, 2, half, 1), WIDE),
            shape((NZ, 2, half, PAIR), LOW),
        ],
        compiler_params=PARAMS,
        cost_estimate=cost("attend"),
        name="attend",
    )(queries.reshape(NZ, 2, 2, half, PAIR), kv0, kv1, qdoc, kdoc0, kdoc1)


def attend_back_kernel(
    q_ref, g_ref, o_ref, log_ref, kv0_ref, kv1_ref, qdoc_ref, kdoc0_ref, kdoc1_ref,
    dq_ref, dkv0_ref, dkv1_ref,
):
    scale = HEAD_DIM ** (-0.5)
    rows = q_ref.shape[3]

    @pl.when((pl.program_id(0) == 0) & (pl.program_id(1) == 0))
    def _():
        dkv0_ref[...] = jnp.zeros_like(dkv0_ref)
        dkv1_ref[...] = jnp.zeros_like(dkv1_ref)

    queries = q_ref[0].reshape(4 * rows, PAIR)
    high_lanes = lax.broadcasted_iota(jnp.int32, (rows, PAIR), 1) >= HEAD_DIM
    parts = []
    for x in range(2):
        packed = g_ref[0, x].astype(WIDE)
        parts.append(jnp.where(high_lanes, pltpu.roll(packed, HEAD_DIM, 1), 0.0))
        parts.append(jnp.where(high_lanes, packed, 0.0))
    wide = jnp.concatenate(parts, axis=0)
    grads = wide.astype(LOW)
    delta = jnp.sum(wide * o_ref[0].reshape(4 * rows, PAIR), axis=-1, keepdims=True)
    doc, log_total = qdoc_ref[0].reshape(4 * rows, 1), log_ref[0].reshape(4 * rows, 1)
    total = jnp.zeros((4 * rows, PAIR), WIDE)
    for kv_ref, kdoc_ref, dkv_ref in (
        (kv0_ref, kdoc0_ref, dkv0_ref),
        (kv1_ref, kdoc1_ref, dkv1_ref),
    ):
        keys = kv_ref[...]
        raw = dot_nt(queries, keys)
        probs = jnp.where(doc == key_row(kdoc_ref), jnp.exp(raw * scale - log_total), 0.0)
        dprobs = dot_nt(grads, keys)
        dscores = (probs * (dprobs - delta) * scale).astype(LOW)
        total = total + dot_nn(dscores, keys)
        dkv_ref[...] += dot_tn(dscores, queries) + dot_tn(probs.astype(LOW), grads)
    dq_ref[0] = total.reshape(2, 2, rows, PAIR)


def attend_back(queries, grads, out, log_total, kv0, kv1, qdoc, kdoc0, kdoc1):
    rows, keys = kdoc0.shape[1], kv0.shape[0]
    half = rows // 2
    grid, part, pack, kv, docs = attend_specs(rows, keys, kdoc0.shape[0])
    return pl.pallas_call(
        attend_back_kernel,
        grid=grid,
        in_specs=[part(PAIR), pack, part(PAIR), part(1), kv, kv, part(1), docs, docs],
        out_specs=[part(PAIR), kv, kv],
        out_shape=[
            shape((NZ, 2, 2, half, PAIR), WIDE),
            shape((keys, PAIR), WIDE),
            shape((keys, PAIR), WIDE),
        ],
        compiler_params=PARAMS,
        cost_estimate=cost("attend_back"),
        name="attend_back",
    )(queries.reshape(NZ, 2, 2, half, PAIR), grads, out, log_total, kv0, kv1, qdoc, kdoc0, kdoc1)


def branch_kernel(idx, got, slabs, low, part, held, sems):
    copy = slab_copy(slabs, slabs.shape[1] - held.shape[1], held, sems)
    copy.start()
    half = got.shape[1]
    for h in range(NZ * 2):
        lanes = slice(h * HEAD_DIM, (h + 1) * HEAD_DIM)
        low[:half, lanes] = got[h, :, :HEAD_DIM]
        low[half:, lanes] = got[h, :, HEAD_DIM:]
    part[...] = dot_nt(low[...], finish(copy, held)).astype(LOW)


def normalize(value):
    center = value - jnp.mean(value, axis=-1, keepdims=True)
    spread = jnp.mean(center * center, axis=-1, keepdims=True)
    inverse = lax.rsqrt(spread + NORM_EPSILON)
    return center * inverse, inverse


def pair(own, other):
    return own[...].astype(WIDE) + other[...].astype(WIDE)


def forward_kernel(
    idx, own, other, tokens, bias, gain, shift, hidden_bias, attended, slabs,
    first, unitary, inverse, hidden_in, keep, send, part,
    low, hidden, expand, sems1, contract, sems2,
):
    copy1 = slab_copy(slabs, 0, expand, sems1)
    copy2 = slab_copy(slabs, expand.shape[1], contract, sems2)
    copy1.start()
    copy2.start()
    value = tokens[...].astype(WIDE) + (pair(own, other) + bias[...])
    unitary[...], inverse[...] = normalize(value)
    first[...] = unitary[...] * gain[...] + shift[...]
    low[...] = first[...].astype(LOW)
    value = dot_nn(low[...], finish(copy1, expand)) + hidden_bias[...]
    hidden_in[...] = value
    hidden[...] = (0.5 * value * (1.0 + lax.erf(value * (0.5**0.5)))).astype(LOW)
    part[...] = dot_nt(hidden[...], finish(copy2, contract)).astype(LOW)
    rows, width = low.shape
    few = rows * QUAD // width
    for out, x in ((keep, idx[2]), (send, 1 - idx[2])):
        out[:rows, :] = low[...]
        out[rows : 2 * rows, :] = columns_of(hidden, x, width)
        for i in range(width // QUAD):
            out[2 * rows :, i * QUAD : (i + 1) * QUAD] = attended[
                i * few : (i + 1) * few, pl.ds(pl.multiple_of(x * QUAD, QUAD), QUAD)
            ]


def columns_of(ref, x, span):
    return ref[:, pl.ds(pl.multiple_of(x * span, 128), span)]


def unit_scale(value):
    return lax.rsqrt(jnp.sum(value * value, axis=-1, keepdims=True) + UNIT_EPSILON)


def second_kernel(
    idx, own, other, first, bias, gain, shift, head, query, kdoc,
    low, unitary, inverse, embed, unit, expo, totals,
):
    value = first[...] + (pair(own, other) + bias[...])
    unitary[...], inverse[...] = normalize(value)
    low[...] = (unitary[...] * gain[...] + shift[...]).astype(LOW)
    embed[...] = dot_nn(low[...], head[...].astype(LOW))
    unit[...] = (embed[...] * unit_scale(embed[...])).astype(LOW)
    expo[...] = jnp.exp(dot_nt(unit[...], query[...]) / SOFTMAX_TEMPER)
    totals[...] = dot_nn(member(idx, kdoc, totals.shape[0]), expo[...], PRECISE)


def query_kernel(idx, vecs, out):
    value = vecs[...].astype(WIDE)
    out[...] = (value * unit_scale(value)).astype(LOW)


def member(idx, kdoc, docs):
    row = kdoc[pl.ds((idx[0] * NZ + idx[1]) * 2 + idx[2], 1), :]
    label = lax.broadcasted_iota(jnp.int32, (docs, row.shape[1]), 0)
    return jnp.where(row == label, 1.0, 0.0)


def group_sum(value, length):
    column = lax.broadcasted_iota(jnp.int32, value.shape, 1)
    span = value.shape[1]
    step = 1
    while step < length:
        ahead, behind = pltpu.roll(value, span - step, 1), pltpu.roll(value, step, 1)
        value = value + jnp.where((column & step) == 0, ahead, behind)
        step *= 2
    return value


def loss_of(count, totals, kdocs, positive):
    docs, columns = totals.shape
    length = columns // count
    label = lax.broadcasted_iota(jnp.int32, (docs, 1), 0)
    tokens = jnp.zeros((docs, 1), WIDE)
    for ref in kdocs:
        tokens = tokens + jnp.sum(jnp.where(key_row(ref) == label, 1.0, 0.0), axis=1, keepdims=True)
    doc_score = group_sum(SOFTMAX_TEMPER * (jnp.log(totals) - jnp.log(tokens)), length)
    best = jnp.max(doc_score, axis=0, keepdims=True)
    shifted = jnp.exp(doc_score - best)
    shifted_sum = jnp.sum(shifted, axis=0, keepdims=True)
    chosen = jnp.where(label == positive, 1.0, 0.0)
    each = best + jnp.log(shifted_sum) - jnp.sum(doc_score * chosen, axis=0, keepdims=True)
    loss = jnp.sum(each, axis=1, keepdims=True) / columns
    return loss, (shifted / shifted_sum - chosen) / (totals * count)


def core_sum_kernel(idx, keep, got, own, send):
    own[...] = keep[0] + got[0].astype(WIDE)
    send[...] = (keep[1] + got[1].astype(WIDE)).astype(LOW)


def query_sum_kernel(idx, own, other, *outs):
    for z, out in enumerate(outs):
        out[...] = (own[z] + other[z].astype(WIDE)).astype(out.dtype)


def unit_back(value, grad):
    scale = unit_scale(value)
    along = jnp.sum(grad * value, axis=-1, keepdims=True)
    return scale * grad - value * (along * scale * scale * scale)


def query_back_kernel(idx, own, r1, r2, r3, value, out):
    total = own[...] + r1[...].astype(WIDE) + (r2[...].astype(WIDE) + r3[...].astype(WIDE))
    shares = value.shape[0]
    out[:shares, :] = unit_back(value[...].astype(WIDE), total[:shares]).astype(LOW)
    out[shares:, :] = total[shares:].astype(LOW)


def spread_kernel(idx, got, queries, head, *vectors):
    rows = got.shape[1]
    chunk = head.shape[0] // (NZ * 4)
    shares = rows - chunk - 16
    pieces = []
    for i in range(NZ * 4):
        queries[i * shares : (i + 1) * shares, :] = got[i, :shares, :].astype(WIDE)
        head[i * chunk : (i + 1) * chunk, :] = got[i, shares : shares + chunk, :].astype(WIDE)
        pieces.append(got[i, shares + chunk :, :].astype(WIDE))
    row = 0
    for out in vectors:
        for i in range(0, out.shape[0], 8):
            out[i : i + 8, :] = pieces[row // 16][row % 16 : row % 16 + 8]
            row += 8


def norm_back(grad, gain, unitary, inverse):
    scaled = grad * gain
    along = jnp.mean(scaled * unitary, axis=-1, keepdims=True)
    return inverse * (scaled - jnp.mean(scaled, axis=-1, keepdims=True) - unitary * along)


def column_sum(value):
    return jnp.sum(value, axis=0, keepdims=True)


def middle_kernel(
    count, idx, t0, t1, t2, t3, kdoc0, kdoc1, positive, expo, query, unit,
    embed, low, head, cotangent, unitary, inverse, gain, hidden_in, slabs,
    grad_in, keep, send, part, loss, q0, q1,
    similar, grad_low, grad_hidden_in, head_part, rows_part, expand, sems1, contract, sems2,
):
    copy1 = slab_copy(slabs, 0, expand, sems1)
    copy2 = slab_copy(slabs, expand.shape[1], contract, sems2)
    copy2.start()
    copy1.start()
    totals = (t0[...] + t1[...]) + (t2[...] + t3[...])
    value, coefficient = loss_of(count, totals, (kdoc0, kdoc1), positive[...])
    loss[...] = jnp.broadcast_to(value, loss.shape)
    here = member(idx, kdoc0, totals.shape[0])
    similar[...] = (dot_tn(here, coefficient, PRECISE) * expo[...]).astype(LOW)
    grad_embed = unit_back(embed[...], dot_nn(similar[...], query[...])).astype(LOW)
    rows, width = embed.shape[0], low.shape[1]
    head_part[...] = dot_tn(low[...], grad_embed)
    grad_second = dot_nt(grad_embed, head[...].astype(LOW)) + cotangent[...].astype(WIDE)
    grad_in[...] = norm_back(grad_second, gain[...], unitary[...], inverse[...])
    grad_low[...] = grad_in[...].astype(LOW)
    sums = [
        column_sum(grad_low[...].astype(WIDE)),
        column_sum(grad_second * unitary[...]),
        column_sum(grad_second),
    ]
    value = hidden_in[...]
    grad = dot_nn(grad_low[...], finish(copy2, contract))
    bell = jnp.exp(-0.5 * value * value) * (1.0 / math.sqrt(2.0 * math.pi))
    slope = 0.5 * (1.0 + lax.erf(value * (0.5**0.5))) + value * bell
    grad_hidden_in[...] = (slope * grad).astype(LOW)
    sums.append(column_sum(grad_hidden_in[...].astype(WIDE)))
    part[...] = dot_nt(grad_hidden_in[...], finish(copy1, expand)).astype(LOW)
    for out, x in ((keep, idx[2]), (send, 1 - idx[2])):
        out[:rows, :] = grad_low[...]
        out[rows:, :] = columns_of(grad_hidden_in, x, width)
    rows_part[...] = jnp.zeros_like(rows_part)
    at = 0
    for value in sums:
        for i in range(value.shape[1] // PAIR):
            rows_part[at : at + 1, :] = value[:, i * PAIR : (i + 1) * PAIR]
            at += 1
    chunk = width // (NZ * 4)
    shares = q0.shape[2] - chunk - 16
    for mask in range(4):
        there = (idx[2] * 2 + idx[3]) ^ mask
        for z in range(NZ):
            out = (q0, q1)[mask % 2].at[mask // 2]
            at = (idx[1] ^ z) * 4 + there
            columns_here = pl.ds(pl.multiple_of(at * shares, shares), shares)
            out[z, :shares, :] = dot_tn(similar[:, columns_here], unit[...]).astype(out.dtype)
            out[z, shares : shares + chunk, :] = head_part[
                pl.ds(pl.multiple_of(at * chunk, chunk), chunk), :
            ].astype(out.dtype)
            out[z, shares + chunk :, :] = rows_part[
                pl.ds(pl.multiple_of(at * 16, 16), 16), :
            ].astype(out.dtype)


def slab_products(idx, left, right, outs, at):
    slab = outs[0].shape[-2]
    for z, out in enumerate(outs):
        mine = []
        for x in range(2):
            spot = (idx[1] ^ z) * 2 + (idx[2] ^ x)
            lanes = left[:, pl.ds(pl.multiple_of(spot * 2 * slab, 2 * slab), 2 * slab)]
            mine.append(jnp.where(idx[3] == 0, lanes[:, :slab], lanes[:, slab:]))
        both_rows = dot_tn(jnp.concatenate(mine, axis=1), right)
        for x in range(2):
            out[at + (x,)] = both_rows[x * slab : (x + 1) * slab].astype(out.dtype)


def weights_kernel(idx, f0, f1, f2, f3, g0, g1, g2, g3, own, s1, s2, s3, left, right):
    rows = g0.shape[0] // 2
    firsts, grads = (f0, f1, f2, f3), (g0, g1, g2, g3)
    for at, lefts, rights in ((0, grads, firsts), (1, firsts, grads)):
        for i in range(4):
            left[i * rows : (i + 1) * rows, :] = lefts[i][:rows, :]
            right[i * rows : (i + 1) * rows, :] = rights[i][rows : 2 * rows, :]
        slab_products(idx, left, right[...], (own, s1, s2, s3), (at,))


def output_kernel(idx, f0, f1, f2, f3, g0, g1, g2, g3, own, s1, s2, s3, left, right):
    rows, width = g0.shape
    few = rows * QUAD // width
    for i, (f, g) in enumerate(zip((f0, f1, f2, f3), (g0, g1, g2, g3))):
        left[i * rows : (i + 1) * rows, :] = g[...]
        for j in range(width // QUAD):
            right[i * rows + j * few : i * rows + (j + 1) * few, :] = f[
                2 * rows :, j * QUAD : (j + 1) * QUAD
            ]
    slab_products(idx, left, right[...], (own, s1, s2, s3), ())


def line_sum_kernel(idx, a0, a1, a2, a3, b0, b1, b2, b3, keep, keep_out, send):
    span = keep.shape[-1]
    total = a0[...] + a1[...].astype(WIDE) + (a2[...].astype(WIDE) + a3[...].astype(WIDE))
    keep[...] = total[:, 0]
    send[:, :span] = total[0, 1].astype(LOW)
    send[:, span : 2 * span] = total[1, 1].astype(LOW)
    total = b0[...] + b1[...].astype(WIDE) + (b2[...].astype(WIDE) + b3[...].astype(WIDE))
    keep_out[...] = total[0]
    send[:, 2 * span :] = total[1].astype(LOW)


def columns_kernel(idx, keep, keep_out, got, contract, expand, output):
    span = keep.shape[-1]
    for at, mine, out in ((0, keep[0], contract), (span, keep[1], expand), (2 * span, keep_out[...], output)):
        cols = mine.shape[1]
        out[:, pl.ds(pl.multiple_of(idx[2] * cols, 128), cols)] = mine
        out[:, pl.ds(pl.multiple_of((1 - idx[2]) * cols, 128), cols)] = got[
            :, at : at + cols
        ].astype(WIDE)


def first_back_kernel(
    idx, own, other, grad_second_in, unitary, inverse, gain, slabs,
    grad_in, grad_low, vectors, pack, held, sems,
):
    copy = slab_copy(slabs, slabs.shape[1] - held.shape[1], held, sems)
    copy.start()
    grad_first = grad_second_in[...] + pair(own, other)
    grad_in[...] = norm_back(grad_first, gain[...], unitary[...], inverse[...])
    grad_low[...] = grad_in[...].astype(LOW)
    vectors[...] = jnp.zeros_like(vectors)
    vectors[0:1, :] = column_sum(grad_low[...].astype(WIDE))
    vectors[1:2, :] = column_sum(grad_first * unitary[...])
    vectors[2:3, :] = column_sum(grad_first)
    grad = dot_nn(grad_low[...], finish(copy, held)).astype(LOW)
    half = pack.shape[1]
    for h in range(NZ * 2):
        lanes = slice(h * HEAD_DIM, (h + 1) * HEAD_DIM)
        pack[h, :, :HEAD_DIM] = grad[:half, lanes]
        pack[h, :, HEAD_DIM:] = grad[half:, lanes]


def triple_kernel(idx, dq, dkv, got, cosine, sine, out):
    rows = dq.shape[0]
    low_lanes = lax.broadcasted_iota(jnp.int32, (rows, PAIR), 1) < HEAD_DIM
    grads = dkv[...] + got[...]
    both_parts = jnp.where(low_lanes, dq[...], pltpu.roll(grads, HEAD_DIM, 1))
    turned = turn(both_parts, cosine[...], -sine[...])
    out[:, :PAIR] = turned.astype(LOW)
    out[:, PAIR:] = jnp.where(low_lanes, 0.0, grads).astype(LOW)


def extra_rows(bias, vectors):
    cols = bias.shape[1]
    rows = [bias]
    for i in range(3):
        for j in range(vectors.shape[1] // cols):
            rows.append(vectors[i : i + 1, j * cols : (j + 1) * cols])
    return jnp.concatenate(rows + [jnp.zeros((16 - len(rows), cols), WIDE)], axis=0)


def triple_weight_kernel(idx, *refs):
    sheets, (grad, vectors, keep, send, total) = refs[:8], refs[8:]
    mz, mx, mc = idx[1], idx[2], idx[3]
    rows = sheets[0].shape[0]
    slab = keep.shape[1] - 16
    for z in range(NZ):
        for x in range(2):
            spot = (mz ^ z) * 2 + (mx ^ x)
            at = pl.ds(pl.multiple_of(spot * rows, rows), rows)
            part = dot_tn(sheets[z * 2 + x][...], grad[at, :])
            if z + x == 0:
                total[...] = part
            else:
                total[...] += part
    extra = extra_rows(column_sum(grad[...].astype(WIDE)), vectors).astype(LOW)
    for spot in range(NZ * 2):
        for out, c in ((keep, mc), (send, 1 - mc)):
            at = pl.ds(pl.multiple_of((spot * 2 + c) * slab, slab), slab)
            out[spot, :slab, :] = total[at, :].astype(LOW)
            out[spot, slab:, :] = extra


def pair_sum_kernel(idx, one, two, out):
    out[...] = (one[...].astype(WIDE) + two[...].astype(WIDE)).astype(out.dtype)


def triple_out_kernel(idx, got, weight, bias, *vectors):
    slab = weight.shape[1]
    total = 0.0
    for spot in range(NZ * 2):
        at = spot * HEAD_DIM
        here = got[spot].astype(WIDE)
        for part, lane in enumerate(LANES):
            weight[part, :, at : at + HEAD_DIM] = here[:slab, lane : lane + HEAD_DIM]
            bias[part : part + 1, at : at + HEAD_DIM] = here[slab : slab + 1, lane : lane + HEAD_DIM]
        total = total + here[slab:]
    row = 1
    for out in vectors:
        for i in range(0, out.shape[0], 2):
            out[i : i + 1, :] = total[row : row + 1, :PAIR]
            out[i + 1 : i + 2, :] = total[row : row + 1, PAIR:]
            row += 1


def tokens_kernel(idx, got, weight, part, group):
    for h in range(NZ * 2):
        for p, lane in enumerate(LANES):
            at = (p * NZ * 2 + h) * HEAD_DIM
            group[:, at : at + HEAD_DIM] = got[h, :, lane : lane + HEAD_DIM]
    part[...] = dot_nt(group[...], weight[...]).astype(LOW)


def tokens_sum_kernel(idx, own, other, grad, out):
    out[...] = grad[...] + pair(own, other)


def shards(
    tokens,
    query_vecs,
    out_cotangent,
    doc_lengths,
    live_mask,
    positives,
    triple_weight,
    triple_bias,
    output_weight,
    output_bias,
    first_gain,
    first_shift,
    expand_weight,
    expand_bias,
    contract_weight,
    contract_bias,
    second_gain,
    second_shift,
    head_weight,
):
    outer = lax.axis_size("o")
    mo, mz, mx, mc, my = [lax.axis_index(a) for a in ("o", "z", "x", "c", "y")]
    index = jnp.stack([mo, mz, mx, mc, my]).astype(jnp.int32)
    rows, width = tokens.shape
    half = rows // 2
    slab = triple_weight.shape[0]
    docs = doc_lengths.shape[0]
    queries_count = positives.shape[0]
    blocks = outer * NZ * 4
    span = expand_weight.shape[1]
    quarter = span // 2
    proj = head_weight.shape[1]
    line = lambda vector: vector.reshape(1, -1)

    def widen(value):
        return lax.all_gather(value, "o") if outer > 1 else value[None]

    def narrow(value):
        return lax.psum_scatter(value, "o") if outer > 1 else value[0]

    def sum_outer(value):
        return lax.psum(value, "o") if outer > 1 else value

    by_z = [tokens] + [xor_z(tokens, m) for m in (1, 2, 3)]
    sheets = [tokens, flip(tokens, "x"), by_z[1], flip(by_z[1], "x")]

    heads, low_slab, triple_slab = whole(
        prep_kernel,
        "prep",
        index,
        (
            triple_weight.transpose(1, 0, 2),
            output_weight.T,
            expand_weight,
            contract_weight.T,
            line(live_mask),
        ),
        [shape((NZ * 2, slab + 16, QUAD), LOW)]
        + [shape((slab, n), LOW) for n in (2 * span + 2 * QUAD, 6 * QUAD)],
    )
    heads = lax.all_to_all(heads, ("z", "x"), 0, 0)
    for piece in by_z[2:]:
        sheets += [piece, flip(after(piece, heads), "x")]
    heads_other = flip(after(heads, sheets[1], sheets[3]), "c")
    if outer > 1:
        pack = widen(both(heads, heads_other, mc)).transpose(0, 2, 1, 3, 4)
        head_triple = pack[..., :slab, :].reshape(width, QUAD)
        live0, live1 = [
            pick(pack, c, 2)[..., slab, :rows].astype(WIDE).reshape(-1, rows) for c in (mc, 1 - mc)
        ]
    else:
        head_triple, live0, live1 = whole(
            heads_kernel,
            "heads",
            index,
            (heads, heads_other),
            [shape((width, QUAD), LOW)] + [shape((NZ * 2, rows), WIDE)] * 2,
        )

    where = jnp.arange(rows, dtype=jnp.int32) * blocks
    rank = jnp.arange(NZ * 2, dtype=jnp.int32) * 2

    def key_doc(live, c):
        block = jnp.arange(outer * NZ * 2, dtype=jnp.int32) * 2 + c
        doc = doc_layout(doc_lengths, block[:, None] + where[None, :])[0]
        return jnp.where(live > 0, doc, -1)

    kdoc0, kdoc1 = key_doc(live0, mc), key_doc(live1, 1 - mc)
    own_places = (mo * NZ * 4 + rank + mc)[:, None] + where[None, :]
    own_doc, own_position = doc_layout(doc_lengths, own_places.reshape(-1))
    lane = jnp.arange(PAIR) % (HEAD_DIM // 2)
    exponent = (2 * lane).astype(WIDE) / HEAD_DIM
    angles = own_position.astype(WIDE)[:, None] * jnp.exp(-math.log(10000.0) * exponent)[None, :]
    sign = jnp.where(jnp.arange(PAIR) % HEAD_DIM < HEAD_DIM // 2, -1.0, 1.0).astype(WIDE)
    cosine, sine = jnp.cos(angles), jnp.sin(angles) * sign[None, :]
    qdoc = own_doc.reshape(NZ, 2, 2, half, 1)
    query_unit = whole(
        query_kernel, "query_units", index, (query_vecs,), [shape(query_vecs.shape, LOW)]
    )[0]
    shares = query_vecs.shape[0] // (NZ * 4)
    positive = line(jnp.repeat(positives, query_vecs.shape[0] // queries_count))

    gathered = lax.all_gather(after(low_slab, *by_z[1:]), BLK, axis=0, tiled=True)
    triple_low = lax.all_gather(after(triple_slab, gathered), BLK, axis=0, tiled=True)

    count = NZ * 2 * rows
    queries, kv = whole(
        project_kernel,
        "project",
        index,
        (*sheets, head_triple, cosine, sine, triple_bias),
        [shape((count, PAIR), LOW)] * 2,
    )
    kv0, kv1 = [widen(v).reshape(-1, PAIR) for v in (kv, flip(kv, "c"))]
    meta = (qdoc, kdoc0, kdoc1)
    out, log_total, pack = attend(queries, kv0, kv1, *meta)
    wide_rows, low_rows, thin_rows = [shape((rows, n), t) for n, t in ((width, WIDE), (width, LOW), (1, WIDE))]

    def to_blocks(value):
        return lax.all_to_all(value.reshape((NZ * 2,) + value.shape[-2:]), ("z", "x"), 0, 0)

    pack = to_blocks(pack)
    attended_low, part = whole(
        branch_kernel,
        "branch",
        index,
        (pack,),
        [shape((rows, 2 * QUAD), LOW), low_rows],
        slab_scratch(width, 2 * QUAD),
        (gathered,),
    )
    both_slabs = slab_scratch(width, span) * 2
    few = rows * QUAD // width
    first, unitary1, inverse1, hidden_in, keep, send, part = whole(
        forward_kernel,
        "forward",
        index,
        (
            part, flip(part, "y"), tokens, line(output_bias), line(first_gain), line(first_shift),
            line(expand_bias), attended_low,
        ),
        [wide_rows, wide_rows, thin_rows, shape((rows, span), WIDE)]
        + [shape((2 * rows + few, width), LOW)] * 2
        + [low_rows],
        [pltpu.VMEM((rows, width), LOW), pltpu.VMEM((rows, span), LOW)] + both_slabs,
        (gathered,),
    )

    def over_z(parts):
        return [parts[0]] + [xor_z(parts[m], m) for m in (1, 2, 3)]

    def four_cores(keep, send):
        two = [keep, flip(send, "x")]
        return two + [flip(value, "c") for value in two]

    firsts = four_cores(keep, send)
    my_tokens = query_unit.shape[0]
    part_other = flip(part, "y")
    second_low, unitary2, inverse2, embed, unit_low, expo, totals = whole(
        second_kernel,
        "second",
        index,
        (
            part, part_other, first, line(contract_bias), line(second_gain), line(second_shift),
            head_weight, query_unit, kdoc0,
        ),
        [low_rows, wide_rows, thin_rows, shape((rows, proj), WIDE), shape((rows, proj), LOW)]
        + [shape((rows, my_tokens), WIDE), shape((docs, my_tokens), WIDE)],
    )

    def tree(own, one, two, three):
        return (own + one) + (two + three)

    totals = sum_outer(tree(totals, *[xor_s(totals, m) for m in (1, 2, 3)]))
    chunk = width // (NZ * 4)
    message = (NZ, shares + chunk + 16, proj)
    grad_second_in, keep, send, part, loss, *query_parts = whole(
        partial(middle_kernel, queries_count),
        "middle",
        index,
        (
            totals, *[xor_z(totals, m) for m in (1, 2, 3)], kdoc0, kdoc1, positive, expo, query_unit,
            unit_low, embed, second_low, head_weight, out_cotangent, unitary2, inverse2,
            line(second_gain), hidden_in,
        ),
        [wide_rows]
        + [shape((2 * rows, width), LOW)] * 2
        + [low_rows, shape((8, proj), WIDE), shape((2,) + message, WIDE), shape((2,) + message, LOW)],
        [
            pltpu.VMEM((rows, my_tokens), LOW),
            pltpu.VMEM((rows, width), LOW),
            pltpu.VMEM((rows, span), LOW),
            pltpu.VMEM((width, proj), WIDE),
            pltpu.VMEM((NZ * 4 * 16, proj), WIDE),
        ]
        + both_slabs,
        (gathered,),
    )
    grads = four_cores(keep, send)
    part_other = flip(part, "y")
    grad_first_in, grad_branch, vectors1, pack = whole(
        first_back_kernel,
        "first_back",
        index,
        (part, part_other, grad_second_in, unitary1, inverse1, line(first_gain)),
        [wide_rows, low_rows, shape((8, width), WIDE), shape((NZ * 2, half, PAIR), LOW)],
        slab_scratch(width, 2 * QUAD),
        (gathered,),
    )
    grad_out = to_blocks(pack)

    branches = four_cores(grad_branch, grad_branch)
    dims, dims_out = (2, 2, slab, quarter), (2, slab, QUAD)
    left_right = [pltpu.VMEM((4 * rows, width), LOW)]
    if outer == 1:
        weight_parts = whole(
            weights_kernel,
            "weights",
            index,
            (*firsts, *grads),
            [shape(dims, WIDE)] + [shape(dims, LOW)] * 3,
            left_right * 2,
        )
        output_parts = whole(
            output_kernel,
            "output",
            index,
            (*firsts, *branches),
            [shape(dims_out, WIDE)] + [shape(dims_out, LOW)] * 3,
            left_right + [pltpu.VMEM((4 * rows, QUAD), LOW)],
        )
    else:

        def parts_of(left, right):
            part = dot_tn(jnp.concatenate(left), jnp.concatenate(right))
            part = pick(narrow(part.reshape(outer, NZ, 2, 2, slab, -1)), mc, 2)
            for axis, spot in ((0, mz), (1, mx)):
                part = jnp.take(part, jnp.arange(part.shape[axis]) ^ spot, axis=axis)
            return part

        top, mid = slice(0, rows), slice(rows, 2 * rows)
        wide = [f[2 * rows :].reshape(few, 4, QUAD).transpose(1, 0, 2).reshape(rows, QUAD) for f in firsts]
        weight_parts = jnp.stack(
            [
                parts_of([g[top] for g in grads], [f[mid] for f in firsts]),
                parts_of([f[top] for f in firsts], [g[mid] for g in grads]),
            ],
            axis=1,
        )
        output_parts = parts_of(branches, wide)
        weight_parts = [weight_parts[0]] + [weight_parts[m].astype(LOW) for m in (1, 2, 3)]
        output_parts = [output_parts[0]] + [output_parts[m].astype(LOW) for m in (1, 2, 3)]

    two = [shape(message, WIDE), shape(message, LOW)]
    parts = whole(core_sum_kernel, "query_c", index, (query_parts[0], flip(query_parts[1], "c")), two)
    parts = whole(
        query_sum_kernel,
        "query_sum",
        index,
        (parts[0], flip(parts[1], "x")),
        [shape(message[1:], WIDE)] + [shape(message[1:], LOW)] * 3,
    )
    parts = [sum_outer(p) for p in parts]
    block = (mz * 2 + mx) * 2 + mc
    own_queries = lax.dynamic_slice_in_dim(query_vecs, block * shares, shares, 0)
    mine = whole(
        query_back_kernel, "query_back", index, (*over_z(parts), own_queries), [shape(message[1:], LOW)]
    )[0]
    grad_query, dkv0, dkv1 = attend_back(
        after(queries, weight_parts[0]), grad_out.reshape(NZ, 2, half, PAIR), out, log_total, kv0, kv1, *meta
    )

    weight_in, output_in = over_z(weight_parts), over_z(output_parts)
    dkv0, dkv1 = [narrow(v.reshape(outer, -1, PAIR)) for v in (dkv0, dkv1)]
    grad_triple = whole(
        triple_kernel,
        "triple",
        index,
        (after(grad_query.reshape(count, PAIR), mine, weight_in[1]), dkv0, flip(dkv1, "c"), cosine, sine),
        [shape((count, QUAD), LOW)],
    )[0]

    block_triple = to_blocks(grad_triple.reshape(NZ * 2, rows, QUAD))
    dims = (NZ * 2, slab + 16, QUAD)
    if outer == 1:
        keep, send = whole(
            triple_weight_kernel,
            "triple_weight",
            index,
            (*sheets, grad_triple, vectors1),
            [shape(dims, LOW)] * 2,
            [pltpu.VMEM((width, QUAD), WIDE)],
        )
    else:
        ordered = place(
            [((mz ^ (i // 2)) * 2 + (mx ^ (i % 2)), sheet) for i, sheet in enumerate(sheets)]
        ).reshape(count, width)
        part = narrow(dot_tn(ordered, grad_triple).reshape(outer, NZ * 2, 2, slab, QUAD))
        bias = sum_outer(jnp.sum(grad_triple, axis=0, dtype=WIDE))
        bias = extra_rows(line(bias), sum_outer(vectors1))
        bias = jnp.broadcast_to(bias, (NZ * 2, 2, 16, QUAD))
        part = jnp.concatenate([part, bias], axis=2).astype(LOW)
        keep, send = pick(part, mc, 1), pick(part, 1 - mc, 1)
    packed = whole(
        pair_sum_kernel, "pair_sum", index, (keep, flip(send, "c")), [shape(dims, LOW)]
    )[0]
    vector = shape((width // PAIR, PAIR), WIDE)
    triple_grad, triple_bias_grad, output_bias_grad, gain_one, shift_one = whole(
        triple_out_kernel,
        "triple_out",
        index,
        (lax.all_to_all(after(packed, block_triple), ("z", "x"), 0, 0),),
        [shape((3, slab, 2 * QUAD), WIDE), shape((3, 2 * QUAD), WIDE)] + [vector] * 3,
    )
    part = whole(
        tokens_kernel,
        "tokens",
        index,
        (after(block_triple, keep, output_parts[0], weight_in[2]), triple_low),
        [low_rows],
        [pltpu.VMEM((rows, 6 * QUAD), LOW)],
    )[0]
    keep, keep_out, send = whole(
        line_sum_kernel,
        "line_sum",
        index,
        (after(weight_in[0], part), *weight_in[1:], *output_in),
        [shape((2, slab, quarter), WIDE), shape((slab, QUAD), WIDE), shape((slab, 2 * quarter + QUAD), LOW)],
    )
    contract_grad, expand_grad, output_grad = whole(
        columns_kernel,
        "columns",
        index,
        (keep, keep_out, flip(send, "x")),
        [shape((slab, n), WIDE) for n in (span, span, 2 * QUAD)],
    )
    tokens_grad = whole(
        tokens_sum_kernel, "tokens_sum", index, (part, flip(part, "y"), grad_first_in), [wide_rows]
    )[0]

    queries_grad, head_grad, contract_bias_grad, gain_two, shift_two, expand_bias_grad = whole(
        spread_kernel,
        "spread",
        index,
        (lax.all_gather(mine, ("z", "x", "c")).reshape(NZ * 4, *message[1:]),),
        [shape((query_vecs.shape[0], proj), WIDE), shape((width, proj), WIDE)]
        + [vector] * 3
        + [shape((span // PAIR, PAIR), WIDE)],
    )

    return (
        second_low,
        loss[0, 0],
        tokens_grad,
        queries_grad,
        triple_grad.transpose(1, 0, 2),
        triple_bias_grad,
        output_grad.T,
        output_bias_grad.reshape(-1),
        gain_one.reshape(-1),
        shift_one.reshape(-1),
        expand_grad,
        expand_bias_grad.reshape(-1),
        contract_grad.T,
        contract_bias_grad.reshape(-1),
        gain_two.reshape(-1),
        shift_two.reshape(-1),
        head_grad,
    )


def solution(mesh):
    outer = mesh.shape["blk"] // 16
    five = Mesh(mesh.devices.reshape(outer, NZ, 2, 2, mesh.shape["tensor"]), BLK + ("y",))
    blk, tensor = BLK, "y"
    return jax.shard_map(
        shards,
        mesh=five,
        in_specs=(
            P(blk, None),
            P(),
            P(blk, None),
            P(),
            P(blk),
            P(),
            P(blk, None, tensor),
            P(None, tensor),
            P(tensor, blk),
            P(),
            P(),
            P(),
            P(blk, tensor),
            P(tensor),
            P(tensor, blk),
            P(),
            P(),
            P(),
            P(),
        ),
        out_specs=(
            P(blk, None),
            P(),
            P(blk, None),
            P(),
            P(blk, None, tensor),
            P(None, tensor),
            P(tensor, blk),
            P(),
            P(),
            P(),
            P(blk, tensor),
            P(tensor),
            P(tensor, blk),
            P(),
            P(),
            P(),
            P(),
        ),
        check_vma=False,
    )
```

profile of v0, /device:TPU:0, one launch (start us, length us, event | category | flops | bytes accessed | tf_op | source)
XLA Modules:
  0.0 359.4 jit_solution(6012949161848769066)
XLA Ops:
  7.2 3.1 collective-permute-start.1
  10.3 2.6 collective-permute-start.3
  13.6 2.6 prep.1
  16.1 5.6 %collective-permute-done.1.refs_2_ = bf16[128,1024]{1,0:T(8,128)(2,1)S(1)} collective-permute-done((bf16[128,1024]{1,0:T(8,128)(2,1)}, bf16[128,1024]{1,0:T(8,128)(2,1)S(1)}, u32[]{:S(2)}, u32[]{:S(2)}) %collective-permute-start.1) | collective-permute-done | bytes 262176 | tf_op jit(solution)/shard_map/ppermute | solution.py:33
  21.7 10.2 %collective-permute-done.3.refs_4_ = bf16[128,1024]{1,0:T(8,128)(2,1)S(1)} collective-permute-done((bf16[128,1024]{1,0:T(8,128)(2,1)}, bf16[128,1024]{1,0:T(8,128)(2,1)S(1)}, u32[]{:S(2)}, u32[]{:S(2)}) %collective-permute-start.3) | collective-permute-done | bytes 262176 | tf_op jit(solution)/shard_map/ppermute | solution.py:33
  31.9 1.6 collective-permute-start
  33.5 7.0 %all-to-all-start = ((bf16[8,80,256]{2,1,0:T(8,128)(2,1)}), bf16[8,80,256]{2,1,0:T(8,128)(2,1)S(1)}, u32[]{:S(2)}, u32[]{:S(2)}) async-start(bf16[8,80,256]{2,1,0:T(8,128)(2,1)} %get-tuple-element.101), calls=%async_computation | async-start | bytes 655360 | tf_op jit(solution)/shard_map/all_to_all | solution.py:758
  41.0 2.0 collective-permute-start.2
  43.1 12.2 %collective-permute-done.2.refs_3_ = bf16[128,1024]{1,0:T(8,128)(2,1)S(1)} collective-permute-done((bf16[128,1024]{1,0:T(8,128)(2,1)S(1)}, bf16[128,1024]{1,0:T(8,128)(2,1)S(1)}, u32[]{:S(2)}, u32[]{:S(2)}) %collective-permute-start.2) | collective-permute-done | bytes 262176 | tf_op jit(solution)/shard_map/ppermute | solution.py:41
  55.3 3.1 fusion
  58.4 2.1 collective-permute-start.4
  61.2 1.9 heads.1
  63.2 4.4 %collective-permute-done.4.refs_5_ = bf16[128,1024]{1,0:T(8,128)(2,1)S(1)} collective-permute-done((bf16[128,1024]{1,0:T(8,128)(2,1)S(1)}, bf16[128,1024]{1,0:T(8,128)(2,1)S(1)}, u32[]{:S(2)}, u32[]{:S(2)}) %collective-permute-start.4) | collective-permute-done | bytes 262176 | tf_op jit(solution)/shard_map/ppermute | solution.py:41
  67.6 5.4 %collective-permute-done.6.refs_7_ = bf16[128,1024]{1,0:T(8,128)(2,1)S(1)} collective-permute-done((bf16[128,1024]{1,0:T(8,128)(2,1)S(1)}, bf16[128,1024]{1,0:T(8,128)(2,1)S(1)}, u32[]{:S(2)}, u32[]{:S(2)}) %collective-permute-start.6) | collective-permute-done | bytes 262176 | tf_op jit(solution)/shard_map/ppermute | solution.py:41
  73.7 4.3 %project.1 = (bf16[1024,128]{1,0:T(8,128)(2,1)}, bf16[1024,128]{1,0:T(8,128)(2,1)}) custom-call(s32[5]{0:T(128)} %stack.20.idx, bf16[128,1024]{1,0:T(8,128)(2,1)} %refs_0_.3, bf16[128,1024]{1,0:T(8,128)(2,1)} %copy-done.28, bf16[128,1024]{1,0:T(8,128)(2,1)} %copy-done.25, bf16[128,1024]{1,0:T(8,128)(2,1)} %copy-done.29, bf16[128,1024]{1,0:T(8,128)(2,1)} %copy-done.26, ...), custom_call_target="tpu_custom_call" | custom-call | flops 4369999872 | bytes 14060000 | tf_op jit(solution)/shard_map/project/pallas_call | solution.py:115
  80.8 7.5 %attend.1 = (f32[4,2,2,64,128]{4,3,2,1,0:T(8,128)}, f32[4,2,2,64,1]{4,3,2,1,0:T(8,128)}, bf16[4,2,64,128]{3,2,1,0:T(8,128)(2,1)}) custom-call(bf16[4,2,2,64,128]{4,3,2,1,0:T(8,128)(2,1)} %bitcast.61, bf16[1024,128]{1,0:T(8,128)(2,1)} %get-tuple-element.107.kv0_ref, bf16[1024,128]{1,0:T(8,128)(2,1)} %copy-done.32, s32[4,2,2,64,1]{4,3,2,1,0:T(8,128)} %sub.34.qdoc_ref, ...), custom_call_target="tpu_custom_call" | custom-call | flops 8625000448 | bytes 27750000 | tf_op jit(solution)/shard_map/attend/pallas_call | solution.py:253
  88.3 16.8 %all_to_all.25.got = bf16[8,64,128]{2,1,0:T(8,128)(2,1)} all-to-all(bf16[8,64,128]{2,1,0:T(8,128)(2,1)} %bitcast.42), channel_id=1, replica_groups=mesh['o'=1,'z'=4,'x'=2,'c'=2,'y'=2] {'z','x'}, dimensions={0} | all-to-all | bytes 262144 | tf_op jit(solution)/shard_map/all_to_all | solution.py:817
  105.1 14.7 %all-gather.5.cloned.1.call-done.slabs = bf16[1024,4608]{1,0:T(8,128)(2,1)} async-done(((bf16[64,4608]{1,0:T(8,128)(2,1)}), bf16[1024,4608]{1,0:T(8,128)(2,1)}) %all-gather.5.cloned.1.call-update) | async-done | bytes 9437200 | tf_op jit(solution)/shard_map/all_gather | solution.py:800
  119.8 3.3 branch.1
  123.2 1.5 collective-permute-start.9
  124.7 7.2 %collective-permute-done.9.other = bf16[128,1024]{1,0:T(8,128)(2,1)S(1)} collective-permute-done((bf16[128,1024]{1,0:T(8,128)(2,1)}, bf16[128,1024]{1,0:T(8,128)(2,1)S(1)}, u32[]{:S(2)}, u32[]{:S(2)}) %collective-permute-start.9) | collective-permute-done | bytes 262176 | tf_op jit(solution)/shard_map/ppermute | solution.py:41
  132.6 7.2 %forward.1 = (f32[128,1024]{1,0:T(8,128)}, f32[128,1024]{1,0:T(8,128)}, f32[128,1]{1,0:T(8,128)}, f32[128,2048]{1,0:T(8,128)}, bf16[288,1024]{1,0:T(8,128)(2,1)}...) custom-call(s32[5]{0:T(128)} %stack.20.idx, bf16[128,1024]{1,0:T(8,128)(2,1)} %get-tuple-element.113.own, ...), custom_call_target="tpu_custom_call" | custom-call | flops 8855000064 | bytes 28490000 | tf_op jit(solution)/shard_map/forward/pallas_call | solution.py:115
  139.9 1.5 collective-permute-start.10
  141.4 2.8 query_units.1.query
  144.2 3.5 collective-permute-done.10.other
  148.5 4.4 %second.1 = (bf16[128,1024]{1,0:T(8,128)(2,1)}, f32[128,1024]{1,0:T(8,128)}, f32[128,1]{1,0:T(8,128)}, f32[128,128]{1,0:T(8,128)}, bf16[128,128]{1,0:T(8,128)(2,...) custom-call(s32[5]{0:T(128)} %stack.20.idx, bf16[128,1024]{1,0:T(8,128)(2,1)} %get-tuple-element.115.own, ...), custom_call_target="tpu_custom_call" | custom-call | flops 4140000000 | bytes 13320000 | tf_op jit(solution)/shard_map/second/pallas_call | solution.py:115
  152.9 2.1 collective-permute-start.12
  155.1 2.8 collective-permute-done.12
  161.2 2.7 collective-permute-start.15
  166.9 2.3 collective-permute-done.15.t2
  170.7 11.0 %middle.1 = (f32[128,1024]{1,0:T(8,128)}, bf16[256,1024]{1,0:T(8,128)(2,1)}, bf16[256,1024]{1,0:T(8,128)(2,1)}, bf16[128,1024]{1,0:T(8,128)(2,1)}, f32[8,128]{1,...) custom-call(s32[5]{0:T(128)} %stack.20.idx, f32[4,4096]{1,0:T(4,128)} %copy-done.4, ...), custom_call_target="tpu_custom_call" | custom-call | flops 13799999488 | bytes 44400000 | tf_op jit(solution)/shard_map/middle/pallas_call | solution.py:115
  182.5 1.5 collective-permute-start.23
  184.2 2.7 collective-permute-done.17.f1
  186.9 4.5 %collective-permute-done.23.other = bf16[128,1024]{1,0:T(8,128)(2,1)S(1)} collective-permute-done((bf16[128,1024]{1,0:T(8,128)(2,1)}, bf16[128,1024]{1,0:T(8,128)(2,1)S(1)}, u32[]{:S(2)}, u32[]{:S(2)}) %collective-permute-start.23) | collective-permute-done | bytes 262176 | tf_op jit(solution)/shard_map/ppermute | solution.py:41
  191.4 8.6 %collective-permute-done.20.g1 = bf16[256,1024]{1,0:T(8,128)(2,1)} collective-permute-done((bf16[256,1024]{1,0:T(8,128)(2,1)}, bf16[256,1024]{1,0:T(8,128)(2,1)}, u32[]{:S(2)}, u32[]{:S(2)}) %collective-permute-start.20) | collective-permute-done | bytes 524320 | tf_op jit(solution)/shard_map/ppermute | solution.py:41
  200.1 3.9 %first_back.1 = (f32[128,1024]{1,0:T(8,128)}, bf16[128,1024]{1,0:T(8,128)(2,1)}, f32[8,1024]{1,0:T(8,128)}, bf16[8,64,128]{2,1,0:T(8,128)(2,1)}) custom-call(s32[5]{0:T(128)} %stack.20.idx, bf16[128,1024]{1,0:T(8,128)(2,1)} %get-tuple-element.132.own, bf16[128,1024]{1,0:T(8,128)(2,1)} %copy-done.36, f32[128,1024]{1,0:T(8,128)} %get-tuple-element.133.grad_second_in, ...), custom_call_target="tpu_custom_call" | custom-call | flops 4369999872 | bytes 14060000 | tf_op jit(solution)/shard_map/first_back/pallas_call | solution.py:115
  204.0 4.2 %all-to-all-start.2 = ((bf16[8,64,128]{2,1,0:T(8,128)(2,1)}), bf16[8,64,128]{2,1,0:T(8,128)(2,1)S(1)}, u32[]{:S(2)}, u32[]{:S(2)}) async-start(bf16[8,64,128]{2,1,0:T(8,128)(2,1)} %get-tuple-element.136), calls=%async_computation.2 | async-start | bytes 262144 | tf_op jit(solution)/shard_map/all_to_all | solution.py:817
  209.1 2.5 query_c.1
  211.7 2.0 collective-permute-start.25
  214.7 6.1 %weights.1 = (f32[2,2,64,1024]{3,2,1,0:T(8,128)}, bf16[2,2,64,1024]{3,2,1,0:T(8,128)(2,1)}, bf16[2,2,64,1024]{3,2,1,0:T(8,128)(2,1)}, bf16[2,2,64,1024]{3,2,1,0:T(8,128)(2,1)}) custom-call(s32[5]{0:T(128)} %stack.20.idx, bf16[288,1024]{1,0:T(8,128)(2,1)} %get-tuple-element.126.f0, bf16[288,1024]{1,0:T(8,128)(2,1)} %copy-done.10, ...), custom_call_target="tpu_custom_call" | custom-call | flops 5980000256 | bytes 19240000 | tf_op jit(solution)/shard_map/weights/pallas_call | solution.py:115
  222.9 9.8 %attend_back.1 = (f32[4,2,2,64,128]{4,3,2,1,0:T(8,128)}, f32[1024,128]{1,0:T(8,128)}, f32[1024,128]{1,0:T(8,128)}) custom-call(bf16[4,2,2,64,128]{4,3,2,1,0:T(8,128)(2,1)} %bitcast.62, bf16[4,2,64,128]{3,2,1,0:T(8,128)(2,1)} %bitcast.41, f32[4,2,2,64,128]{4,3,2,1,0:T(8,128)} %get-tuple-element.137.o_ref, f32[4,2,2,64,1]{4,3,2,1,0:T(8,128)} %get-tuple-element.138.log_ref, ...), custom_call_target="tpu_custom_call" | custom-call | flops 11269999616 | bytes 36260000 | tf_op jit(solution)/shard_map/attend_back/pallas_call | solution.py:311
  233.5 2.0 query_sum.1
  236.0 2.3 collective-permute-start.27
  238.4 1.5 collective-permute-start.28
  242.4 3.7 %collective-permute-done.28.r3 = bf16[336,128]{1,0:T(8,128)(2,1)S(1)} collective-permute-done((bf16[336,128]{1,0:T(8,128)(2,1)}, bf16[336,128]{1,0:T(8,128)(2,1)S(1)}, u32[]{:S(2)}, u32[]{:S(2)}) %collective-permute-start.28) | collective-permute-done | bytes 86048 | tf_op jit(solution)/shard_map/ppermute | solution.py:33
  246.8 1.8 query_back.1
  249.6 3.0 triple.1.refs_8_
  252.5 4.7 %all-to-all-start.3 = ((bf16[8,128,256]{2,1,0:T(8,128)(2,1)}), bf16[8,128,256]{2,1,0:T(8,128)(2,1)S(1)}, u32[]{:S(2)}, u32[]{:S(2)}) async-start(bf16[8,128,256]{2,1,0:T(8,128)(2,1)} %bitcast.40), calls=%async_computation.3 | async-start | bytes 1048576 | tf_op jit(solution)/shard_map/all_to_all | solution.py:817
  257.3 3.9 %triple_weight.1 = (bf16[8,80,256]{2,1,0:T(8,128)(2,1)}, bf16[8,80,256]{2,1,0:T(8,128)(2,1)}) custom-call(s32[5]{0:T(128)} %stack.20.idx, bf16[128,1024]{1,0:T(8,128)(2,1)} %refs_0_.3, bf16[128,1024]{1,0:T(8,128)(2,1)} %copy-done.28, bf16[128,1024]{1,0:T(8,128)(2,1)} %copy-done.25, bf16[128,1024]{1,0:T(8,128)(2,1)} %copy-done.29, ...), custom_call_target="tpu_custom_call" | custom-call | flops 4369999872 | bytes 14060000 | tf_op jit(solution)/shard_map/triple_weight/pallas_call | solution.py:115
  261.1 2.1 collective-permute-start.31
  263.9 1.9 pair_sum.1
  265.9 8.7 %all-to-all-done.3.got = bf16[8,128,256]{2,1,0:T(8,128)(2,1)S(1)} async-done(((bf16[8,128,256]{2,1,0:T(8,128)(2,1)}), bf16[8,128,256]{2,1,0:T(8,128)(2,1)S(1)}, u32[]{:S(2)}, u32[]{:S(2)}) %all-to-all-start.3) | async-done | bytes 524320 | tf_op jit(solution)/shard_map/all_to_all | solution.py:817
  274.6 3.5 all-to-all-start.4
  278.1 2.9 collective-permute-start.34
  284.2 3.9 %output.1 = (f32[2,64,256]{2,1,0:T(8,128)}, bf16[2,64,256]{2,1,0:T(8,128)(2,1)}, bf16[2,64,256]{2,1,0:T(8,128)(2,1)}, bf16[2,64,256]{2,1,0:T(8,128)(2,1)}) custom-call(s32[5]{0:T(128)} %stack.20.idx, bf16[288,1024]{1,0:T(8,128)(2,1)} %get-tuple-element.126.f0, bf16[288,1024]{1,0:T(8,128)(2,1)} %copy-done.10, bf16[288,1024]{1,0:T(8,128)(2,1)} %copy-done.11, ...), custom_call_target="tpu_custom_call" | custom-call | flops 2644999936 | bytes 8510000 | tf_op jit(solution)/shard_map/output/pallas_call | solution.py:115
  288.1 1.5 collective-permute-start.38
  290.1 2.4 collective-permute-start.40
  294.0 36.1 %collective-permute-done.34.a2 = bf16[2,2,64,1024]{3,2,1,0:T(8,128)(2,1)S(1)} collective-permute-done((bf16[2,2,64,1024]{3,2,1,0:T(8,128)(2,1)S(1)}, bf16[2,2,64,1024]{3,2,1,0:T(8,128)(2,1)S(1)}, u32[]{:S(2)}, u32[]{:S(2)}) %collective-permute-start.34) | collective-permute-done | bytes 524320 | tf_op jit(solution)/shard_map/ppermute | solution.py:33
  330.8 1.9 triple_out.1
  332.7 3.9 %tokens.3.own = bf16[128,1024]{1,0:T(8,128)(2,1)} custom-call(s32[5]{0:T(128)} %stack.20.idx, bf16[8,128,256]{2,1,0:T(8,128)(2,1)} %copy-done, bf16[1024,1536]{1,0:T(8,128)(2,1)} %all-gather.7.cloned.1.call-done.weight), custom_call_target="tpu_custom_call" | custom-call | flops 4485000192 | bytes 14430000 | tf_op jit(solution)/shard_map/tokens/pallas_call | solution.py:115
  339.4 2.8 line_sum.1
  343.5 2.9 spread.1
  347.1 2.1 tokens_sum.1
  350.7 2.2 columns.1
  (185 shorter events, 38.2 us)
Async XLA Ops:
  7.2 112.6 %all-gather.5.cloned.1.call-start = ((), (), s32[]{:S(2)}) async-start(), calls=%async_computation.5 | async-start | bytes 10027008 | tf_op jit(solution)/shard_map/all_gather | solution.py:800
  7.2 14.5 %collective-permute-start.1 = (bf16[128,1024]{1,0:T(8,128)(2,1)}, bf16[128,1024]{1,0:T(8,128)(2,1)S(1)}, u32[]{:S(2)}, u32[]{:S(2)}) collective-permute-start(bf16[128,1024]{1,0:T(8,128)(2,1)} %refs_0_.3), channel_id=1, source_target_pairs={{0,8},{8,0},{16,24},{24,16},{1,9},{9,1},{17,25},{25,17},{2,10},{10... | collective-permute-start | bytes 786440 | tf_op jit(solution)/shard_map/ppermute | solution.py:33
  10.3 21.6 %collective-permute-start.3 = (bf16[128,1024]{1,0:T(8,128)(2,1)}, bf16[128,1024]{1,0:T(8,128)(2,1)S(1)}, u32[]{:S(2)}, u32[]{:S(2)}) collective-permute-start(bf16[128,1024]{1,0:T(8,128)(2,1)} %refs_0_.3), channel_id=1, source_target_pairs={{0,16},{8,24},{16,0},{24,8},{1,17},{9,25},{17,1},{25,9},{2,18},{10... | collective-permute-start | bytes 786440 | tf_op jit(solution)/shard_map/ppermute | solution.py:33
  12.9 19.0 %collective-permute-start.5 = (bf16[128,1024]{1,0:T(8,128)(2,1)}, bf16[128,1024]{1,0:T(8,128)(2,1)S(1)}, u32[]{:S(2)}, u32[]{:S(2)}) collective-permute-start(bf16[128,1024]{1,0:T(8,128)(2,1)} %refs_0_.3), channel_id=1, source_target_pairs={{0,24},{8,16},{16,8},{24,0},{1,25},{9,17},{17,9},{25,1},{2,26},{10... | collective-permute-start | bytes 786440 | tf_op jit(solution)/shard_map/ppermute | solution.py:33
  13.5 18.4 %copy-start.24 = (bf16[128,1024]{1,0:T(8,128)(2,1)S(1)}, bf16[128,1024]{1,0:T(8,128)(2,1)}, u32[]{:S(2)}) copy-start(bf16[128,1024]{1,0:T(8,128)(2,1)} %refs_0_.3) | copy-start | bytes 786436
  13.5 27.0 %copy-start.50 = (s32[4]{0:T(128)S(1)}, s32[4]{0:T(128)}, u32[]{:S(2)}) copy-start(s32[4]{0:T(128)} %param.22) | copy-start | bytes 52
  21.7 41.5 %copy-start.25 = (bf16[128,1024]{1,0:T(8,128)(2,1)}, bf16[128,1024]{1,0:T(8,128)(2,1)S(1)}, u32[]{:S(2)}) copy-start(bf16[128,1024]{1,0:T(8,128)(2,1)S(1)} %collective-permute-done.1.refs_2_) | copy-start | bytes 786436
  31.9 31.3 %copy-start.26 = (bf16[128,1024]{1,0:T(8,128)(2,1)}, bf16[128,1024]{1,0:T(8,128)(2,1)S(1)}, u32[]{:S(2)}) copy-start(bf16[128,1024]{1,0:T(8,128)(2,1)S(1)} %collective-permute-done.3.refs_4_) | copy-start | bytes 786436
  31.9 31.3 %copy-start.27 = (bf16[128,1024]{1,0:T(8,128)(2,1)}, bf16[128,1024]{1,0:T(8,128)(2,1)S(1)}, u32[]{:S(2)}) copy-start(bf16[128,1024]{1,0:T(8,128)(2,1)S(1)} %collective-permute-done.5.refs_6_) | copy-start | bytes 786436
  31.9 11.2 %collective-permute-start = (bf16[128,1024]{1,0:T(8,128)(2,1)S(1)}, bf16[128,1024]{1,0:T(8,128)(2,1)S(1)}, u32[]{:S(2)}, u32[]{:S(2)}) collective-permute-start(bf16[128,1024]{1,0:T(8,128)(2,1)S(1)} %copy-done.24), channel_id=1, source_target_pairs={{0,4},{4,0},{1,5},{5,1},{2,6},{6,2},{3,7},{7,3},{8,12},{12,8},{9,1... | collective-permute-start | bytes 786440 | tf_op jit(solution)/shard_map/ppermute | solution.py:41
  33.5 21.8 %all-to-all-start = ((bf16[8,80,256]{2,1,0:T(8,128)(2,1)}), bf16[8,80,256]{2,1,0:T(8,128)(2,1)S(1)}, u32[]{:S(2)}, u32[]{:S(2)}) async-start(bf16[8,80,256]{2,1,0:T(8,128)(2,1)} %get-tuple-element.101), calls=%async_computation | async-start | bytes 655360 | tf_op jit(solution)/shard_map/all_to_all | solution.py:758
  40.5 292.1 %all-gather.7.cloned.1.call-start = ((), (), s32[]{:S(2)}) async-start(), calls=%async_computation.6 | async-start | bytes 3342336 | tf_op jit(solution)/shard_map/all_gather | solution.py:801
  41.0 14.3 %collective-permute-start.2 = (bf16[128,1024]{1,0:T(8,128)(2,1)S(1)}, bf16[128,1024]{1,0:T(8,128)(2,1)S(1)}, u32[]{:S(2)}, u32[]{:S(2)}) collective-permute-start(bf16[128,1024]{1,0:T(8,128)(2,1)S(1)} %collective-permute-done.1.refs_2_), channel_id=1, source_target_pairs={{0,4},{4,0},{1,5},{5,1},{2,6},{6,2},{3,7},{7,3},{8,12},{12,8},{9,1... | collective-permute-start | bytes 786440 | tf_op jit(solution)/shard_map/ppermute | solution.py:41
  43.1 20.1 %copy-start.28 = (bf16[128,1024]{1,0:T(8,128)(2,1)}, bf16[128,1024]{1,0:T(8,128)(2,1)S(1)}, u32[]{:S(2)}) copy-start(bf16[128,1024]{1,0:T(8,128)(2,1)S(1)} %collective-permute-done.refs_1_) | copy-start | bytes 786436
  55.3 5.3 %collective-permute-start.7 = (bf16[8,80,256]{2,1,0:T(8,128)(2,1)S(1)}, bf16[8,80,256]{2,1,0:T(8,128)(2,1)S(1)}, u32[]{:S(2)}, u32[]{:S(2)}) collective-permute-start(bf16[8,80,256]{2,1,0:T(8,128)(2,1)S(1)} %all-to-all-done.own), channel_id=1, source_target_pairs={{0,2},{2,0},{1,3},{3,1},{4,6},{6,4},{5,7},{7,5},{8,10},{10,8},{9,1... | collective-permute-start | bytes 983048 | tf_op jit(solution)/shard_map/ppermute | solution.py:41
  58.4 9.2 %collective-permute-start.4 = (bf16[128,1024]{1,0:T(8,128)(2,1)S(1)}, bf16[128,1024]{1,0:T(8,128)(2,1)S(1)}, u32[]{:S(2)}, u32[]{:S(2)}) collective-permute-start(bf16[128,1024]{1,0:T(8,128)(2,1)S(1)} %collective-permute-done.3.refs_4_), channel_id=1, source_target_pairs={{0,4},{4,0},{1,5},{5,1},{2,6},{6,2},{3,7},{7,3},{8,12},{12,8},{9,1... | collective-permute-start | bytes 786440 | tf_op jit(solution)/shard_map/ppermute | solution.py:41
  60.5 12.6 %collective-permute-start.6 = (bf16[128,1024]{1,0:T(8,128)(2,1)S(1)}, bf16[128,1024]{1,0:T(8,128)(2,1)S(1)}, u32[]{:S(2)}, u32[]{:S(2)}) collective-permute-start(bf16[128,1024]{1,0:T(8,128)(2,1)S(1)} %collective-permute-done.5.refs_6_), channel_id=1, source_target_pairs={{0,4},{4,0},{1,5},{5,1},{2,6},{6,2},{3,7},{7,3},{8,12},{12,8},{9,1... | collective-permute-start | bytes 786440 | tf_op jit(solution)/shard_map/ppermute | solution.py:41
  78.0 2.1 collective-permute-start.8
  123.2 8.7 %collective-permute-start.9 = (bf16[128,1024]{1,0:T(8,128)(2,1)}, bf16[128,1024]{1,0:T(8,128)(2,1)S(1)}, u32[]{:S(2)}, u32[]{:S(2)}) collective-permute-start(bf16[128,1024]{1,0:T(8,128)(2,1)} %get-tuple-element.113.own), channel_id=1, source_target_pairs={{0,1},{1,0},{2,3},{3,2},{4,5},{5,4},{6,7},{7,6},{8,9},{9,8},{10,11... | collective-permute-start | bytes 786440 | tf_op jit(solution)/shard_map/ppermute | solution.py:41
  139.9 7.9 %collective-permute-start.10 = (bf16[128,1024]{1,0:T(8,128)(2,1)}, bf16[128,1024]{1,0:T(8,128)(2,1)S(1)}, u32[]{:S(2)}, u32[]{:S(2)}) collective-permute-start(bf16[128,1024]{1,0:T(8,128)(2,1)} %get-tuple-element.115.own), channel_id=1, source_target_pairs={{0,1},{1,0},{2,3},{3,2},{4,5},{5,4},{6,7},{7,6},{8,9},{9,8},{10,11... | collective-permute-start | bytes 786440 | tf_op jit(solution)/shard_map/ppermute | solution.py:41
  148.5 16.2 %copy-start.7 = (s32[128]{0:T(128)S(1)}, s32[128]{0:T(128)}, u32[]{:S(2)}) copy-start(s32[128]{0:T(128)} %param.24) | copy-start | bytes 1540
  148.5 17.0 %copy-start.13 = (bf16[288,1024]{1,0:T(8,128)(2,1)S(1)}, bf16[288,1024]{1,0:T(8,128)(2,1)}, u32[]{:S(2)}) copy-start(bf16[288,1024]{1,0:T(8,128)(2,1)} %get-tuple-element.127) | copy-start | bytes 1769476
  152.9 2.2 collective-permute-start.11
  152.9 5.0 %collective-permute-start.12 = (f32[4,4096]{1,0:T(4,128)}, f32[4,4096]{1,0:T(4,128)S(1)}, u32[]{:S(2)}, u32[]{:S(2)}) collective-permute-start(f32[4,4096]{1,0:T(4,128)} %get-tuple-element.118), channel_id=1, source_target_pairs={{0,4},{2,6},{4,0},{6,2},{1,5},{3,7},{5,1},{7,3},{8,12},{10,14},{12... | collective-permute-start | bytes 196616 | tf_op jit(solution)/shard_map/ppermute | solution.py:37
  155.0 4.3 %collective-permute-start.13 = (f32[4,4096]{1,0:T(4,128)}, f32[4,4096]{1,0:T(4,128)S(1)}, u32[]{:S(2)}, u32[]{:S(2)}) collective-permute-start(f32[4,4096]{1,0:T(4,128)} %get-tuple-element.118), channel_id=1, source_target_pairs={{0,6},{2,4},{4,2},{6,0},{1,7},{3,5},{5,3},{7,1},{8,14},{10,12},{12... | collective-permute-start | bytes 196616 | tf_op jit(solution)/shard_map/ppermute | solution.py:37
  160.2 9.9 %copy-start.4 = (f32[4,4096]{1,0:T(4,128)}, f32[4,4096]{1,0:T(4,128)S(1)}, u32[]{:S(2)}) copy-start(f32[4,4096]{1,0:T(4,128)S(1)} %add_add_fusion.t0) | copy-start | bytes 196612
  160.2 6.7 %collective-permute-start.14 = (f32[4,4096]{1,0:T(4,128)S(1)}, f32[4,4096]{1,0:T(4,128)S(1)}, u32[]{:S(2)}, u32[]{:S(2)}) collective-permute-start(f32[4,4096]{1,0:T(4,128)S(1)} %add_add_fusion.t0), channel_id=1, source_target_pairs={{0,8},{8,0},{16,24},{24,16},{1,9},{9,1},{17,25},{25,17},{2,10},{10... | collective-permute-start | bytes 196616 | tf_op jit(solution)/shard_map/ppermute | solution.py:33
  161.2 8.1 %collective-permute-start.15 = (f32[4,4096]{1,0:T(4,128)S(1)}, f32[4,4096]{1,0:T(4,128)S(1)}, u32[]{:S(2)}, u32[]{:S(2)}) collective-permute-start(f32[4,4096]{1,0:T(4,128)S(1)} %add_add_fusion.t0), channel_id=1, source_target_pairs={{0,16},{8,24},{16,0},{24,8},{1,17},{9,25},{17,1},{25,9},{2,18},{10... | collective-permute-start | bytes 196616 | tf_op jit(solution)/shard_map/ppermute | solution.py:33
  163.9 6.2 %collective-permute-start.16 = (f32[4,4096]{1,0:T(4,128)S(1)}, f32[4,4096]{1,0:T(4,128)S(1)}, u32[]{:S(2)}, u32[]{:S(2)}) collective-permute-start(f32[4,4096]{1,0:T(4,128)S(1)} %add_add_fusion.t0), channel_id=1, source_target_pairs={{0,24},{8,16},{16,8},{24,0},{1,25},{9,17},{17,9},{25,1},{2,26},{10... | collective-permute-start | bytes 196616 | tf_op jit(solution)/shard_map/ppermute | solution.py:33
  165.4 21.5 %collective-permute-start.17 = (bf16[288,1024]{1,0:T(8,128)(2,1)S(1)}, bf16[288,1024]{1,0:T(8,128)(2,1)S(1)}, u32[]{:S(2)}, u32[]{:S(2)}) collective-permute-start(bf16[288,1024]{1,0:T(8,128)(2,1)S(1)} %copy-done.13), channel_id=1, source_target_pairs={{0,4},{4,0},{1,5},{5,1},{2,6},{6,2},{3,7},{7,3},{8,12},{12,8},{9,1... | collective-permute-start | bytes 1769480 | tf_op jit(solution)/shard_map/ppermute | solution.py:41
  170.7 13.3 %copy-start.9 = (bf16[288,1024]{1,0:T(8,128)(2,1)S(1)}, bf16[288,1024]{1,0:T(8,128)(2,1)}, u32[]{:S(2)}) copy-start(bf16[288,1024]{1,0:T(8,128)(2,1)} %get-tuple-element.126.f0) | copy-start | bytes 1769476
  181.8 18.3 %collective-permute-start.20 = (bf16[256,1024]{1,0:T(8,128)(2,1)}, bf16[256,1024]{1,0:T(8,128)(2,1)}, u32[]{:S(2)}, u32[]{:S(2)}) collective-permute-start(bf16[256,1024]{1,0:T(8,128)(2,1)} %get-tuple-element.129), channel_id=1, source_target_pairs={{0,4},{4,0},{1,5},{5,1},{2,6},{6,2},{3,7},{7,3},{8,12},{12,8},{9,1... | collective-permute-start | bytes 1572872 | tf_op jit(solution)/shard_map/ppermute | solution.py:41
  182.5 25.8 %collective-permute-start.24 = (bf16[2,4,336,128]{3,2,1,0:T(8,128)(2,1)}, bf16[2,4,336,128]{3,2,1,0:T(8,128)(2,1)S(1)}, u32[]{:S(2)}, u32[]{:S(2)}) collective-permute-start(bf16[2,4,336,128]{3,2,1,0:T(8,128)(2,1)} %get-tuple-element.141), channel_id=1, source_target_pairs={{0,2},{2,0},{1,3},{3,1},{4,6},{6,4},{5,7},{7,5},{8,10},{10,8},{9,1... | collective-permute-start | bytes 2064392 | tf_op jit(solution)/shard_map/ppermute | solution.py:41
  182.5 8.9 %collective-permute-start.23 = (bf16[128,1024]{1,0:T(8,128)(2,1)}, bf16[128,1024]{1,0:T(8,128)(2,1)S(1)}, u32[]{:S(2)}, u32[]{:S(2)}) collective-permute-start(bf16[128,1024]{1,0:T(8,128)(2,1)} %get-tuple-element.132.own), channel_id=1, source_target_pairs={{0,1},{1,0},{2,3},{3,2},{4,5},{5,4},{6,7},{7,6},{8,9},{9,8},{10,11... | collective-permute-start | bytes 786440 | tf_op jit(solution)/shard_map/ppermute | solution.py:41
  184.0 29.7 %collective-permute-start.18 = (bf16[288,1024]{1,0:T(8,128)(2,1)S(1)}, bf16[288,1024]{1,0:T(8,128)(2,1)S(1)}, u32[]{:S(2)}, u32[]{:S(2)}) collective-permute-start(bf16[288,1024]{1,0:T(8,128)(2,1)S(1)} %copy-done.9), channel_id=1, source_target_pairs={{0,2},{2,0},{1,3},{3,1},{4,6},{6,4},{5,7},{7,5},{8,10},{10,8},{9,1... | collective-permute-start | bytes 1769480 | tf_op jit(solution)/shard_map/ppermute | solution.py:41
  186.9 17.1 %copy-start.10 = (bf16[288,1024]{1,0:T(8,128)(2,1)}, bf16[288,1024]{1,0:T(8,128)(2,1)S(1)}, u32[]{:S(2)}) copy-start(bf16[288,1024]{1,0:T(8,128)(2,1)S(1)} %collective-permute-done.17.f1) | copy-start | bytes 1769476
  186.9 26.7 %collective-permute-start.21 = (bf16[256,1024]{1,0:T(8,128)(2,1)}, bf16[256,1024]{1,0:T(8,128)(2,1)}, u32[]{:S(2)}, u32[]{:S(2)}) collective-permute-start(bf16[256,1024]{1,0:T(8,128)(2,1)} %get-tuple-element.128.g0), channel_id=1, source_target_pairs={{0,2},{2,0},{1,3},{3,1},{4,6},{6,4},{5,7},{7,5},{8,10},{10,8},{9,1... | collective-permute-start | bytes 1572872 | tf_op jit(solution)/shard_map/ppermute | solution.py:41
  191.4 8.6 %copy-start.36 = (bf16[128,1024]{1,0:T(8,128)(2,1)}, bf16[128,1024]{1,0:T(8,128)(2,1)S(1)}, u32[]{:S(2)}) copy-start(bf16[128,1024]{1,0:T(8,128)(2,1)S(1)} %collective-permute-done.23.other) | copy-start | bytes 786436
  191.4 22.2 %collective-permute-start.19 = (bf16[288,1024]{1,0:T(8,128)(2,1)S(1)}, bf16[288,1024]{1,0:T(8,128)(2,1)S(1)}, u32[]{:S(2)}, u32[]{:S(2)}) collective-permute-start(bf16[288,1024]{1,0:T(8,128)(2,1)S(1)} %collective-permute-done.17.f1), channel_id=1, source_target_pairs={{0,2},{2,0},{1,3},{3,1},{4,6},{6,4},{5,7},{7,5},{8,10},{10,8},{9,1... | collective-permute-start | bytes 1769480 | tf_op jit(solution)/shard_map/ppermute | solution.py:41
  200.1 13.6 %collective-permute-start.22 = (bf16[256,1024]{1,0:T(8,128)(2,1)}, bf16[256,1024]{1,0:T(8,128)(2,1)}, u32[]{:S(2)}, u32[]{:S(2)}) collective-permute-start(bf16[256,1024]{1,0:T(8,128)(2,1)} %collective-permute-done.20.g1), channel_id=1, source_target_pairs={{0,2},{2,0},{1,3},{3,1},{4,6},{6,4},{5,7},{7,5},{8,10},{10,8},{9,1... | collective-permute-start | bytes 1572872 | tf_op jit(solution)/shard_map/ppermute | solution.py:41
  204.0 18.2 %all-to-all-start.2 = ((bf16[8,64,128]{2,1,0:T(8,128)(2,1)}), bf16[8,64,128]{2,1,0:T(8,128)(2,1)S(1)}, u32[]{:S(2)}, u32[]{:S(2)}) async-start(bf16[8,64,128]{2,1,0:T(8,128)(2,1)} %get-tuple-element.136), calls=%async_computation.2 | async-start | bytes 262144 | tf_op jit(solution)/shard_map/all_to_all | solution.py:817
  208.2 135.3 %all-gather.9.cloned.1.call-start = ((), (), s32[]{:S(2)}) async-start(), calls=%async_computation.7 | async-start | bytes 1462272 | tf_op jit(solution)/shard_map/all_gather | solution.py:1042
  211.7 21.1 %collective-permute-start.25 = (bf16[4,336,128]{2,1,0:T(8,128)(2,1)}, bf16[4,336,128]{2,1,0:T(8,128)(2,1)S(1)}, u32[]{:S(2)}, u32[]{:S(2)}) collective-permute-start(bf16[4,336,128]{2,1,0:T(8,128)(2,1)} %get-tuple-element.143), channel_id=1, source_target_pairs={{0,4},{4,0},{1,5},{5,1},{2,6},{6,2},{3,7},{7,3},{8,12},{12,8},{9,1... | collective-permute-start | bytes 1032200 | tf_op jit(solution)/shard_map/ppermute | solution.py:41
  220.7 27.9 %collective-permute-start.29 = (bf16[2,2,64,1024]{3,2,1,0:T(8,128)(2,1)}, bf16[2,2,64,1024]{3,2,1,0:T(8,128)(2,1)S(1)}, u32[]{:S(2)}, u32[]{:S(2)}) collective-permute-start(bf16[2,2,64,1024]{3,2,1,0:T(8,128)(2,1)} %get-tuple-element.148), channel_id=1, source_target_pairs={{0,8},{8,0},{16,24},{24,16},{1,9},{9,1},{17,25},{25,17},{2,10},{10... | collective-permute-start | bytes 1572872 | tf_op jit(solution)/shard_map/ppermute | solution.py:33
  232.7 16.0 %collective-permute-start.30 = (f32[1024,128]{1,0:T(8,128)}, f32[1024,128]{1,0:T(8,128)S(1)}, u32[]{:S(2)}, u32[]{:S(2)}) collective-permute-start(f32[1024,128]{1,0:T(8,128)} %get-tuple-element.151), channel_id=1, source_target_pairs={{0,2},{2,0},{1,3},{3,1},{4,6},{6,4},{5,7},{7,5},{8,10},{10,8},{9,1... | collective-permute-start | bytes 1572872 | tf_op jit(solution)/shard_map/ppermute | solution.py:41
  235.5 7.0 %collective-permute-start.26 = (bf16[336,128]{1,0:T(8,128)(2,1)}, bf16[336,128]{1,0:T(8,128)(2,1)S(1)}, u32[]{:S(2)}, u32[]{:S(2)}) collective-permute-start(bf16[336,128]{1,0:T(8,128)(2,1)} %get-tuple-element.145), channel_id=1, source_target_pairs={{0,8},{8,0},{16,24},{24,16},{1,9},{9,1},{17,25},{25,17},{2,10},{10... | collective-permute-start | bytes 258056 | tf_op jit(solution)/shard_map/ppermute | solution.py:33
  236.0 6.4 %collective-permute-start.27 = (bf16[336,128]{1,0:T(8,128)(2,1)}, bf16[336,128]{1,0:T(8,128)(2,1)S(1)}, u32[]{:S(2)}, u32[]{:S(2)}) collective-permute-start(bf16[336,128]{1,0:T(8,128)(2,1)} %get-tuple-element.146), channel_id=1, source_target_pairs={{0,16},{8,24},{16,0},{24,8},{1,17},{9,25},{17,1},{25,9},{2,18},{10... | collective-permute-start | bytes 258056 | tf_op jit(solution)/shard_map/ppermute | solution.py:33
  238.4 7.8 %collective-permute-start.28 = (bf16[336,128]{1,0:T(8,128)(2,1)}, bf16[336,128]{1,0:T(8,128)(2,1)S(1)}, u32[]{:S(2)}, u32[]{:S(2)}) collective-permute-start(bf16[336,128]{1,0:T(8,128)(2,1)} %get-tuple-element.147), channel_id=1, source_target_pairs={{0,24},{8,16},{16,8},{24,0},{1,25},{9,17},{17,9},{25,1},{2,26},{10... | collective-permute-start | bytes 258056 | tf_op jit(solution)/shard_map/ppermute | solution.py:33
  252.5 22.1 %all-to-all-start.3 = ((bf16[8,128,256]{2,1,0:T(8,128)(2,1)}), bf16[8,128,256]{2,1,0:T(8,128)(2,1)S(1)}, u32[]{:S(2)}, u32[]{:S(2)}) async-start(bf16[8,128,256]{2,1,0:T(8,128)(2,1)} %bitcast.40), calls=%async_computation.3 | async-start | bytes 1048576 | tf_op jit(solution)/shard_map/all_to_all | solution.py:817
  261.1 2.1 collective-permute-start.36
  261.1 19.9 %collective-permute-start.31 = (bf16[128,1024]{1,0:T(8,128)(2,1)S(1)}, bf16[128,1024]{1,0:T(8,128)(2,1)S(1)}, u32[]{:S(2)}, u32[]{:S(2)}) collective-permute-start(bf16[128,1024]{1,0:T(8,128)(2,1)S(1)} %copy-done.33), channel_id=1, source_target_pairs={{0,4},{4,0},{1,5},{5,1},{2,6},{6,2},{3,7},{7,3},{8,12},{12,8},{9,1... | collective-permute-start | bytes 786440 | tf_op jit(solution)/shard_map/ppermute | solution.py:41
  263.9 14.2 %copy-start.16 = (bf16[2,2,64,1024]{3,2,1,0:T(8,128)(2,1)S(1)}, bf16[2,2,64,1024]{3,2,1,0:T(8,128)(2,1)}, u32[]{:S(2)}) copy-start(bf16[2,2,64,1024]{3,2,1,0:T(8,128)(2,1)} %get-tuple-element.156) | copy-start | bytes 1572868
  274.6 13.5 %copy-start = (bf16[8,128,256]{2,1,0:T(8,128)(2,1)}, bf16[8,128,256]{2,1,0:T(8,128)(2,1)S(1)}, u32[]{:S(2)}) copy-start(bf16[8,128,256]{2,1,0:T(8,128)(2,1)S(1)} %all-to-all-done.3.got) | copy-start | bytes 1572868
  274.6 55.4 %all-to-all-start.4 = ((bf16[8,80,256]{2,1,0:T(8,128)(2,1)}), bf16[8,80,256]{2,1,0:T(8,128)(2,1)S(1)}, u32[]{:S(2)}, u32[]{:S(2)}) async-start(bf16[8,80,256]{2,1,0:T(8,128)(2,1)} %pair_sum.1), calls=%async_computation.4 | async-start | bytes 655360 | tf_op jit(solution)/shard_map/all_to_all | solution.py:1009
  278.1 51.9 %collective-permute-start.34 = (bf16[2,2,64,1024]{3,2,1,0:T(8,128)(2,1)S(1)}, bf16[2,2,64,1024]{3,2,1,0:T(8,128)(2,1)S(1)}, u32[]{:S(2)}, u32[]{:S(2)}) collective-permute-start(bf16[2,2,64,1024]{3,2,1,0:T(8,128)(2,1)S(1)} %copy-done.16), channel_id=1, source_target_pairs={{0,16},{8,24},{16,0},{24,8},{1,17},{9,25},{17,1},{25,9},{2,18},{10... | collective-permute-start | bytes 1572872 | tf_op jit(solution)/shard_map/ppermute | solution.py:33
  281.0 1.7 collective-permute-start.32
  281.0 1.9 collective-permute-start.33
  282.7 9.8 %copy-start.14 = (bf16[2,2,64,1024]{3,2,1,0:T(8,128)(2,1)S(1)}, bf16[2,2,64,1024]{3,2,1,0:T(8,128)(2,1)}, u32[]{:S(2)}) copy-start(bf16[2,2,64,1024]{3,2,1,0:T(8,128)(2,1)} %get-tuple-element.167) | copy-start | bytes 1572868
  288.1 49.9 %collective-permute-start.38 = (bf16[2,64,256]{2,1,0:T(8,128)(2,1)}, bf16[2,64,256]{2,1,0:T(8,128)(2,1)S(1)}, u32[]{:S(2)}, u32[]{:S(2)}) collective-permute-start(bf16[2,64,256]{2,1,0:T(8,128)(2,1)} %get-tuple-element.168), channel_id=1, source_target_pairs={{0,8},{8,0},{16,24},{24,16},{1,9},{9,1},{17,25},{25,17},{2,10},{10... | collective-permute-start | bytes 196616 | tf_op jit(solution)/shard_map/ppermute | solution.py:33
  289.6 48.4 %collective-permute-start.39 = (bf16[2,64,256]{2,1,0:T(8,128)(2,1)}, bf16[2,64,256]{2,1,0:T(8,128)(2,1)S(1)}, u32[]{:S(2)}, u32[]{:S(2)}) collective-permute-start(bf16[2,64,256]{2,1,0:T(8,128)(2,1)} %get-tuple-element.169), channel_id=1, source_target_pairs={{0,16},{8,24},{16,0},{24,8},{1,17},{9,25},{17,1},{25,9},{2,18},{10... | collective-permute-start | bytes 196616 | tf_op jit(solution)/shard_map/ppermute | solution.py:33
  290.1 47.8 %collective-permute-start.40 = (bf16[2,64,256]{2,1,0:T(8,128)(2,1)}, bf16[2,64,256]{2,1,0:T(8,128)(2,1)S(1)}, u32[]{:S(2)}, u32[]{:S(2)}) collective-permute-start(bf16[2,64,256]{2,1,0:T(8,128)(2,1)} %get-tuple-element.170), channel_id=1, source_target_pairs={{0,24},{8,16},{16,8},{24,0},{1,25},{9,17},{17,9},{25,1},{2,26},{10... | collective-permute-start | bytes 196616 | tf_op jit(solution)/shard_map/ppermute | solution.py:33
  292.5 45.5 %collective-permute-start.37 = (bf16[2,2,64,1024]{3,2,1,0:T(8,128)(2,1)S(1)}, bf16[2,2,64,1024]{3,2,1,0:T(8,128)(2,1)S(1)}, u32[]{:S(2)}, u32[]{:S(2)}) collective-permute-start(bf16[2,2,64,1024]{3,2,1,0:T(8,128)(2,1)S(1)} %copy-done.14), channel_id=1, source_target_pairs={{0,24},{8,16},{16,8},{24,0},{1,25},{9,17},{17,9},{25,1},{2,26},{10... | collective-permute-start | bytes 1572872 | tf_op jit(solution)/shard_map/ppermute | solution.py:33
  336.6 9.8 %collective-permute-start.35 = (bf16[128,1024]{1,0:T(8,128)(2,1)}, bf16[128,1024]{1,0:T(8,128)(2,1)S(1)}, u32[]{:S(2)}, u32[]{:S(2)}) collective-permute-start(bf16[128,1024]{1,0:T(8,128)(2,1)} %tokens.3.own), channel_id=1, source_target_pairs={{0,1},{1,0},{2,3},{3,2},{4,5},{5,4},{6,7},{7,6},{8,9},{9,8},{10,11... | collective-permute-start | bytes 786440 | tf_op jit(solution)/shard_map/ppermute | solution.py:41
  342.1 7.8 %collective-permute-start.41 = (bf16[64,2304]{1,0:T(8,128)(2,1)}, bf16[64,2304]{1,0:T(8,128)(2,1)S(1)}, u32[]{:S(2)}, u32[]{:S(2)}) collective-permute-start(bf16[64,2304]{1,0:T(8,128)(2,1)} %get-tuple-element.173), channel_id=1, source_target_pairs={{0,4},{4,0},{1,5},{5,1},{2,6},{6,2},{3,7},{7,3},{8,12},{12,8},{9,1... | collective-permute-start | bytes 884744 | tf_op jit(solution)/shard_map/ppermute | solution.py:41
  (36 other events, 74.6 us)
Sparse Core Ops, SparseCore 0:
  32.1 87.7 all-gather.4
  144.4 54.3 all-gather.6
  248.8 57.5 all-gather.8
where the time goes:
time: 364 us; the launch traced here: 359 us
  waiting for transfers between devices  137 us (38%)
  Pallas kernels  99.6 us (27%)
  starting transfers between devices  66.7 us (18%)
  local copies, waits for them, and re-layouts  19.7 us (5%)
  blocking collectives  16.8 us (5%)
  between operations  14.2 us (4%)
  other arithmetic  5.07 us (1%)
    pallas_call x23, Pallas kernels, whole(): pl.pallas_call(kernel, in_specs=[pl.BlockSpec(memory_space=pltpu.SMEM)] +...  82.3 us
    ppermute x15, waiting for transfers between devices, xor_z(): return lax.ppermute(value, 'z', [(i, i ^ mask) for i in FOUR])  60.1 us
    ppermute x24, waiting for transfers between devices, flip(): return lax.ppermute(value, axis, [(0, 1), (1, 0)])  49.5 us
    ppermute x15, starting transfers between devices, xor_z(): return lax.ppermute(value, 'z', [(i, i ^ mask) for i in FOUR])  24.8 us
    ppermute x24, starting transfers between devices, flip(): return lax.ppermute(value, axis, [(0, 1), (1, 0)])  20.1 us
    all_to_all x1, blocking collectives, to_blocks(): lax.all_to_all(value.reshape((NZ * 2,) + value.shape[-2:]), ('z', 'x'), 0...  16.8 us
    all_gather x1, waiting for transfers between devices, shards(): lax.all_gather(after(low_slab, *by_z[1:]), BLK, axis=0, tiled=True)  14.7 us
    unnamed x102, local copies, waits for them, and re-layouts  14.5 us
  transfers between devices with their start and end apart: 49, of which 22 were waited for; matrix products, arithmetic and copies ran while one was open for 3% of the time, Pallas kernels for 24%

commit v1 on v0

--- a/solution.py
+++ b/solution.py
@@ -131,12 +131,38 @@
     return pltpu.make_async_copy(there, weight, sems.at[0])
 
 
+def piece_copies(idx, pieces, weight, sems):
+    if len(pieces) == 1:
+        return [pltpu.make_async_copy(pieces[0], weight, sems.at[0])]
+    count, rows, cols = pieces[0].shape
+    slab = (rows - 16) // 3
+    copies = []
+    for c, piece in enumerate(pieces):
+        for spot in range(count):
+            row = (spot * 2 + (idx[3] ^ c)) * slab
+            for i in range(2):
+                here = piece.at[spot, pl.ds((i + 1) * slab + 16, slab), :]
+                there = weight.at[pl.ds(pl.multiple_of(row, slab), slab), pl.ds(i * cols, cols)]
+                copies.append(pltpu.make_async_copy(here, there, sems.at[len(copies)]))
+    return copies
+
+
+def piece_scratch(rows, cols):
+    return [pltpu.VMEM((rows, cols), LOW), pltpu.SemaphoreType.DMA((NZ * 8,))]
+
+
 def slab_scratch(rows, cols):
     return [pltpu.VMEM((rows, cols), LOW), pltpu.SemaphoreType.DMA((1,))]
 
 
-def finish(copy, weight):
-    copy.wait()
+def start(copies):
+    for copy in copies:
+        copy.start()
+
+
+def finish(copies, weight):
+    for copy in copies:
+        copy.wait()
     return weight[...]
 
 
@@ -148,17 +174,18 @@
         for part, lane in enumerate(LANES):
             heads[spot, :slab, lane : lane + HEAD_DIM] = tw[part, :, at : at + HEAD_DIM].astype(LOW)
         heads[spot, :slab, PAIR : PAIR + HEAD_DIM] = jnp.zeros((slab, HEAD_DIM), LOW)
-        heads[spot, slab:, : live.shape[1]] = alive
-        heads[spot, slab:, PAIR:] = jnp.zeros((16, PAIR), LOW)
+        heads[spot, slab : slab + 16, : live.shape[1]] = alive
+        heads[spot, slab : slab + 16, PAIR:] = jnp.zeros((16, PAIR), LOW)
+        heads[spot, slab + 16 : 2 * slab + 16, :] = ow[:, :QUAD].astype(LOW)
+        heads[spot, 2 * slab + 16 :, :] = ow[:, QUAD:].astype(LOW)
     low[:, :span] = ew[...].astype(LOW)
-    low[:, span : 2 * span] = cw[...].astype(LOW)
-    low[:, 2 * span :] = ow[...].astype(LOW)
+    low[:, span:] = cw[...].astype(LOW)
     for part in range(3):
         tri[:, part * 2 * QUAD : (part + 1) * 2 * QUAD] = tw[part].astype(LOW)
 
 
 def heads_kernel(idx, own, other, weight, live0, live1):
-    slab, mc = own.shape[1] - 16, idx[3]
+    slab, mc = (own.shape[1] - 16) // 3, idx[3]
     for spot in range(NZ * 2):
         for source, c, live in ((own, mc, live0), (other, 1 - mc, live1)):
             rows = pl.ds(pl.multiple_of((spot * 2 + c) * slab, slab), slab)
@@ -180,32 +207,45 @@
     return value * cosine + swap_halves(value) * sine
 
 
+def sheet_rows(idx, sheets):
+    rows = sheets[0].shape[0]
+    half = rows // 2
+    parts = []
+    for x in range(2):
+        spot = idx[1] * 2 + (idx[2] ^ x)
+        parts.append((sheets[x][...], pl.ds(pl.multiple_of(spot * rows, rows), rows)))
+    for at, sheet in enumerate(sheets[2:]):
+        z, y = at // 2 + 1, at % 2
+        for x in range(2):
+            spot = (idx[1] ^ z) * 2 + (idx[2] ^ x)
+            row = spot * rows + (idx[4] ^ y) * half
+            parts.append((sheet[x], pl.ds(pl.multiple_of(row, half), half)))
+    return parts
+
+
 def project_kernel(idx, *refs):
     sheets, (weight, cosine, sine, bias, query, kv) = refs[:8], refs[8:]
-    rows = sheets[0].shape[0]
+    parts = sheet_rows(idx, sheets)
     mz, mx = idx[1], idx[2]
     mine = mz * 2 + mx
-    parts = []
+    biases = []
     for part in range(3):
         total = jnp.zeros((1, HEAD_DIM), WIDE)
         for h in range(NZ * 2):
             here = bias[part : part + 1, h * HEAD_DIM : (h + 1) * HEAD_DIM]
             total = jnp.where(mine == h, here, total)
-        parts.append(total)
+        biases.append(total)
     empty = jnp.zeros((1, HEAD_DIM), WIDE)
-    offset = jnp.concatenate([parts[0], parts[1], empty, parts[2]], axis=1)
+    offset = jnp.concatenate([biases[0], biases[1], empty, biases[2]], axis=1)
     weights = weight[...]
-    low_lanes = lax.broadcasted_iota(jnp.int32, (rows, PAIR), 1) < HEAD_DIM
-    for z in range(NZ):
-        for x in range(2):
-            spot = (mz ^ z) * 2 + (mx ^ x)
-            at = pl.ds(pl.multiple_of(spot * rows, rows), rows)
-            triple = dot_nn(sheets[z * 2 + x][...], weights) + offset
-            turned = turn(triple[:, :PAIR], cosine[at, :], sine[at, :])
-            query[at, :] = jnp.where(low_lanes, turned, 0.0).astype(LOW)
-            kv[at, :] = jnp.where(
-                low_lanes, pltpu.roll(turned, HEAD_DIM, 1), triple[:, PAIR:]
-            ).astype(LOW)
+    for value, at in parts:
+        low_lanes = lax.broadcasted_iota(jnp.int32, (value.shape[0], PAIR), 1) < HEAD_DIM
+        triple = dot_nn(value, weights) + offset
+        turned = turn(triple[:, :PAIR], cosine[at, :], sine[at, :])
+        query[at, :] = jnp.where(low_lanes, turned, 0.0).astype(LOW)
+        kv[at, :] = jnp.where(
+            low_lanes, pltpu.roll(turned, HEAD_DIM, 1), triple[:, PAIR:]
+        ).astype(LOW)
 
 
 def key_row(ref):
@@ -324,9 +364,10 @@
     )(queries.reshape(NZ, 2, 2, half, PAIR), grads, out, log_total, kv0, kv1, qdoc, kdoc0, kdoc1)
 
 
-def branch_kernel(idx, got, slabs, low, part, held, sems):
-    copy = slab_copy(slabs, slabs.shape[1] - held.shape[1], held, sems)
-    copy.start()
+def branch_kernel(pieces, idx, got, *refs):
+    slabs, (low, part, held, sems) = refs[:pieces], refs[pieces:]
+    copy = piece_copies(idx, slabs, held, sems)
+    start(copy)
     half = got.shape[1]
     for h in range(NZ * 2):
         lanes = slice(h * HEAD_DIM, (h + 1) * HEAD_DIM)
@@ -351,10 +392,9 @@
     first, unitary, inverse, hidden_in, keep, send, part,
     low, hidden, expand, sems1, contract, sems2,
 ):
-    copy1 = slab_copy(slabs, 0, expand, sems1)
-    copy2 = slab_copy(slabs, expand.shape[1], contract, sems2)
-    copy1.start()
-    copy2.start()
+    copy1 = [slab_copy(slabs, 0, expand, sems1)]
+    copy2 = [slab_copy(slabs, expand.shape[1], contract, sems2)]
+    start(copy1 + copy2)
     value = tokens[...].astype(WIDE) + (pair(own, other) + bias[...])
     unitary[...], inverse[...] = normalize(value)
     first[...] = unitary[...] * gain[...] + shift[...]
@@ -395,7 +435,9 @@
     totals[...] = dot_nn(member(idx, kdoc, totals.shape[0]), expo[...], PRECISE)
 
 
-def query_kernel(idx, vecs, out):
+def query_kernel(idx, vecs, out, own):
+    block, shares = (idx[1] * 2 + idx[2]) * 2 + idx[3], own.shape[0]
+    own[...] = vecs[pl.ds(pl.multiple_of(block * shares, shares), shares), :]
     value = vecs[...].astype(WIDE)
     out[...] = (value * unit_scale(value)).astype(LOW)
 
@@ -434,14 +476,11 @@
     return loss, (shifted / shifted_sum - chosen) / (totals * count)
 
 
-def core_sum_kernel(idx, keep, got, own, send):
-    own[...] = keep[0] + got[0].astype(WIDE)
-    send[...] = (keep[1] + got[1].astype(WIDE)).astype(LOW)
-
-
-def query_sum_kernel(idx, own, other, *outs):
-    for z, out in enumerate(outs):
-        out[...] = (own[z] + other[z].astype(WIDE)).astype(out.dtype)
+def core_sum_kernel(idx, pack, keep, got, out):
+    half = pack.shape[1]
+    for spot in range(pack.shape[0]):
+        out[spot, :half, :] = pack[spot]
+        out[spot, half:, :] = (keep[spot] + got[spot].astype(WIDE)).astype(LOW)
 
 
 def unit_back(value, grad):
@@ -450,9 +489,11 @@
     return scale * grad - value * (along * scale * scale * scale)
 
 
-def query_back_kernel(idx, own, r1, r2, r3, value, out):
-    total = own[...] + r1[...].astype(WIDE) + (r2[...].astype(WIDE) + r3[...].astype(WIDE))
-    shares = value.shape[0]
+def query_back_kernel(half, idx, got, value, out):
+    total = [got[spot, half:, :].astype(WIDE) for spot in range(NZ * 2)]
+    while len(total) > 1:
+        total = [a + b for a, b in zip(total[::2], total[1::2])]
+    total, shares = total[0], value.shape[0]
     out[:shares, :] = unit_back(value[...].astype(WIDE), total[:shares]).astype(LOW)
     out[shares:, :] = total[shares:].astype(LOW)
 
@@ -460,12 +501,12 @@
 def spread_kernel(idx, got, queries, head, *vectors):
     rows = got.shape[1]
     chunk = head.shape[0] // (NZ * 4)
-    shares = rows - chunk - 16
+    shares = rows - 2 * chunk
     pieces = []
     for i in range(NZ * 4):
         queries[i * shares : (i + 1) * shares, :] = got[i, :shares, :].astype(WIDE)
         head[i * chunk : (i + 1) * chunk, :] = got[i, shares : shares + chunk, :].astype(WIDE)
-        pieces.append(got[i, shares + chunk :, :].astype(WIDE))
+        pieces.append(got[i, shares + chunk : shares + chunk + 16, :].astype(WIDE))
     row = 0
     for out in vectors:
         for i in range(0, out.shape[0], 8):
@@ -489,10 +530,9 @@
     grad_in, keep, send, part, loss, q0, q1,
     similar, grad_low, grad_hidden_in, head_part, rows_part, expand, sems1, contract, sems2,
 ):
-    copy1 = slab_copy(slabs, 0, expand, sems1)
-    copy2 = slab_copy(slabs, expand.shape[1], contract, sems2)
-    copy2.start()
-    copy1.start()
+    copy1 = [slab_copy(slabs, 0, expand, sems1)]
+    copy2 = [slab_copy(slabs, expand.shape[1], contract, sems2)]
+    start(copy2 + copy1)
     totals = (t0[...] + t1[...]) + (t2[...] + t3[...])
     value, coefficient = loss_of(count, totals, (kdoc0, kdoc1), positive[...])
     loss[...] = jnp.broadcast_to(value, loss.shape)
@@ -526,23 +566,22 @@
             rows_part[at : at + 1, :] = value[:, i * PAIR : (i + 1) * PAIR]
             at += 1
     chunk = width // (NZ * 4)
-    shares = q0.shape[2] - chunk - 16
-    for mask in range(4):
-        there = (idx[2] * 2 + idx[3]) ^ mask
-        for z in range(NZ):
-            out = (q0, q1)[mask % 2].at[mask // 2]
-            at = (idx[1] ^ z) * 4 + there
+    shares = q0.shape[1] - 2 * chunk
+    for z in range(NZ * 2):
+        for c, out in enumerate((q0, q1)):
+            at = z * 2 + (idx[3] ^ c)
             columns_here = pl.ds(pl.multiple_of(at * shares, shares), shares)
             out[z, :shares, :] = dot_tn(similar[:, columns_here], unit[...]).astype(out.dtype)
             out[z, shares : shares + chunk, :] = head_part[
                 pl.ds(pl.multiple_of(at * chunk, chunk), chunk), :
             ].astype(out.dtype)
-            out[z, shares + chunk :, :] = rows_part[
+            out[z, shares + chunk : shares + chunk + 16, :] = rows_part[
                 pl.ds(pl.multiple_of(at * 16, 16), 16), :
             ].astype(out.dtype)
-
-
-def slab_products(idx, left, right, outs, at):
+            out[z, shares + chunk + 16 :, :] = jnp.zeros((chunk - 16, PAIR), out.dtype)
+
+
+def slab_products(idx, left, right, outs):
     slab = outs[0].shape[-2]
     for z, out in enumerate(outs):
         mine = []
@@ -552,20 +591,21 @@
             mine.append(jnp.where(idx[3] == 0, lanes[:, :slab], lanes[:, slab:]))
         both_rows = dot_tn(jnp.concatenate(mine, axis=1), right)
         for x in range(2):
-            out[at + (x,)] = both_rows[x * slab : (x + 1) * slab].astype(out.dtype)
-
-
-def weights_kernel(idx, f0, f1, f2, f3, g0, g1, g2, g3, own, s1, s2, s3, left, right):
+            out[x] = both_rows[x * slab : (x + 1) * slab].astype(out.dtype)
+
+
+def weights_kernel(idx, f0, f1, f2, f3, g0, g1, g2, g3, *refs):
+    (*outs, left, right) = refs
     rows = g0.shape[0] // 2
     firsts, grads = (f0, f1, f2, f3), (g0, g1, g2, g3)
-    for at, lefts, rights in ((0, grads, firsts), (1, firsts, grads)):
+    for lefts, rights, group in ((grads, firsts, outs[:4]), (firsts, grads, outs[4:])):
         for i in range(4):
             left[i * rows : (i + 1) * rows, :] = lefts[i][:rows, :]
             right[i * rows : (i + 1) * rows, :] = rights[i][rows : 2 * rows, :]
-        slab_products(idx, left, right[...], (own, s1, s2, s3), (at,))
-
-
-def output_kernel(idx, f0, f1, f2, f3, g0, g1, g2, g3, own, s1, s2, s3, left, right):
+        slab_products(idx, left, right[...], group)
+
+
+def output_kernel(idx, f0, f1, f2, f3, g0, g1, g2, g3, e1, e2, e3, own, s1, s2, s3, left, right):
     rows, width = g0.shape
     few = rows * QUAD // width
     for i, (f, g) in enumerate(zip((f0, f1, f2, f3), (g0, g1, g2, g3))):
@@ -574,18 +614,26 @@
             right[i * rows + j * few : i * rows + (j + 1) * few, :] = f[
                 2 * rows :, j * QUAD : (j + 1) * QUAD
             ]
-    slab_products(idx, left, right[...], (own, s1, s2, s3), ())
-
-
-def line_sum_kernel(idx, a0, a1, a2, a3, b0, b1, b2, b3, keep, keep_out, send):
-    span = keep.shape[-1]
-    total = a0[...] + a1[...].astype(WIDE) + (a2[...].astype(WIDE) + a3[...].astype(WIDE))
-    keep[...] = total[:, 0]
-    send[:, :span] = total[0, 1].astype(LOW)
-    send[:, span : 2 * span] = total[1, 1].astype(LOW)
-    total = b0[...] + b1[...].astype(WIDE) + (b2[...].astype(WIDE) + b3[...].astype(WIDE))
-    keep_out[...] = total[0]
-    send[:, 2 * span :] = total[1].astype(LOW)
+    span = e1.shape[-1]
+    for out, expand in ((s1, e1), (s2, e2), (s3, e3)):
+        out[:, :, :span] = expand[...]
+    slab_products(
+        idx, left, right[...], [own] + [out.at[:, :, span:] for out in (s1, s2, s3)]
+    )
+
+
+def line_sum_kernel(idx, c0, c1, c2, c3, e0, o0, b1, b2, b3, keep, keep_out, send):
+    span = c0.shape[2]
+    for x in range(2):
+        wide = c0[x] + c1[x].astype(WIDE) + (c2[x].astype(WIDE) + c3[x].astype(WIDE))
+        both = b1[x].astype(WIDE) + (b2[x].astype(WIDE) + b3[x].astype(WIDE))
+        expand, thin = e0[x] + both[:, :span], o0[x] + both[:, span:]
+        if x == 0:
+            keep[0], keep[1], keep_out[...] = wide, expand, thin
+        else:
+            send[:, :span] = wide.astype(LOW)
+            send[:, span : 2 * span] = expand.astype(LOW)
+            send[:, 2 * span :] = thin.astype(LOW)
 
 
 def columns_kernel(idx, keep, keep_out, got, contract, expand, output):
@@ -599,11 +647,11 @@
 
 
 def first_back_kernel(
-    idx, own, other, grad_second_in, unitary, inverse, gain, slabs,
-    grad_in, grad_low, vectors, pack, held, sems,
+    pieces, idx, own, other, grad_second_in, unitary, inverse, gain, *refs
 ):
-    copy = slab_copy(slabs, slabs.shape[1] - held.shape[1], held, sems)
-    copy.start()
+    slabs, (grad_in, grad_low, vectors, pack, held, sems) = refs[:pieces], refs[pieces:]
+    copy = piece_copies(idx, slabs, held, sems)
+    start(copy)
     grad_first = grad_second_in[...] + pair(own, other)
     grad_in[...] = norm_back(grad_first, gain[...], unitary[...], inverse[...])
     grad_low[...] = grad_in[...].astype(LOW)
@@ -640,18 +688,14 @@
 
 def triple_weight_kernel(idx, *refs):
     sheets, (grad, vectors, keep, send, total) = refs[:8], refs[8:]
-    mz, mx, mc = idx[1], idx[2], idx[3]
-    rows = sheets[0].shape[0]
+    mc = idx[3]
     slab = keep.shape[1] - 16
-    for z in range(NZ):
-        for x in range(2):
-            spot = (mz ^ z) * 2 + (mx ^ x)
-            at = pl.ds(pl.multiple_of(spot * rows, rows), rows)
-            part = dot_tn(sheets[z * 2 + x][...], grad[at, :])
-            if z + x == 0:
-                total[...] = part
-            else:
-                total[...] += part
+    for i, (value, at) in enumerate(sheet_rows(idx, sheets)):
+        part = dot_tn(value, grad[at, :])
+        if i == 0:
+            total[...] = part
+        else:
+            total[...] += part
     extra = extra_rows(column_sum(grad[...].astype(WIDE)), vectors).astype(LOW)
     for spot in range(NZ * 2):
         for out, c in ((keep, mc), (send, 1 - mc)):
@@ -738,8 +782,40 @@
     def sum_outer(value):
         return lax.psum(value, "o") if outer > 1 else value
 
-    by_z = [tokens] + [xor_z(tokens, m) for m in (1, 2, 3)]
-    sheets = [tokens, flip(tokens, "x"), by_z[1], flip(by_z[1], "x")]
+    def stage(work):
+        like = jax.eval_shape(work)
+        idle = lambda: jax.tree.map(lambda leaf: jnp.zeros(leaf.shape, leaf.dtype), like)
+        return lax.cond(doc_lengths[0] >= 0, work, idle)
+
+    def key_doc(live, c):
+        block = jnp.arange(outer * NZ * 2, dtype=jnp.int32) * 2 + c
+        doc = doc_layout(doc_lengths, block[:, None] + where[None, :])[0]
+        return jnp.where(live > 0, doc, -1)
+
+    def head_weights(heads, heads_other):
+        if outer > 1:
+            pack = widen(both(heads, heads_other, mc)).transpose(0, 2, 1, 3, 4)
+            head_triple = pack[..., :slab, :].reshape(width, QUAD)
+            outs = pack[..., slab + 16 :, :].reshape(-1, 2, slab, QUAD).transpose(0, 2, 1, 3)
+            outs = (outs.reshape(width, 2 * QUAD),)
+            live0, live1 = [
+                pick(pack, c, 2)[..., slab, :rows].astype(WIDE).reshape(-1, rows)
+                for c in (mc, 1 - mc)
+            ]
+        else:
+            outs = (heads, heads_other)
+            head_triple, live0, live1 = whole(
+                heads_kernel,
+                "heads",
+                index,
+                (heads, heads_other),
+                [shape((width, QUAD), LOW)] + [shape((NZ * 2, rows), WIDE)] * 2,
+            )
+        return head_triple, key_doc(live0, mc), key_doc(live1, 1 - mc), outs
+
+    half_tokens = lax.dynamic_slice_in_dim(tokens, my * half, half, 0)
+    by_z = [half_tokens] + [xor_z(half_tokens, m) for m in (1, 2, 3)]
+    own_other = flip(tokens, "x")
 
     heads, low_slab, triple_slab = whole(
         prep_kernel,
@@ -752,88 +828,100 @@
             contract_weight.T,
             line(live_mask),
         ),
-        [shape((NZ * 2, slab + 16, QUAD), LOW)]
-        + [shape((slab, n), LOW) for n in (2 * span + 2 * QUAD, 6 * QUAD)],
-    )
-    heads = lax.all_to_all(heads, ("z", "x"), 0, 0)
-    for piece in by_z[2:]:
-        sheets += [piece, flip(after(piece, heads), "x")]
-    heads_other = flip(after(heads, sheets[1], sheets[3]), "c")
-    if outer > 1:
-        pack = widen(both(heads, heads_other, mc)).transpose(0, 2, 1, 3, 4)
-        head_triple = pack[..., :slab, :].reshape(width, QUAD)
-        live0, live1 = [
-            pick(pack, c, 2)[..., slab, :rows].astype(WIDE).reshape(-1, rows) for c in (mc, 1 - mc)
-        ]
-    else:
-        head_triple, live0, live1 = whole(
-            heads_kernel,
-            "heads",
-            index,
-            (heads, heads_other),
-            [shape((width, QUAD), LOW)] + [shape((NZ * 2, rows), WIDE)] * 2,
-        )
+        [shape((NZ * 2, 3 * slab + 16, QUAD), LOW)]
+        + [shape((slab, n), LOW) for n in (2 * span, 6 * QUAD)],
+    )
 
     where = jnp.arange(rows, dtype=jnp.int32) * blocks
     rank = jnp.arange(NZ * 2, dtype=jnp.int32) * 2
-
-    def key_doc(live, c):
-        block = jnp.arange(outer * NZ * 2, dtype=jnp.int32) * 2 + c
-        doc = doc_layout(doc_lengths, block[:, None] + where[None, :])[0]
-        return jnp.where(live > 0, doc, -1)
-
-    kdoc0, kdoc1 = key_doc(live0, mc), key_doc(live1, 1 - mc)
-    own_places = (mo * NZ * 4 + rank + mc)[:, None] + where[None, :]
-    own_doc, own_position = doc_layout(doc_lengths, own_places.reshape(-1))
-    lane = jnp.arange(PAIR) % (HEAD_DIM // 2)
-    exponent = (2 * lane).astype(WIDE) / HEAD_DIM
-    angles = own_position.astype(WIDE)[:, None] * jnp.exp(-math.log(10000.0) * exponent)[None, :]
-    sign = jnp.where(jnp.arange(PAIR) % HEAD_DIM < HEAD_DIM // 2, -1.0, 1.0).astype(WIDE)
-    cosine, sine = jnp.cos(angles), jnp.sin(angles) * sign[None, :]
-    qdoc = own_doc.reshape(NZ, 2, 2, half, 1)
-    query_unit = whole(
-        query_kernel, "query_units", index, (query_vecs,), [shape(query_vecs.shape, LOW)]
-    )[0]
     shares = query_vecs.shape[0] // (NZ * 4)
-    positive = line(jnp.repeat(positives, query_vecs.shape[0] // queries_count))
-
+    by_z = list(lax.optimization_barrier((*by_z, heads, own_other))[:NZ])
+    by_x = [flip(piece, "x") for piece in by_z[1:]]
     gathered = lax.all_gather(after(low_slab, *by_z[1:]), BLK, axis=0, tiled=True)
-    triple_low = lax.all_gather(after(triple_slab, gathered), BLK, axis=0, tiled=True)
+
+    def tables_stage():
+        own_places = (mo * NZ * 4 + rank + mc)[:, None] + where[None, :]
+        own_doc, own_position = doc_layout(doc_lengths, own_places.reshape(-1))
+        lane = jnp.arange(PAIR) % (HEAD_DIM // 2)
+        exponent = (2 * lane).astype(WIDE) / HEAD_DIM
+        angles = own_position.astype(WIDE)[:, None] * jnp.exp(-math.log(10000.0) * exponent)[None, :]
+        sign = jnp.where(jnp.arange(PAIR) % HEAD_DIM < HEAD_DIM // 2, -1.0, 1.0).astype(WIDE)
+        tables = jnp.cos(angles), jnp.sin(angles) * sign[None, :]
+        units = whole(
+            query_kernel,
+            "query_units",
+            index,
+            (after(query_vecs, by_z[1]),),
+            [shape(query_vecs.shape, LOW), shape((shares, proj), LOW)],
+        )
+        positive = line(jnp.repeat(positives, query_vecs.shape[0] // queries_count))
+        return tables, list(units), positive, own_doc.reshape(NZ, 2, 2, half, 1)
+
+    (cosine, sine), (query_unit, own_queries), positive, qdoc = stage(tables_stage)
+    positive, qdoc = lax.optimization_barrier((positive, qdoc))
+    by_x = list(lax.optimization_barrier((*by_x, cosine))[:3])
+
+    sheets = [tokens, own_other]
+    for piece, turned in zip(by_z[1:], by_x):
+        two = jnp.stack([piece, turned])
+        sheets += [two, flip(two, "y")]
+
+    def head_stage():
+        got = lax.all_to_all(after(heads, sheets[2], sheets[4], sheets[6]), ("z", "x"), 0, 0)
+        return head_weights(got, flip(got, "c"))
+
+    head_triple, kdoc0, kdoc1, outs = stage(head_stage)
+    pieces = len(outs)
+    sheets = list(lax.optimization_barrier((*sheets, head_triple))[: len(sheets)])
 
     count = NZ * 2 * rows
-    queries, kv = whole(
-        project_kernel,
-        "project",
-        index,
-        (*sheets, head_triple, cosine, sine, triple_bias),
-        [shape((count, PAIR), LOW)] * 2,
-    )
-    kv0, kv1 = [widen(v).reshape(-1, PAIR) for v in (kv, flip(kv, "c"))]
+
+    def project_stage():
+        queries, kv = whole(
+            project_kernel,
+            "project",
+            index,
+            (*sheets, head_triple, cosine, sine, triple_bias),
+            [shape((count, PAIR), LOW)] * 2,
+        )
+        return queries, kv, flip(kv, "c")
+
+    queries, kv, kv_other = stage(project_stage)
+    kv0, kv1 = [widen(v).reshape(-1, PAIR) for v in (kv, kv_other)]
     meta = (qdoc, kdoc0, kdoc1)
-    out, log_total, pack = attend(queries, kv0, kv1, *meta)
-    wide_rows, low_rows, thin_rows = [shape((rows, n), t) for n, t in ((width, WIDE), (width, LOW), (1, WIDE))]
 
     def to_blocks(value):
         return lax.all_to_all(value.reshape((NZ * 2,) + value.shape[-2:]), ("z", "x"), 0, 0)
 
-    pack = to_blocks(pack)
-    attended_low, part = whole(
-        branch_kernel,
-        "branch",
-        index,
-        (pack,),
-        [shape((rows, 2 * QUAD), LOW), low_rows],
-        slab_scratch(width, 2 * QUAD),
-        (gathered,),
-    )
+    def attention_stage():
+        out, log_total, pack = attend(queries, kv0, kv1, *meta)
+        return out, log_total, to_blocks(pack)
+
+    out, log_total, pack = stage(attention_stage)
+    wide_rows, low_rows, thin_rows = [shape((rows, n), t) for n, t in ((width, WIDE), (width, LOW), (1, WIDE))]
+    def branch_stage():
+        low, part = whole(
+            partial(branch_kernel, pieces),
+            "branch",
+            index,
+            (pack,),
+            [shape((rows, 2 * QUAD), LOW), low_rows],
+            piece_scratch(width, 2 * QUAD),
+            outs,
+        )
+        return low, part, flip(part, "y")
+
+    attended_low, part, part_other = stage(branch_stage)
+    gathered = after(gathered, part)
     both_slabs = slab_scratch(width, span) * 2
+    triple_low = lax.all_gather(after(triple_slab, part), BLK, axis=0, tiled=True)
     few = rows * QUAD // width
     first, unitary1, inverse1, hidden_in, keep, send, part = whole(
         forward_kernel,
         "forward",
         index,
         (
-            part, flip(part, "y"), tokens, line(output_bias), line(first_gain), line(first_shift),
+            part, part_other, tokens, line(output_bias), line(first_gain), line(first_shift),
             line(expand_bias), attended_low,
         ),
         [wide_rows, wide_rows, thin_rows, shape((rows, span), WIDE)]
@@ -850,178 +938,224 @@
         two = [keep, flip(send, "x")]
         return two + [flip(value, "c") for value in two]
 
-    firsts = four_cores(keep, send)
+    first_keep, first_other, first_across = keep, flip(send, "x"), flip(keep, "c")
     my_tokens = query_unit.shape[0]
-    part_other = flip(part, "y")
-    second_low, unitary2, inverse2, embed, unit_low, expo, totals = whole(
-        second_kernel,
-        "second",
-        index,
-        (
-            part, part_other, first, line(contract_bias), line(second_gain), line(second_shift),
-            head_weight, query_unit, kdoc0,
-        ),
-        [low_rows, wide_rows, thin_rows, shape((rows, proj), WIDE), shape((rows, proj), LOW)]
-        + [shape((rows, my_tokens), WIDE), shape((docs, my_tokens), WIDE)],
-    )
+
+    def second_stage():
+        return whole(
+            second_kernel,
+            "second",
+            index,
+            (
+                part, flip(part, "y"), first, line(contract_bias), line(second_gain),
+                line(second_shift), head_weight, query_unit, kdoc0,
+            ),
+            [low_rows, wide_rows, thin_rows, shape((rows, proj), WIDE), shape((rows, proj), LOW)]
+            + [shape((rows, my_tokens), WIDE), shape((docs, my_tokens), WIDE)],
+        )
+
+    second_low, unitary2, inverse2, embed, unit_low, expo, totals = stage(second_stage)
+    firsts = [first_keep, first_other, first_across, flip(first_other, "c")]
+    totals = after(totals, first_other, first_across)
 
     def tree(own, one, two, three):
         return (own + one) + (two + three)
 
-    totals = sum_outer(tree(totals, *[xor_s(totals, m) for m in (1, 2, 3)]))
     chunk = width // (NZ * 4)
-    message = (NZ, shares + chunk + 16, proj)
-    grad_second_in, keep, send, part, loss, *query_parts = whole(
-        partial(middle_kernel, queries_count),
-        "middle",
+    message = (NZ * 2, shares + 2 * chunk, proj)
+    def middle_stage():
+        sums = sum_outer(tree(totals, *[xor_s(totals, m) for m in (1, 2, 3)]))
+        return whole(
+            partial(middle_kernel, queries_count),
+            "middle",
+            index,
+            (
+                sums, *[xor_z(sums, m) for m in (1, 2, 3)], kdoc0, kdoc1, positive, expo, query_unit,
+                unit_low, embed, second_low, head_weight, out_cotangent, unitary2, inverse2,
+                line(second_gain), hidden_in,
+            ),
+            [wide_rows]
+            + [shape((2 * rows, width), LOW)] * 2
+            + [low_rows, shape((8, proj), WIDE), shape(message, WIDE), shape(message, LOW)],
+            [
+                pltpu.VMEM((rows, my_tokens), LOW),
+                pltpu.VMEM((rows, width), LOW),
+                pltpu.VMEM((rows, span), LOW),
+                pltpu.VMEM((width, proj), WIDE),
+                pltpu.VMEM((NZ * 4 * 16, proj), WIDE),
+            ]
+            + both_slabs,
+            (gathered,),
+        )
+
+    grad_second_in, keep, send, part, loss, *query_parts = stage(middle_stage)
+
+    keep_other, keep_across = flip(send, "x"), flip(keep, "c")
+    message_other = flip(query_parts[1], "c")
+
+    def first_stage():
+        return whole(
+            partial(first_back_kernel, pieces),
+            "first_back",
+            index,
+            (part, flip(part, "y"), grad_second_in, unitary1, inverse1, line(first_gain)),
+            [wide_rows, low_rows, shape((8, width), WIDE), shape((NZ * 2, half, PAIR), LOW)],
+            piece_scratch(width, 2 * QUAD),
+            outs,
+        )
+
+    grad_first_in, grad_branch, vectors1, pack = stage(first_stage)
+    keep_other, message_other = lax.optimization_barrier((keep_other, message_other, grad_branch))[:2]
+    grads = [keep, keep_other, keep_across, flip(keep_other, "c")]
+    pack = whole(
+        core_sum_kernel,
+        "query_c",
         index,
-        (
-            totals, *[xor_z(totals, m) for m in (1, 2, 3)], kdoc0, kdoc1, positive, expo, query_unit,
-            unit_low, embed, second_low, head_weight, out_cotangent, unitary2, inverse2,
-            line(second_gain), hidden_in,
-        ),
-        [wide_rows]
-        + [shape((2 * rows, width), LOW)] * 2
-        + [low_rows, shape((8, proj), WIDE), shape((2,) + message, WIDE), shape((2,) + message, LOW)],
-        [
-            pltpu.VMEM((rows, my_tokens), LOW),
-            pltpu.VMEM((rows, width), LOW),
-            pltpu.VMEM((rows, span), LOW),
-            pltpu.VMEM((width, proj), WIDE),
-            pltpu.VMEM((NZ * 4 * 16, proj), WIDE),
-        ]
-        + both_slabs,
-        (gathered,),
-    )
-    grads = four_cores(keep, send)
-    part_other = flip(part, "y")
-    grad_first_in, grad_branch, vectors1, pack = whole(
-        first_back_kernel,
-        "first_back",
+        (pack, query_parts[0], message_other),
+        [shape((NZ * 2, half + message[1], proj), LOW)],
+    )[0]
+
+    dims, dims_out = (2, slab, quarter), (2, slab, QUAD)
+    dims_both = (2, slab, quarter + QUAD)
+    left_right = [pltpu.VMEM((4 * rows, width), LOW)]
+
+    def parts_of(left, right):
+        part = dot_tn(jnp.concatenate(left), jnp.concatenate(right))
+        part = pick(narrow(part.reshape(outer, NZ, 2, 2, slab, -1)), mc, 2)
+        for axis, spot in ((0, mz), (1, mx)):
+            part = jnp.take(part, jnp.arange(part.shape[axis]) ^ spot, axis=axis)
+        return part
+
+    def low_parts(parts):
+        return [parts[0]] + [parts[m].astype(LOW) for m in (1, 2, 3)]
+
+    def weights_stage():
+        got = to_blocks(pack)
+        got = got, flip(grad_branch, "x"), flip(grad_branch, "c")
+        if outer == 1:
+            parts = whole(
+                weights_kernel,
+                "weights",
+                index,
+                (*firsts, *grads),
+                ([shape(dims, WIDE)] + [shape(dims, LOW)] * 3) * 2,
+                left_right * 2,
+            )
+            return got, list(parts)
+        top, mid = slice(0, rows), slice(rows, 2 * rows)
+        contract = parts_of([g[top] for g in grads], [f[mid] for f in firsts])
+        expand = parts_of([f[top] for f in firsts], [g[mid] for g in grads])
+        return got, low_parts(contract) + low_parts(expand)
+
+    (grad_out, branch_other, branch_across), weight_parts = stage(weights_stage)
+    contract_parts, expand_parts = weight_parts[:4], weight_parts[4:]
+    mine = whole(
+        partial(query_back_kernel, half),
+        "query_back",
         index,
-        (part, part_other, grad_second_in, unitary1, inverse1, line(first_gain)),
-        [wide_rows, low_rows, shape((8, width), WIDE), shape((NZ * 2, half, PAIR), LOW)],
-        slab_scratch(width, 2 * QUAD),
-        (gathered,),
-    )
-    grad_out = to_blocks(pack)
-
-    branches = four_cores(grad_branch, grad_branch)
-    dims, dims_out = (2, 2, slab, quarter), (2, slab, QUAD)
-    left_right = [pltpu.VMEM((4 * rows, width), LOW)]
-    if outer == 1:
-        weight_parts = whole(
-            weights_kernel,
-            "weights",
+        (sum_outer(grad_out), own_queries),
+        [shape(message[1:], LOW)],
+    )[0]
+    spread = lax.all_gather(mine, ("z", "x", "c"))
+    contract_in = over_z([mine, *lax.optimization_barrier((*contract_parts[1:], mine))[:3]])[1:]
+
+    def attend_stage():
+        grad_query, dkv0, dkv1 = attend_back(
+            queries, grad_out.reshape(NZ, 2, -1, PAIR), out, log_total, kv0, kv1, *meta
+        )
+        dkv0, dkv1 = [narrow(v.reshape(outer, -1, PAIR)) for v in (dkv0, dkv1)]
+        triple = whole(
+            triple_kernel,
+            "triple",
             index,
-            (*firsts, *grads),
-            [shape(dims, WIDE)] + [shape(dims, LOW)] * 3,
-            left_right * 2,
-        )
-        output_parts = whole(
-            output_kernel,
-            "output",
-            index,
-            (*firsts, *branches),
-            [shape(dims_out, WIDE)] + [shape(dims_out, LOW)] * 3,
-            left_right + [pltpu.VMEM((4 * rows, QUAD), LOW)],
-        )
-    else:
-
-        def parts_of(left, right):
-            part = dot_tn(jnp.concatenate(left), jnp.concatenate(right))
-            part = pick(narrow(part.reshape(outer, NZ, 2, 2, slab, -1)), mc, 2)
-            for axis, spot in ((0, mz), (1, mx)):
-                part = jnp.take(part, jnp.arange(part.shape[axis]) ^ spot, axis=axis)
-            return part
-
-        top, mid = slice(0, rows), slice(rows, 2 * rows)
-        wide = [f[2 * rows :].reshape(few, 4, QUAD).transpose(1, 0, 2).reshape(rows, QUAD) for f in firsts]
-        weight_parts = jnp.stack(
-            [
-                parts_of([g[top] for g in grads], [f[mid] for f in firsts]),
-                parts_of([f[top] for f in firsts], [g[mid] for g in grads]),
-            ],
-            axis=1,
-        )
-        output_parts = parts_of(branches, wide)
-        weight_parts = [weight_parts[0]] + [weight_parts[m].astype(LOW) for m in (1, 2, 3)]
-        output_parts = [output_parts[0]] + [output_parts[m].astype(LOW) for m in (1, 2, 3)]
-
-    two = [shape(message, WIDE), shape(message, LOW)]
-    parts = whole(core_sum_kernel, "query_c", index, (query_parts[0], flip(query_parts[1], "c")), two)
-    parts = whole(
-        query_sum_kernel,
-        "query_sum",
-        index,
-        (parts[0], flip(parts[1], "x")),
-        [shape(message[1:], WIDE)] + [shape(message[1:], LOW)] * 3,
-    )
-    parts = [sum_outer(p) for p in parts]
-    block = (mz * 2 + mx) * 2 + mc
-    own_queries = lax.dynamic_slice_in_dim(query_vecs, block * shares, shares, 0)
-    mine = whole(
-        query_back_kernel, "query_back", index, (*over_z(parts), own_queries), [shape(message[1:], LOW)]
-    )[0]
-    grad_query, dkv0, dkv1 = attend_back(
-        after(queries, weight_parts[0]), grad_out.reshape(NZ, 2, half, PAIR), out, log_total, kv0, kv1, *meta
-    )
-
-    weight_in, output_in = over_z(weight_parts), over_z(output_parts)
-    dkv0, dkv1 = [narrow(v.reshape(outer, -1, PAIR)) for v in (dkv0, dkv1)]
-    grad_triple = whole(
-        triple_kernel,
-        "triple",
-        index,
-        (after(grad_query.reshape(count, PAIR), mine, weight_in[1]), dkv0, flip(dkv1, "c"), cosine, sine),
-        [shape((count, QUAD), LOW)],
-    )[0]
-
-    block_triple = to_blocks(grad_triple.reshape(NZ * 2, rows, QUAD))
-    dims = (NZ * 2, slab + 16, QUAD)
-    if outer == 1:
-        keep, send = whole(
-            triple_weight_kernel,
-            "triple_weight",
-            index,
-            (*sheets, grad_triple, vectors1),
-            [shape(dims, LOW)] * 2,
-            [pltpu.VMEM((width, QUAD), WIDE)],
-        )
-    else:
-        ordered = place(
-            [((mz ^ (i // 2)) * 2 + (mx ^ (i % 2)), sheet) for i, sheet in enumerate(sheets)]
-        ).reshape(count, width)
+            (grad_query.reshape(count, PAIR), dkv0, flip(dkv1, "c"), cosine, sine),
+            [shape((count, QUAD), LOW)],
+        )[0]
+        return triple, flip(branch_other, "c")
+
+    grad_triple, branch_last = stage(attend_stage)
+    branches = [grad_branch, branch_other, branch_across, branch_last]
+    grad_triple, *contract_in = lax.optimization_barrier((grad_triple, *contract_in))
+
+    dims_triple = (NZ * 2, slab + 16, QUAD)
+    vector = shape((width // PAIR, PAIR), WIDE)
+
+    def triple_parts():
+        if outer == 1:
+            return whole(
+                triple_weight_kernel,
+                "triple_weight",
+                index,
+                (*sheets, grad_triple, vectors1),
+                [shape(dims_triple, LOW)] * 2,
+                [pltpu.VMEM((width, QUAD), WIDE)],
+            )
+        ordered = [(mz * 2 + (mx ^ x), sheets[x]) for x in range(2)]
+        for m in (1, 2, 3):
+            two = both(*sheets[2 * m : 2 * m + 2], my)
+            for x in range(2):
+                ordered.append(((mz ^ m) * 2 + (mx ^ x), two[:, x].reshape(rows, width)))
+        ordered = place(ordered).reshape(count, width)
         part = narrow(dot_tn(ordered, grad_triple).reshape(outer, NZ * 2, 2, slab, QUAD))
         bias = sum_outer(jnp.sum(grad_triple, axis=0, dtype=WIDE))
         bias = extra_rows(line(bias), sum_outer(vectors1))
         bias = jnp.broadcast_to(bias, (NZ * 2, 2, 16, QUAD))
         part = jnp.concatenate([part, bias], axis=2).astype(LOW)
-        keep, send = pick(part, mc, 1), pick(part, 1 - mc, 1)
-    packed = whole(
-        pair_sum_kernel, "pair_sum", index, (keep, flip(send, "c")), [shape(dims, LOW)]
-    )[0]
-    vector = shape((width // PAIR, PAIR), WIDE)
+        return pick(part, mc, 1), pick(part, 1 - mc, 1)
+
+    def output_parts_of():
+        if outer == 1:
+            return whole(
+                output_kernel,
+                "output",
+                index,
+                (*firsts, *branches, *expand_parts[1:]),
+                [shape(dims_out, WIDE)] + [shape(dims_both, LOW)] * 3,
+                left_right + [pltpu.VMEM((4 * rows, QUAD), LOW)],
+            )
+        wide = [f[2 * rows :].reshape(few, 4, QUAD).transpose(1, 0, 2).reshape(rows, QUAD) for f in firsts]
+        parts = low_parts(parts_of(branches, wide))
+        return parts[:1] + [jnp.concatenate(both, axis=-1) for both in zip(expand_parts[1:], parts[1:])]
+
+    def triple_stage():
+        block_triple = to_blocks(grad_triple.reshape(NZ * 2, rows, QUAD))
+        keep, send = triple_parts()
+        output_parts = output_parts_of()
+        packed = whole(
+            pair_sum_kernel, "pair_sum", index, (keep, flip(send, "c")), [shape(dims_triple, LOW)]
+        )[0]
+        return block_triple, packed, list(output_parts)
+
+    block_triple, packed, output_parts = stage(triple_stage)
+    both_in = over_z([expand_parts[0]] + list(output_parts[1:]))[1:]
+
+    def tokens_stage():
+        part = whole(
+            tokens_kernel,
+            "tokens",
+            index,
+            (block_triple, triple_low),
+            [low_rows],
+            [pltpu.VMEM((rows, 6 * QUAD), LOW)],
+        )[0]
+        return whole(
+            tokens_sum_kernel, "tokens_sum", index, (part, flip(part, "y"), grad_first_in), [wide_rows]
+        )[0]
+
+    tokens_grad = stage(tokens_stage)
     triple_grad, triple_bias_grad, output_bias_grad, gain_one, shift_one = whole(
         triple_out_kernel,
         "triple_out",
         index,
-        (lax.all_to_all(after(packed, block_triple), ("z", "x"), 0, 0),),
+        (lax.all_to_all(after(packed, tokens_grad), ("z", "x"), 0, 0),),
         [shape((3, slab, 2 * QUAD), WIDE), shape((3, 2 * QUAD), WIDE)] + [vector] * 3,
     )
-    part = whole(
-        tokens_kernel,
-        "tokens",
-        index,
-        (after(block_triple, keep, output_parts[0], weight_in[2]), triple_low),
-        [low_rows],
-        [pltpu.VMEM((rows, 6 * QUAD), LOW)],
-    )[0]
+    contract_own, spread = after(contract_parts[0], tokens_grad), after(spread, tokens_grad)
     keep, keep_out, send = whole(
         line_sum_kernel,
         "line_sum",
         index,
-        (after(weight_in[0], part), *weight_in[1:], *output_in),
+        (contract_own, *contract_in, expand_parts[0], output_parts[0], *both_in),
         [shape((2, slab, quarter), WIDE), shape((slab, QUAD), WIDE), shape((slab, 2 * quarter + QUAD), LOW)],
     )
     contract_grad, expand_grad, output_grad = whole(
@@ -1031,15 +1165,11 @@
         (keep, keep_out, flip(send, "x")),
         [shape((slab, n), WIDE) for n in (span, span, 2 * QUAD)],
     )
-    tokens_grad = whole(
-        tokens_sum_kernel, "tokens_sum", index, (part, flip(part, "y"), grad_first_in), [wide_rows]
-    )[0]
-
     queries_grad, head_grad, contract_bias_grad, gain_two, shift_two, expand_bias_grad = whole(
         spread_kernel,
         "spread",
         index,
-        (lax.all_gather(mine, ("z", "x", "c")).reshape(NZ * 4, *message[1:]),),
+        (spread.reshape(NZ * 4, *message[1:]),),
         [shape((query_vecs.shape[0], proj), WIDE), shape((width, proj), WIDE)]
         + [vector] * 3
         + [shape((span // PAIR, PAIR), WIDE)],
@@ -1047,7 +1177,7 @@
 
     return (
         second_low,
-        loss[0, 0],
+        after(loss, tokens_grad)[0, 0],
         tokens_grad,
         queries_grad,
         triple_grad.transpose(1, 0, 2),

time: 364 us -> 335 us (0.920)
  waiting for transfers between devices: 137 us -> 95.6 us
  blocking collectives: 16.8 us -> 47.1 us
  local copies, waits for them, and re-layouts: 19.7 us -> 11 us
  starting transfers between devices: 66.7 us -> 60.8 us
  Pallas kernels: 99.6 us -> 94.3 us
    ppermute x15 -> x12, waiting for transfers between devices: 60.1 us -> 25.4 us  [xor_z(): return lax.ppermute(value, 'z', [(i, i ^ mask) for i in FOUR])]
    all_to_all x0 -> x1, blocking collectives: none -> 32.2 us  [head_stage(): lax.all_to_all(after(heads, sheets[2], sheets[4], sheets[6]), ('z', 'x'),...]
    all_gather x1, waiting for transfers between devices: 14.7 us -> 0.02 us  [shards(): lax.all_gather(after(low_slab, *by_z[1:]), BLK, axis=0, tiled=True)]
    unnamed x102 -> x50, local copies, waits for them, and re-layouts: 14.5 us -> 2.9 us
    all_to_all x2, waiting for transfers between devices: 8.71 us -> 16.2 us  [to_blocks(): lax.all_to_all(value.reshape((NZ * 2,) + value.shape[-2:]), ('z', 'x'), 0...]
    all_to_all x2 -> x1, starting transfers between devices: 10.6 us -> 4.38 us  [shards(): lax.all_to_all(after(packed, tokens_grad), ('z', 'x'), 0, 0)]
    all_to_all x2, starting transfers between devices: 8.96 us -> 15.1 us  [to_blocks(): lax.all_to_all(value.reshape((NZ * 2,) + value.shape[-2:]), ('z', 'x'), 0...]
    ppermute x15 -> x12, starting transfers between devices: 24.8 us -> 19 us  [xor_z(): return lax.ppermute(value, 'z', [(i, i ^ mask) for i in FOUR])]
  transfers between devices with their start and end apart: 49 -> 47, of which waited for: 22 -> 20; matrix products, arithmetic and copies ran while one was open for 3% -> 3% of each run, Pallas kernels for 24% -> 28%
where the time goes in v1:
time: 335 us; the launch traced here: 331 us
  waiting for transfers between devices  95.6 us (29%)
  Pallas kernels  94.3 us (28%)
  starting transfers between devices  60.8 us (18%)
  blocking collectives  47.1 us (14%)
  between operations  14.2 us (4%)
  local copies, waits for them, and re-layouts  11 us (3%)
  other arithmetic  7.76 us (2%)
    pallas_call x22, Pallas kernels, whole(): pl.pallas_call(kernel, in_specs=[pl.BlockSpec(memory_space=pltpu.SMEM)] +...  77.2 us
    ppermute x26, waiting for transfers between devices, flip(): return lax.ppermute(value, axis, [(0, 1), (1, 0)])  45 us
    all_to_all x1, blocking collectives, head_stage(): lax.all_to_all(after(heads, sheets[2], sheets[4], sheets[6]), ('z', 'x'),...  32.2 us
    ppermute x12, waiting for transfers between devices, xor_z(): return lax.ppermute(value, 'z', [(i, i ^ mask) for i in FOUR])  25.4 us
    ppermute x26, starting transfers between devices, flip(): return lax.ppermute(value, axis, [(0, 1), (1, 0)])  20.4 us
    ppermute x12, starting transfers between devices, xor_z(): return lax.ppermute(value, 'z', [(i, i ^ mask) for i in FOUR])  19 us
    all_to_all x2, waiting for transfers between devices, to_blocks(): lax.all_to_all(value.reshape((NZ * 2,) + value.shape[-2:]), ('z', 'x'), 0...  16.2 us
    all_to_all x2, starting transfers between devices, to_blocks(): lax.all_to_all(value.reshape((NZ * 2,) + value.shape[-2:]), ('z', 'x'), 0...  15.1 us
  transfers between devices with their start and end apart: 47, of which 20 were waited for; matrix products, arithmetic and copies ran while one was open for 3% of the time, Pallas kernels for 28%

profile of v1, /device:TPU:0, one launch (start us, length us, event | category | flops | bytes accessed | tf_op | source)
XLA Modules:
  0.0 331.0 jit_solution(3996469487578489503)
XLA Ops:
  8.2 3.1 collective-permute-start.18
  11.2 2.6 collective-permute-start.19
  15.6 2.5 prep.1
  18.1 6.0 %collective-permute-done.19 = bf16[64,1024]{1,0:T(8,128)(2,1)S(1)} collective-permute-done((bf16[64,1024]{1,0:T(8,128)(2,1)S(1)}, bf16[64,1024]{1,0:T(8,128)(2,1)S(1)}, u32[]{:S(2)}, u32[]{:S(2)}) %collective-permute-start.19) | collective-permute-done | bytes 131104 | tf_op jit(solution)/shard_map/ppermute | solution.py:33
  28.0 5.1 %conditional.12 = (f32[1024,128]{1,0:T(8,128)S(1)}, f32[1024,128]{1,0:T(8,128)S(1)}, bf16[4096,128]{1,0:T(8,128)(2,1)S(1)}, bf16[256,128]{1,0:T(8,128)(2,1)}, s3...) conditional(s32[]{:T(128)} %bitcast.16, () %tuple.128, (s32[8]{0:T(128)S(1)}, s32[]{:T(128)}, ...), branch_computations={%region_0.0_spmd, %region_1.5_spmd} | conditional | flops 3220288000 | bytes 11506648 | solution.py:788
  28.4 1.9 fusion
  30.4 2.4 query_units.3
  41.0 38.4 %conditional.13 = (bf16[1024,256]{1,0:T(8,128)(2,1)S(1)}, s32[8,128]{1,0:T(8,128)S(1)}, s32[8,128]{1,0:T(8,128)S(1)}, bf16[8,208,256]{2,1,0:T(8,128)(2,1)}, bf16[8,208,256]{2,1,0:T(8,128)(2,1)}) conditional(s32[]{:T(128)} %bitcast.16, () %tuple.131, (bf16[8,208,256]{2,1,0:T(8,128)(2,1)S(1)}, s32[5]{0:T(128)S(1)}, s32[4]{0:T(128)S(1)}, s32[]{:T(128)}, ...), branch_computations={%region_5.6_spmd, %region_6.10_spmd} | conditional | flops 2300030720 | bytes 12562312 | solution.py:788
  41.0 32.2 %all_to_all.21.own = bf16[8,208,256]{2,1,0:T(8,128)(2,1)} all-to-all(bf16[8,208,256]{2,1,0:T(8,128)(2,1)S(1)} %get-tuple-element.290), channel_id=1, replica_groups=mesh['o'=1,'z'=4,'x'=2,'c'=2,'y'=2] {'z','x'}, dimensions={0} | all-to-all | bytes 1703936 | tf_op jit(solution)/shard_map/cond/branch_1_fun/all_to_all | solution.py:870
  73.5 2.4 collective-permute-done.10.other
  75.9 2.1 heads.1
  79.4 5.5 %conditional.14 = (bf16[1024,128]{1,0:T(8,128)(2,1)}, bf16[1024,128]{1,0:T(8,128)(2,1)}, bf16[1024,128]{1,0:T(8,128)(2,1)}) conditional(s32[]{:T(128)} %bitcast.16, () %tuple.126, (s32[5]{0:T(128)S(1)}, bf16[128,1024]{1,0:T(8,128)(2,1)}, bf16[128,1024]{1,0:T(8,128)(2,1)}, bf16[2,64,1024]{2,1,0:T(8,128)(2,1)}, bf16[2,64,1024]{2,1,0:T(8,128)(2,1)}, ...), branch_computations={%region_10.11_spmd, %region_11.12_spmd} | conditional | flops 4369999872 | bytes 15108640 | solution.py:788
  79.4 3.6 %project.1 = (bf16[1024,128]{1,0:T(8,128)(2,1)}, bf16[1024,128]{1,0:T(8,128)(2,1)}) custom-call(s32[5]{0:T(128)S(1)} %get-tuple-element.298.idx, bf16[128,1024]{1,0:T(8,128)(2,1)} %get-tuple-element.299.refs_0_, bf16[128,1024]{1,0:T(8,128)(2,1)} %get-tuple-element.300.refs_1_, bf16[2,64,1024]{2,1,0:T(8,128)(2,1)} %get-tuple-element.301.refs_2_, ...), custom_call_target="tpu_custom_call" | custom-call | flops 4369999872 | bytes 14060000 | tf_op jit(solution)/shard_map/cond/branch_1_fun/project/pallas_call | solution.py:115
  85.0 23.3 %conditional.15 = (f32[4,2,2,64,128]{4,3,2,1,0:T(8,128)}, f32[4,2,2,64,1]{4,3,2,1,0:T(8,128)}, bf16[8,64,128]{2,1,0:T(8,128)(2,1)S(1)}) conditional(s32[]{:T(128)} %bitcast.16, () %tuple.125, (bf16[1024,128]{1,0:T(8,128)(2,1)}, bf16[1024,128]{1,0:T(8,128)(2,1)}, bf16[1024,128]{1,0:T(8,128)(2,1)}, s32[4,2,2,64,1]{3,2,1,0,4:T(2,128)S(1)}, ...), branch_computations={%region_12.13_spmd, %region_13.14_spmd} | conditional | flops 8625000448 | bytes 28020360 | solution.py:788
  86.0 7.4 %attend.1 = (f32[4,2,2,64,128]{4,3,2,1,0:T(8,128)}, f32[4,2,2,64,1]{4,3,2,1,0:T(8,128)}, bf16[4,2,64,128]{3,2,1,0:T(8,128)(2,1)}) custom-call(bf16[4,2,2,64,128]{4,3,2,1,0:T(8,128)(2,1)} %bitcast.5.q_ref, bf16[1024,128]{1,0:T(8,128)(2,1)} %get-tuple-element.314.kv0_ref, bf16[1024,128]{1,0:T(8,128)(2,1)} %get-tuple-element.315.kv1_ref, ...), custom_call_target="tpu_custom_call" | custom-call | flops 8625000448 | bytes 27750000 | tf_op jit(solution)/shard_map/cond/branch_1_fun/attend/pallas_call | solution.py:293
  93.4 14.8 %all_to_all.22 = bf16[8,64,128]{2,1,0:T(8,128)(2,1)S(1)} all-to-all(bf16[8,64,128]{2,1,0:T(8,128)(2,1)} %bitcast.53), channel_id=1, replica_groups=mesh['o'=1,'z'=4,'x'=2,'c'=2,'y'=2] {'z','x'}, dimensions={0} | all-to-all | bytes 262144 | tf_op jit(solution)/shard_map/cond/branch_1_fun/all_to_all | solution.py:894
  108.3 11.2 %conditional.16 = (bf16[128,512]{1,0:T(8,128)(2,1)S(1)}, bf16[128,1024]{1,0:T(8,128)(2,1)}, bf16[128,1024]{1,0:T(8,128)(2,1)}) conditional(s32[]{:T(128)} %bitcast.16, () %tuple.124, (s32[5]{0:T(128)S(1)}, bf16[8,64,128]{2,1,0:T(8,128)(2,1)S(1)}, bf16[8,208,256]{2,1,0:T(8,128)(2,1)}, bf16[8,208,256]{2,1,0:T(8,128)(2,1)}) %tuple.137), branch_computations={%region_14.15_spmd, %region_15.16_spmd} | conditional | flops 4024999936 | bytes 13998640 | solution.py:788
  108.3 3.2 branch.1
  113.0 6.5 %collective-permute-done.1 = bf16[128,1024]{1,0:T(8,128)(2,1)} collective-permute-done((bf16[128,1024]{1,0:T(8,128)(2,1)}, bf16[128,1024]{1,0:T(8,128)(2,1)}, u32[]{:S(2)}, u32[]{:S(2)}) %collective-permute-start.1) | collective-permute-done | bytes 262176 | tf_op jit(solution)/shard_map/cond/branch_1_fun/ppermute | solution.py:41
  119.6 7.2 %forward.1 = (f32[128,1024]{1,0:T(8,128)}, f32[128,1024]{1,0:T(8,128)}, f32[128,1]{1,0:T(8,128)}, f32[128,2048]{1,0:T(8,128)}, bf16[288,1024]{1,0:T(8,128)(2,1)}...) custom-call(s32[5]{0:T(128)S(1)} %stack.47.idx, bf16[128,1024]{1,0:T(8,128)(2,1)} %get-tuple-element.592.own, ...), custom_call_target="tpu_custom_call" | custom-call | flops 8855000064 | bytes 28490000 | tf_op jit(solution)/shard_map/forward/pallas_call | solution.py:115
  128.0 13.1 %conditional.17 = ((bf16[128,1024]{1,0:T(8,128)(2,1)}, f32[128,1024]{1,0:T(8,128)}, f32[128,1]{1,0:T(8,128)S(1)}, f32[128,128]{1,0:T(8,128)}, bf16[128,128]{1,0:...) conditional(s32[]{:T(128)} %bitcast.16, () %tuple.123, (bf16[128,1024]{1,0:T(8,128)(2,1)}, ...), branch_computations={%region_16.17_spmd, %region_17.18_spmd} | conditional | flops 4140000000 | bytes 15417228 | solution.py:788
  129.3 7.6 %collective-permute-done.2.other = bf16[128,1024]{1,0:T(8,128)(2,1)S(1)} collective-permute-done((bf16[128,1024]{1,0:T(8,128)(2,1)}, bf16[128,1024]{1,0:T(8,128)(2,1)S(1)}, u32[]{:S(2)}, u32[]{:S(2)}) %collective-permute-start.2) | collective-permute-done | bytes 262176 | tf_op jit(solution)/shard_map/cond/branch_1_fun/ppermute | solution.py:41
  137.7 3.4 %second.1 = (bf16[128,1024]{1,0:T(8,128)(2,1)}, f32[128,1024]{1,0:T(8,128)}, f32[128,1]{1,0:T(8,128)S(1)}, f32[128,128]{1,0:T(8,128)}, bf16[128,128]{1,0:T(8,128...) custom-call(s32[5]{0:T(128)S(1)} %get-tuple-element.328.idx, bf16[128,1024]{1,0:T(8,128)(2,1)} %get-tuple-element.329.own, ...), custom_call_target="tpu_custom_call" | custom-call | flops 4140000000 | bytes 13320000 | tf_op jit(solution)/shard_map/cond/branch_1_fun/second/pallas_call | solution.py:115
  141.1 1.9 collective-permute-done.27
  143.0 30.0 %conditional.18 = ((f32[128,1024]{1,0:T(8,128)}, bf16[256,1024]{1,0:T(8,128)(2,1)}, bf16[256,1024]{1,0:T(8,128)(2,1)}, bf16[128,1024]{1,0:T(8,128)(2,1)}, f32[8,...) conditional(s32[]{:T(128)} %bitcast.16, () %tuple.141, (f32[4,4096]{1,0:T(4,128)S(1)}, ...), branch_computations={%region_18.19_spmd, %region_19.20_spmd} | conditional | flops 13800048640 | bytes 47349588 | solution.py:788
  145.0 3.1 collective-permute-done.12
  150.2 3.1 collective-permute-start.16
  153.3 2.0 collective-permute-done.14.t1
  155.3 3.3 collective-permute-done.15.t2
  160.9 12.1 %middle.1 = (f32[128,1024]{1,0:T(8,128)}, bf16[256,1024]{1,0:T(8,128)(2,1)}, bf16[256,1024]{1,0:T(8,128)(2,1)}, bf16[128,1024]{1,0:T(8,128)(2,1)}, f32[8,128]{1,...) custom-call(s32[5]{0:T(128)} %copy-done.24, f32[4,4096]{1,0:T(4,128)} %copy-done.15, ...), custom_call_target="tpu_custom_call" | custom-call | flops 13799999488 | bytes 44400000 | tf_op jit(solution)/shard_map/cond/branch_1_fun/middle/pallas_call | solution.py:115
  173.0 2.0 collective-permute-start.30
  176.7 12.5 %conditional.19 = ((f32[128,1024]{1,0:T(8,128)S(1)}, bf16[128,1024]{1,0:T(8,128)(2,1)S(1)}, f32[8,1024]{1,0:T(8,128)S(1)}, bf16[8,64,128]{2,1,0:T(8,128)(2,1)S(1)})) conditional(s32[]{:T(128)} %bitcast.16, () %tuple.148, (bf16[128,1024]{1,0:T(8,128)(2,1)}, f32[1024]{0:T(1024)}, s32[5]{0:T(128)}, f32[128,1024]{1,0:T(8,128)}, ...), branch_computations={%region_20.21_spmd, %region_21.22_spmd} | conditional | flops 4369999872 | bytes 16157228 | solution.py:788
  177.3 7.9 %collective-permute-done.3.other = bf16[128,1024]{1,0:T(8,128)(2,1)S(1)} collective-permute-done((bf16[128,1024]{1,0:T(8,128)(2,1)}, bf16[128,1024]{1,0:T(8,128)(2,1)S(1)}, u32[]{:S(2)}, u32[]{:S(2)}) %collective-permute-start.3) | collective-permute-done | bytes 262176 | tf_op jit(solution)/shard_map/cond/branch_1_fun/ppermute | solution.py:41
  185.9 3.4 %first_back.1 = (f32[128,1024]{1,0:T(8,128)S(1)}, bf16[128,1024]{1,0:T(8,128)(2,1)S(1)}, f32[8,1024]{1,0:T(8,128)S(1)}, bf16[8,64,128]{2,1,0:T(8,128)(2,1)S(1)}) custom-call(s32[5]{0:T(128)} %get-tuple-element.354.idx, bf16[128,1024]{1,0:T(8,128)(2,1)} %get-tuple-element.355.own, bf16[128,1024]{1,0:T(8,128)(2,1)} %copy-done.31, ...), custom_call_target="tpu_custom_call" | custom-call | flops 4369999872 | bytes 14060000 | tf_op jit(solution)/shard_map/cond/branch_1_fun/first_back/pallas_call | solution.py:115
  190.2 2.7 query_c.1
  193.0 30.6 %conditional.20 = (bf16[8,448,128]{2,1,0:T(8,128)(2,1)}, bf16[128,1024]{1,0:T(8,128)(2,1)}, bf16[128,1024]{1,0:T(8,128)(2,1)}, f32[2,64,1024]{2,1,0:T(8,128)S(1)...) conditional(s32[]{:T(128)} %bitcast.16, () %tuple.147, ...), branch_computations={%region_22.23_spmd, %region_23.24_spmd} | conditional | flops 5980000256 | bytes 24089864 | solution.py:788
  193.0 7.5 %all-to-all-start.1 = ((bf16[8,448,128]{2,1,0:T(8,128)(2,1)}), bf16[8,448,128]{2,1,0:T(8,128)(2,1)}, u32[]{:S(2)}, u32[]{:S(2)}) async-start(bf16[8,448,128]{2,1,0:T(8,128)(2,1)} %get-tuple-element.362), calls=%async_computation.1 | async-start | bytes 1835008 | tf_op jit(solution)/shard_map/cond/branch_1_fun/all_to_all | solution.py:894
  200.5 2.0 collective-permute-start.4
  202.5 5.6 %weights.1 = (f32[2,64,1024]{2,1,0:T(8,128)S(1)}, bf16[2,64,1024]{2,1,0:T(8,128)(2,1)}, bf16[2,64,1024]{2,1,0:T(8,128)(2,1)}, bf16[2,64,1024]{2,1,0:T(8,128)(2,1...) custom-call(s32[5]{0:T(128)S(1)} %get-tuple-element.364.idx, ...), custom_call_target="tpu_custom_call" | custom-call | flops 5980000256 | bytes 19240000 | tf_op jit(solution)/shard_map/cond/branch_1_fun/weights/pallas_call | solution.py:115
  208.1 8.8 %collective-permute-done.4 = bf16[128,1024]{1,0:T(8,128)(2,1)} collective-permute-done((bf16[128,1024]{1,0:T(8,128)(2,1)S(1)}, bf16[128,1024]{1,0:T(8,128)(2,1)}, u32[]{:S(2)}, u32[]{:S(2)}) %collective-permute-start.4) | collective-permute-done | bytes 262176 | tf_op jit(solution)/shard_map/cond/branch_1_fun/ppermute | solution.py:41
  217.0 6.6 %all-to-all-done.1 = bf16[8,448,128]{2,1,0:T(8,128)(2,1)} async-done(((bf16[8,448,128]{2,1,0:T(8,128)(2,1)}), bf16[8,448,128]{2,1,0:T(8,128)(2,1)}, u32[]{:S(2)}, u32[]{:S(2)}) %all-to-all-start.1) | async-done | bytes 917536 | tf_op jit(solution)/shard_map/cond/branch_1_fun/all_to_all | solution.py:894
  223.6 2.1 query_back.1
  227.3 2.9 collective-permute-start.36
  230.1 16.3 %conditional.21 = (bf16[1024,256]{1,0:T(8,128)(2,1)}, bf16[128,1024]{1,0:T(8,128)(2,1)}) conditional(s32[]{:T(128)} %bitcast.16, () %tuple.146, (bf16[1024,128]{1,0:T(8,128)(2,1)}, bf16[8,448,128]{2,1,0:T(8,128)(2,1)}, f32[4,2,2,64,128]{4,3,2,1,0:T(8,128)S(1)}, f32[4,2,2,64,1]{4,3,2,1,0:T(8,128)}, bf16[1024,128]{1,0:T(8,128)(2,1)}, ...), branch_computations={%region_24.25_spmd, %region_25.26_spmd} | conditional | flops 14604999680 | bytes 52241196 | solution.py:788
  231.2 9.6 %attend_back.1 = (f32[4,2,2,64,128]{4,3,2,1,0:T(8,128)}, f32[1024,128]{1,0:T(8,128)}, f32[1024,128]{1,0:T(8,128)}) custom-call(bf16[4,2,2,64,128]{4,3,2,1,0:T(8,128)(2,1)} %bitcast.12.q_ref, bf16[4,2,448,128]{3,2,1,0:T(8,128)(2,1)} %bitcast.13.g_ref, f32[4,2,2,64,128]{4,3,2,1,0:T(8,128)S(1)} %get-tuple-element.384.o_ref, ...), custom_call_target="tpu_custom_call" | custom-call | flops 11269999616 | bytes 36260000 | tf_op jit(solution)/shard_map/cond/branch_1_fun/attend_back/pallas_call | solution.py:351
  243.8 2.6 triple.1
  246.5 3.8 %collective-permute-done.35.c2 = bf16[2,64,1024]{2,1,0:T(8,128)(2,1)} collective-permute-done((bf16[2,64,1024]{2,1,0:T(8,128)(2,1)}, bf16[2,64,1024]{2,1,0:T(8,128)(2,1)}, u32[]{:S(2)}, u32[]{:S(2)}) %collective-permute-start.35) | collective-permute-done | bytes 262176 | tf_op jit(solution)/shard_map/ppermute | solution.py:33
  250.3 27.8 %conditional.22 = (bf16[8,128,256]{2,1,0:T(8,128)(2,1)}, bf16[8,80,256]{2,1,0:T(8,128)(2,1)}, f32[2,64,256]{2,1,0:T(8,128)S(1)}, bf16[2,64,1280]{2,1,0:T(8,128)(...) conditional(s32[]{:T(128)} %bitcast.16, () %tuple.145, ...), branch_computations={%region_26.27_spmd, %region_27.28_spmd} | conditional | flops 9084999680 | bytes 37618868 | solution.py:788
  250.3 7.6 %all-to-all-start.2 = ((bf16[8,128,256]{2,1,0:T(8,128)(2,1)}), bf16[8,128,256]{2,1,0:T(8,128)(2,1)}, u32[]{:S(2)}, u32[]{:S(2)}) async-start(bf16[8,128,256]{2,1,0:T(8,128)(2,1)} %bitcast.15), calls=%async_computation.2 | async-start | bytes 1048576 | tf_op jit(solution)/shard_map/cond/branch_1_fun/all_to_all | solution.py:894
  257.9 4.7 %triple_weight.1 = (bf16[8,80,256]{2,1,0:T(8,128)(2,1)}, bf16[8,80,256]{2,1,0:T(8,128)(2,1)}) custom-call(s32[5]{0:T(128)S(1)} %get-tuple-element.398.idx, bf16[128,1024]{1,0:T(8,128)(2,1)} %get-tuple-element.399.refs_0_, bf16[128,1024]{1,0:T(8,128)(2,1)} %get-tuple-element.400.refs_1_, bf16[2,64,1024]{2,1,0:T(8,128)(2,1)} %get-tuple-element.401.refs_2_, ...), custom_call_target="tpu_custom_call" | custom-call | flops 4369999872 | bytes 14060000 | tf_op jit(solution)/shard_map/cond/branch_1_fun/triple_weight/pallas_call | solution.py:115
  262.7 3.2 output.1
  266.6 1.9 pair_sum.1
  268.5 9.6 %all-to-all-done.2 = bf16[8,128,256]{2,1,0:T(8,128)(2,1)} async-done(((bf16[8,128,256]{2,1,0:T(8,128)(2,1)}), bf16[8,128,256]{2,1,0:T(8,128)(2,1)}, u32[]{:S(2)}, u32[]{:S(2)}) %all-to-all-start.2) | async-done | bytes 524320 | tf_op jit(solution)/shard_map/cond/branch_1_fun/all_to_all | solution.py:894
  279.8 2.6 collective-permute-start.39
  282.5 12.6 %conditional.23 = (f32[128,1024]{1,0:T(8,128)S(1)}) conditional(s32[]{:T(128)} %bitcast.16, () %tuple.144, (s32[5]{0:T(128)S(1)}, bf16[8,128,256]{2,1,0:T(8,128)(2,1)}, bf16[1024,1536]{1,0:T(8,128)(2,1)}, f32[128,1024]{1,0:T(8,128)S(1)}) %tuple.222), branch_computations={%region_28.29_spmd, %region_29.30_spmd} | conditional | flops 6900000256 | bytes 24297228 | solution.py:788
  282.5 3.9 %tokens.2.own = bf16[128,1024]{1,0:T(8,128)(2,1)} custom-call(s32[5]{0:T(128)S(1)} %get-tuple-element.425.idx, bf16[8,128,256]{2,1,0:T(8,128)(2,1)} %get-tuple-element.426.got, bf16[1024,1536]{1,0:T(8,128)(2,1)} %get-tuple-element.427.weight), custom_call_target="tpu_custom_call" | custom-call | flops 4485000192 | bytes 14430000 | tf_op jit(solution)/shard_map/cond/branch_1_fun/tokens/pallas_call | solution.py:115
  286.8 6.5 %collective-permute-done.9.other = bf16[128,1024]{1,0:T(8,128)(2,1)S(1)} collective-permute-done((bf16[128,1024]{1,0:T(8,128)(2,1)}, bf16[128,1024]{1,0:T(8,128)(2,1)S(1)}, u32[]{:S(2)}, u32[]{:S(2)}) %collective-permute-start.9) | collective-permute-done | bytes 262176 | tf_op jit(solution)/shard_map/cond/branch_1_fun/ppermute | solution.py:41
  295.1 4.4 %all-to-all-start.4 = ((bf16[8,80,256]{2,1,0:T(8,128)(2,1)}), bf16[8,80,256]{2,1,0:T(8,128)(2,1)S(1)}, u32[]{:S(2)}, u32[]{:S(2)}) async-start(bf16[8,80,256]{2,1,0:T(8,128)(2,1)} %get-tuple-element.653), calls=%async_computation.4 | async-start | bytes 655360 | tf_op jit(solution)/shard_map/all_to_all | solution.py:1150
  299.5 8.5 %collective-permute-done.38.b2 = bf16[2,64,1280]{2,1,0:T(8,128)(2,1)} collective-permute-done((bf16[2,64,1280]{2,1,0:T(8,128)(2,1)S(1)}, bf16[2,64,1280]{2,1,0:T(8,128)(2,1)}, u32[]{:S(2)}, u32[]{:S(2)}) %collective-permute-start.38) | collective-permute-done | bytes 327712 | tf_op jit(solution)/shard_map/ppermute | solution.py:33
  308.0 2.4 line_sum.1
  310.9 5.1 %all-to-all-done.4.got = bf16[8,80,256]{2,1,0:T(8,128)(2,1)S(1)} async-done(((bf16[8,80,256]{2,1,0:T(8,128)(2,1)}), bf16[8,80,256]{2,1,0:T(8,128)(2,1)S(1)}, u32[]{:S(2)}, u32[]{:S(2)}) %all-to-all-start.4) | async-done | bytes 327712 | tf_op jit(solution)/shard_map/all_to_all | solution.py:1150
  316.7 1.9 triple_out.1
  319.3 2.2 columns.1
  321.6 3.0 spread.1
  (179 shorter events, 47.0 us)
Async XLA Ops:
  7.2 112.4 %all-gather.5.cloned.1.call-start = ((), (), s32[]{:S(2)}) async-start(), calls=%async_computation.5 | async-start | bytes 8912896 | tf_op jit(solution)/shard_map/all_gather | solution.py:840
  8.2 10.0 %collective-permute-start.18 = (bf16[64,1024]{1,0:T(8,128)(2,1)S(1)}, bf16[64,1024]{1,0:T(8,128)(2,1)S(1)}, u32[]{:S(2)}, u32[]{:S(2)}) collective-permute-start(bf16[64,1024]{1,0:T(8,128)(2,1)S(1)} %constant_dynamic-slice_fusion), channel_id=1, source_target_pairs={{0,8},{8,0},{16,24},{24,16},{1,9},{9,1},{17,25},{25,17},{2,10},{10... | collective-permute-start | bytes 393224 | tf_op jit(solution)/shard_map/ppermute | solution.py:33
  11.2 12.9 %collective-permute-start.19 = (bf16[64,1024]{1,0:T(8,128)(2,1)S(1)}, bf16[64,1024]{1,0:T(8,128)(2,1)S(1)}, u32[]{:S(2)}, u32[]{:S(2)}) collective-permute-start(bf16[64,1024]{1,0:T(8,128)(2,1)S(1)} %constant_dynamic-slice_fusion), channel_id=1, source_target_pairs={{0,16},{8,24},{16,0},{24,8},{1,17},{9,25},{17,1},{25,9},{2,18},{10... | collective-permute-start | bytes 393224 | tf_op jit(solution)/shard_map/ppermute | solution.py:33
  13.8 10.3 %collective-permute-start.20 = (bf16[64,1024]{1,0:T(8,128)(2,1)S(1)}, bf16[64,1024]{1,0:T(8,128)(2,1)S(1)}, u32[]{:S(2)}, u32[]{:S(2)}) collective-permute-start(bf16[64,1024]{1,0:T(8,128)(2,1)S(1)} %constant_dynamic-slice_fusion), channel_id=1, source_target_pairs={{0,24},{8,16},{16,8},{24,0},{1,25},{9,17},{17,9},{25,1},{2,26},{10... | collective-permute-start | bytes 393224 | tf_op jit(solution)/shard_map/ppermute | solution.py:33
  13.8 10.3 %collective-permute-start.17 = (bf16[128,1024]{1,0:T(8,128)(2,1)}, bf16[128,1024]{1,0:T(8,128)(2,1)S(1)}, u32[]{:S(2)}, u32[]{:S(2)}) collective-permute-start(bf16[128,1024]{1,0:T(8,128)(2,1)} %tokens.3), channel_id=1, source_target_pairs={{0,4},{4,0},{1,5},{5,1},{2,6},{6,2},{3,7},{7,3},{8,12},{12,8},{9,1... | collective-permute-start | bytes 786440 | tf_op jit(solution)/shard_map/ppermute | solution.py:41
  15.6 127.4 %copy-start.22 = (s32[5]{0:T(128)}, s32[5]{0:T(128)S(1)}, u32[]{:S(2)}) copy-start(s32[5]{0:T(128)S(1)} %stack.47.idx) | copy-start | bytes 64
  15.6 12.2 %copy-start.38 = (s32[4]{0:T(128)S(1)}, s32[4]{0:T(128)}, u32[]{:S(2)}) copy-start(s32[4]{0:T(128)} %param.46) | copy-start | bytes 52
  15.6 12.3 %copy-start.21 = (s32[128]{0:T(128)S(1)}, s32[128]{0:T(128)}, u32[]{:S(2)}) copy-start(s32[128]{0:T(128)} %param.48) | copy-start | bytes 1540
  18.1 9.8 %copy-start.13 = (bf16[64,1024]{1,0:T(8,128)(2,1)}, bf16[64,1024]{1,0:T(8,128)(2,1)S(1)}, u32[]{:S(2)}) copy-start(bf16[64,1024]{1,0:T(8,128)(2,1)S(1)} %collective-permute-done.18) | copy-start | bytes 393220
  24.2 258.3 %all-gather.7.cloned.1.call-start = ((), (), s32[]{:S(2)}) async-start(), calls=%async_computation.6 | async-start | bytes 3342336 | tf_op jit(solution)/shard_map/all_gather | solution.py:917
  24.3 8.8 %collective-permute-start.21 = (bf16[64,1024]{1,0:T(8,128)(2,1)S(1)}, bf16[64,1024]{1,0:T(8,128)(2,1)}, u32[]{:S(2)}, u32[]{:S(2)}) collective-permute-start(bf16[64,1024]{1,0:T(8,128)(2,1)S(1)} %collective-permute-done.18), channel_id=1, source_target_pairs={{0,4},{4,0},{1,5},{5,1},{2,6},{6,2},{3,7},{7,3},{8,12},{12,8},{9,1... | collective-permute-start | bytes 393224 | tf_op jit(solution)/shard_map/ppermute | solution.py:41
  25.8 7.2 %collective-permute-start.22 = (bf16[64,1024]{1,0:T(8,128)(2,1)S(1)}, bf16[64,1024]{1,0:T(8,128)(2,1)}, u32[]{:S(2)}, u32[]{:S(2)}) collective-permute-start(bf16[64,1024]{1,0:T(8,128)(2,1)S(1)} %collective-permute-done.19), channel_id=1, source_target_pairs={{0,4},{4,0},{1,5},{5,1},{2,6},{6,2},{3,7},{7,3},{8,12},{12,8},{9,1... | collective-permute-start | bytes 393224 | tf_op jit(solution)/shard_map/ppermute | solution.py:41
  26.4 6.7 %collective-permute-start.23 = (bf16[64,1024]{1,0:T(8,128)(2,1)S(1)}, bf16[64,1024]{1,0:T(8,128)(2,1)}, u32[]{:S(2)}, u32[]{:S(2)}) collective-permute-start(bf16[64,1024]{1,0:T(8,128)(2,1)S(1)} %collective-permute-done.20), channel_id=1, source_target_pairs={{0,4},{4,0},{1,5},{5,1},{2,6},{6,2},{3,7},{7,3},{8,12},{12,8},{9,1... | collective-permute-start | bytes 393224 | tf_op jit(solution)/shard_map/ppermute | solution.py:41
  33.0 46.4 %copy-start = (f32[1024,128]{1,0:T(8,128)}, f32[1024,128]{1,0:T(8,128)S(1)}, u32[]{:S(2)}) copy-start(f32[1024,128]{1,0:T(8,128)S(1)} %get-tuple-element.567) | copy-start | bytes 1572868
  33.0 46.4 %copy-start.2 = (f32[1024,128]{1,0:T(8,128)}, f32[1024,128]{1,0:T(8,128)S(1)}, u32[]{:S(2)}) copy-start(f32[1024,128]{1,0:T(8,128)S(1)} %get-tuple-element.580) | copy-start | bytes 1572868
  34.6 44.8 %collective-permute-start.26 = (bf16[2,64,1024]{2,1,0:T(8,128)(2,1)S(1)}, bf16[2,64,1024]{2,1,0:T(8,128)(2,1)}, u32[]{:S(2)}, u32[]{:S(2)}) collective-permute-start(bf16[2,64,1024]{2,1,0:T(8,128)(2,1)S(1)} %pad_maximum_fusion.2), channel_id=1, source_target_pairs={{0,1},{1,0},{2,3},{3,2},{4,5},{5,4},{6,7},{7,6},{8,9},{9,8},{10,11... | collective-permute-start | bytes 786440 | tf_op jit(solution)/shard_map/ppermute | solution.py:41
  37.1 42.3 %copy-start.7 = (bf16[2,64,1024]{2,1,0:T(8,128)(2,1)}, bf16[2,64,1024]{2,1,0:T(8,128)(2,1)S(1)}, u32[]{:S(2)}) copy-start(bf16[2,64,1024]{2,1,0:T(8,128)(2,1)S(1)} %pad_maximum_fusion.1) | copy-start | bytes 786436
  37.1 42.2 %collective-permute-start.25 = (bf16[2,64,1024]{2,1,0:T(8,128)(2,1)S(1)}, bf16[2,64,1024]{2,1,0:T(8,128)(2,1)}, u32[]{:S(2)}, u32[]{:S(2)}) collective-permute-start(bf16[2,64,1024]{2,1,0:T(8,128)(2,1)S(1)} %pad_maximum_fusion.1), channel_id=1, source_target_pairs={{0,1},{1,0},{2,3},{3,2},{4,5},{5,4},{6,7},{7,6},{8,9},{9,8},{10,11... | collective-permute-start | bytes 786440 | tf_op jit(solution)/shard_map/ppermute | solution.py:41
  39.5 39.9 %collective-permute-start.24 = (bf16[2,64,1024]{2,1,0:T(8,128)(2,1)}, bf16[2,64,1024]{2,1,0:T(8,128)(2,1)}, u32[]{:S(2)}, u32[]{:S(2)}) collective-permute-start(bf16[2,64,1024]{2,1,0:T(8,128)(2,1)} %pad_maximum_fusion), channel_id=1, source_target_pairs={{0,1},{1,0},{2,3},{3,2},{4,5},{5,4},{6,7},{7,6},{8,9},{9,8},{10,11... | collective-permute-start | bytes 786440 | tf_op jit(solution)/shard_map/ppermute | solution.py:41
  40.9 38.4 %copy-start.36 = (f32[3,512]{1,0:T(4,128)S(1)}, f32[3,512]{1,0:T(4,128)}, u32[]{:S(2)}) copy-start(f32[3,512]{1,0:T(4,128)} %param.50) | copy-start | bytes 18436
  73.2 2.7 collective-permute-start.10
  83.1 1.9 collective-permute-start
  108.3 11.3 %copy-start.16 = (bf16[128,1024]{1,0:T(8,128)(2,1)S(1)}, bf16[128,1024]{1,0:T(8,128)(2,1)}, u32[]{:S(2)}) copy-start(bf16[128,1024]{1,0:T(8,128)(2,1)} %tokens.3) | copy-start | bytes 786436
  108.3 11.3 %copy-start.37 = (f32[1024]{0:T(1024)S(1)}, f32[1024]{0:T(1024)}, u32[]{:S(2)}) copy-start(f32[1024]{0:T(1024)} %param.53) | copy-start | bytes 12292
  111.5 8.0 %collective-permute-start.1 = (bf16[128,1024]{1,0:T(8,128)(2,1)}, bf16[128,1024]{1,0:T(8,128)(2,1)}, u32[]{:S(2)}, u32[]{:S(2)}) collective-permute-start(bf16[128,1024]{1,0:T(8,128)(2,1)} %get-tuple-element.780), channel_id=1, source_target_pairs={{0,1},{1,0},{2,3},{3,2},{4,5},{5,4},{6,7},{7,6},{8,9},{9,8},{10,11... | collective-permute-start | bytes 786440 | tf_op jit(solution)/shard_map/cond/branch_1_fun/ppermute | solution.py:41
  119.5 202.0 %all-gather.9.cloned.1.call-start = ((), (), s32[]{:S(2)}) async-start(), calls=%async_computation.7 | async-start | bytes 1671168 | tf_op jit(solution)/shard_map/all_gather | solution.py:1059
  126.8 16.2 %collective-permute-start.27 = (bf16[288,1024]{1,0:T(8,128)(2,1)}, bf16[288,1024]{1,0:T(8,128)(2,1)}, u32[]{:S(2)}, u32[]{:S(2)}) collective-permute-start(bf16[288,1024]{1,0:T(8,128)(2,1)} %get-tuple-element.603), channel_id=1, source_target_pairs={{0,4},{4,0},{1,5},{5,1},{2,6},{6,2},{3,7},{7,3},{8,12},{12,8},{9,1... | collective-permute-start | bytes 1769480 | tf_op jit(solution)/shard_map/ppermute | solution.py:41
  128.0 15.0 %collective-permute-start.28 = (bf16[288,1024]{1,0:T(8,128)(2,1)}, bf16[288,1024]{1,0:T(8,128)(2,1)}, u32[]{:S(2)}, u32[]{:S(2)}) collective-permute-start(bf16[288,1024]{1,0:T(8,128)(2,1)} %get-tuple-element.604), channel_id=1, source_target_pairs={{0,2},{2,0},{1,3},{3,1},{4,6},{6,4},{5,7},{7,5},{8,10},{10,8},{9,1... | collective-permute-start | bytes 1769480 | tf_op jit(solution)/shard_map/ppermute | solution.py:41
  128.0 8.9 %collective-permute-start.2 = (bf16[128,1024]{1,0:T(8,128)(2,1)}, bf16[128,1024]{1,0:T(8,128)(2,1)S(1)}, u32[]{:S(2)}, u32[]{:S(2)}) collective-permute-start(bf16[128,1024]{1,0:T(8,128)(2,1)} %get-tuple-element.329.own), channel_id=1, source_target_pairs={{0,1},{1,0},{2,3},{3,2},{4,5},{5,4},{6,7},{7,6},{8,9},{9,8},{10,11... | collective-permute-start | bytes 786440 | tf_op jit(solution)/shard_map/cond/branch_1_fun/ppermute | solution.py:41
  143.0 17.3 %copy-start.24 = (s32[5]{0:T(128)}, s32[5]{0:T(128)S(1)}, u32[]{:S(2)}) copy-start(s32[5]{0:T(128)S(1)} %get-tuple-element.337.idx) | copy-start | bytes 64 | tf_op jit(solution)/shard_map/cond
  143.0 1.9 collective-permute-start.11
  143.1 5.0 %collective-permute-start.12 = (f32[4,4096]{1,0:T(4,128)S(1)}, f32[4,4096]{1,0:T(4,128)S(1)}, u32[]{:S(2)}, u32[]{:S(2)}) collective-permute-start(f32[4,4096]{1,0:T(4,128)S(1)} %get-tuple-element.338), channel_id=1, source_target_pairs={{0,4},{2,6},{4,0},{6,2},{1,5},{3,7},{5,1},{7,3},{8,12},{10,14},{12... | collective-permute-start | bytes 196616 | tf_op jit(solution)/shard_map/cond/branch_1_fun/ppermute | solution.py:37
  143.8 5.0 %collective-permute-start.13 = (f32[4,4096]{1,0:T(4,128)S(1)}, f32[4,4096]{1,0:T(4,128)S(1)}, u32[]{:S(2)}, u32[]{:S(2)}) collective-permute-start(f32[4,4096]{1,0:T(4,128)S(1)} %get-tuple-element.338), channel_id=1, source_target_pairs={{0,6},{2,4},{4,2},{6,0},{1,7},{3,5},{5,3},{7,1},{8,14},{10,12},{12... | collective-permute-start | bytes 196616 | tf_op jit(solution)/shard_map/cond/branch_1_fun/ppermute | solution.py:37
  148.9 11.5 %copy-start.15 = (f32[4,4096]{1,0:T(4,128)}, f32[4,4096]{1,0:T(4,128)S(1)}, u32[]{:S(2)}) copy-start(f32[4,4096]{1,0:T(4,128)S(1)} %add_add_fusion.t0) | copy-start | bytes 196612 | tf_op jit(solution)/shard_map/cond
  148.9 6.5 %collective-permute-start.14 = (f32[4,4096]{1,0:T(4,128)S(1)}, f32[4,4096]{1,0:T(4,128)S(1)}, u32[]{:S(2)}, u32[]{:S(2)}) collective-permute-start(f32[4,4096]{1,0:T(4,128)S(1)} %add_add_fusion.t0), channel_id=1, source_target_pairs={{0,8},{8,0},{16,24},{24,16},{1,9},{9,1},{17,25},{25,17},{2,10},{10... | collective-permute-start | bytes 196616 | tf_op jit(solution)/shard_map/cond/branch_1_fun/ppermute | solution.py:33
  148.9 9.7 %collective-permute-start.15 = (f32[4,4096]{1,0:T(4,128)S(1)}, f32[4,4096]{1,0:T(4,128)S(1)}, u32[]{:S(2)}, u32[]{:S(2)}) collective-permute-start(f32[4,4096]{1,0:T(4,128)S(1)} %add_add_fusion.t0), channel_id=1, source_target_pairs={{0,16},{8,24},{16,0},{24,8},{1,17},{9,25},{17,1},{25,9},{2,18},{10... | collective-permute-start | bytes 196616 | tf_op jit(solution)/shard_map/cond/branch_1_fun/ppermute | solution.py:33
  150.2 10.1 %collective-permute-start.16 = (f32[4,4096]{1,0:T(4,128)S(1)}, f32[4,4096]{1,0:T(4,128)S(1)}, u32[]{:S(2)}, u32[]{:S(2)}) collective-permute-start(f32[4,4096]{1,0:T(4,128)S(1)} %add_add_fusion.t0), channel_id=1, source_target_pairs={{0,24},{8,16},{16,8},{24,0},{1,25},{9,17},{17,9},{25,1},{2,26},{10... | collective-permute-start | bytes 196616 | tf_op jit(solution)/shard_map/cond/branch_1_fun/ppermute | solution.py:33
  173.0 16.2 %collective-permute-start.30 = (bf16[8,384,128]{2,1,0:T(8,128)(2,1)}, bf16[8,384,128]{2,1,0:T(8,128)(2,1)S(1)}, u32[]{:S(2)}, u32[]{:S(2)}) collective-permute-start(bf16[8,384,128]{2,1,0:T(8,128)(2,1)} %get-tuple-element.621), channel_id=1, source_target_pairs={{0,2},{2,0},{1,3},{3,1},{4,6},{6,4},{5,7},{7,5},{8,10},{10,8},{9,1... | collective-permute-start | bytes 2359304 | tf_op jit(solution)/shard_map/ppermute | solution.py:41
  175.1 14.2 %collective-permute-start.29 = (bf16[256,1024]{1,0:T(8,128)(2,1)}, bf16[256,1024]{1,0:T(8,128)(2,1)S(1)}, u32[]{:S(2)}, u32[]{:S(2)}) collective-permute-start(bf16[256,1024]{1,0:T(8,128)(2,1)} %get-tuple-element.620), channel_id=1, source_target_pairs={{0,4},{4,0},{1,5},{5,1},{2,6},{6,2},{3,7},{7,3},{8,12},{12,8},{9,1... | collective-permute-start | bytes 1572872 | tf_op jit(solution)/shard_map/ppermute | solution.py:41
  176.2 16.7 %collective-permute-start.31 = (bf16[288,1024]{1,0:T(8,128)(2,1)}, bf16[288,1024]{1,0:T(8,128)(2,1)}, u32[]{:S(2)}, u32[]{:S(2)}) collective-permute-start(bf16[288,1024]{1,0:T(8,128)(2,1)} %collective-permute-done.27), channel_id=1, source_target_pairs={{0,2},{2,0},{1,3},{3,1},{4,6},{6,4},{5,7},{7,5},{8,10},{10,8},{9,1... | collective-permute-start | bytes 1769480 | tf_op jit(solution)/shard_map/ppermute | solution.py:41
  176.2 16.7 %collective-permute-start.32 = (bf16[256,1024]{1,0:T(8,128)(2,1)}, bf16[256,1024]{1,0:T(8,128)(2,1)S(1)}, u32[]{:S(2)}, u32[]{:S(2)}) collective-permute-start(bf16[256,1024]{1,0:T(8,128)(2,1)} %get-tuple-element.624), channel_id=1, source_target_pairs={{0,2},{2,0},{1,3},{3,1},{4,6},{6,4},{5,7},{7,5},{8,10},{10,8},{9,1... | collective-permute-start | bytes 1572872 | tf_op jit(solution)/shard_map/ppermute | solution.py:41
  176.7 8.5 %collective-permute-start.3 = (bf16[128,1024]{1,0:T(8,128)(2,1)}, bf16[128,1024]{1,0:T(8,128)(2,1)S(1)}, u32[]{:S(2)}, u32[]{:S(2)}) collective-permute-start(bf16[128,1024]{1,0:T(8,128)(2,1)} %get-tuple-element.355.own), channel_id=1, source_target_pairs={{0,1},{1,0},{2,3},{3,2},{4,5},{5,4},{6,7},{7,6},{8,9},{9,8},{10,11... | collective-permute-start | bytes 786440 | tf_op jit(solution)/shard_map/cond/branch_1_fun/ppermute | solution.py:41
  189.3 3.6 %collective-permute-start.33 = (bf16[256,1024]{1,0:T(8,128)(2,1)S(1)}, bf16[256,1024]{1,0:T(8,128)(2,1)}, u32[]{:S(2)}, u32[]{:S(2)}) collective-permute-start(bf16[256,1024]{1,0:T(8,128)(2,1)S(1)} %collective-permute-done.29), channel_id=1, source_target_pairs={{0,2},{2,0},{1,3},{3,1},{4,6},{6,4},{5,7},{7,5},{8,10},{10,8},{9,1... | collective-permute-start | bytes 1572872 | tf_op jit(solution)/shard_map/ppermute | solution.py:41
  192.9 30.6 %copy-start.17 = (bf16[256,128]{1,0:T(8,128)(2,1)S(1)}, bf16[256,128]{1,0:T(8,128)(2,1)}, u32[]{:S(2)}) copy-start(bf16[256,128]{1,0:T(8,128)(2,1)} %get-tuple-element.634.value) | copy-start | bytes 196612
  193.0 30.5 %all-to-all-start.1 = ((bf16[8,448,128]{2,1,0:T(8,128)(2,1)}), bf16[8,448,128]{2,1,0:T(8,128)(2,1)}, u32[]{:S(2)}, u32[]{:S(2)}) async-start(bf16[8,448,128]{2,1,0:T(8,128)(2,1)} %get-tuple-element.362), calls=%async_computation.1 | async-start | bytes 1835008 | tf_op jit(solution)/shard_map/cond/branch_1_fun/all_to_all | solution.py:894
  200.5 16.5 %collective-permute-start.4 = (bf16[128,1024]{1,0:T(8,128)(2,1)S(1)}, bf16[128,1024]{1,0:T(8,128)(2,1)}, u32[]{:S(2)}, u32[]{:S(2)}) collective-permute-start(bf16[128,1024]{1,0:T(8,128)(2,1)S(1)} %get-tuple-element.363), channel_id=1, source_target_pairs={{0,4},{4,0},{1,5},{5,1},{2,6},{6,2},{3,7},{7,3},{8,12},{12,8},{9,1... | collective-permute-start | bytes 786440 | tf_op jit(solution)/shard_map/cond/branch_1_fun/ppermute | solution.py:41
  202.5 14.5 %collective-permute-start.5 = (bf16[128,1024]{1,0:T(8,128)(2,1)S(1)}, bf16[128,1024]{1,0:T(8,128)(2,1)}, u32[]{:S(2)}, u32[]{:S(2)}) collective-permute-start(bf16[128,1024]{1,0:T(8,128)(2,1)S(1)} %get-tuple-element.363), channel_id=1, source_target_pairs={{0,2},{2,0},{1,3},{3,1},{4,6},{6,4},{5,7},{7,5},{8,10},{10,8},{9,1... | collective-permute-start | bytes 786440 | tf_op jit(solution)/shard_map/cond/branch_1_fun/ppermute | solution.py:41
  223.5 6.6 %copy-start.1 = (f32[1024,128]{1,0:T(8,128)S(1)}, f32[1024,128]{1,0:T(8,128)}, u32[]{:S(2)}) copy-start(f32[1024,128]{1,0:T(8,128)} %copy-done) | copy-start | bytes 1572868
  223.5 6.6 %copy-start.3 = (f32[1024,128]{1,0:T(8,128)S(1)}, f32[1024,128]{1,0:T(8,128)}, u32[]{:S(2)}) copy-start(f32[1024,128]{1,0:T(8,128)} %copy-done.2) | copy-start | bytes 1572868
  223.5 6.6 %copy-start.4 = (f32[4,2,2,64,128]{4,3,2,1,0:T(8,128)S(1)}, f32[4,2,2,64,128]{4,3,2,1,0:T(8,128)}, u32[]{:S(2)}) copy-start(f32[4,2,2,64,128]{4,3,2,1,0:T(8,128)} %get-tuple-element.627) | copy-start | bytes 1572868
  225.7 20.8 %collective-permute-start.34 = (bf16[2,64,1024]{2,1,0:T(8,128)(2,1)}, bf16[2,64,1024]{2,1,0:T(8,128)(2,1)}, u32[]{:S(2)}, u32[]{:S(2)}) collective-permute-start(bf16[2,64,1024]{2,1,0:T(8,128)(2,1)} %get-tuple-element.635), channel_id=1, source_target_pairs={{0,8},{8,0},{16,24},{24,16},{1,9},{9,1},{17,25},{25,17},{2,10},{10... | collective-permute-start | bytes 786440 | tf_op jit(solution)/shard_map/ppermute | solution.py:33
  225.8 24.5 %collective-permute-start.35 = (bf16[2,64,1024]{2,1,0:T(8,128)(2,1)}, bf16[2,64,1024]{2,1,0:T(8,128)(2,1)}, u32[]{:S(2)}, u32[]{:S(2)}) collective-permute-start(bf16[2,64,1024]{2,1,0:T(8,128)(2,1)} %get-tuple-element.636), channel_id=1, source_target_pairs={{0,16},{8,24},{16,0},{24,8},{1,17},{9,25},{17,1},{25,9},{2,18},{10... | collective-permute-start | bytes 786440 | tf_op jit(solution)/shard_map/ppermute | solution.py:33
  227.3 23.0 %collective-permute-start.36 = (bf16[2,64,1024]{2,1,0:T(8,128)(2,1)}, bf16[2,64,1024]{2,1,0:T(8,128)(2,1)}, u32[]{:S(2)}, u32[]{:S(2)}) collective-permute-start(bf16[2,64,1024]{2,1,0:T(8,128)(2,1)} %get-tuple-element.637), channel_id=1, source_target_pairs={{0,24},{8,16},{16,8},{24,0},{1,25},{9,17},{17,9},{25,1},{2,26},{10... | collective-permute-start | bytes 786440 | tf_op jit(solution)/shard_map/ppermute | solution.py:33
  240.8 2.2 collective-permute-start.6
  240.9 5.5 %collective-permute-start.7 = (bf16[128,1024]{1,0:T(8,128)(2,1)}, bf16[128,1024]{1,0:T(8,128)(2,1)}, u32[]{:S(2)}, u32[]{:S(2)}) collective-permute-start(bf16[128,1024]{1,0:T(8,128)(2,1)} %get-tuple-element.396), channel_id=1, source_target_pairs={{0,2},{2,0},{1,3},{3,1},{4,6},{6,4},{5,7},{7,5},{8,10},{10,8},{9,1... | collective-permute-start | bytes 786440 | tf_op jit(solution)/shard_map/cond/branch_1_fun/ppermute | solution.py:41
  250.3 27.8 %all-to-all-start.2 = ((bf16[8,128,256]{2,1,0:T(8,128)(2,1)}), bf16[8,128,256]{2,1,0:T(8,128)(2,1)}, u32[]{:S(2)}, u32[]{:S(2)}) async-start(bf16[8,128,256]{2,1,0:T(8,128)(2,1)} %bitcast.15), calls=%async_computation.2 | async-start | bytes 1048576 | tf_op jit(solution)/shard_map/cond/branch_1_fun/all_to_all | solution.py:894
  262.6 3.2 collective-permute-start.8
  278.1 21.4 %collective-permute-start.37 = (bf16[2,64,1280]{2,1,0:T(8,128)(2,1)S(1)}, bf16[2,64,1280]{2,1,0:T(8,128)(2,1)}, u32[]{:S(2)}, u32[]{:S(2)}) collective-permute-start(bf16[2,64,1280]{2,1,0:T(8,128)(2,1)S(1)} %get-tuple-element.663), channel_id=1, source_target_pairs={{0,8},{8,0},{16,24},{24,16},{1,9},{9,1},{17,25},{25,17},{2,10},{10... | collective-permute-start | bytes 983048 | tf_op jit(solution)/shard_map/ppermute | solution.py:33
  278.8 29.2 %collective-permute-start.38 = (bf16[2,64,1280]{2,1,0:T(8,128)(2,1)S(1)}, bf16[2,64,1280]{2,1,0:T(8,128)(2,1)}, u32[]{:S(2)}, u32[]{:S(2)}) collective-permute-start(bf16[2,64,1280]{2,1,0:T(8,128)(2,1)S(1)} %get-tuple-element.664), channel_id=1, source_target_pairs={{0,16},{8,24},{16,0},{24,8},{1,17},{9,25},{17,1},{25,9},{2,18},{10... | collective-permute-start | bytes 983048 | tf_op jit(solution)/shard_map/ppermute | solution.py:33
  279.8 28.2 %collective-permute-start.39 = (bf16[2,64,1280]{2,1,0:T(8,128)(2,1)S(1)}, bf16[2,64,1280]{2,1,0:T(8,128)(2,1)}, u32[]{:S(2)}, u32[]{:S(2)}) collective-permute-start(bf16[2,64,1280]{2,1,0:T(8,128)(2,1)S(1)} %get-tuple-element.665), channel_id=1, source_target_pairs={{0,24},{8,16},{16,8},{24,0},{1,25},{9,17},{17,9},{25,1},{2,26},{10... | collective-permute-start | bytes 983048 | tf_op jit(solution)/shard_map/ppermute | solution.py:33
  286.4 6.8 %collective-permute-start.9 = (bf16[128,1024]{1,0:T(8,128)(2,1)}, bf16[128,1024]{1,0:T(8,128)(2,1)S(1)}, u32[]{:S(2)}, u32[]{:S(2)}) collective-permute-start(bf16[128,1024]{1,0:T(8,128)(2,1)} %tokens.2.own), channel_id=1, source_target_pairs={{0,1},{1,0},{2,3},{3,2},{4,5},{5,4},{6,7},{7,6},{8,9},{9,8},{10,11... | collective-permute-start | bytes 786440 | tf_op jit(solution)/shard_map/cond/branch_1_fun/ppermute | solution.py:41
  295.1 15.3 %copy-start.5 = (f32[128,1024]{1,0:T(8,128)}, f32[128,1024]{1,0:T(8,128)S(1)}, u32[]{:S(2)}) copy-start(f32[128,1024]{1,0:T(8,128)S(1)} %get-tuple-element.859) | copy-start | bytes 1572868
  295.1 20.9 %all-to-all-start.4 = ((bf16[8,80,256]{2,1,0:T(8,128)(2,1)}), bf16[8,80,256]{2,1,0:T(8,128)(2,1)S(1)}, u32[]{:S(2)}, u32[]{:S(2)}) async-start(bf16[8,80,256]{2,1,0:T(8,128)(2,1)} %get-tuple-element.653), calls=%async_computation.4 | async-start | bytes 655360 | tf_op jit(solution)/shard_map/all_to_all | solution.py:1150
  310.4 8.2 %collective-permute-start.40 = (bf16[64,2304]{1,0:T(8,128)(2,1)}, bf16[64,2304]{1,0:T(8,128)(2,1)S(1)}, u32[]{:S(2)}, u32[]{:S(2)}) collective-permute-start(bf16[64,2304]{1,0:T(8,128)(2,1)} %get-tuple-element.668), channel_id=1, source_target_pairs={{0,4},{4,0},{1,5},{5,1},{2,6},{6,2},{3,7},{7,3},{8,12},{12,8},{9,1... | collective-permute-start | bytes 884744 | tf_op jit(solution)/shard_map/ppermute | solution.py:41
  (22 other events, 59.1 us)
Sparse Core Ops, SparseCore 0:
  24.3 88.7 all-gather.4
  119.7 50.1 all-gather.6
  225.8 52.8 all-gather.8

commit v2 on v1

--- a/solution.py
+++ b/solution.py
@@ -96,8 +96,8 @@
 
 TAKES = dict(
     prep=2.5, heads=2.0, project=3.8, attend=7.5, branch=3.5, forward=7.7, second=3.6, middle=12.0, first_back=3.8, attend_back=9.8, triple=2.9, triple_weight=3.8, tokens=3.9,
-    tokens_sum=2.1, weights=5.2, output=2.3, core_sum=3.9, line_sum=2.7, columns=2.2, pair_sum=1.8,
-    triple_out=1.9, query_units=2.8, query_sum=1.9, query_c=2.5, query_back=1.6, spread=3.5,
+    tokens_sum=2.1, weights=5.2, output=2.3, core_sum=3.9, line_sum=2.7, pair=2.0, columns=2.2, pair_sum=1.8,
+    triple_out=1.9, query_units=2.8, query_back=3.5, spread=3.5,
 )
 
 
@@ -424,13 +424,14 @@
 
 def second_kernel(
     idx, own, other, first, bias, gain, shift, head, query, kdoc,
-    low, unitary, inverse, embed, unit, expo, totals,
+    low, unitary, inverse, embed, unit, expo, totals, message,
 ):
     value = first[...] + (pair(own, other) + bias[...])
     unitary[...], inverse[...] = normalize(value)
     low[...] = (unitary[...] * gain[...] + shift[...]).astype(LOW)
     embed[...] = dot_nn(low[...], head[...].astype(LOW))
     unit[...] = (embed[...] * unit_scale(embed[...])).astype(LOW)
+    message[...] = unit[...].astype(WIDE)
     expo[...] = jnp.exp(dot_nt(unit[...], query[...]) / SOFTMAX_TEMPER)
     totals[...] = dot_nn(member(idx, kdoc, totals.shape[0]), expo[...], PRECISE)
 
@@ -476,32 +477,62 @@
     return loss, (shifted / shifted_sum - chosen) / (totals * count)
 
 
-def core_sum_kernel(idx, pack, keep, got, out):
-    half = pack.shape[1]
-    for spot in range(pack.shape[0]):
-        out[spot, :half, :] = pack[spot]
-        out[spot, half:, :] = (keep[spot] + got[spot].astype(WIDE)).astype(LOW)
-
-
 def unit_back(value, grad):
     scale = unit_scale(value)
     along = jnp.sum(grad * value, axis=-1, keepdims=True)
     return scale * grad - value * (along * scale * scale * scale)
 
 
-def query_back_kernel(half, idx, got, value, out):
-    total = [got[spot, half:, :].astype(WIDE) for spot in range(NZ * 2)]
-    while len(total) > 1:
-        total = [a + b for a, b in zip(total[::2], total[1::2])]
-    total, shares = total[0], value.shape[0]
-    out[:shares, :] = unit_back(value[...].astype(WIDE), total[:shares]).astype(LOW)
-    out[shares:, :] = total[shares:].astype(LOW)
+def query_back_kernel(half, idx, kdoc0, kdoc1, coefficients, value, units, got, out):
+    shares = value.shape[0]
+    block = (idx[1] * 2 + idx[2]) * 2 + idx[3]
+    columns_here = pl.ds(pl.multiple_of(block * shares, shares), shares)
+    coefficient = coefficients[:, columns_here]
+    docs = coefficient.shape[0]
+    pads = jnp.zeros((-docs % 8, shares), WIDE)
+    coefficient = jnp.transpose(jnp.concatenate([coefficient, pads]) if docs % 8 else coefficient)
+    queries = value[...].astype(WIDE)
+    query = (queries * unit_scale(queries)).astype(LOW)
+    rows, group = kdoc0.shape[1], 4
+    count = units.shape[0] // rows
+
+    def add(at, total):
+        labels = []
+        for step in range(group):
+            block = at * group + step
+            spot = block // 2
+            labels.append(
+                jnp.where(block % 2 == idx[3], kdoc0[pl.ds(spot, 1), :], kdoc1[pl.ds(spot, 1), :])
+            )
+        row = jnp.concatenate(labels, axis=1)
+        unit = units[pl.ds(at * group * rows, group * rows), :].astype(LOW)
+        if docs <= 8:
+            chosen = jnp.zeros((shares, group * rows), WIDE)
+            for doc in range(docs):
+                chosen = jnp.where(row == doc, coefficient[:, doc : doc + 1], chosen)
+        else:
+            label = lax.broadcasted_iota(jnp.int32, (coefficient.shape[1], group * rows), 0)
+            chosen = dot_nn(coefficient, jnp.where(row == label, 1.0, 0.0), PRECISE)
+        expo = jnp.exp(dot_nt(query, unit) / SOFTMAX_TEMPER)
+        return total + dot_nn((chosen * expo).astype(LOW), unit)
+
+    steps, total = count // group, jnp.zeros(queries.shape, WIDE)
+    if steps <= 4:
+        for at in range(steps):
+            total = add(at, total)
+    else:
+        total = lax.fori_loop(0, steps, add, total)
+    out[:shares, :] = unit_back(queries, total).astype(LOW)
+    sums = [got[spot, half:, :].astype(WIDE) for spot in range(NZ * 2)]
+    while len(sums) > 1:
+        sums = [a + b for a, b in zip(sums[::2], sums[1::2])]
+    out[shares:, :] = sums[0].astype(LOW)
 
 
 def spread_kernel(idx, got, queries, head, *vectors):
     rows = got.shape[1]
     chunk = head.shape[0] // (NZ * 4)
-    shares = rows - 2 * chunk
+    shares = rows - chunk - 16
     pieces = []
     for i in range(NZ * 4):
         queries[i * shares : (i + 1) * shares, :] = got[i, :shares, :].astype(WIDE)
@@ -527,7 +558,7 @@
 def middle_kernel(
     count, idx, t0, t1, t2, t3, kdoc0, kdoc1, positive, expo, query, unit,
     embed, low, head, cotangent, unitary, inverse, gain, hidden_in, slabs,
-    grad_in, keep, send, part, loss, q0, q1,
+    grad_in, keep, send, part, loss, coefficients, sums0, sums1,
     similar, grad_low, grad_hidden_in, head_part, rows_part, expand, sems1, contract, sems2,
 ):
     copy1 = [slab_copy(slabs, 0, expand, sems1)]
@@ -536,6 +567,7 @@
     totals = (t0[...] + t1[...]) + (t2[...] + t3[...])
     value, coefficient = loss_of(count, totals, (kdoc0, kdoc1), positive[...])
     loss[...] = jnp.broadcast_to(value, loss.shape)
+    coefficients[...] = coefficient
     here = member(idx, kdoc0, totals.shape[0])
     similar[...] = (dot_tn(here, coefficient, PRECISE) * expo[...]).astype(LOW)
     grad_embed = unit_back(embed[...], dot_nn(similar[...], query[...])).astype(LOW)
@@ -566,19 +598,15 @@
             rows_part[at : at + 1, :] = value[:, i * PAIR : (i + 1) * PAIR]
             at += 1
     chunk = width // (NZ * 4)
-    shares = q0.shape[1] - 2 * chunk
-    for z in range(NZ * 2):
-        for c, out in enumerate((q0, q1)):
-            at = z * 2 + (idx[3] ^ c)
-            columns_here = pl.ds(pl.multiple_of(at * shares, shares), shares)
-            out[z, :shares, :] = dot_tn(similar[:, columns_here], unit[...]).astype(out.dtype)
-            out[z, shares : shares + chunk, :] = head_part[
+    for spot in range(NZ * 2):
+        for out, c in ((sums0, idx[3]), (sums1, 1 - idx[3])):
+            at = spot * 2 + c
+            out[spot, :chunk, :] = head_part[
                 pl.ds(pl.multiple_of(at * chunk, chunk), chunk), :
             ].astype(out.dtype)
-            out[z, shares + chunk : shares + chunk + 16, :] = rows_part[
-                pl.ds(pl.multiple_of(at * 16, 16), 16), :
-            ].astype(out.dtype)
-            out[z, shares + chunk + 16 :, :] = jnp.zeros((chunk - 16, PAIR), out.dtype)
+            out[spot, chunk:, :] = rows_part[pl.ds(pl.multiple_of(at * 16, 16), 16), :].astype(
+                out.dtype
+            )
 
 
 def slab_products(idx, left, right, outs):
@@ -595,17 +623,27 @@
 
 
 def weights_kernel(idx, f0, f1, f2, f3, g0, g1, g2, g3, *refs):
-    (*outs, left, right) = refs
+    keep0, send0, keep1, send1, left, right = refs
     rows = g0.shape[0] // 2
     firsts, grads = (f0, f1, f2, f3), (g0, g1, g2, g3)
-    for lefts, rights, group in ((grads, firsts, outs[:4]), (firsts, grads, outs[4:])):
+    for keep, send, lefts, rights in ((keep0, send0, grads, firsts), (keep1, send1, firsts, grads)):
         for i in range(4):
             left[i * rows : (i + 1) * rows, :] = lefts[i][:rows, :]
             right[i * rows : (i + 1) * rows, :] = rights[i][rows : 2 * rows, :]
-        slab_products(idx, left, right[...], group)
-
-
-def output_kernel(idx, f0, f1, f2, f3, g0, g1, g2, g3, e1, e2, e3, own, s1, s2, s3, left, right):
+        slab_products(idx, left, right[...], [keep.at[0], send.at[0], keep.at[1], send.at[1]])
+
+
+def pair_kernel(idx, *refs):
+    count = (len(refs) - 1) // 3
+    gots, owns, send, at = refs[: 2 * count], refs[2 * count : -1], refs[-1], 0
+    for i, own in enumerate(owns):
+        keep, got, span = gots[2 * i], gots[2 * i + 1], own.shape[-1]
+        own[...] = keep[0] + got[0].astype(WIDE)
+        send[:, :, at : at + span] = (keep[1] + got[1].astype(WIDE)).astype(LOW)
+        at += span
+
+
+def output_kernel(idx, f0, f1, f2, f3, g0, g1, g2, g3, keep, send, left, right):
     rows, width = g0.shape
     few = rows * QUAD // width
     for i, (f, g) in enumerate(zip((f0, f1, f2, f3), (g0, g1, g2, g3))):
@@ -614,26 +652,20 @@
             right[i * rows + j * few : i * rows + (j + 1) * few, :] = f[
                 2 * rows :, j * QUAD : (j + 1) * QUAD
             ]
-    span = e1.shape[-1]
-    for out, expand in ((s1, e1), (s2, e2), (s3, e3)):
-        out[:, :, :span] = expand[...]
-    slab_products(
-        idx, left, right[...], [own] + [out.at[:, :, span:] for out in (s1, s2, s3)]
-    )
-
-
-def line_sum_kernel(idx, c0, c1, c2, c3, e0, o0, b1, b2, b3, keep, keep_out, send):
-    span = c0.shape[2]
-    for x in range(2):
-        wide = c0[x] + c1[x].astype(WIDE) + (c2[x].astype(WIDE) + c3[x].astype(WIDE))
-        both = b1[x].astype(WIDE) + (b2[x].astype(WIDE) + b3[x].astype(WIDE))
-        expand, thin = e0[x] + both[:, :span], o0[x] + both[:, span:]
-        if x == 0:
-            keep[0], keep[1], keep_out[...] = wide, expand, thin
-        else:
-            send[:, :span] = wide.astype(LOW)
-            send[:, span : 2 * span] = expand.astype(LOW)
-            send[:, 2 * span :] = thin.astype(LOW)
+    slab_products(idx, left, right[...], [keep.at[0], send.at[0], keep.at[1], send.at[1]])
+
+
+def line_sum_kernel(idx, own0, got0, own1, own2, got, keep, keep_out, send):
+    at = 0
+    for own, other, out in (
+        (own0, got0[...], keep.at[0]),
+        (own1, got[:, :, : own1.shape[-1]], keep.at[1]),
+        (own2, got[:, :, own1.shape[-1] :], keep_out),
+    ):
+        span = own.shape[-1]
+        out[...] = own[0] + other[0].astype(WIDE)
+        send[:, at : at + span] = (own[1] + other[1].astype(WIDE)).astype(LOW)
+        at += span
 
 
 def columns_kernel(idx, keep, keep_out, got, contract, expand, output):
@@ -647,7 +679,7 @@
 
 
 def first_back_kernel(
-    pieces, idx, own, other, grad_second_in, unitary, inverse, gain, *refs
+    pieces, idx, own, other, grad_second_in, unitary, inverse, gain, sums0, sums1, *refs
 ):
     slabs, (grad_in, grad_low, vectors, pack, held, sems) = refs[:pieces], refs[pieces:]
     copy = piece_copies(idx, slabs, held, sems)
@@ -660,11 +692,12 @@
     vectors[1:2, :] = column_sum(grad_first * unitary[...])
     vectors[2:3, :] = column_sum(grad_first)
     grad = dot_nn(grad_low[...], finish(copy, held)).astype(LOW)
-    half = pack.shape[1]
+    half = grad.shape[0] // 2
     for h in range(NZ * 2):
         lanes = slice(h * HEAD_DIM, (h + 1) * HEAD_DIM)
-        pack[h, :, :HEAD_DIM] = grad[:half, lanes]
-        pack[h, :, HEAD_DIM:] = grad[half:, lanes]
+        pack[h, :half, :HEAD_DIM] = grad[:half, lanes]
+        pack[h, :half, HEAD_DIM:] = grad[half:, lanes]
+        pack[h, half:, :] = (sums0[h] + sums1[h].astype(WIDE)).astype(LOW)
 
 
 def triple_kernel(idx, dq, dkv, got, cosine, sine, out):
@@ -726,12 +759,15 @@
             row += 1
 
 
-def tokens_kernel(idx, got, weight, part, group):
+def tokens_kernel(idx, got, message, part, group, held, sems):
+    copy = slab_copy(message, 0, held, sems)
+    copy.start()
     for h in range(NZ * 2):
         for p, lane in enumerate(LANES):
             at = (p * NZ * 2 + h) * HEAD_DIM
             group[:, at : at + HEAD_DIM] = got[h, :, lane : lane + HEAD_DIM]
-    part[...] = dot_nt(group[...], weight[...]).astype(LOW)
+    copy.wait()
+    part[...] = dot_nt(group[...], held[...]).astype(LOW)
 
 
 def tokens_sum_kernel(idx, own, other, grad, out):
@@ -836,10 +872,14 @@
     rank = jnp.arange(NZ * 2, dtype=jnp.int32) * 2
     shares = query_vecs.shape[0] // (NZ * 4)
     by_z = list(lax.optimization_barrier((*by_z, heads, own_other))[:NZ])
-    by_x = [flip(piece, "x") for piece in by_z[1:]]
     gathered = lax.all_gather(after(low_slab, *by_z[1:]), BLK, axis=0, tiled=True)
 
-    def tables_stage():
+    def heads_stage():
+        got = lax.all_to_all(heads, ("z", "x"), 0, 0)
+        sheets = [tokens, own_other]
+        for piece in by_z[1:]:
+            two = jnp.stack([piece, flip(piece, "x")])
+            sheets += [two, flip(two, "y")]
         own_places = (mo * NZ * 4 + rank + mc)[:, None] + where[None, :]
         own_doc, own_position = doc_layout(doc_lengths, own_places.reshape(-1))
         lane = jnp.arange(PAIR) % (HEAD_DIM // 2)
@@ -851,29 +891,19 @@
             query_kernel,
             "query_units",
             index,
-            (after(query_vecs, by_z[1]),),
+            (query_vecs,),
             [shape(query_vecs.shape, LOW), shape((shares, proj), LOW)],
         )
         positive = line(jnp.repeat(positives, query_vecs.shape[0] // queries_count))
-        return tables, list(units), positive, own_doc.reshape(NZ, 2, 2, half, 1)
-
-    (cosine, sine), (query_unit, own_queries), positive, qdoc = stage(tables_stage)
+        got = after(got, sheets[3], sheets[5], sheets[7], tables[0], units[0])
+        head = head_weights(got, flip(got, "c"))
+        return head, sheets[2:], tables, list(units), positive, own_doc.reshape(NZ, 2, 2, half, 1)
+
+    head, sheets, (cosine, sine), (query_unit, own_queries), positive, qdoc = stage(heads_stage)
+    head_triple, kdoc0, kdoc1, outs = head
+    pieces = len(outs)
+    sheets = [tokens, own_other] + sheets
     positive, qdoc = lax.optimization_barrier((positive, qdoc))
-    by_x = list(lax.optimization_barrier((*by_x, cosine))[:3])
-
-    sheets = [tokens, own_other]
-    for piece, turned in zip(by_z[1:], by_x):
-        two = jnp.stack([piece, turned])
-        sheets += [two, flip(two, "y")]
-
-    def head_stage():
-        got = lax.all_to_all(after(heads, sheets[2], sheets[4], sheets[6]), ("z", "x"), 0, 0)
-        return head_weights(got, flip(got, "c"))
-
-    head_triple, kdoc0, kdoc1, outs = stage(head_stage)
-    pieces = len(outs)
-    sheets = list(lax.optimization_barrier((*sheets, head_triple))[: len(sheets)])
-
     count = NZ * 2 * rows
 
     def project_stage():
@@ -950,11 +980,12 @@
                 part, flip(part, "y"), first, line(contract_bias), line(second_gain),
                 line(second_shift), head_weight, query_unit, kdoc0,
             ),
-            [low_rows, wide_rows, thin_rows, shape((rows, proj), WIDE), shape((rows, proj), LOW)]
-            + [shape((rows, my_tokens), WIDE), shape((docs, my_tokens), WIDE)],
+            [low_rows, wide_rows, thin_rows] + [shape((rows, proj), t) for t in (WIDE, LOW)]
+            + [shape((rows, my_tokens), WIDE), shape((docs, my_tokens), WIDE)]
+            + [shape((rows, proj), WIDE)],
         )
 
-    second_low, unitary2, inverse2, embed, unit_low, expo, totals = stage(second_stage)
+    second_low, unitary2, inverse2, embed, unit_low, expo, totals, message = stage(second_stage)
     firsts = [first_keep, first_other, first_across, flip(first_other, "c")]
     totals = after(totals, first_other, first_across)
 
@@ -962,7 +993,7 @@
         return (own + one) + (two + three)
 
     chunk = width // (NZ * 4)
-    message = (NZ * 2, shares + 2 * chunk, proj)
+    sums_dims = (NZ * 2, chunk + 16, proj)
     def middle_stage():
         sums = sum_outer(tree(totals, *[xor_s(totals, m) for m in (1, 2, 3)]))
         return whole(
@@ -976,7 +1007,8 @@
             ),
             [wide_rows]
             + [shape((2 * rows, width), LOW)] * 2
-            + [low_rows, shape((8, proj), WIDE), shape(message, WIDE), shape(message, LOW)],
+            + [low_rows, shape((8, proj), WIDE), shape((docs, my_tokens), WIDE)]
+            + [shape(sums_dims, WIDE), shape(sums_dims, LOW)],
             [
                 pltpu.VMEM((rows, my_tokens), LOW),
                 pltpu.VMEM((rows, width), LOW),
@@ -988,33 +1020,30 @@
             (gathered,),
         )
 
-    grad_second_in, keep, send, part, loss, *query_parts = stage(middle_stage)
-
+    grad_second_in, keep, send, part, loss, coefficients, sums_own, sums_send = stage(middle_stage)
+
+    triple_low, part = lax.optimization_barrier((triple_low, part))
+    units = lax.all_gather(after(message, part), BLK, axis=0, tiled=True)
     keep_other, keep_across = flip(send, "x"), flip(keep, "c")
-    message_other = flip(query_parts[1], "c")
 
     def first_stage():
         return whole(
             partial(first_back_kernel, pieces),
             "first_back",
             index,
-            (part, flip(part, "y"), grad_second_in, unitary1, inverse1, line(first_gain)),
-            [wide_rows, low_rows, shape((8, width), WIDE), shape((NZ * 2, half, PAIR), LOW)],
+            (
+                part, flip(part, "y"), grad_second_in, unitary1, inverse1, line(first_gain),
+                sums_own, flip(sums_send, "c"),
+            ),
+            [wide_rows, low_rows, shape((8, width), WIDE)]
+            + [shape((NZ * 2, half + chunk + 16, PAIR), LOW)],
             piece_scratch(width, 2 * QUAD),
             outs,
         )
 
     grad_first_in, grad_branch, vectors1, pack = stage(first_stage)
-    keep_other, message_other = lax.optimization_barrier((keep_other, message_other, grad_branch))[:2]
+    keep_other = after(keep_other, grad_branch)
     grads = [keep, keep_other, keep_across, flip(keep_other, "c")]
-    pack = whole(
-        core_sum_kernel,
-        "query_c",
-        index,
-        (pack, query_parts[0], message_other),
-        [shape((NZ * 2, half + message[1], proj), LOW)],
-    )[0]
-
     dims, dims_out = (2, slab, quarter), (2, slab, QUAD)
     dims_both = (2, slab, quarter + QUAD)
     left_right = [pltpu.VMEM((4 * rows, width), LOW)]
@@ -1031,33 +1060,26 @@
 
     def weights_stage():
         got = to_blocks(pack)
-        got = got, flip(grad_branch, "x"), flip(grad_branch, "c")
+        other = flip(grad_branch, "x")
+        got = got, [grad_branch, other, flip(grad_branch, "c"), flip(other, "c")]
         if outer == 1:
             parts = whole(
                 weights_kernel,
                 "weights",
                 index,
                 (*firsts, *grads),
-                ([shape(dims, WIDE)] + [shape(dims, LOW)] * 3) * 2,
+                [shape((2,) + dims, WIDE), shape((2,) + dims, LOW)] * 2,
                 left_right * 2,
             )
             return got, list(parts)
         top, mid = slice(0, rows), slice(rows, 2 * rows)
         contract = parts_of([g[top] for g in grads], [f[mid] for f in firsts])
         expand = parts_of([f[top] for f in firsts], [g[mid] for g in grads])
-        return got, low_parts(contract) + low_parts(expand)
-
-    (grad_out, branch_other, branch_across), weight_parts = stage(weights_stage)
-    contract_parts, expand_parts = weight_parts[:4], weight_parts[4:]
-    mine = whole(
-        partial(query_back_kernel, half),
-        "query_back",
-        index,
-        (sum_outer(grad_out), own_queries),
-        [shape(message[1:], LOW)],
-    )[0]
-    spread = lax.all_gather(mine, ("z", "x", "c"))
-    contract_in = over_z([mine, *lax.optimization_barrier((*contract_parts[1:], mine))[:3]])[1:]
+        return got, [part for p in (contract, expand) for part in (p[::2], p[1::2].astype(LOW))]
+
+    (grad_out, branches), weight_parts = stage(weights_stage)
+    contract_keep, contract_send, expand_keep, expand_send = weight_parts
+    contract_got, expand_got = xor_z(contract_send, 1), xor_z(expand_send, 1)
 
     def attend_stage():
         grad_query, dkv0, dkv1 = attend_back(
@@ -1071,12 +1093,22 @@
             (grad_query.reshape(count, PAIR), dkv0, flip(dkv1, "c"), cosine, sine),
             [shape((count, QUAD), LOW)],
         )[0]
-        return triple, flip(branch_other, "c")
-
-    grad_triple, branch_last = stage(attend_stage)
-    branches = [grad_branch, branch_other, branch_across, branch_last]
-    grad_triple, *contract_in = lax.optimization_barrier((grad_triple, *contract_in))
-
+        mine = whole(
+            partial(query_back_kernel, half),
+            "query_back",
+            index,
+            (kdoc0, kdoc1, coefficients, own_queries, units, sum_outer(grad_out)),
+            [shape((shares + chunk + 16, proj), LOW)],
+        )[0]
+        return triple, mine
+
+    grad_triple, mine = stage(attend_stage)
+    grad_triple, contract_got = lax.optimization_barrier((grad_triple, contract_got))
+    contract_own, contract_send = whole(
+        pair_kernel, "pair", index, (contract_keep, contract_got), [shape(dims, t) for t in (WIDE, LOW)]
+    )
+    contract_got = xor_z(contract_send, 2)
+    grad_triple = after(grad_triple, contract_own)
     dims_triple = (NZ * 2, slab + 16, QUAD)
     vector = shape((width // PAIR, PAIR), WIDE)
 
@@ -1109,13 +1141,13 @@
                 output_kernel,
                 "output",
                 index,
-                (*firsts, *branches, *expand_parts[1:]),
-                [shape(dims_out, WIDE)] + [shape(dims_both, LOW)] * 3,
+                (*firsts, *branches),
+                [shape((2,) + dims_out, t) for t in (WIDE, LOW)],
                 left_right + [pltpu.VMEM((4 * rows, QUAD), LOW)],
             )
         wide = [f[2 * rows :].reshape(few, 4, QUAD).transpose(1, 0, 2).reshape(rows, QUAD) for f in firsts]
-        parts = low_parts(parts_of(branches, wide))
-        return parts[:1] + [jnp.concatenate(both, axis=-1) for both in zip(expand_parts[1:], parts[1:])]
+        parts = parts_of(branches, wide)
+        return parts[::2], parts[1::2].astype(LOW)
 
     def triple_stage():
         block_triple = to_blocks(grad_triple.reshape(NZ * 2, rows, QUAD))
@@ -1124,55 +1156,69 @@
         packed = whole(
             pair_sum_kernel, "pair_sum", index, (keep, flip(send, "c")), [shape(dims_triple, LOW)]
         )[0]
-        return block_triple, packed, list(output_parts)
-
-    block_triple, packed, output_parts = stage(triple_stage)
-    both_in = over_z([expand_parts[0]] + list(output_parts[1:]))[1:]
+        return block_triple, packed, output_parts[0], xor_z(output_parts[1], 1)
+
+    block_triple, packed, output_keep, output_got = stage(triple_stage)
+    block_triple, contract_got, expand_got = lax.optimization_barrier(
+        (block_triple, contract_got, expand_got)
+    )
+    expand_own, output_own, both_send = whole(
+        pair_kernel,
+        "pair",
+        index,
+        (expand_keep, expand_got, output_keep, output_got),
+        [shape(dims, WIDE), shape(dims_out, WIDE), shape(dims_both, LOW)],
+    )
+    both_got = xor_z(both_send, 2)
+    block_triple = after(block_triple, expand_own)
+    spread = lax.all_gather(after(mine, expand_own), ("z", "x", "c"))
 
     def tokens_stage():
         part = whole(
             tokens_kernel,
             "tokens",
             index,
-            (block_triple, triple_low),
+            (block_triple,),
             [low_rows],
-            [pltpu.VMEM((rows, 6 * QUAD), LOW)],
+            [pltpu.VMEM((rows, 6 * QUAD), LOW)] + slab_scratch(width, 6 * QUAD),
+            (triple_low,),
         )[0]
-        return whole(
+        tokens_grad = whole(
             tokens_sum_kernel, "tokens_sum", index, (part, flip(part, "y"), grad_first_in), [wide_rows]
         )[0]
-
-    tokens_grad = stage(tokens_stage)
+        return tokens_grad, lax.all_to_all(after(packed, part), ("z", "x"), 0, 0)
+
+    tokens_grad, packed = stage(tokens_stage)
+    contract_own, spread = after(contract_own, tokens_grad), after(spread, tokens_grad)
+    keep, keep_out, send = whole(
+        line_sum_kernel,
+        "line_sum",
+        index,
+        (contract_own, contract_got, expand_own, output_own, both_got),
+        [shape((2, slab, quarter), WIDE), shape((slab, QUAD), WIDE), shape((slab, 2 * quarter + QUAD), LOW)],
+    )
+    queries_grad, head_grad, contract_bias_grad, gain_two, shift_two, expand_bias_grad = whole(
+        spread_kernel,
+        "spread",
+        index,
+        (spread.reshape(NZ * 4, -1, proj),),
+        [shape((query_vecs.shape[0], proj), WIDE), shape((width, proj), WIDE)]
+        + [vector] * 3
+        + [shape((span // PAIR, PAIR), WIDE)],
+    )
     triple_grad, triple_bias_grad, output_bias_grad, gain_one, shift_one = whole(
         triple_out_kernel,
         "triple_out",
         index,
-        (lax.all_to_all(after(packed, tokens_grad), ("z", "x"), 0, 0),),
+        (after(packed, send),),
         [shape((3, slab, 2 * QUAD), WIDE), shape((3, 2 * QUAD), WIDE)] + [vector] * 3,
-    )
-    contract_own, spread = after(contract_parts[0], tokens_grad), after(spread, tokens_grad)
-    keep, keep_out, send = whole(
-        line_sum_kernel,
-        "line_sum",
-        index,
-        (contract_own, *contract_in, expand_parts[0], output_parts[0], *both_in),
-        [shape((2, slab, quarter), WIDE), shape((slab, QUAD), WIDE), shape((slab, 2 * quarter + QUAD), LOW)],
     )
     contract_grad, expand_grad, output_grad = whole(
         columns_kernel,
         "columns",
         index,
-        (keep, keep_out, flip(send, "x")),
+        (keep, keep_out, after(flip(send, "x"), queries_grad)),
         [shape((slab, n), WIDE) for n in (span, span, 2 * QUAD)],
-    )
-    queries_grad, head_grad, contract_bias_grad, gain_two, shift_two, expand_bias_grad = whole(
-        spread_kernel,
-        "spread",
-        index,
-        (spread.reshape(NZ * 4, *message[1:]),),
-        [shape((query_vecs.shape[0], proj), WIDE), shape((width, proj), WIDE)]
-        + [vector] * 3
-        + [shape((span // PAIR, PAIR), WIDE)],
     )
 
     return (

time: 335 us -> 319 us (0.952)
  blocking collectives: 47.1 us -> 11.7 us
  waiting for transfers between devices: 95.6 us -> 115 us
    all_to_all x1 -> x0, blocking collectives: 32.2 us -> none  [head_stage(): lax.all_to_all(after(heads, sheets[2], sheets[4], sheets[6]), ('z', 'x'),...]
    all_to_all x1 -> x2, waiting for transfers between devices: 5.05 us -> 25 us  [the longest x1 16.8 us: heads_stage(): got = lax.all_to_all(heads, ('z', 'x'), 0, 0)]
    all_gather x1 -> x2, waiting for transfers between devices: 0.01 us -> 11.3 us  [the longest x1 9.55 us: shards(): spread = lax.all_gather(after(mine, expand_own), ('z', 'x', 'c'))]
    ppermute x12 -> x11, waiting for transfers between devices: 25.4 us -> 16.3 us  [xor_z(): return lax.ppermute(value, 'z', [(i, i ^ mask) for i in FOUR])]
    all_to_all x2, waiting for transfers between devices: 16.2 us -> 10.8 us  [to_blocks(): lax.all_to_all(value.reshape((NZ * 2,) + value.shape[-2:]), ('z', 'x'), 0...]
    all_to_all x2, starting transfers between devices: 15.1 us -> 10.9 us  [to_blocks(): lax.all_to_all(value.reshape((NZ * 2,) + value.shape[-2:]), ('z', 'x'), 0...]
    all_to_all x1 -> x2, starting transfers between devices: 4.38 us -> 8.32 us  [the longest x1 4.23 us: heads_stage(): got = lax.all_to_all(heads, ('z', 'x'), 0, 0)]
    ppermute x12 -> x11, starting transfers between devices: 19 us -> 16.7 us  [xor_z(): return lax.ppermute(value, 'z', [(i, i ^ mask) for i in FOUR])]
  transfers between devices with their start and end apart: 47 -> 48, of which waited for: 20 -> 26; matrix products, arithmetic and copies ran while one was open for 3% -> 4% of each run, Pallas kernels for 28% -> 29%
where the time goes in v2:
time: 319 us; the launch traced here: 317 us
  waiting for transfers between devices  115 us (36%)
  Pallas kernels  96.4 us (30%)
  starting transfers between devices  59.8 us (19%)
  between operations  14.1 us (4%)
  local copies, waits for them, and re-layouts  12.7 us (4%)
  blocking collectives  11.7 us (4%)
  other arithmetic  7.33 us (2%)
    pallas_call x23, Pallas kernels, whole(): pl.pallas_call(kernel, in_specs=[pl.BlockSpec(memory_space=pltpu.SMEM)] +...  79.2 us
    ppermute x26, waiting for transfers between devices, flip(): return lax.ppermute(value, axis, [(0, 1), (1, 0)])  44.9 us
    ppermute x26, starting transfers between devices, flip(): return lax.ppermute(value, axis, [(0, 1), (1, 0)])  21.8 us
    all_to_all x1, waiting for transfers between devices, heads_stage(): got = lax.all_to_all(heads, ('z', 'x'), 0, 0)  16.8 us
    ppermute x11, starting transfers between devices, xor_z(): return lax.ppermute(value, 'z', [(i, i ^ mask) for i in FOUR])  16.7 us
    ppermute x11, waiting for transfers between devices, xor_z(): return lax.ppermute(value, 'z', [(i, i ^ mask) for i in FOUR])  16.3 us
    all_to_all x1, blocking collectives, to_blocks(): lax.all_to_all(value.reshape((NZ * 2,) + value.shape[-2:]), ('z', 'x'), 0...  11.7 us
    all_to_all x2, starting transfers between devices, to_blocks(): lax.all_to_all(value.reshape((NZ * 2,) + value.shape[-2:]), ('z', 'x'), 0...  10.9 us
  transfers between devices with their start and end apart: 48, of which 26 were waited for; matrix products, arithmetic and copies ran while one was open for 4% of the time, Pallas kernels for 29%

profile of v2, /device:TPU:0, one launch (start us, length us, event | category | flops | bytes accessed | tf_op | source)
XLA Modules:
  0.0 317.4 jit_solution(9175462648033197152)
XLA Ops:
  8.2 3.1 collective-permute-start.26
  11.2 2.6 collective-permute-start.27
  15.6 2.7 prep.1
  18.4 5.8 %collective-permute-done.27 = bf16[64,1024]{1,0:T(8,128)(2,1)S(1)} collective-permute-done((bf16[64,1024]{1,0:T(8,128)(2,1)S(1)}, bf16[64,1024]{1,0:T(8,128)(2,1)S(1)}, u32[]{:S(2)}, u32[]{:S(2)}) %collective-permute-start.27) | collective-permute-done | bytes 131104 | tf_op jit(solution)/shard_map/ppermute | solution.py:33
  24.4 51.7 %conditional.11 = (bf16[1024,256]{1,0:T(8,128)(2,1)S(1)}, s32[8,128]{1,0:T(8,128)S(1)}, s32[8,128]{1,0:T(8,128)S(1)}, bf16[8,208,256]{2,1,0:T(8,128)(2,1)}, bf16...) conditional(s32[]{:T(128)} %bitcast.20, () %tuple.121, ...), branch_computations={%region_0.0_spmd, %region_1.7_spmd} | conditional | flops 5520711680 | bytes 31215688 | solution.py:824
  28.0 4.2 %all-to-all-start.4 = ((bf16[8,208,256]{2,1,0:T(8,128)(2,1)}), bf16[8,208,256]{2,1,0:T(8,128)(2,1)}, u32[]{:S(2)}, u32[]{:S(2)}) async-start(bf16[8,208,256]{2,1,0:T(8,128)(2,1)} %get-tuple-element.250), calls=%async_computation.4 | async-start | bytes 1703936 | tf_op jit(solution)/shard_map/cond/branch_1_fun/all_to_all | solution.py:878
  32.7 1.9 query_units.1
  40.6 3.1 fusion
  44.9 5.1 %collective-permute-done.15 = bf16[2,64,1024]{2,1,0:T(8,128)(2,1)} collective-permute-done((bf16[2,64,1024]{2,1,0:T(8,128)(2,1)}, bf16[2,64,1024]{2,1,0:T(8,128)(2,1)}, u32[]{:S(2)}, u32[]{:S(2)}) %collective-permute-start.15) | collective-permute-done | bytes 262176 | tf_op jit(solution)/shard_map/cond/branch_1_fun/ppermute | solution.py:41
  50.0 2.8 collective-permute-done.17
  52.8 16.8 %all-to-all-done.4.own = bf16[8,208,256]{2,1,0:T(8,128)(2,1)} async-done(((bf16[8,208,256]{2,1,0:T(8,128)(2,1)}), bf16[8,208,256]{2,1,0:T(8,128)(2,1)}, u32[]{:S(2)}, u32[]{:S(2)}) %all-to-all-start.4) | async-done | bytes 852000 | tf_op jit(solution)/shard_map/cond/branch_1_fun/all_to_all | solution.py:878
  69.8 2.5 collective-permute-done.18.other
  72.3 2.3 heads.1
  76.6 5.9 %conditional.12 = (bf16[1024,128]{1,0:T(8,128)(2,1)}, bf16[1024,128]{1,0:T(8,128)(2,1)}, bf16[1024,128]{1,0:T(8,128)(2,1)}) conditional(s32[]{:T(128)} %bitcast.20, () %tuple.120, (s32[5]{0:T(128)S(1)}, bf16[128,1024]{1,0:T(8,128)(2,1)S(1)}, bf16[128,1024]{1,0:T(8,128)(2,1)S(1)}, bf16[2,64,1024]{2,1,0:T(8,128)(2,1)}, bf16[2,64,1024]{2,1,0:T(8,128)(2,1)}, ...), branch_computations={%region_7.8_spmd, %region_8.9_spmd} | conditional | flops 4369999872 | bytes 15108640 | solution.py:824
  76.6 4.0 %project.1 = (bf16[1024,128]{1,0:T(8,128)(2,1)}, bf16[1024,128]{1,0:T(8,128)(2,1)}) custom-call(s32[5]{0:T(128)S(1)} %get-tuple-element.268.idx, bf16[128,1024]{1,0:T(8,128)(2,1)S(1)} %get-tuple-element.269.refs_0_, bf16[128,1024]{1,0:T(8,128)(2,1)S(1)} %get-tuple-element.270.refs_1_, bf16[2,64,1024]{2,1,0:T(8,128)(2,1)} %get-tuple-element.271.refs_2_, ...), custom_call_target="tpu_custom_call" | custom-call | flops 4369999872 | bytes 14060000 | tf_op jit(solution)/shard_map/cond/branch_1_fun/project/pallas_call | solution.py:115
  82.5 20.2 %conditional.13 = (f32[4,2,2,64,128]{4,3,2,1,0:T(8,128)}, f32[4,2,2,64,1]{4,3,2,1,0:T(8,128)}, bf16[8,64,128]{2,1,0:T(8,128)(2,1)S(1)}) conditional(s32[]{:T(128)} %bitcast.20, () %tuple.119, (bf16[1024,128]{1,0:T(8,128)(2,1)}, bf16[1024,128]{1,0:T(8,128)(2,1)}, bf16[1024,128]{1,0:T(8,128)(2,1)}, s32[4,2,2,64,1]{3,2,1,0,4:T(2,128)S(1)}, ...), branch_computations={%region_9.10_spmd, %region_10.11_spmd} | conditional | flops 8625000448 | bytes 28020360 | solution.py:824
  83.5 7.4 %attend.1 = (f32[4,2,2,64,128]{4,3,2,1,0:T(8,128)}, f32[4,2,2,64,1]{4,3,2,1,0:T(8,128)}, bf16[4,2,64,128]{3,2,1,0:T(8,128)(2,1)}) custom-call(bf16[4,2,2,64,128]{4,3,2,1,0:T(8,128)(2,1)} %bitcast.9.q_ref, bf16[1024,128]{1,0:T(8,128)(2,1)} %get-tuple-element.284.kv0_ref, bf16[1024,128]{1,0:T(8,128)(2,1)} %get-tuple-element.285.kv1_ref, ...), custom_call_target="tpu_custom_call" | custom-call | flops 8625000448 | bytes 27750000 | tf_op jit(solution)/shard_map/cond/branch_1_fun/attend/pallas_call | solution.py:293
  91.0 11.7 %all_to_all.20 = bf16[8,64,128]{2,1,0:T(8,128)(2,1)S(1)} all-to-all(bf16[8,64,128]{2,1,0:T(8,128)(2,1)} %bitcast.50), channel_id=1, replica_groups=mesh['o'=1,'z'=4,'x'=2,'c'=2,'y'=2] {'z','x'}, dimensions={0} | all-to-all | bytes 262144 | tf_op jit(solution)/shard_map/cond/branch_1_fun/all_to_all | solution.py:924
  102.7 11.2 %conditional.14 = (bf16[128,512]{1,0:T(8,128)(2,1)S(1)}, bf16[128,1024]{1,0:T(8,128)(2,1)}, bf16[128,1024]{1,0:T(8,128)(2,1)}) conditional(s32[]{:T(128)} %bitcast.20, () %tuple.118, (s32[5]{0:T(128)S(1)}, bf16[8,64,128]{2,1,0:T(8,128)(2,1)S(1)}, bf16[8,208,256]{2,1,0:T(8,128)(2,1)}, bf16[8,208,256]{2,1,0:T(8,128)(2,1)}) %tuple.127), branch_computations={%region_11.12_spmd, %region_12.13_spmd} | conditional | flops 4024999936 | bytes 13998640 | solution.py:824
  102.7 3.2 %branch.1 = (bf16[128,512]{1,0:T(8,128)(2,1)S(1)}, bf16[128,1024]{1,0:T(8,128)(2,1)}) custom-call(s32[5]{0:T(128)S(1)} %get-tuple-element.292.idx, bf16[8,64,128]{2,1,0:T(8,128)(2,1)S(1)} %get-tuple-element.293.got, bf16[8,208,256]{2,1,0:T(8,128)(2,1)} %get-tuple-element.294.refs_0_, bf16[8,208,256]{2,1,0:T(8,128)(2,1)} %get-tuple-element.295.refs_1_), custom_call_target="tpu_custom_call" | custom-call | flops 4024999936 | bytes 12950000 | tf_op jit(solution)/shard_map/cond/branch_1_fun/branch/pallas_call | solution.py:115
  107.4 6.5 %collective-permute-done.1 = bf16[128,1024]{1,0:T(8,128)(2,1)} collective-permute-done((bf16[128,1024]{1,0:T(8,128)(2,1)}, bf16[128,1024]{1,0:T(8,128)(2,1)}, u32[]{:S(2)}, u32[]{:S(2)}) %collective-permute-start.1) | collective-permute-done | bytes 262176 | tf_op jit(solution)/shard_map/cond/branch_1_fun/ppermute | solution.py:41
  114.8 7.2 %forward.1 = (f32[128,1024]{1,0:T(8,128)}, f32[128,1024]{1,0:T(8,128)}, f32[128,1]{1,0:T(8,128)}, f32[128,2048]{1,0:T(8,128)}, bf16[288,1024]{1,0:T(8,128)(2,1)}...) custom-call(s32[5]{0:T(128)S(1)} %stack.47.idx, bf16[128,1024]{1,0:T(8,128)(2,1)} %get-tuple-element.558.own, ...), custom_call_target="tpu_custom_call" | custom-call | flops 8855000064 | bytes 28490000 | tf_op jit(solution)/shard_map/forward/pallas_call | solution.py:115
  123.8 13.4 %conditional.15 = ((bf16[128,1024]{1,0:T(8,128)(2,1)}, f32[128,1024]{1,0:T(8,128)}, f32[128,1]{1,0:T(8,128)}, f32[128,128]{1,0:T(8,128)}, bf16[128,128]{1,0:T(8,...) conditional(s32[]{:T(128)} %bitcast.20, () %tuple.117, ...), branch_computations={%region_13.14_spmd, %region_14.15_spmd} | conditional | flops 4140000000 | bytes 15417228 | solution.py:824
  125.6 7.4 %collective-permute-done.2.other = bf16[128,1024]{1,0:T(8,128)(2,1)S(1)} collective-permute-done((bf16[128,1024]{1,0:T(8,128)(2,1)}, bf16[128,1024]{1,0:T(8,128)(2,1)S(1)}, u32[]{:S(2)}, u32[]{:S(2)}) %collective-permute-start.2) | collective-permute-done | bytes 262176 | tf_op jit(solution)/shard_map/cond/branch_1_fun/ppermute | solution.py:41
  133.7 3.5 %second.1 = (bf16[128,1024]{1,0:T(8,128)(2,1)}, f32[128,1024]{1,0:T(8,128)}, f32[128,1]{1,0:T(8,128)}, f32[128,128]{1,0:T(8,128)}, bf16[128,128]{1,0:T(8,128)(2,...) custom-call(s32[5]{0:T(128)S(1)} %get-tuple-element.298.idx, ...), custom_call_target="tpu_custom_call" | custom-call | flops 4140000000 | bytes 13320000 | tf_op jit(solution)/shard_map/cond/branch_1_fun/second/pallas_call | solution.py:115
  137.2 2.7 collective-permute-done.29
  139.9 30.5 %conditional.16 = ((f32[128,1024]{1,0:T(8,128)}, bf16[256,1024]{1,0:T(8,128)(2,1)}, bf16[256,1024]{1,0:T(8,128)(2,1)}, bf16[128,1024]{1,0:T(8,128)(2,1)S(1)}, f3...) conditional(s32[]{:T(128)} %bitcast.20, () %tuple.131, ...), branch_computations={%region_15.16_spmd, %region_16.17_spmd} | conditional | flops 13800048640 | bytes 47366000 | solution.py:824
  142.9 3.2 %collective-permute-done.20 = f32[4,4096]{1,0:T(4,128)S(1)} collective-permute-done((f32[4,4096]{1,0:T(4,128)S(1)}, f32[4,4096]{1,0:T(4,128)S(1)}, u32[]{:S(2)}, u32[]{:S(2)}) %collective-permute-start.20) | collective-permute-done | bytes 65568 | tf_op jit(solution)/shard_map/cond/branch_1_fun/ppermute | solution.py:37
  146.2 2.4 collective-permute-done.21
  149.2 3.9 %collective-permute-start.24 = (f32[4,4096]{1,0:T(4,128)S(1)}, f32[4,4096]{1,0:T(4,128)S(1)}, u32[]{:S(2)}, u32[]{:S(2)}) collective-permute-start(f32[4,4096]{1,0:T(4,128)S(1)} %add_add_fusion.t0), channel_id=1, source_target_pairs={{0,24},{8,16},{16,8},{24,0},{1,25},{9,17},{17,9},{25,1},{2,26},{10... | collective-permute-start | bytes 196616 | tf_op jit(solution)/shard_map/cond/branch_1_fun/ppermute | solution.py:33
  153.1 3.2 collective-permute-done.22.t1
  156.3 4.0 %collective-permute-done.23.t2 = f32[4,4096]{1,0:T(4,128)S(1)} collective-permute-done((f32[4,4096]{1,0:T(4,128)S(1)}, f32[4,4096]{1,0:T(4,128)S(1)}, u32[]{:S(2)}, u32[]{:S(2)}) %collective-permute-start.23) | collective-permute-done | bytes 65568 | tf_op jit(solution)/shard_map/cond/branch_1_fun/ppermute | solution.py:33
  160.9 9.6 %middle.1 = (f32[128,1024]{1,0:T(8,128)}, bf16[256,1024]{1,0:T(8,128)(2,1)}, bf16[256,1024]{1,0:T(8,128)(2,1)}, bf16[128,1024]{1,0:T(8,128)(2,1)S(1)}, f32[8,128...) custom-call(s32[5]{0:T(128)} %copy-done.12, f32[4,4096]{1,0:T(4,128)} %copy-done.4, ...), custom_call_target="tpu_custom_call" | custom-call | flops 13799999488 | bytes 44400000 | tf_op jit(solution)/shard_map/cond/branch_1_fun/middle/pallas_call | solution.py:115
  172.6 13.4 %conditional.17 = ((f32[128,1024]{1,0:T(8,128)}, bf16[128,1024]{1,0:T(8,128)(2,1)S(1)}, f32[8,1024]{1,0:T(8,128)}, bf16[8,144,128]{2,1,0:T(8,128)(2,1)})) conditional(s32[]{:T(128)} %bitcast.20, () %tuple.138, (bf16[128,1024]{1,0:T(8,128)(2,1)S(1)}, f32[1024]{0:T(1024)}, bf16[8,80,128]{2,1,0:T(8,128)(2,1)}, s32[5]{0:T(128)}, ...), branch_computations={%region_17.18_spmd, %region_18.19_spmd} | conditional | flops 4369999872 | bytes 18516620 | solution.py:824
  175.9 5.1 %collective-permute-done.3.other = bf16[128,1024]{1,0:T(8,128)(2,1)S(1)} collective-permute-done((bf16[128,1024]{1,0:T(8,128)(2,1)S(1)}, bf16[128,1024]{1,0:T(8,128)(2,1)S(1)}, u32[]{:S(2)}, u32[]{:S(2)}) %collective-permute-start.3) | collective-permute-done | bytes 262176 | tf_op jit(solution)/shard_map/cond/branch_1_fun/ppermute | solution.py:41
  181.7 4.2 %first_back.1 = (f32[128,1024]{1,0:T(8,128)}, bf16[128,1024]{1,0:T(8,128)(2,1)S(1)}, f32[8,1024]{1,0:T(8,128)}, bf16[8,144,128]{2,1,0:T(8,128)(2,1)}) custom-call(s32[5]{0:T(128)} %get-tuple-element.324.idx, bf16[128,1024]{1,0:T(8,128)(2,1)} %copy-done.3, bf16[128,1024]{1,0:T(8,128)(2,1)} %copy-done.28, f32[128,1024]{1,0:T(8,128)} %get-tuple-element.326.grad_second_in, ...), custom_call_target="tpu_custom_call" | custom-call | flops 4369999872 | bytes 14060000 | tf_op jit(solution)/shard_map/cond/branch_1_fun/first_back/pallas_call | solution.py:115
  188.0 21.6 %conditional.18 = (bf16[8,144,128]{2,1,0:T(8,128)(2,1)}, bf16[128,1024]{1,0:T(8,128)(2,1)}, bf16[128,1024]{1,0:T(8,128)(2,1)}, bf16[128,1024]{1,0:T(8,128)(2,1)}...) conditional(s32[]{:T(128)} %bitcast.20, () %tuple.137, ...), branch_computations={%region_19.20_spmd, %region_20.21_spmd} | conditional | flops 5980000256 | bytes 32445840 | solution.py:824
  189.3 6.7 %all-to-all-start.1 = ((bf16[8,144,128]{2,1,0:T(8,128)(2,1)}), bf16[8,144,128]{2,1,0:T(8,128)(2,1)}, u32[]{:S(2)}, u32[]{:S(2)}) async-start(bf16[8,144,128]{2,1,0:T(8,128)(2,1)} %get-tuple-element.334), calls=%async_computation.1 | async-start | bytes 589824 | tf_op jit(solution)/shard_map/cond/branch_1_fun/all_to_all | solution.py:924
  196.5 5.3 %weights.1 = (f32[2,2,64,1024]{3,2,1,0:T(8,128)S(1)}, bf16[2,2,64,1024]{3,2,1,0:T(8,128)(2,1)S(1)}, f32[2,2,64,1024]{3,2,1,0:T(8,128)S(1)}, bf16[2,2,64,1024]{3,2,1,0:T(8,128)(2,1)S(1)}) custom-call(s32[5]{0:T(128)} %get-tuple-element.336.idx, bf16[288,1024]{1,0:T(8,128)(2,1)} %get-tuple-element.337.f0, bf16[288,1024]{1,0:T(8,128)(2,1)} %get-tuple-element.338.f1, ...), custom_call_target="tpu_custom_call" | custom-call | flops 5980000256 | bytes 19240000 | tf_op jit(solution)/shard_map/cond/branch_1_fun/weights/pallas_call | solution.py:115
  202.6 7.0 %all-to-all-done.1 = bf16[8,144,128]{2,1,0:T(8,128)(2,1)} async-done(((bf16[8,144,128]{2,1,0:T(8,128)(2,1)}), bf16[8,144,128]{2,1,0:T(8,128)(2,1)}, u32[]{:S(2)}, u32[]{:S(2)}) %all-to-all-start.1) | async-done | bytes 294944 | tf_op jit(solution)/shard_map/cond/branch_1_fun/all_to_all | solution.py:924
  213.3 17.2 %conditional.19 = (bf16[1024,256]{1,0:T(8,128)(2,1)}, bf16[336,128]{1,0:T(8,128)(2,1)S(1)}) conditional(s32[]{:T(128)} %bitcast.20, () %tuple.136, (bf16[1024,128]{1,0:T(8,128)(2,1)}, bf16[8,144,128]{2,1,0:T(8,128)(2,1)}, f32[4,2,2,64,128]{4,3,2,1,0:T(8,128)}, f32[4,2,2,64,1]{4,3,2,1,0:T(8,128)}, bf16[1024,128]{1,0:T(8,128)(2,1)}, ...), branch_computations={%region_21.22_spmd, %region_22.23_spmd} | conditional | flops 18630000640 | bytes 68337024 | solution.py:824
  214.4 9.8 %attend_back.1 = (f32[4,2,2,64,128]{4,3,2,1,0:T(8,128)}, f32[1024,128]{1,0:T(8,128)}, f32[1024,128]{1,0:T(8,128)}) custom-call(bf16[4,2,2,64,128]{4,3,2,1,0:T(8,128)(2,1)} %bitcast.16.q_ref, bf16[4,2,144,128]{3,2,1,0:T(8,128)(2,1)} %bitcast.17.g_ref, f32[4,2,2,64,128]{4,3,2,1,0:T(8,128)} %get-tuple-element.352.o_ref, ...), custom_call_target="tpu_custom_call" | custom-call | flops 11269999616 | bytes 36260000 | tf_op jit(solution)/shard_map/cond/branch_1_fun/attend_back/pallas_call | solution.py:351
  224.5 2.3 query_back.1
  227.6 3.0 triple.1
  230.6 2.1 pair.2
  232.7 2.3 collective-permute-start.36
  235.0 24.3 %conditional.20 = (bf16[8,128,256]{2,1,0:T(8,128)(2,1)}, bf16[8,80,256]{2,1,0:T(8,128)(2,1)}, f32[2,2,64,256]{3,2,1,0:T(8,128)S(1)}, bf16[2,2,64,256]{3,2,1,0:T(8,128)(2,1)}) conditional(s32[]{:T(128)} %bitcast.20, () %tuple.135, (bf16[1024,256]{1,0:T(8,128)(2,1)}, s32[5]{0:T(128)S(1)}, bf16[128,1024]{1,0:T(8,128)(2,1)S(1)}, ...), branch_computations={%region_23.24_spmd, %region_24.25_spmd} | conditional | flops 9084999680 | bytes 36308088 | solution.py:824
  235.0 4.2 %all-to-all-start.2 = ((bf16[8,128,256]{2,1,0:T(8,128)(2,1)}), bf16[8,128,256]{2,1,0:T(8,128)(2,1)}, u32[]{:S(2)}, u32[]{:S(2)}) async-start(bf16[8,128,256]{2,1,0:T(8,128)(2,1)} %bitcast.19), calls=%async_computation.2 | async-start | bytes 1048576 | tf_op jit(solution)/shard_map/cond/branch_1_fun/all_to_all | solution.py:924
  239.2 4.6 %triple_weight.1 = (bf16[8,80,256]{2,1,0:T(8,128)(2,1)}, bf16[8,80,256]{2,1,0:T(8,128)(2,1)}) custom-call(s32[5]{0:T(128)S(1)} %get-tuple-element.368.idx, bf16[128,1024]{1,0:T(8,128)(2,1)S(1)} %get-tuple-element.369.refs_0_, bf16[128,1024]{1,0:T(8,128)(2,1)S(1)} %get-tuple-element.370.refs_1_, bf16[2,64,1024]{2,1,0:T(8,128)(2,1)} %get-tuple-element.371.refs_2_, ...), custom_call_target="tpu_custom_call" | custom-call | flops 4369999872 | bytes 14060000 | tf_op jit(solution)/shard_map/cond/branch_1_fun/triple_weight/pallas_call | solution.py:115
  243.8 3.7 %output.1 = (f32[2,2,64,256]{3,2,1,0:T(8,128)S(1)}, bf16[2,2,64,256]{3,2,1,0:T(8,128)(2,1)}) custom-call(s32[5]{0:T(128)S(1)} %get-tuple-element.368.idx, bf16[288,1024]{1,0:T(8,128)(2,1)} %get-tuple-element.380.f0, bf16[288,1024]{1,0:T(8,128)(2,1)} %get-tuple-element.381.f1, bf16[288,1024]{1,0:T(8,128)(2,1)} %get-tuple-element.382.f2, ...), custom_call_target="tpu_custom_call" | custom-call | flops 2644999936 | bytes 8510000 | tf_op jit(solution)/shard_map/cond/branch_1_fun/output/pallas_call | solution.py:115
  250.2 1.9 pair_sum.1
  252.0 3.3 %collective-permute-done.10 = bf16[2,2,64,256]{3,2,1,0:T(8,128)(2,1)} collective-permute-done((bf16[2,2,64,256]{3,2,1,0:T(8,128)(2,1)}, bf16[2,2,64,256]{3,2,1,0:T(8,128)(2,1)}, u32[]{:S(2)}, u32[]{:S(2)}) %collective-permute-start.10) | collective-permute-done | bytes 131104 | tf_op jit(solution)/shard_map/cond/branch_1_fun/ppermute | solution.py:33
  255.4 3.9 %all-to-all-done.2 = bf16[8,128,256]{2,1,0:T(8,128)(2,1)} async-done(((bf16[8,128,256]{2,1,0:T(8,128)(2,1)}), bf16[8,128,256]{2,1,0:T(8,128)(2,1)}, u32[]{:S(2)}, u32[]{:S(2)}) %all-to-all-start.2) | async-done | bytes 524320 | tf_op jit(solution)/shard_map/cond/branch_1_fun/all_to_all | solution.py:924
  259.3 2.2 pair.3
  261.9 26.6 %conditional.21 = (f32[128,1024]{1,0:T(8,128)S(1)}, bf16[8,80,256]{2,1,0:T(8,128)(2,1)}) conditional(s32[]{:T(128)} %bitcast.20, () %tuple.134, (s32[5]{0:T(128)S(1)}, bf16[8,128,256]{2,1,0:T(8,128)(2,1)}, bf16[1024,1536]{1,0:T(8,128)(2,1)}, f32[128,1024]{1,0:T(8,128)S(1)}, bf16[8,80,256]{2,1,0:T(8,128)(2,1)}) %tuple.215), branch_computations={%region_25.26_spmd, %region_26.27_spmd} | conditional | flops 6900000256 | bytes 25280308 | solution.py:824
  261.9 4.8 %tokens.2.own = bf16[128,1024]{1,0:T(8,128)(2,1)} custom-call(s32[5]{0:T(128)S(1)} %get-tuple-element.390.idx, bf16[8,128,256]{2,1,0:T(8,128)(2,1)} %get-tuple-element.391.got, bf16[1024,1536]{1,0:T(8,128)(2,1)} %get-tuple-element.392.message), custom_call_target="tpu_custom_call" | custom-call | flops 4485000192 | bytes 14430000 | tf_op jit(solution)/shard_map/cond/branch_1_fun/tokens/pallas_call | solution.py:115
  266.7 4.1 %all-to-all-start.3 = ((bf16[8,80,256]{2,1,0:T(8,128)(2,1)}), bf16[8,80,256]{2,1,0:T(8,128)(2,1)}, u32[]{:S(2)}, u32[]{:S(2)}) async-start(bf16[8,80,256]{2,1,0:T(8,128)(2,1)} %get-tuple-element.395), calls=%async_computation.3 | async-start | bytes 655360 | tf_op jit(solution)/shard_map/cond/branch_1_fun/all_to_all | solution.py:1189
  272.7 5.8 %collective-permute-done.11.other = bf16[128,1024]{1,0:T(8,128)(2,1)S(1)} collective-permute-done((bf16[128,1024]{1,0:T(8,128)(2,1)}, bf16[128,1024]{1,0:T(8,128)(2,1)S(1)}, u32[]{:S(2)}, u32[]{:S(2)}) %collective-permute-start.11) | collective-permute-done | bytes 262176 | tf_op jit(solution)/shard_map/cond/branch_1_fun/ppermute | solution.py:41
  280.3 8.2 %all-to-all-done.3 = bf16[8,80,256]{2,1,0:T(8,128)(2,1)} async-done(((bf16[8,80,256]{2,1,0:T(8,128)(2,1)}), bf16[8,80,256]{2,1,0:T(8,128)(2,1)}, u32[]{:S(2)}, u32[]{:S(2)}) %all-to-all-start.3) | async-done | bytes 327712 | tf_op jit(solution)/shard_map/cond/branch_1_fun/all_to_all | solution.py:1189
  290.4 2.5 line_sum.1
  293.6 1.9 triple_out.1
  295.5 9.5 %all-gather.12.cloned.1.call-done = bf16[5376,128]{1,0:T(8,128)(2,1)} async-done(((bf16[336,128]{1,0:T(8,128)(2,1)}), bf16[5376,128]{1,0:T(8,128)(2,1)}) %all-gather.12.cloned.1.call-update) | async-done | bytes 1376272 | tf_op jit(solution)/shard_map/all_gather | solution.py:1174
  305.1 2.9 spread.1
  308.7 2.2 columns.1
  (189 shorter events, 56.5 us)
Async XLA Ops:
  7.2 107.6 %all-gather.6.cloned.1.call-start = ((), (), s32[]{:S(2)}) async-start(), calls=%async_computation.5 | async-start | bytes 8912896 | tf_op jit(solution)/shard_map/all_gather | solution.py:875
  8.2 10.2 %collective-permute-start.26 = (bf16[64,1024]{1,0:T(8,128)(2,1)S(1)}, bf16[64,1024]{1,0:T(8,128)(2,1)S(1)}, u32[]{:S(2)}, u32[]{:S(2)}) collective-permute-start(bf16[64,1024]{1,0:T(8,128)(2,1)S(1)} %constant_dynamic-slice_fusion), channel_id=1, source_target_pairs={{0,8},{8,0},{16,24},{24,16},{1,9},{9,1},{17,25},{25,17},{2,10},{10... | collective-permute-start | bytes 393224 | tf_op jit(solution)/shard_map/ppermute | solution.py:33
  11.2 12.9 %collective-permute-start.27 = (bf16[64,1024]{1,0:T(8,128)(2,1)S(1)}, bf16[64,1024]{1,0:T(8,128)(2,1)S(1)}, u32[]{:S(2)}, u32[]{:S(2)}) collective-permute-start(bf16[64,1024]{1,0:T(8,128)(2,1)S(1)} %constant_dynamic-slice_fusion), channel_id=1, source_target_pairs={{0,16},{8,24},{16,0},{24,8},{1,17},{9,25},{17,1},{25,9},{2,18},{10... | collective-permute-start | bytes 393224 | tf_op jit(solution)/shard_map/ppermute | solution.py:33
  13.8 10.3 %collective-permute-start.28 = (bf16[64,1024]{1,0:T(8,128)(2,1)S(1)}, bf16[64,1024]{1,0:T(8,128)(2,1)S(1)}, u32[]{:S(2)}, u32[]{:S(2)}) collective-permute-start(bf16[64,1024]{1,0:T(8,128)(2,1)S(1)} %constant_dynamic-slice_fusion), channel_id=1, source_target_pairs={{0,24},{8,16},{16,8},{24,0},{1,25},{9,17},{17,9},{25,1},{2,26},{10... | collective-permute-start | bytes 393224 | tf_op jit(solution)/shard_map/ppermute | solution.py:33
  13.8 10.3 %collective-permute-start.25 = (bf16[128,1024]{1,0:T(8,128)(2,1)}, bf16[128,1024]{1,0:T(8,128)(2,1)S(1)}, u32[]{:S(2)}, u32[]{:S(2)}) collective-permute-start(bf16[128,1024]{1,0:T(8,128)(2,1)} %tokens.3), channel_id=1, source_target_pairs={{0,4},{4,0},{1,5},{5,1},{2,6},{6,2},{3,7},{7,3},{8,12},{12,8},{9,1... | collective-permute-start | bytes 786440 | tf_op jit(solution)/shard_map/ppermute | solution.py:41
  15.6 124.3 %copy-start.10 = (s32[5]{0:T(128)}, s32[5]{0:T(128)S(1)}, u32[]{:S(2)}) copy-start(s32[5]{0:T(128)S(1)} %stack.47.idx) | copy-start | bytes 64
  15.6 8.6 %copy-start.41 = (s32[4]{0:T(128)S(1)}, s32[4]{0:T(128)}, u32[]{:S(2)}) copy-start(s32[4]{0:T(128)} %param.44) | copy-start | bytes 52
  15.6 8.7 %copy-start.9 = (s32[128]{0:T(128)S(1)}, s32[128]{0:T(128)}, u32[]{:S(2)}) copy-start(s32[128]{0:T(128)} %param.46) | copy-start | bytes 1540
  24.2 51.9 %copy-start.25 = (bf16[128,1024]{1,0:T(8,128)(2,1)}, bf16[128,1024]{1,0:T(8,128)(2,1)S(1)}, u32[]{:S(2)}) copy-start(bf16[128,1024]{1,0:T(8,128)(2,1)S(1)} %collective-permute-done.25) | copy-start | bytes 786436
  24.2 146.3 %all-gather.8.cloned.1.call-start = ((), (), s32[]{:S(2)}) async-start(), calls=%async_computation.6 | async-start | bytes 3342336 | tf_op jit(solution)/shard_map/all_gather | solution.py:947
  24.3 51.7 %copy-start.5 = (bf16[128,1024]{1,0:T(8,128)(2,1)S(1)}, bf16[128,1024]{1,0:T(8,128)(2,1)}, u32[]{:S(2)}) copy-start(bf16[128,1024]{1,0:T(8,128)(2,1)} %tokens.3) | copy-start | bytes 786436
  24.4 51.7 %copy-start.35 = (f32[3,512]{1,0:T(4,128)S(1)}, f32[3,512]{1,0:T(4,128)}, u32[]{:S(2)}) copy-start(f32[3,512]{1,0:T(4,128)} %param.48) | copy-start | bytes 18436
  24.4 10.2 %collective-permute-start.12 = (bf16[64,1024]{1,0:T(8,128)(2,1)S(1)}, bf16[64,1024]{1,0:T(8,128)(2,1)S(1)}, u32[]{:S(2)}, u32[]{:S(2)}) collective-permute-start(bf16[64,1024]{1,0:T(8,128)(2,1)S(1)} %get-tuple-element.251), channel_id=1, source_target_pairs={{0,4},{4,0},{1,5},{5,1},{2,6},{6,2},{3,7},{7,3},{8,12},{12,8},{9,1... | collective-permute-start | bytes 393224 | tf_op jit(solution)/shard_map/cond/branch_1_fun/ppermute | solution.py:41
  26.0 10.9 %collective-permute-start.14 = (bf16[64,1024]{1,0:T(8,128)(2,1)S(1)}, bf16[64,1024]{1,0:T(8,128)(2,1)S(1)}, u32[]{:S(2)}, u32[]{:S(2)}) collective-permute-start(bf16[64,1024]{1,0:T(8,128)(2,1)S(1)} %get-tuple-element.252), channel_id=1, source_target_pairs={{0,4},{4,0},{1,5},{5,1},{2,6},{6,2},{3,7},{7,3},{8,12},{12,8},{9,1... | collective-permute-start | bytes 393224 | tf_op jit(solution)/shard_map/cond/branch_1_fun/ppermute | solution.py:41
  26.5 11.6 %collective-permute-start.16 = (bf16[64,1024]{1,0:T(8,128)(2,1)S(1)}, bf16[64,1024]{1,0:T(8,128)(2,1)S(1)}, u32[]{:S(2)}, u32[]{:S(2)}) collective-permute-start(bf16[64,1024]{1,0:T(8,128)(2,1)S(1)} %get-tuple-element.253), channel_id=1, source_target_pairs={{0,4},{4,0},{1,5},{5,1},{2,6},{6,2},{3,7},{7,3},{8,12},{12,8},{9,1... | collective-permute-start | bytes 393224 | tf_op jit(solution)/shard_map/cond/branch_1_fun/ppermute | solution.py:41
  28.0 41.6 %all-to-all-start.4 = ((bf16[8,208,256]{2,1,0:T(8,128)(2,1)}), bf16[8,208,256]{2,1,0:T(8,128)(2,1)}, u32[]{:S(2)}, u32[]{:S(2)}) async-start(bf16[8,208,256]{2,1,0:T(8,128)(2,1)} %get-tuple-element.250), calls=%async_computation.4 | async-start | bytes 1703936 | tf_op jit(solution)/shard_map/cond/branch_1_fun/all_to_all | solution.py:878
  35.3 9.6 %collective-permute-start.13 = (bf16[2,64,1024]{2,1,0:T(8,128)(2,1)}, bf16[2,64,1024]{2,1,0:T(8,128)(2,1)}, u32[]{:S(2)}, u32[]{:S(2)}) collective-permute-start(bf16[2,64,1024]{2,1,0:T(8,128)(2,1)} %pad_maximum_fusion), channel_id=1, source_target_pairs={{0,1},{1,0},{2,3},{3,2},{4,5},{5,4},{6,7},{7,6},{8,9},{9,8},{10,11... | collective-permute-start | bytes 786440 | tf_op jit(solution)/shard_map/cond/branch_1_fun/ppermute | solution.py:41
  37.6 12.4 %collective-permute-start.15 = (bf16[2,64,1024]{2,1,0:T(8,128)(2,1)}, bf16[2,64,1024]{2,1,0:T(8,128)(2,1)}, u32[]{:S(2)}, u32[]{:S(2)}) collective-permute-start(bf16[2,64,1024]{2,1,0:T(8,128)(2,1)} %pad_maximum_fusion.1), channel_id=1, source_target_pairs={{0,1},{1,0},{2,3},{3,2},{4,5},{5,4},{6,7},{7,6},{8,9},{9,8},{10,11... | collective-permute-start | bytes 786440 | tf_op jit(solution)/shard_map/cond/branch_1_fun/ppermute | solution.py:41
  38.8 14.0 %collective-permute-start.17 = (bf16[2,64,1024]{2,1,0:T(8,128)(2,1)}, bf16[2,64,1024]{2,1,0:T(8,128)(2,1)}, u32[]{:S(2)}, u32[]{:S(2)}) collective-permute-start(bf16[2,64,1024]{2,1,0:T(8,128)(2,1)} %pad_maximum_fusion.2), channel_id=1, source_target_pairs={{0,1},{1,0},{2,3},{3,2},{4,5},{5,4},{6,7},{7,6},{8,9},{9,8},{10,11... | collective-permute-start | bytes 786440 | tf_op jit(solution)/shard_map/cond/branch_1_fun/ppermute | solution.py:41
  69.6 2.7 collective-permute-start.18
  80.6 1.9 collective-permute-start
  102.7 12.1 %copy-start.40 = (f32[1024]{0:T(1024)S(1)}, f32[1024]{0:T(1024)}, u32[]{:S(2)}) copy-start(f32[1024]{0:T(1024)} %param.51) | copy-start | bytes 12292
  105.9 8.0 %collective-permute-start.1 = (bf16[128,1024]{1,0:T(8,128)(2,1)}, bf16[128,1024]{1,0:T(8,128)(2,1)}, u32[]{:S(2)}, u32[]{:S(2)}) collective-permute-start(bf16[128,1024]{1,0:T(8,128)(2,1)} %get-tuple-element.771), channel_id=1, source_target_pairs={{0,1},{1,0},{2,3},{3,2},{4,5},{5,4},{6,7},{7,6},{8,9},{9,8},{10,11... | collective-permute-start | bytes 786440 | tf_op jit(solution)/shard_map/cond/branch_1_fun/ppermute | solution.py:41
  113.9 99.5 %all-gather.10.cloned.1.call-start = ((), (), s32[]{:S(2)}) async-start(), calls=%async_computation.7 | async-start | bytes 1114112 | tf_op jit(solution)/shard_map/all_gather | solution.py:1026
  114.8 9.0 %copy-start.36 = (f32[1024]{0:T(1024)S(1)}, f32[1024]{0:T(1024)}, u32[]{:S(2)}) copy-start(f32[1024]{0:T(1024)} %param.56) | copy-start | bytes 12292
  114.8 9.0 %copy-start.37 = (f32[1024]{0:T(1024)S(1)}, f32[1024]{0:T(1024)}, u32[]{:S(2)}) copy-start(f32[1024]{0:T(1024)} %param.58) | copy-start | bytes 12292
  114.8 9.0 %copy-start.38 = (f32[1024]{0:T(1024)S(1)}, f32[1024]{0:T(1024)}, u32[]{:S(2)}) copy-start(f32[1024]{0:T(1024)} %param.57) | copy-start | bytes 12292
  122.0 18.0 %collective-permute-start.29 = (bf16[288,1024]{1,0:T(8,128)(2,1)}, bf16[288,1024]{1,0:T(8,128)(2,1)}, u32[]{:S(2)}, u32[]{:S(2)}) collective-permute-start(bf16[288,1024]{1,0:T(8,128)(2,1)} %get-tuple-element.569), channel_id=1, source_target_pairs={{0,4},{4,0},{1,5},{5,1},{2,6},{6,2},{3,7},{7,3},{8,12},{12,8},{9,1... | collective-permute-start | bytes 1769480 | tf_op jit(solution)/shard_map/ppermute | solution.py:41
  123.8 16.2 %collective-permute-start.30 = (bf16[288,1024]{1,0:T(8,128)(2,1)}, bf16[288,1024]{1,0:T(8,128)(2,1)}, u32[]{:S(2)}, u32[]{:S(2)}) collective-permute-start(bf16[288,1024]{1,0:T(8,128)(2,1)} %get-tuple-element.570), channel_id=1, source_target_pairs={{0,2},{2,0},{1,3},{3,1},{4,6},{6,4},{5,7},{7,5},{8,10},{10,8},{9,1... | collective-permute-start | bytes 1769480 | tf_op jit(solution)/shard_map/ppermute | solution.py:41
  124.0 9.0 %collective-permute-start.2 = (bf16[128,1024]{1,0:T(8,128)(2,1)}, bf16[128,1024]{1,0:T(8,128)(2,1)S(1)}, u32[]{:S(2)}, u32[]{:S(2)}) collective-permute-start(bf16[128,1024]{1,0:T(8,128)(2,1)} %get-tuple-element.299.own), channel_id=1, source_target_pairs={{0,1},{1,0},{2,3},{3,2},{4,5},{5,4},{6,7},{7,6},{8,9},{9,8},{10,11... | collective-permute-start | bytes 786440 | tf_op jit(solution)/shard_map/cond/branch_1_fun/ppermute | solution.py:41
  141.1 1.9 collective-permute-start.19
  141.1 5.1 %collective-permute-start.20 = (f32[4,4096]{1,0:T(4,128)S(1)}, f32[4,4096]{1,0:T(4,128)S(1)}, u32[]{:S(2)}, u32[]{:S(2)}) collective-permute-start(f32[4,4096]{1,0:T(4,128)S(1)} %get-tuple-element.308), channel_id=1, source_target_pairs={{0,4},{2,6},{4,0},{6,2},{1,5},{3,7},{5,1},{7,3},{8,12},{10,14},{12... | collective-permute-start | bytes 196616 | tf_op jit(solution)/shard_map/cond/branch_1_fun/ppermute | solution.py:37
  142.8 5.8 %collective-permute-start.21 = (f32[4,4096]{1,0:T(4,128)S(1)}, f32[4,4096]{1,0:T(4,128)S(1)}, u32[]{:S(2)}, u32[]{:S(2)}) collective-permute-start(f32[4,4096]{1,0:T(4,128)S(1)} %get-tuple-element.308), channel_id=1, source_target_pairs={{0,6},{2,4},{4,2},{6,0},{1,7},{3,5},{5,3},{7,1},{8,14},{10,12},{12... | collective-permute-start | bytes 196616 | tf_op jit(solution)/shard_map/cond/branch_1_fun/ppermute | solution.py:37
  148.6 11.6 %copy-start.4 = (f32[4,4096]{1,0:T(4,128)}, f32[4,4096]{1,0:T(4,128)S(1)}, u32[]{:S(2)}) copy-start(f32[4,4096]{1,0:T(4,128)S(1)} %add_add_fusion.t0) | copy-start | bytes 196612 | tf_op jit(solution)/shard_map/cond
  148.7 7.6 %collective-permute-start.22 = (f32[4,4096]{1,0:T(4,128)S(1)}, f32[4,4096]{1,0:T(4,128)S(1)}, u32[]{:S(2)}, u32[]{:S(2)}) collective-permute-start(f32[4,4096]{1,0:T(4,128)S(1)} %add_add_fusion.t0), channel_id=1, source_target_pairs={{0,8},{8,0},{16,24},{24,16},{1,9},{9,1},{17,25},{25,17},{2,10},{10... | collective-permute-start | bytes 196616 | tf_op jit(solution)/shard_map/cond/branch_1_fun/ppermute | solution.py:33
  148.7 11.5 %collective-permute-start.23 = (f32[4,4096]{1,0:T(4,128)S(1)}, f32[4,4096]{1,0:T(4,128)S(1)}, u32[]{:S(2)}, u32[]{:S(2)}) collective-permute-start(f32[4,4096]{1,0:T(4,128)S(1)} %add_add_fusion.t0), channel_id=1, source_target_pairs={{0,16},{8,24},{16,0},{24,8},{1,17},{9,25},{17,1},{25,9},{2,18},{10... | collective-permute-start | bytes 196616 | tf_op jit(solution)/shard_map/cond/branch_1_fun/ppermute | solution.py:33
  149.2 11.0 %collective-permute-start.24 = (f32[4,4096]{1,0:T(4,128)S(1)}, f32[4,4096]{1,0:T(4,128)S(1)}, u32[]{:S(2)}, u32[]{:S(2)}) collective-permute-start(f32[4,4096]{1,0:T(4,128)S(1)} %add_add_fusion.t0), channel_id=1, source_target_pairs={{0,24},{8,16},{16,8},{24,0},{1,25},{9,17},{17,9},{25,1},{2,26},{10... | collective-permute-start | bytes 196616 | tf_op jit(solution)/shard_map/cond/branch_1_fun/ppermute | solution.py:33
  170.5 134.5 %all-gather.12.cloned.1.call-start = ((), (), s32[]{:S(2)}) async-start(), calls=%async_computation.8 | async-start | bytes 1462272 | tf_op jit(solution)/shard_map/all_gather | solution.py:1174
  170.6 15.4 %collective-permute-start.32 = (bf16[256,1024]{1,0:T(8,128)(2,1)}, bf16[256,1024]{1,0:T(8,128)(2,1)S(1)}, u32[]{:S(2)}, u32[]{:S(2)}) collective-permute-start(bf16[256,1024]{1,0:T(8,128)(2,1)} %get-tuple-element.592), channel_id=1, source_target_pairs={{0,4},{4,0},{1,5},{5,1},{2,6},{6,2},{3,7},{7,3},{8,12},{12,8},{9,1... | collective-permute-start | bytes 1572872 | tf_op jit(solution)/shard_map/ppermute | solution.py:41
  172.1 14.0 %collective-permute-start.31 = (bf16[288,1024]{1,0:T(8,128)(2,1)}, bf16[288,1024]{1,0:T(8,128)(2,1)S(1)}, u32[]{:S(2)}, u32[]{:S(2)}) collective-permute-start(bf16[288,1024]{1,0:T(8,128)(2,1)} %collective-permute-done.29), channel_id=1, source_target_pairs={{0,2},{2,0},{1,3},{3,1},{4,6},{6,4},{5,7},{7,5},{8,10},{10,8},{9,1... | collective-permute-start | bytes 1769480 | tf_op jit(solution)/shard_map/ppermute | solution.py:41
  172.3 13.8 %collective-permute-start.33 = (bf16[256,1024]{1,0:T(8,128)(2,1)}, bf16[256,1024]{1,0:T(8,128)(2,1)S(1)}, u32[]{:S(2)}, u32[]{:S(2)}) collective-permute-start(bf16[256,1024]{1,0:T(8,128)(2,1)} %get-tuple-element.591), channel_id=1, source_target_pairs={{0,2},{2,0},{1,3},{3,1},{4,6},{6,4},{5,7},{7,5},{8,10},{10,8},{9,1... | collective-permute-start | bytes 1572872 | tf_op jit(solution)/shard_map/ppermute | solution.py:41
  172.6 8.4 %collective-permute-start.3 = (bf16[128,1024]{1,0:T(8,128)(2,1)S(1)}, bf16[128,1024]{1,0:T(8,128)(2,1)S(1)}, u32[]{:S(2)}, u32[]{:S(2)}) collective-permute-start(bf16[128,1024]{1,0:T(8,128)(2,1)S(1)} %get-tuple-element.325.own), channel_id=1, source_target_pairs={{0,1},{1,0},{2,3},{3,2},{4,5},{5,4},{6,7},{7,6},{8,9},{9,8},{10,11... | collective-permute-start | bytes 786440 | tf_op jit(solution)/shard_map/cond/branch_1_fun/ppermute | solution.py:41
  174.3 1.6 collective-permute-start.4
  186.0 2.0 collective-permute-start.34
  188.0 8.5 %copy-start.18 = (bf16[256,1024]{1,0:T(8,128)(2,1)}, bf16[256,1024]{1,0:T(8,128)(2,1)S(1)}, u32[]{:S(2)}) copy-start(bf16[256,1024]{1,0:T(8,128)(2,1)S(1)} %get-tuple-element.342.g1) | copy-start | bytes 1572868 | tf_op jit(solution)/shard_map/cond
  188.0 8.5 %copy-start.19 = (bf16[256,1024]{1,0:T(8,128)(2,1)}, bf16[256,1024]{1,0:T(8,128)(2,1)S(1)}, u32[]{:S(2)}) copy-start(bf16[256,1024]{1,0:T(8,128)(2,1)S(1)} %get-tuple-element.343.g2) | copy-start | bytes 1572868 | tf_op jit(solution)/shard_map/cond
  188.0 8.6 %copy-start.20 = (bf16[256,1024]{1,0:T(8,128)(2,1)}, bf16[256,1024]{1,0:T(8,128)(2,1)S(1)}, u32[]{:S(2)}) copy-start(bf16[256,1024]{1,0:T(8,128)(2,1)S(1)} %get-tuple-element.344.g3) | copy-start | bytes 1572868 | tf_op jit(solution)/shard_map/cond
  188.0 8.5 %collective-permute-start.5 = (bf16[128,1024]{1,0:T(8,128)(2,1)S(1)}, bf16[128,1024]{1,0:T(8,128)(2,1)}, u32[]{:S(2)}, u32[]{:S(2)}) collective-permute-start(bf16[128,1024]{1,0:T(8,128)(2,1)S(1)} %get-tuple-element.823), channel_id=1, source_target_pairs={{0,4},{4,0},{1,5},{5,1},{2,6},{6,2},{3,7},{7,3},{8,12},{12,8},{9,1... | collective-permute-start | bytes 786440 | tf_op jit(solution)/shard_map/cond/branch_1_fun/ppermute | solution.py:41
  189.3 13.3 %collective-permute-start.6 = (bf16[128,1024]{1,0:T(8,128)(2,1)S(1)}, bf16[128,1024]{1,0:T(8,128)(2,1)}, u32[]{:S(2)}, u32[]{:S(2)}) collective-permute-start(bf16[128,1024]{1,0:T(8,128)(2,1)S(1)} %get-tuple-element.823), channel_id=1, source_target_pairs={{0,2},{2,0},{1,3},{3,1},{4,6},{6,4},{5,7},{7,5},{8,10},{10,8},{9,1... | collective-permute-start | bytes 786440 | tf_op jit(solution)/shard_map/cond/branch_1_fun/ppermute | solution.py:41
  189.3 20.2 %all-to-all-start.1 = ((bf16[8,144,128]{2,1,0:T(8,128)(2,1)}), bf16[8,144,128]{2,1,0:T(8,128)(2,1)}, u32[]{:S(2)}, u32[]{:S(2)}) async-start(bf16[8,144,128]{2,1,0:T(8,128)(2,1)} %get-tuple-element.334), calls=%async_computation.1 | async-start | bytes 589824 | tf_op jit(solution)/shard_map/cond/branch_1_fun/all_to_all | solution.py:924
  196.5 13.1 %collective-permute-start.7 = (bf16[128,1024]{1,0:T(8,128)(2,1)}, bf16[128,1024]{1,0:T(8,128)(2,1)}, u32[]{:S(2)}, u32[]{:S(2)}) collective-permute-start(bf16[128,1024]{1,0:T(8,128)(2,1)} %collective-permute-done.5), channel_id=1, source_target_pairs={{0,2},{2,0},{1,3},{3,1},{4,6},{6,4},{5,7},{7,5},{8,10},{10,8},{9,1... | collective-permute-start | bytes 786440 | tf_op jit(solution)/shard_map/cond/branch_1_fun/ppermute | solution.py:41
  209.6 21.0 %collective-permute-start.35 = (bf16[2,2,64,1024]{3,2,1,0:T(8,128)(2,1)S(1)}, bf16[2,2,64,1024]{3,2,1,0:T(8,128)(2,1)}, u32[]{:S(2)}, u32[]{:S(2)}) collective-permute-start(bf16[2,2,64,1024]{3,2,1,0:T(8,128)(2,1)S(1)} %get-tuple-element.602), channel_id=1, source_target_pairs={{0,8},{8,0},{16,24},{24,16},{1,9},{9,1},{17,25},{25,17},{2,10},{10... | collective-permute-start | bytes 1572872 | tf_op jit(solution)/shard_map/ppermute | solution.py:33
  210.8 48.5 %collective-permute-start.37 = (bf16[2,2,64,1024]{3,2,1,0:T(8,128)(2,1)S(1)}, bf16[2,2,64,1024]{3,2,1,0:T(8,128)(2,1)}, u32[]{:S(2)}, u32[]{:S(2)}) collective-permute-start(bf16[2,2,64,1024]{3,2,1,0:T(8,128)(2,1)S(1)} %get-tuple-element.615), channel_id=1, source_target_pairs={{0,8},{8,0},{16,24},{24,16},{1,9},{9,1},{17,25},{25,17},{2,10},{10... | collective-permute-start | bytes 1572872 | tf_op jit(solution)/shard_map/ppermute | solution.py:33
  214.4 10.1 %copy-start.13 = (s32[5]{0:T(128)S(1)}, s32[5]{0:T(128)}, u32[]{:S(2)}) copy-start(s32[5]{0:T(128)} %get-tuple-element.349.idx) | copy-start | bytes 64 | tf_op jit(solution)/shard_map/cond
  214.4 10.1 %copy-start.14 = (f32[2048,128]{1,0:T(8,128)S(1)}, f32[2048,128]{1,0:T(8,128)}, u32[]{:S(2)}) copy-start(f32[2048,128]{1,0:T(8,128)} %get-tuple-element.366.units) | copy-start | bytes 3145732 | tf_op jit(solution)/shard_map/cond
  224.2 2.6 collective-permute-start.8
  232.7 26.6 %collective-permute-start.36 = (bf16[2,64,1024]{2,1,0:T(8,128)(2,1)}, bf16[2,64,1024]{2,1,0:T(8,128)(2,1)S(1)}, u32[]{:S(2)}, u32[]{:S(2)}) collective-permute-start(bf16[2,64,1024]{2,1,0:T(8,128)(2,1)} %get-tuple-element.614), channel_id=1, source_target_pairs={{0,16},{8,24},{16,0},{24,8},{1,17},{9,25},{17,1},{25,9},{2,18},{10... | collective-permute-start | bytes 786440 | tf_op jit(solution)/shard_map/ppermute | solution.py:33
  235.0 24.3 %all-to-all-start.2 = ((bf16[8,128,256]{2,1,0:T(8,128)(2,1)}), bf16[8,128,256]{2,1,0:T(8,128)(2,1)}, u32[]{:S(2)}, u32[]{:S(2)}) async-start(bf16[8,128,256]{2,1,0:T(8,128)(2,1)} %bitcast.19), calls=%async_computation.2 | async-start | bytes 1048576 | tf_op jit(solution)/shard_map/cond/branch_1_fun/all_to_all | solution.py:924
  243.8 5.6 %collective-permute-start.9 = (bf16[8,80,256]{2,1,0:T(8,128)(2,1)}, bf16[8,80,256]{2,1,0:T(8,128)(2,1)S(1)}, u32[]{:S(2)}, u32[]{:S(2)}) collective-permute-start(bf16[8,80,256]{2,1,0:T(8,128)(2,1)} %get-tuple-element.379), channel_id=1, source_target_pairs={{0,2},{2,0},{1,3},{3,1},{4,6},{6,4},{5,7},{7,5},{8,10},{10,8},{9,1... | collective-permute-start | bytes 983048 | tf_op jit(solution)/shard_map/cond/branch_1_fun/ppermute | solution.py:41
  247.6 7.8 %collective-permute-start.10 = (bf16[2,2,64,256]{3,2,1,0:T(8,128)(2,1)}, bf16[2,2,64,256]{3,2,1,0:T(8,128)(2,1)}, u32[]{:S(2)}, u32[]{:S(2)}) collective-permute-start(bf16[2,2,64,256]{3,2,1,0:T(8,128)(2,1)} %get-tuple-element.389), channel_id=1, source_target_pairs={{0,8},{8,0},{16,24},{24,16},{1,9},{9,1},{17,25},{25,17},{2,10},{10... | collective-permute-start | bytes 393224 | tf_op jit(solution)/shard_map/cond/branch_1_fun/ppermute | solution.py:33
  261.5 28.2 %collective-permute-start.38 = (bf16[2,64,1280]{2,1,0:T(8,128)(2,1)}, bf16[2,64,1280]{2,1,0:T(8,128)(2,1)S(1)}, u32[]{:S(2)}, u32[]{:S(2)}) collective-permute-start(bf16[2,64,1280]{2,1,0:T(8,128)(2,1)} %get-tuple-element.636), channel_id=1, source_target_pairs={{0,16},{8,24},{16,0},{24,8},{1,17},{9,25},{17,1},{25,9},{2,18},{10... | collective-permute-start | bytes 983048 | tf_op jit(solution)/shard_map/ppermute | solution.py:33
  266.7 21.8 %all-to-all-start.3 = ((bf16[8,80,256]{2,1,0:T(8,128)(2,1)}), bf16[8,80,256]{2,1,0:T(8,128)(2,1)}, u32[]{:S(2)}, u32[]{:S(2)}) async-start(bf16[8,80,256]{2,1,0:T(8,128)(2,1)} %get-tuple-element.395), calls=%async_computation.3 | async-start | bytes 655360 | tf_op jit(solution)/shard_map/cond/branch_1_fun/all_to_all | solution.py:1189
  270.8 7.6 %collective-permute-start.11 = (bf16[128,1024]{1,0:T(8,128)(2,1)}, bf16[128,1024]{1,0:T(8,128)(2,1)S(1)}, u32[]{:S(2)}, u32[]{:S(2)}) collective-permute-start(bf16[128,1024]{1,0:T(8,128)(2,1)} %tokens.2.own), channel_id=1, source_target_pairs={{0,1},{1,0},{2,3},{3,2},{4,5},{5,4},{6,7},{7,6},{8,9},{9,8},{10,11... | collective-permute-start | bytes 786440 | tf_op jit(solution)/shard_map/cond/branch_1_fun/ppermute | solution.py:41
  292.9 15.0 %collective-permute-start.39 = (bf16[64,2304]{1,0:T(8,128)(2,1)}, bf16[64,2304]{1,0:T(8,128)(2,1)S(1)}, u32[]{:S(2)}, u32[]{:S(2)}) collective-permute-start(bf16[64,2304]{1,0:T(8,128)(2,1)} %get-tuple-element.637), channel_id=1, source_target_pairs={{0,4},{4,0},{1,5},{5,1},{2,6},{6,2},{3,7},{7,3},{8,12},{12,8},{9,1... | collective-permute-start | bytes 884744 | tf_op jit(solution)/shard_map/ppermute | solution.py:41
  (26 other events, 69.6 us)
Sparse Core Ops, SparseCore 0:
  24.3 90.3 all-gather.5
  117.0 50.6 all-gather.7
  170.6 42.6 all-gather.9
  261.7 43.3 all-gather.11

commit v3 on v2

--- a/solution.py
+++ b/solution.py
@@ -135,13 +135,14 @@
     if len(pieces) == 1:
         return [pltpu.make_async_copy(pieces[0], weight, sems.at[0])]
     count, rows, cols = pieces[0].shape
-    slab = (rows - 16) // 3
+    slab = HEAD_DIM
+    behind = slab + extra_count(slab)
     copies = []
     for c, piece in enumerate(pieces):
         for spot in range(count):
             row = (spot * 2 + (idx[3] ^ c)) * slab
             for i in range(2):
-                here = piece.at[spot, pl.ds((i + 1) * slab + 16, slab), :]
+                here = piece.at[spot, pl.ds(behind + i * slab, slab), :]
                 there = weight.at[pl.ds(pl.multiple_of(row, slab), slab), pl.ds(i * cols, cols)]
                 copies.append(pltpu.make_async_copy(here, there, sems.at[len(copies)]))
     return copies
@@ -166,18 +167,40 @@
     return weight[...]
 
 
+def extra_count(slab):
+    return 0 if slab >= HEAD_DIM else 16
+
+
+def put_extra(message, slab, extra):
+    if extra_count(slab):
+        message[slab : slab + 16, :] = extra
+        return
+    for i in range(4):
+        message[i * 16 : (i + 1) * 16, PAIR : PAIR + HEAD_DIM] = extra[
+            :, i * HEAD_DIM : (i + 1) * HEAD_DIM
+        ]
+
+
+def get_extra(message, slab):
+    if extra_count(slab):
+        return message[slab : slab + 16, :]
+    lanes = slice(PAIR, PAIR + HEAD_DIM)
+    return jnp.concatenate([message[i * 16 : (i + 1) * 16, lanes] for i in range(4)], axis=1)
+
+
 def prep_kernel(idx, tw, ow, ew, cw, live, heads, low, tri):
     slab, span = ew.shape
     alive = jnp.broadcast_to(live[...], (16, live.shape[1])).astype(WIDE).astype(LOW)
+    alive = jnp.concatenate([alive, jnp.zeros((16, QUAD - live.shape[1]), LOW)], axis=1)
+    behind = slab + extra_count(slab)
     for spot in range(NZ * 2):
         at = spot * HEAD_DIM
         for part, lane in enumerate(LANES):
             heads[spot, :slab, lane : lane + HEAD_DIM] = tw[part, :, at : at + HEAD_DIM].astype(LOW)
         heads[spot, :slab, PAIR : PAIR + HEAD_DIM] = jnp.zeros((slab, HEAD_DIM), LOW)
-        heads[spot, slab : slab + 16, : live.shape[1]] = alive
-        heads[spot, slab : slab + 16, PAIR:] = jnp.zeros((16, PAIR), LOW)
-        heads[spot, slab + 16 : 2 * slab + 16, :] = ow[:, :QUAD].astype(LOW)
-        heads[spot, 2 * slab + 16 :, :] = ow[:, QUAD:].astype(LOW)
+        put_extra(heads.at[spot], slab, alive)
+        heads[spot, behind : behind + slab, :] = ow[:, :QUAD].astype(LOW)
+        heads[spot, behind + slab :, :] = ow[:, QUAD:].astype(LOW)
     low[:, :span] = ew[...].astype(LOW)
     low[:, span:] = cw[...].astype(LOW)
     for part in range(3):
@@ -185,12 +208,12 @@
 
 
 def heads_kernel(idx, own, other, weight, live0, live1):
-    slab, mc = (own.shape[1] - 16) // 3, idx[3]
+    slab, mc = HEAD_DIM, idx[3]
     for spot in range(NZ * 2):
         for source, c, live in ((own, mc, live0), (other, 1 - mc, live1)):
             rows = pl.ds(pl.multiple_of((spot * 2 + c) * slab, slab), slab)
             weight[rows, :] = source[spot, :slab, :]
-            live[spot : spot + 1, :] = source[spot, slab : slab + 16, :PAIR].astype(WIDE)[:1]
+            live[spot : spot + 1, :] = get_extra(source.at[spot], slab)[:, :PAIR].astype(WIDE)[:1]
 
 
 def swap_halves(value):
@@ -242,7 +265,7 @@
         low_lanes = lax.broadcasted_iota(jnp.int32, (value.shape[0], PAIR), 1) < HEAD_DIM
         triple = dot_nn(value, weights) + offset
         turned = turn(triple[:, :PAIR], cosine[at, :], sine[at, :])
-        query[at, :] = jnp.where(low_lanes, turned, 0.0).astype(LOW)
+        query[at, :] = jnp.where(low_lanes, turned * HEAD_DIM ** (-0.5), 0.0).astype(LOW)
         kv[at, :] = jnp.where(
             low_lanes, pltpu.roll(turned, HEAD_DIM, 1), triple[:, PAIR:]
         ).astype(LOW)
@@ -253,22 +276,46 @@
     return jnp.concatenate([rows[i : i + 1] for i in range(rows.shape[0])], axis=1)
 
 
-def attend_kernel(q_ref, kv0_ref, kv1_ref, qdoc_ref, kdoc0_ref, kdoc1_ref, out_ref, log_ref, pack_ref):
-    scale = HEAD_DIM ** (-0.5)
-    rows = q_ref.shape[3]
+def places_of(token, rows, half, blocks, idx, z, part):
+    x, upper, row = token // (2 * rows), token // rows % 2, token % rows
+    block = ((idx[0] * NZ + z) * 2 + x) * 2 + idx[3]
+    return (upper * half + part * rows + row) * blocks + block
+
+
+def docs_of(places, lens):
+    doc, begin = jnp.full(places.shape, -1, jnp.int32), jnp.int32(0)
+    for i in range(lens.shape[0]):
+        doc = jnp.where(begin <= places, doc + 1, doc)
+        begin = begin + lens[i]
+    return doc
+
+
+def as_row(column):
+    count = column.shape[0]
+    row = lax.broadcasted_iota(jnp.int32, (count, count), 0)
+    same = row == lax.broadcasted_iota(jnp.int32, (count, count), 1)
+    return jnp.sum(jnp.where(same, column, 0.0), axis=0, keepdims=True)
+
+
+def attend_kernel(
+    blocks, idx, lens, q_ref, kv0_ref, kv1_ref, kdoc0_ref, kdoc1_ref, out_ref, log_ref, pack_ref
+):
+    rows, half = q_ref.shape[3], kdoc0_ref.shape[1] // 2
     queries = q_ref[0].reshape(4 * rows, PAIR)
     kv = (kv0_ref[...], kv1_ref[...])
-    doc = qdoc_ref[0].reshape(4 * rows, 1)
-    allowed = [doc == key_row(ref) for ref in (kdoc0_ref, kdoc1_ref)]
+    token = lax.broadcasted_iota(jnp.int32, (4 * rows, 1), 0)
+    z, part = pl.program_id(0), pl.program_id(1)
+    doc = docs_of(places_of(token, rows, half, blocks, idx, z, part), lens)
     scores = [
-        jnp.where(ok, dot_nt(queries, keys) * scale, FLOOR_SCORE) for ok, keys in zip(allowed, kv)
+        jnp.where(doc == key_row(ref), dot_nt(queries, keys), FLOOR_SCORE)
+        for ref, keys in zip((kdoc0_ref, kdoc1_ref), kv)
     ]
     peak = jnp.maximum(*[jnp.max(s, axis=-1, keepdims=True) for s in scores])
-    weights = [jnp.where(ok, jnp.exp(s - peak), 0.0) for ok, s in zip(allowed, scores)]
+    weights = [jnp.exp(s - peak) for s in scores]
     total = sum(jnp.sum(w, axis=-1, keepdims=True) for w in weights)
     mixed = sum(dot_nn(w.astype(LOW), keys) for w, keys in zip(weights, kv)) / total
     out_ref[0] = mixed.reshape(2, 2, rows, PAIR)
-    log_ref[0] = (peak + jnp.log(total)).reshape(2, 2, rows, 1)
+    log_ref[0, 0] = as_row(peak + jnp.log(total))
     low_lanes = lax.broadcasted_iota(jnp.int32, (rows, PAIR), 1) < HEAD_DIM
     for x in range(2):
         upper = mixed[2 * x * rows : (2 * x + 1) * rows]
@@ -282,41 +329,49 @@
     full = lambda n, m: pl.BlockSpec((n, m), lambda i, j: (0, 0))
     part = lambda m: pl.BlockSpec((1, 2, 2, size, m), lambda i, j: (i, 0, 0, j, 0))
     pack = pl.BlockSpec((1, 2, size, PAIR), lambda i, j: (i, 0, j, 0))
+    logs = pl.BlockSpec((1, 1, 1, 4 * size), lambda i, j: (i, j, 0, 0))
     kv, docs = full(keys, PAIR), full(key_rows, rows)
-    return (NZ, half // size), part, pack, kv, docs
-
-
-def attend(queries, kv0, kv1, qdoc, kdoc0, kdoc1):
+    return (NZ, half // size), part, pack, logs, kv, docs
+
+
+SCALARS = [pl.BlockSpec(memory_space=pltpu.SMEM)] * 2
+
+
+def attend(blocks, index, lens, queries, kv0, kv1, kdoc0, kdoc1):
     rows = kdoc0.shape[1]
     half = rows // 2
-    grid, part, pack, kv, docs = attend_specs(rows, kv0.shape[0], kdoc0.shape[0])
+    grid, part, pack, logs, kv, docs = attend_specs(rows, kv0.shape[0], kdoc0.shape[0])
     return pl.pallas_call(
-        attend_kernel,
+        partial(attend_kernel, blocks),
         grid=grid,
-        in_specs=[part(PAIR), kv, kv, part(1), docs, docs],
-        out_specs=[part(PAIR), part(1), pack],
+        in_specs=SCALARS + [part(PAIR), kv, kv, docs, docs],
+        out_specs=[part(PAIR), logs, pack],
         out_shape=[
             shape((NZ, 2, 2, half, PAIR), WIDE),
-            shape((NZ, 2, 2, half, 1), WIDE),
+            shape((NZ, grid[1], 1, 4 * half // grid[1]), WIDE),
             shape((NZ, 2, half, PAIR), LOW),
         ],
         compiler_params=PARAMS,
         cost_estimate=cost("attend"),
         name="attend",
-    )(queries.reshape(NZ, 2, 2, half, PAIR), kv0, kv1, qdoc, kdoc0, kdoc1)
+    )(index, lens, queries.reshape(NZ, 2, 2, half, PAIR), kv0, kv1, kdoc0, kdoc1)
 
 
 def attend_back_kernel(
-    q_ref, g_ref, o_ref, log_ref, kv0_ref, kv1_ref, qdoc_ref, kdoc0_ref, kdoc1_ref,
-    dq_ref, dkv0_ref, dkv1_ref,
+    blocks, idx, lens, q_ref, g_ref, o_ref, log_ref, kv0_ref, kv1_ref, kdoc0_ref, kdoc1_ref,
+    dq_ref, dkv0_ref, dkv1_ref, column0, column1,
 ):
-    scale = HEAD_DIM ** (-0.5)
-    rows = q_ref.shape[3]
-
-    @pl.when((pl.program_id(0) == 0) & (pl.program_id(1) == 0))
+    rows, width = q_ref.shape[3], kdoc0_ref.shape[1]
+    z, part = pl.program_id(0), pl.program_id(1)
+
+    @pl.when((z == 0) & (part == 0))
     def _():
         dkv0_ref[...] = jnp.zeros_like(dkv0_ref)
         dkv1_ref[...] = jnp.zeros_like(dkv1_ref)
+        for ref, column in ((kdoc0_ref, column0), (kdoc1_ref, column1)):
+            turned = jnp.transpose(ref[...].astype(WIDE))
+            for i in range(ref.shape[0]):
+                column[i * width : (i + 1) * width, :] = turned[:, i : i + 1]
 
     queries = q_ref[0].reshape(4 * rows, PAIR)
     high_lanes = lax.broadcasted_iota(jnp.int32, (rows, PAIR), 1) >= HEAD_DIM
@@ -327,41 +382,44 @@
         parts.append(jnp.where(high_lanes, packed, 0.0))
     wide = jnp.concatenate(parts, axis=0)
     grads = wide.astype(LOW)
-    delta = jnp.sum(wide * o_ref[0].reshape(4 * rows, PAIR), axis=-1, keepdims=True)
-    doc, log_total = qdoc_ref[0].reshape(4 * rows, 1), log_ref[0].reshape(4 * rows, 1)
+    delta = as_row(jnp.sum(wide * o_ref[0].reshape(4 * rows, PAIR), axis=-1, keepdims=True))
+    token = lax.broadcasted_iota(jnp.int32, (1, 4 * rows), 1)
+    doc = docs_of(places_of(token, rows, width // 2, blocks, idx, z, part), lens).astype(WIDE)
+    log_total = log_ref[0, 0]
     total = jnp.zeros((4 * rows, PAIR), WIDE)
-    for kv_ref, kdoc_ref, dkv_ref in (
-        (kv0_ref, kdoc0_ref, dkv0_ref),
-        (kv1_ref, kdoc1_ref, dkv1_ref),
-    ):
+    for kv_ref, column, dkv_ref in ((kv0_ref, column0, dkv0_ref), (kv1_ref, column1, dkv1_ref)):
         keys = kv_ref[...]
-        raw = dot_nt(queries, keys)
-        probs = jnp.where(doc == key_row(kdoc_ref), jnp.exp(raw * scale - log_total), 0.0)
-        dprobs = dot_nt(grads, keys)
-        dscores = (probs * (dprobs - delta) * scale).astype(LOW)
-        total = total + dot_nn(dscores, keys)
-        dkv_ref[...] += dot_tn(dscores, queries) + dot_tn(probs.astype(LOW), grads)
-    dq_ref[0] = total.reshape(2, 2, rows, PAIR)
-
-
-def attend_back(queries, grads, out, log_total, kv0, kv1, qdoc, kdoc0, kdoc1):
+        raw = dot_nt(keys, queries)
+        probs = jnp.where(column[...] == doc, jnp.exp(raw - log_total), 0.0)
+        dprobs = dot_nt(keys, grads)
+        dscores = (probs * (dprobs - delta)).astype(LOW)
+        total = total + dot_tn(dscores, keys)
+        dkv_ref[...] += dot_nn(dscores, queries) + dot_nn(probs.astype(LOW), grads)
+    dq_ref[0] = (total * HEAD_DIM ** (-0.5)).reshape(2, 2, rows, PAIR)
+
+
+def attend_back(blocks, index, lens, queries, grads, out, log_total, kv0, kv1, kdoc0, kdoc1):
     rows, keys = kdoc0.shape[1], kv0.shape[0]
     half = rows // 2
-    grid, part, pack, kv, docs = attend_specs(rows, keys, kdoc0.shape[0])
+    grid, part, pack, logs, kv, docs = attend_specs(rows, keys, kdoc0.shape[0])
     return pl.pallas_call(
-        attend_back_kernel,
+        partial(attend_back_kernel, blocks),
         grid=grid,
-        in_specs=[part(PAIR), pack, part(PAIR), part(1), kv, kv, part(1), docs, docs],
+        in_specs=SCALARS + [part(PAIR), pack, part(PAIR), logs, kv, kv, docs, docs],
         out_specs=[part(PAIR), kv, kv],
         out_shape=[
             shape((NZ, 2, 2, half, PAIR), WIDE),
             shape((keys, PAIR), WIDE),
             shape((keys, PAIR), WIDE),
         ],
+        scratch_shapes=[pltpu.VMEM((keys, 1), WIDE)] * 2,
         compiler_params=PARAMS,
         cost_estimate=cost("attend_back"),
         name="attend_back",
-    )(queries.reshape(NZ, 2, 2, half, PAIR), grads, out, log_total, kv0, kv1, qdoc, kdoc0, kdoc1)
+    )(
+        index, lens, queries.reshape(NZ, 2, 2, half, PAIR), grads, out, log_total, kv0, kv1,
+        kdoc0, kdoc1,
+    )
 
 
 def branch_kernel(pieces, idx, got, *refs):
@@ -700,14 +758,25 @@
         pack[h, half:, :] = (sums0[h] + sums1[h].astype(WIDE)).astype(LOW)
 
 
-def triple_kernel(idx, dq, dkv, got, cosine, sine, out):
+def triple_kernel(idx, dq, dkv, got, cosine, sine, out, dense):
     rows = dq.shape[0]
     low_lanes = lax.broadcasted_iota(jnp.int32, (rows, PAIR), 1) < HEAD_DIM
     grads = dkv[...] + got[...]
     both_parts = jnp.where(low_lanes, dq[...], pltpu.roll(grads, HEAD_DIM, 1))
     turned = turn(both_parts, cosine[...], -sine[...])
-    out[:, :PAIR] = turned.astype(LOW)
+    turned, value = turned.astype(LOW), grads[:, HEAD_DIM:].astype(LOW)
+    out[:, :PAIR] = turned
     out[:, PAIR:] = jnp.where(low_lanes, 0.0, grads).astype(LOW)
+    rows = dense.shape[1] * 4 // 3
+    half, few = rows // 2, rows // 4
+    for i in range(dense.shape[0]):
+        at = i * rows
+        dense[i, :half, :PAIR] = turned[at : at + half]
+        dense[i, :half, PAIR:] = turned[at + half : at + rows]
+        for j in range(4):
+            dense[i, half:, j * HEAD_DIM : (j + 1) * HEAD_DIM] = value[
+                at + j * few : at + (j + 1) * few
+            ]
 
 
 def extra_rows(bias, vectors):
@@ -722,7 +791,7 @@
 def triple_weight_kernel(idx, *refs):
     sheets, (grad, vectors, keep, send, total) = refs[:8], refs[8:]
     mc = idx[3]
-    slab = keep.shape[1] - 16
+    slab = HEAD_DIM
     for i, (value, at) in enumerate(sheet_rows(idx, sheets)):
         part = dot_tn(value, grad[at, :])
         if i == 0:
@@ -734,7 +803,7 @@
         for out, c in ((keep, mc), (send, 1 - mc)):
             at = pl.ds(pl.multiple_of((spot * 2 + c) * slab, slab), slab)
             out[spot, :slab, :] = total[at, :].astype(LOW)
-            out[spot, slab:, :] = extra
+            put_extra(out.at[spot], slab, extra)
 
 
 def pair_sum_kernel(idx, one, two, out):
@@ -746,11 +815,11 @@
     total = 0.0
     for spot in range(NZ * 2):
         at = spot * HEAD_DIM
-        here = got[spot].astype(WIDE)
+        here, extra = got[spot].astype(WIDE), get_extra(got.at[spot], slab).astype(WIDE)
         for part, lane in enumerate(LANES):
             weight[part, :, at : at + HEAD_DIM] = here[:slab, lane : lane + HEAD_DIM]
-            bias[part : part + 1, at : at + HEAD_DIM] = here[slab : slab + 1, lane : lane + HEAD_DIM]
-        total = total + here[slab:]
+            bias[part : part + 1, at : at + HEAD_DIM] = extra[:1, lane : lane + HEAD_DIM]
+        total = total + extra
     row = 1
     for out in vectors:
         for i in range(0, out.shape[0], 2):
@@ -762,10 +831,21 @@
 def tokens_kernel(idx, got, message, part, group, held, sems):
     copy = slab_copy(message, 0, held, sems)
     copy.start()
+    rows = part.shape[0]
+    half, few = rows // 2, rows // 4
     for h in range(NZ * 2):
-        for p, lane in enumerate(LANES):
+        for p in range(2):
             at = (p * NZ * 2 + h) * HEAD_DIM
-            group[:, at : at + HEAD_DIM] = got[h, :, lane : lane + HEAD_DIM]
+            for i in range(2):
+                lane = i * PAIR + p * HEAD_DIM
+                group[i * half : (i + 1) * half, at : at + HEAD_DIM] = got[
+                    h, :half, lane : lane + HEAD_DIM
+                ]
+        at = (2 * NZ * 2 + h) * HEAD_DIM
+        for j in range(4):
+            group[j * few : (j + 1) * few, at : at + HEAD_DIM] = got[
+                h, half:, j * HEAD_DIM : (j + 1) * HEAD_DIM
+            ]
     copy.wait()
     part[...] = dot_nt(group[...], held[...]).astype(LOW)
 
@@ -864,7 +944,7 @@
             contract_weight.T,
             line(live_mask),
         ),
-        [shape((NZ * 2, 3 * slab + 16, QUAD), LOW)]
+        [shape((NZ * 2, 3 * slab + extra_count(slab), QUAD), LOW)]
         + [shape((slab, n), LOW) for n in (2 * span, 6 * QUAD)],
     )
 
@@ -881,7 +961,7 @@
             two = jnp.stack([piece, flip(piece, "x")])
             sheets += [two, flip(two, "y")]
         own_places = (mo * NZ * 4 + rank + mc)[:, None] + where[None, :]
-        own_doc, own_position = doc_layout(doc_lengths, own_places.reshape(-1))
+        own_position = doc_layout(doc_lengths, own_places.reshape(-1))[1]
         lane = jnp.arange(PAIR) % (HEAD_DIM // 2)
         exponent = (2 * lane).astype(WIDE) / HEAD_DIM
         angles = own_position.astype(WIDE)[:, None] * jnp.exp(-math.log(10000.0) * exponent)[None, :]
@@ -897,13 +977,13 @@
         positive = line(jnp.repeat(positives, query_vecs.shape[0] // queries_count))
         got = after(got, sheets[3], sheets[5], sheets[7], tables[0], units[0])
         head = head_weights(got, flip(got, "c"))
-        return head, sheets[2:], tables, list(units), positive, own_doc.reshape(NZ, 2, 2, half, 1)
-
-    head, sheets, (cosine, sine), (query_unit, own_queries), positive, qdoc = stage(heads_stage)
+        return head, sheets[2:], tables, list(units), positive
+
+    head, sheets, (cosine, sine), (query_unit, own_queries), positive = stage(heads_stage)
     head_triple, kdoc0, kdoc1, outs = head
     pieces = len(outs)
     sheets = [tokens, own_other] + sheets
-    positive, qdoc = lax.optimization_barrier((positive, qdoc))
+    positive = lax.optimization_barrier(positive)
     count = NZ * 2 * rows
 
     def project_stage():
@@ -918,13 +998,14 @@
 
     queries, kv, kv_other = stage(project_stage)
     kv0, kv1 = [widen(v).reshape(-1, PAIR) for v in (kv, kv_other)]
-    meta = (qdoc, kdoc0, kdoc1)
+    meta = (kdoc0, kdoc1)
+    steps = (blocks, index, doc_lengths)
 
     def to_blocks(value):
         return lax.all_to_all(value.reshape((NZ * 2,) + value.shape[-2:]), ("z", "x"), 0, 0)
 
     def attention_stage():
-        out, log_total, pack = attend(queries, kv0, kv1, *meta)
+        out, log_total, pack = attend(*steps, queries, kv0, kv1, *meta)
         return out, log_total, to_blocks(pack)
 
     out, log_total, pack = stage(attention_stage)
@@ -986,8 +1067,7 @@
         )
 
     second_low, unitary2, inverse2, embed, unit_low, expo, totals, message = stage(second_stage)
-    firsts = [first_keep, first_other, first_across, flip(first_other, "c")]
-    totals = after(totals, first_other, first_across)
+    totals = after(totals, first_across)
 
     def tree(own, one, two, three):
         return (own + one) + (two + three)
@@ -1022,7 +1102,7 @@
 
     grad_second_in, keep, send, part, loss, coefficients, sums_own, sums_send = stage(middle_stage)
 
-    triple_low, part = lax.optimization_barrier((triple_low, part))
+    triple_low, part, first_other = lax.optimization_barrier((triple_low, part, first_other))
     units = lax.all_gather(after(message, part), BLK, axis=0, tiled=True)
     keep_other, keep_across = flip(send, "x"), flip(keep, "c")
 
@@ -1043,7 +1123,6 @@
 
     grad_first_in, grad_branch, vectors1, pack = stage(first_stage)
     keep_other = after(keep_other, grad_branch)
-    grads = [keep, keep_other, keep_across, flip(keep_other, "c")]
     dims, dims_out = (2, slab, quarter), (2, slab, QUAD)
     dims_both = (2, slab, quarter + QUAD)
     left_right = [pltpu.VMEM((4 * rows, width), LOW)]
@@ -1060,8 +1139,10 @@
 
     def weights_stage():
         got = to_blocks(pack)
+        firsts = [first_keep, first_other, first_across, flip(first_other, "c")]
+        grads = [keep, keep_other, keep_across, flip(keep_other, "c")]
         other = flip(grad_branch, "x")
-        got = got, [grad_branch, other, flip(grad_branch, "c"), flip(other, "c")]
+        got = got, [other, flip(grad_branch, "c"), flip(other, "c")], firsts[3]
         if outer == 1:
             parts = whole(
                 weights_kernel,
@@ -1077,13 +1158,15 @@
         expand = parts_of([f[top] for f in firsts], [g[mid] for g in grads])
         return got, [part for p in (contract, expand) for part in (p[::2], p[1::2].astype(LOW))]
 
-    (grad_out, branches), weight_parts = stage(weights_stage)
+    (grad_out, branches, first_last), weight_parts = stage(weights_stage)
+    branches = [grad_branch] + branches
+    firsts = [first_keep, first_other, first_across, first_last]
     contract_keep, contract_send, expand_keep, expand_send = weight_parts
     contract_got, expand_got = xor_z(contract_send, 1), xor_z(expand_send, 1)
 
     def attend_stage():
         grad_query, dkv0, dkv1 = attend_back(
-            queries, grad_out.reshape(NZ, 2, -1, PAIR), out, log_total, kv0, kv1, *meta
+            *steps, queries, grad_out.reshape(NZ, 2, -1, PAIR), out, log_total, kv0, kv1, *meta
         )
         dkv0, dkv1 = [narrow(v.reshape(outer, -1, PAIR)) for v in (dkv0, dkv1)]
         triple = whole(
@@ -1091,25 +1174,18 @@
             "triple",
             index,
             (grad_query.reshape(count, PAIR), dkv0, flip(dkv1, "c"), cosine, sine),
-            [shape((count, QUAD), LOW)],
-        )[0]
-        mine = whole(
-            partial(query_back_kernel, half),
-            "query_back",
-            index,
-            (kdoc0, kdoc1, coefficients, own_queries, units, sum_outer(grad_out)),
-            [shape((shares + chunk + 16, proj), LOW)],
-        )[0]
-        return triple, mine
-
-    grad_triple, mine = stage(attend_stage)
+            [shape((count, QUAD), LOW), shape((NZ * 2, rows * 3 // 4, QUAD), LOW)],
+        )
+        return triple
+
+    grad_triple, dense_triple = stage(attend_stage)
     grad_triple, contract_got = lax.optimization_barrier((grad_triple, contract_got))
     contract_own, contract_send = whole(
         pair_kernel, "pair", index, (contract_keep, contract_got), [shape(dims, t) for t in (WIDE, LOW)]
     )
     contract_got = xor_z(contract_send, 2)
-    grad_triple = after(grad_triple, contract_own)
-    dims_triple = (NZ * 2, slab + 16, QUAD)
+    grad_triple, units = lax.optimization_barrier((grad_triple, units, contract_own))[:2]
+    dims_triple = (NZ * 2, slab + extra_count(slab), QUAD)
     vector = shape((width // PAIR, PAIR), WIDE)
 
     def triple_parts():
@@ -1150,15 +1226,22 @@
         return parts[::2], parts[1::2].astype(LOW)
 
     def triple_stage():
-        block_triple = to_blocks(grad_triple.reshape(NZ * 2, rows, QUAD))
+        block_triple = to_blocks(dense_triple)
         keep, send = triple_parts()
         output_parts = output_parts_of()
         packed = whole(
             pair_sum_kernel, "pair_sum", index, (keep, flip(send, "c")), [shape(dims_triple, LOW)]
         )[0]
-        return block_triple, packed, output_parts[0], xor_z(output_parts[1], 1)
-
-    block_triple, packed, output_keep, output_got = stage(triple_stage)
+        mine = whole(
+            partial(query_back_kernel, half),
+            "query_back",
+            index,
+            (kdoc0, kdoc1, coefficients, own_queries, units, sum_outer(grad_out)),
+            [shape((shares + chunk + 16, proj), LOW)],
+        )[0]
+        return block_triple, packed, output_parts[0], xor_z(output_parts[1], 1), mine
+
+    block_triple, packed, output_keep, output_got, mine = stage(triple_stage)
     block_triple, contract_got, expand_got = lax.optimization_barrier(
         (block_triple, contract_got, expand_got)
     )
@@ -1186,9 +1269,10 @@
         tokens_grad = whole(
             tokens_sum_kernel, "tokens_sum", index, (part, flip(part, "y"), grad_first_in), [wide_rows]
         )[0]
-        return tokens_grad, lax.all_to_all(after(packed, part), ("z", "x"), 0, 0)
-
-    tokens_grad, packed = stage(tokens_stage)
+        return tokens_grad
+
+    tokens_grad = stage(tokens_stage)
+    packed = lax.all_to_all(after(packed, tokens_grad), ("z", "x"), 0, 0)
     contract_own, spread = after(contract_own, tokens_grad), after(spread, tokens_grad)
     keep, keep_out, send = whole(
         line_sum_kernel,
@@ -1197,28 +1281,29 @@
         (contract_own, contract_got, expand_own, output_own, both_got),
         [shape((2, slab, quarter), WIDE), shape((slab, QUAD), WIDE), shape((slab, 2 * quarter + QUAD), LOW)],
     )
+    triple_grad, triple_bias_grad, output_bias_grad, gain_one, shift_one = whole(
+        triple_out_kernel,
+        "triple_out",
+        index,
+        (packed,),
+        [shape((3, slab, 2 * QUAD), WIDE), shape((3, 2 * QUAD), WIDE)] + [vector] * 3,
+    )
+    contract_grad, expand_grad, output_grad = whole(
+        columns_kernel,
+        "columns",
+        index,
+        (keep, keep_out, flip(send, "x")),
+        [shape((slab, n), WIDE) for n in (span, span, 2 * QUAD)],
+    )
+
     queries_grad, head_grad, contract_bias_grad, gain_two, shift_two, expand_bias_grad = whole(
         spread_kernel,
         "spread",
         index,
-        (spread.reshape(NZ * 4, -1, proj),),
+        (after(spread, contract_grad).reshape(NZ * 4, -1, proj),),
         [shape((query_vecs.shape[0], proj), WIDE), shape((width, proj), WIDE)]
         + [vector] * 3
         + [shape((span // PAIR, PAIR), WIDE)],
-    )
-    triple_grad, triple_bias_grad, output_bias_grad, gain_one, shift_one = whole(
-        triple_out_kernel,
-        "triple_out",
-        index,
-        (after(packed, send),),
-        [shape((3, slab, 2 * QUAD), WIDE), shape((3, 2 * QUAD), WIDE)] + [vector] * 3,
-    )
-    contract_grad, expand_grad, output_grad = whole(
-        columns_kernel,
-        "columns",
-        index,
-        (keep, keep_out, after(flip(send, "x"), queries_grad)),
-        [shape((slab, n), WIDE) for n in (span, span, 2 * QUAD)],
     )
 
     return (

time: 319 us -> 305 us (0.956)
  waiting for transfers between devices: 115 us -> 102 us
    all_to_all x1, waiting for transfers between devices: 8.19 us -> 1.93 us  [shards(): packed = lax.all_to_all(after(packed, tokens_grad), ('z', 'x'), 0, 0)]
    all_gather x1, waiting for transfers between devices: 9.55 us -> 3.99 us  [shards(): spread = lax.all_gather(after(mine, expand_own), ('z', 'x', 'c'))]
    all_to_all x2, waiting for transfers between devices: 10.8 us -> 6.06 us  [to_blocks(): lax.all_to_all(value.reshape((NZ * 2,) + value.shape[-2:]), ('z', 'x'), 0...]
    ppermute x26, waiting for transfers between devices: 44.9 us -> 48.8 us  [flip(): return lax.ppermute(value, axis, [(0, 1), (1, 0)])]
  transfers between devices with their start and end apart: 48 -> 48, of which waited for: 26 -> 25; matrix products, arithmetic and copies ran while one was open for 4% -> 3% of each run, Pallas kernels for 29% -> 30%
where the time goes in v3:
time: 305 us; the launch traced here: 303 us
  waiting for transfers between devices  102 us (33%)
  Pallas kernels  94.6 us (31%)
  starting transfers between devices  61.5 us (20%)
  between operations  14 us (5%)
  blocking collectives  13.8 us (5%)
  local copies, waits for them, and re-layouts  9.52 us (3%)
  other arithmetic  7.32 us (2%)
    pallas_call x23, Pallas kernels, whole(): pl.pallas_call(kernel, in_specs=[pl.BlockSpec(memory_space=pltpu.SMEM)] +...  78.4 us
    ppermute x26, waiting for transfers between devices, flip(): return lax.ppermute(value, axis, [(0, 1), (1, 0)])  48.8 us
    ppermute x26, starting transfers between devices, flip(): return lax.ppermute(value, axis, [(0, 1), (1, 0)])  21.7 us
    ppermute x11, waiting for transfers between devices, xor_z(): return lax.ppermute(value, 'z', [(i, i ^ mask) for i in FOUR])  17.1 us
    all_to_all x1, waiting for transfers between devices, heads_stage(): got = lax.all_to_all(heads, ('z', 'x'), 0, 0)  16 us
    ppermute x11, starting transfers between devices, xor_z(): return lax.ppermute(value, 'z', [(i, i ^ mask) for i in FOUR])  16 us
    all_to_all x1, blocking collectives, to_blocks(): lax.all_to_all(value.reshape((NZ * 2,) + value.shape[-2:]), ('z', 'x'), 0...  13.8 us
    all_to_all x2, starting transfers between devices, to_blocks(): lax.all_to_all(value.reshape((NZ * 2,) + value.shape[-2:]), ('z', 'x'), 0...  13.1 us
  transfers between devices with their start and end apart: 48, of which 25 were waited for; matrix products, arithmetic and copies ran while one was open for 3% of the time, Pallas kernels for 30%

profile of v3, /device:TPU:0, one launch (start us, length us, event | category | flops | bytes accessed | tf_op | source)
XLA Modules:
  0.0 303.3 jit_solution(16406608627698729060)
XLA Ops:
  8.2 3.1 %collective-permute-start.28 = (bf16[64,1024]{1,0:T(8,128)(2,1)S(1)}, bf16[64,1024]{1,0:T(8,128)(2,1)S(1)}, u32[]{:S(2)}, u32[]{:S(2)}) collective-permute-start(bf16[64,1024]{1,0:T(8,128)(2,1)S(1)} %constant_dynamic-slice_fusion), channel_id=1, source_target_pairs={{0,8},{8,0},{16,24},{24,16},{1,9},{9,1},{17,25},{25,17},{2,10},{10... | collective-permute-start | bytes 393224 | tf_op jit(solution)/shard_map/ppermute | solution.py:33
  11.2 2.6 collective-permute-start.29
  15.7 2.8 prep.1
  18.4 5.8 %collective-permute-done.29 = bf16[64,1024]{1,0:T(8,128)(2,1)S(1)} collective-permute-done((bf16[64,1024]{1,0:T(8,128)(2,1)S(1)}, bf16[64,1024]{1,0:T(8,128)(2,1)S(1)}, u32[]{:S(2)}, u32[]{:S(2)}) %collective-permute-start.29) | collective-permute-done | bytes 131104 | tf_op jit(solution)/shard_map/ppermute | solution.py:33
  24.9 49.8 %conditional.11 = (bf16[1024,256]{1,0:T(8,128)(2,1)S(1)}, s32[8,128]{1,0:T(8,128)S(1)}, s32[8,128]{1,0:T(8,128)S(1)}, bf16[8,192,256]{2,1,0:T(8,128)(2,1)}, bf16...) conditional(s32[]{:T(128)} %bitcast.19, () %tuple.116, ...), branch_computations={%region_0.0_spmd, %region_1.6_spmd} | conditional | flops 5520703488 | bytes 30736448 | solution.py:904
  28.5 4.2 %all-to-all-start.3 = ((bf16[8,192,256]{2,1,0:T(8,128)(2,1)}), bf16[8,192,256]{2,1,0:T(8,128)(2,1)}, u32[]{:S(2)}, u32[]{:S(2)}) async-start(bf16[8,192,256]{2,1,0:T(8,128)(2,1)} %get-tuple-element.257), calls=%async_computation.3 | async-start | bytes 1572864 | tf_op jit(solution)/shard_map/cond/branch_1_fun/all_to_all | solution.py:958
  40.1 3.1 %fusion = (f32[1024,128]{1,0:T(8,128)}, f32[1024,128]{1,0:T(8,128)}) fusion(f32[128]{0:T(128)S(1)} %get-tuple-element.679, f32[128]{0:T(128)S(1)} %get-tuple-element.680, f32[1024]{0:T(1024)S(1)} %subtract_convert_fusion), kind=kLoop, calls=%fused_computation.2 | loop fusion | flops 262144 | bytes 1053696 | tf_op jit(solution)/shard_map/cond/branch_1_fun/mul | solution.py:969
  44.7 5.2 %collective-permute-done.17 = bf16[2,64,1024]{2,1,0:T(8,128)(2,1)} collective-permute-done((bf16[2,64,1024]{2,1,0:T(8,128)(2,1)}, bf16[2,64,1024]{2,1,0:T(8,128)(2,1)}, u32[]{:S(2)}, u32[]{:S(2)}) %collective-permute-start.17) | collective-permute-done | bytes 262176 | tf_op jit(solution)/shard_map/cond/branch_1_fun/ppermute | solution.py:41
  49.8 2.8 collective-permute-done.19
  52.6 16.0 %all-to-all-done.3.own = bf16[8,192,256]{2,1,0:T(8,128)(2,1)} async-done(((bf16[8,192,256]{2,1,0:T(8,128)(2,1)}), bf16[8,192,256]{2,1,0:T(8,128)(2,1)}, u32[]{:S(2)}, u32[]{:S(2)}) %all-to-all-start.3) | async-done | bytes 786464 | tf_op jit(solution)/shard_map/cond/branch_1_fun/all_to_all | solution.py:958
  69.1 2.2 collective-permute-done.20.other
  71.3 2.1 heads.1
  74.7 6.0 %conditional.12 = (bf16[1024,128]{1,0:T(8,128)(2,1)}, bf16[1024,128]{1,0:T(8,128)(2,1)}, bf16[1024,128]{1,0:T(8,128)(2,1)}) conditional(s32[]{:T(128)} %bitcast.19, () %tuple.115, (s32[5]{0:T(128)S(1)}, bf16[128,1024]{1,0:T(8,128)(2,1)S(1)}, bf16[128,1024]{1,0:T(8,128)(2,1)}, bf16[2,64,1024]{2,1,0:T(8,128)(2,1)}, bf16[2,64,1024]{2,1,0:T(8,128)(2,1)}, ...), branch_computations={%region_6.7_spmd, %region_7.8_spmd} | conditional | flops 4369999872 | bytes 15108640 | solution.py:904
  74.8 4.1 %project.1 = (bf16[1024,128]{1,0:T(8,128)(2,1)}, bf16[1024,128]{1,0:T(8,128)(2,1)}) custom-call(s32[5]{0:T(128)S(1)} %get-tuple-element.275.idx, bf16[128,1024]{1,0:T(8,128)(2,1)S(1)} %get-tuple-element.276.refs_0_, bf16[128,1024]{1,0:T(8,128)(2,1)} %get-tuple-element.277.refs_1_, bf16[2,64,1024]{2,1,0:T(8,128)(2,1)} %get-tuple-element.278.refs_2_, ...), custom_call_target="tpu_custom_call" | custom-call | flops 4369999872 | bytes 14060000 | tf_op jit(solution)/shard_map/cond/branch_1_fun/project/pallas_call | solution.py:115
  80.7 20.4 %conditional.13 = (f32[4,2,2,64,128]{4,3,2,1,0:T(8,128)}, f32[4,1,1,256]{3,2,1,0:T(1,128)}, bf16[8,64,128]{2,1,0:T(8,128)(2,1)S(1)}) conditional(s32[]{:T(128)} %bitcast.19, () %tuple.114, (bf16[1024,128]{1,0:T(8,128)(2,1)}, s32[5]{0:T(128)S(1)}, s32[4]{0:T(128)S(1)}, bf16[1024,128]{1,0:T(8,128)(2,1)}, bf16[1024,128]{1,0:T(8,128)(2,1)}, ...), branch_computations={%region_8.9_spmd, %region_9.10_spmd} | conditional | flops 8625000448 | bytes 28012168 | solution.py:904
  80.7 6.5 %attend.1 = (f32[4,2,2,64,128]{4,3,2,1,0:T(8,128)}, f32[4,1,1,256]{3,2,1,0:T(1,128)}, bf16[4,2,64,128]{3,2,1,0:T(8,128)(2,1)}) custom-call(s32[5]{0:T(128)S(1)} %get-tuple-element.290.idx, s32[4]{0:T(128)S(1)} %get-tuple-element.291.lens, bf16[4,2,2,64,128]{4,3,2,1,0:T(8,128)(2,1)} %bitcast.9.q_ref, bf16[1024,128]{1,0:T(8,128)(2,1)} %get-tuple-element.293.kv0_ref, ...), custom_call_target="tpu_custom_call" | custom-call | flops 8625000448 | bytes 27750000 | tf_op jit(solution)/shard_map/cond/branch_1_fun/attend/pallas_call | solution.py:344
  87.2 13.8 %all_to_all.21 = bf16[8,64,128]{2,1,0:T(8,128)(2,1)S(1)} all-to-all(bf16[8,64,128]{2,1,0:T(8,128)(2,1)} %bitcast.49), channel_id=1, replica_groups=mesh['o'=1,'z'=4,'x'=2,'c'=2,'y'=2] {'z','x'}, dimensions={0} | all-to-all | bytes 262144 | tf_op jit(solution)/shard_map/cond/branch_1_fun/all_to_all | solution.py:1005
  101.1 11.3 %conditional.14 = (bf16[128,512]{1,0:T(8,128)(2,1)S(1)}, bf16[128,1024]{1,0:T(8,128)(2,1)}, bf16[128,1024]{1,0:T(8,128)(2,1)}) conditional(s32[]{:T(128)} %bitcast.19, () %tuple.113, (s32[5]{0:T(128)S(1)}, bf16[8,64,128]{2,1,0:T(8,128)(2,1)S(1)}, bf16[8,192,256]{2,1,0:T(8,128)(2,1)}, bf16[8,192,256]{2,1,0:T(8,128)(2,1)}) %tuple.121), branch_computations={%region_10.11_spmd, %region_11.12_spmd} | conditional | flops 4024999936 | bytes 13998640 | solution.py:904
  101.1 3.2 %branch.1 = (bf16[128,512]{1,0:T(8,128)(2,1)S(1)}, bf16[128,1024]{1,0:T(8,128)(2,1)}) custom-call(s32[5]{0:T(128)S(1)} %get-tuple-element.300.idx, bf16[8,64,128]{2,1,0:T(8,128)(2,1)S(1)} %get-tuple-element.301.got, bf16[8,192,256]{2,1,0:T(8,128)(2,1)} %get-tuple-element.302.refs_0_, bf16[8,192,256]{2,1,0:T(8,128)(2,1)} %get-tuple-element.303.refs_1_), custom_call_target="tpu_custom_call" | custom-call | flops 4024999936 | bytes 12950000 | tf_op jit(solution)/shard_map/cond/branch_1_fun/branch/pallas_call | solution.py:115
  105.8 6.5 %collective-permute-done.1 = bf16[128,1024]{1,0:T(8,128)(2,1)} collective-permute-done((bf16[128,1024]{1,0:T(8,128)(2,1)}, bf16[128,1024]{1,0:T(8,128)(2,1)}, u32[]{:S(2)}, u32[]{:S(2)}) %collective-permute-start.1) | collective-permute-done | bytes 262176 | tf_op jit(solution)/shard_map/cond/branch_1_fun/ppermute | solution.py:41
  112.5 2.6 all-gather.6.cloned.1.call-done.slabs
  115.1 7.2 %forward.1 = (f32[128,1024]{1,0:T(8,128)}, f32[128,1024]{1,0:T(8,128)}, f32[128,1]{1,0:T(8,128)}, f32[128,2048]{1,0:T(8,128)}, bf16[288,1024]{1,0:T(8,128)(2,1)}...) custom-call(s32[5]{0:T(128)S(1)} %stack.47.idx, bf16[128,1024]{1,0:T(8,128)(2,1)} %get-tuple-element.561.own, ...), custom_call_target="tpu_custom_call" | custom-call | flops 8855000064 | bytes 28490000 | tf_op jit(solution)/shard_map/forward/pallas_call | solution.py:115
  123.6 12.6 %conditional.15 = ((bf16[128,1024]{1,0:T(8,128)(2,1)}, f32[128,1024]{1,0:T(8,128)}, f32[128,1]{1,0:T(8,128)}, f32[128,128]{1,0:T(8,128)}, bf16[128,128]{1,0:T(8,...) conditional(s32[]{:T(128)} %bitcast.19, () %tuple.112, ...), branch_computations={%region_12.13_spmd, %region_13.14_spmd} | conditional | flops 4140000000 | bytes 15433748 | solution.py:904
  125.2 6.9 %collective-permute-done.2.other = bf16[128,1024]{1,0:T(8,128)(2,1)S(1)} collective-permute-done((bf16[128,1024]{1,0:T(8,128)(2,1)}, bf16[128,1024]{1,0:T(8,128)(2,1)S(1)}, u32[]{:S(2)}, u32[]{:S(2)}) %collective-permute-start.2) | collective-permute-done | bytes 262176 | tf_op jit(solution)/shard_map/cond/branch_1_fun/ppermute | solution.py:41
  132.8 3.4 %second.1 = (bf16[128,1024]{1,0:T(8,128)(2,1)}, f32[128,1024]{1,0:T(8,128)}, f32[128,1]{1,0:T(8,128)}, f32[128,128]{1,0:T(8,128)}, bf16[128,128]{1,0:T(8,128)(2,...) custom-call(s32[5]{0:T(128)} %copy-done.16, bf16[128,1024]{1,0:T(8,128)(2,1)} %get-tuple-element.307.own, ...), custom_call_target="tpu_custom_call" | custom-call | flops 4140000000 | bytes 13320000 | tf_op jit(solution)/shard_map/cond/branch_1_fun/second/pallas_call | solution.py:115
  136.2 29.7 %conditional.16 = ((f32[128,1024]{1,0:T(8,128)}, bf16[256,1024]{1,0:T(8,128)(2,1)}, bf16[256,1024]{1,0:T(8,128)(2,1)}, bf16[128,1024]{1,0:T(8,128)(2,1)}, f32[8,...) conditional(s32[]{:T(128)} %bitcast.19, () %tuple.125, ...), branch_computations={%region_14.15_spmd, %region_15.16_spmd} | conditional | flops 13800048640 | bytes 47349480 | solution.py:904
  138.4 4.1 %collective-permute-done.22 = f32[4,4096]{1,0:T(4,128)S(1)} collective-permute-done((f32[4,4096]{1,0:T(4,128)S(1)}, f32[4,4096]{1,0:T(4,128)S(1)}, u32[]{:S(2)}, u32[]{:S(2)}) %collective-permute-start.22) | collective-permute-done | bytes 65568 | tf_op jit(solution)/shard_map/cond/branch_1_fun/ppermute | solution.py:37
  145.0 2.0 collective-permute-start.26
  147.0 3.6 %collective-permute-done.24.t1 = f32[4,4096]{1,0:T(4,128)S(1)} collective-permute-done((f32[4,4096]{1,0:T(4,128)S(1)}, f32[4,4096]{1,0:T(4,128)S(1)}, u32[]{:S(2)}, u32[]{:S(2)}) %collective-permute-start.24) | collective-permute-done | bytes 65568 | tf_op jit(solution)/shard_map/cond/branch_1_fun/ppermute | solution.py:33
  150.6 4.9 %collective-permute-done.25.t2 = f32[4,4096]{1,0:T(4,128)S(1)} collective-permute-done((f32[4,4096]{1,0:T(4,128)S(1)}, f32[4,4096]{1,0:T(4,128)S(1)}, u32[]{:S(2)}, u32[]{:S(2)}) %collective-permute-start.25) | collective-permute-done | bytes 65568 | tf_op jit(solution)/shard_map/cond/branch_1_fun/ppermute | solution.py:33
  156.2 9.8 %middle.1 = (f32[128,1024]{1,0:T(8,128)}, bf16[256,1024]{1,0:T(8,128)(2,1)}, bf16[256,1024]{1,0:T(8,128)(2,1)}, bf16[128,1024]{1,0:T(8,128)(2,1)}, f32[8,128]{1,...) custom-call(s32[5]{0:T(128)} %get-tuple-element.315.idx, ...), custom_call_target="tpu_custom_call" | custom-call | flops 13799999488 | bytes 44400000 | tf_op jit(solution)/shard_map/cond/branch_1_fun/middle/pallas_call | solution.py:115
  167.9 13.8 %conditional.17 = ((f32[128,1024]{1,0:T(8,128)}, bf16[128,1024]{1,0:T(8,128)(2,1)S(1)}, f32[8,1024]{1,0:T(8,128)S(1)}, bf16[8,144,128]{2,1,0:T(8,128)(2,1)})) conditional(s32[]{:T(128)} %bitcast.19, () %tuple.132, (bf16[128,1024]{1,0:T(8,128)(2,1)}, f32[1024]{0:T(1024)}, bf16[8,80,128]{2,1,0:T(8,128)(2,1)}, s32[5]{0:T(128)}, ...), branch_computations={%region_16.17_spmd, %region_17.18_spmd} | conditional | flops 4369999872 | bytes 17468016 | solution.py:904
  171.0 5.8 %collective-permute-done.3.other = bf16[128,1024]{1,0:T(8,128)(2,1)S(1)} collective-permute-done((bf16[128,1024]{1,0:T(8,128)(2,1)}, bf16[128,1024]{1,0:T(8,128)(2,1)S(1)}, u32[]{:S(2)}, u32[]{:S(2)}) %collective-permute-start.3) | collective-permute-done | bytes 262176 | tf_op jit(solution)/shard_map/cond/branch_1_fun/ppermute | solution.py:41
  177.5 4.1 %first_back.1 = (f32[128,1024]{1,0:T(8,128)}, bf16[128,1024]{1,0:T(8,128)(2,1)S(1)}, f32[8,1024]{1,0:T(8,128)S(1)}, bf16[8,144,128]{2,1,0:T(8,128)(2,1)}) custom-call(s32[5]{0:T(128)} %get-tuple-element.332.idx, bf16[128,1024]{1,0:T(8,128)(2,1)} %get-tuple-element.333.own, bf16[128,1024]{1,0:T(8,128)(2,1)} %copy-done.27, ...), custom_call_target="tpu_custom_call" | custom-call | flops 4369999872 | bytes 14060000 | tf_op jit(solution)/shard_map/cond/branch_1_fun/first_back/pallas_call | solution.py:115
  182.1 21.3 %conditional.18 = (bf16[8,144,128]{2,1,0:T(8,128)(2,1)}, bf16[128,1024]{1,0:T(8,128)(2,1)}, bf16[128,1024]{1,0:T(8,128)(2,1)}, bf16[128,1024]{1,0:T(8,128)(2,1)}...) conditional(s32[]{:T(128)} %bitcast.19, () %tuple.131, ...), branch_computations={%region_18.19_spmd, %region_19.20_spmd} | conditional | flops 5980000256 | bytes 34018756 | solution.py:904
  183.6 6.3 %all-to-all-start.1 = ((bf16[8,144,128]{2,1,0:T(8,128)(2,1)}), bf16[8,144,128]{2,1,0:T(8,128)(2,1)}, u32[]{:S(2)}, u32[]{:S(2)}) async-start(bf16[8,144,128]{2,1,0:T(8,128)(2,1)} %get-tuple-element.342), calls=%async_computation.1 | async-start | bytes 589824 | tf_op jit(solution)/shard_map/cond/branch_1_fun/all_to_all | solution.py:1005
  191.9 5.3 %weights.1 = (f32[2,2,64,1024]{3,2,1,0:T(8,128)S(1)}, bf16[2,2,64,1024]{3,2,1,0:T(8,128)(2,1)S(1)}, f32[2,2,64,1024]{3,2,1,0:T(8,128)S(1)}, bf16[2,2,64,1024]{3,2,1,0:T(8,128)(2,1)S(1)}) custom-call(s32[5]{0:T(128)} %get-tuple-element.345.idx, bf16[288,1024]{1,0:T(8,128)(2,1)} %get-tuple-element.346.f0, bf16[288,1024]{1,0:T(8,128)(2,1)} %get-tuple-element.344.f1, ...), custom_call_target="tpu_custom_call" | custom-call | flops 5980000256 | bytes 19240000 | tf_op jit(solution)/shard_map/cond/branch_1_fun/weights/pallas_call | solution.py:115
  197.3 6.1 %all-to-all-done.1 = bf16[8,144,128]{2,1,0:T(8,128)(2,1)} async-done(((bf16[8,144,128]{2,1,0:T(8,128)(2,1)}), bf16[8,144,128]{2,1,0:T(8,128)(2,1)}, u32[]{:S(2)}, u32[]{:S(2)}) %all-to-all-start.1) | async-done | bytes 294944 | tf_op jit(solution)/shard_map/cond/branch_1_fun/all_to_all | solution.py:1005
  205.4 16.0 %conditional.19 = ((bf16[1024,256]{1,0:T(8,128)(2,1)}, bf16[8,96,256]{2,1,0:T(8,128)(2,1)})) conditional(s32[]{:T(128)} %bitcast.19, () %tuple.130, (bf16[1024,128]{1,0:T(8,128)(2,1)}, bf16[8,144,128]{2,1,0:T(8,128)(2,1)}, s32[5]{0:T(128)}, s32[4]{0:T(128)S(1)}, f32[4,2,2,64,128]{4,3,2,1,0:T(8,128)}, /*index=5*/f32[4,1,1,256]{3,2,1,0:T(1,128)S(1)}, ...), branch_computations={%region_20.21_spmd, %region_21.22_spmd} | conditional | flops 14604999680 | bytes 51184488 | solution.py:904
  205.6 9.7 %attend_back.1 = (f32[4,2,2,64,128]{4,3,2,1,0:T(8,128)}, f32[1024,128]{1,0:T(8,128)}, f32[1024,128]{1,0:T(8,128)}) custom-call(s32[5]{0:T(128)} %get-tuple-element.355.idx, s32[4]{0:T(128)S(1)} %get-tuple-element.356.lens, bf16[4,2,2,64,128]{4,3,2,1,0:T(8,128)(2,1)} %bitcast.16.q_ref, bf16[4,2,144,128]{3,2,1,0:T(8,128)(2,1)} %bitcast.17.g_ref, ...), custom_call_target="tpu_custom_call" | custom-call | flops 11269999616 | bytes 36260000 | tf_op jit(solution)/shard_map/cond/branch_1_fun/attend_back/pallas_call | solution.py:405
  215.4 2.1 collective-permute-done.10.got
  218.3 3.1 %triple.1 = (bf16[1024,256]{1,0:T(8,128)(2,1)}, bf16[8,96,256]{2,1,0:T(8,128)(2,1)}) custom-call(s32[5]{0:T(128)S(1)} %copy-done.17, f32[1024,128]{1,0:T(8,128)} %bitcast.73, f32[1024,128]{1,0:T(8,128)} %get-tuple-element.366.dkv, f32[1024,128]{1,0:T(8,128)} %copy-done.23, f32[1024,128]{1,0:T(8,128)} %get-tuple-element.368.cosine, ...), custom_call_target="tpu_custom_call" | custom-call | flops 3335000064 | bytes 10730000 | tf_op jit(solution)/shard_map/cond/branch_1_fun/triple/pallas_call | solution.py:115
  221.4 2.1 pair.2
  223.5 24.5 %conditional.20 = (bf16[8,96,256]{2,1,0:T(8,128)(2,1)}, bf16[8,64,256]{2,1,0:T(8,128)(2,1)}, f32[2,2,64,256]{3,2,1,0:T(8,128)S(1)}, bf16[2,2,64,256]{3,2,1,0:T(8,128)(2,1)}, bf16[336,128]{1,0:T(8,128)(2,1)S(1)}) conditional(s32[]{:T(128)} %bitcast.19, () %tuple.129, (bf16[8,96,256]{2,1,0:T(8,128)(2,1)}, s32[5]{0:T(128)S(1)}, ...), branch_computations={%region_22.23_spmd, %region_23.24_spmd} | conditional | flops 13109999616 | bytes 49126996 | solution.py:904
  223.5 4.6 %triple_weight.1 = (bf16[8,64,256]{2,1,0:T(8,128)(2,1)}, bf16[8,64,256]{2,1,0:T(8,128)(2,1)}) custom-call(s32[5]{0:T(128)S(1)} %get-tuple-element.371.idx, bf16[128,1024]{1,0:T(8,128)(2,1)} %get-tuple-element.372.refs_0_, bf16[128,1024]{1,0:T(8,128)(2,1)} %get-tuple-element.373.refs_1_, bf16[2,64,1024]{2,1,0:T(8,128)(2,1)} %get-tuple-element.374.refs_2_, ...), custom_call_target="tpu_custom_call" | custom-call | flops 4369999872 | bytes 14060000 | tf_op jit(solution)/shard_map/cond/branch_1_fun/triple_weight/pallas_call | solution.py:115
  228.2 6.9 %all-to-all-start.2 = ((bf16[8,96,256]{2,1,0:T(8,128)(2,1)}), bf16[8,96,256]{2,1,0:T(8,128)(2,1)}, u32[]{:S(2)}, u32[]{:S(2)}) async-start(bf16[8,96,256]{2,1,0:T(8,128)(2,1)} %get-tuple-element.370), calls=%async_computation.2 | async-start | bytes 786432 | tf_op jit(solution)/shard_map/cond/branch_1_fun/all_to_all | solution.py:1005
  235.1 3.9 %output.1 = (f32[2,2,64,256]{3,2,1,0:T(8,128)S(1)}, bf16[2,2,64,256]{3,2,1,0:T(8,128)(2,1)}) custom-call(s32[5]{0:T(128)S(1)} %get-tuple-element.371.idx, bf16[288,1024]{1,0:T(8,128)(2,1)} %get-tuple-element.384.f0, bf16[288,1024]{1,0:T(8,128)(2,1)} %get-tuple-element.385.f1, bf16[288,1024]{1,0:T(8,128)(2,1)} %get-tuple-element.386.f2, ...), custom_call_target="tpu_custom_call" | custom-call | flops 2644999936 | bytes 8510000 | tf_op jit(solution)/shard_map/cond/branch_1_fun/output/pallas_call | solution.py:115
  239.0 2.0 collective-permute-start.12
  241.0 2.3 query_back.1
  245.1 2.8 collective-permute-done.12
  248.0 2.2 pair.3
  252.0 14.3 %conditional.21 = (f32[128,1024]{1,0:T(8,128)S(1)}) conditional(s32[]{:T(128)} %bitcast.19, () %tuple.128, (s32[5]{0:T(128)S(1)}, bf16[8,96,256]{2,1,0:T(8,128)(2,1)}, bf16[1024,1536]{1,0:T(8,128)(2,1)}, f32[128,1024]{1,0:T(8,128)S(1)}) %tuple.212), branch_computations={%region_24.25_spmd, %region_25.26_spmd} | conditional | flops 6900000256 | bytes 24297228 | solution.py:904
  252.0 4.8 %tokens.2.own = bf16[128,1024]{1,0:T(8,128)(2,1)} custom-call(s32[5]{0:T(128)S(1)} %get-tuple-element.400.idx, bf16[8,96,256]{2,1,0:T(8,128)(2,1)} %get-tuple-element.401.got, bf16[1024,1536]{1,0:T(8,128)(2,1)} %get-tuple-element.402.message), custom_call_target="tpu_custom_call" | custom-call | flops 4485000192 | bytes 14430000 | tf_op jit(solution)/shard_map/cond/branch_1_fun/tokens/pallas_call | solution.py:115
  256.7 2.0 collective-permute-start.13
  258.7 5.8 %collective-permute-done.13.other = bf16[128,1024]{1,0:T(8,128)(2,1)S(1)} collective-permute-done((bf16[128,1024]{1,0:T(8,128)(2,1)}, bf16[128,1024]{1,0:T(8,128)(2,1)S(1)}, u32[]{:S(2)}, u32[]{:S(2)}) %collective-permute-start.13) | collective-permute-done | bytes 262176 | tf_op jit(solution)/shard_map/cond/branch_1_fun/ppermute | solution.py:41
  266.3 4.5 %all-to-all-start.4 = ((bf16[8,64,256]{2,1,0:T(8,128)(2,1)}), bf16[8,64,256]{2,1,0:T(8,128)(2,1)S(1)}, u32[]{:S(2)}, u32[]{:S(2)}) async-start(bf16[8,64,256]{2,1,0:T(8,128)(2,1)} %get-tuple-element.646), calls=%async_computation.4 | async-start | bytes 524288 | tf_op jit(solution)/shard_map/all_to_all | solution.py:1275
  271.5 2.5 line_sum.1
  274.0 2.0 collective-permute-start.39
  277.2 1.9 all-to-all-done.4.got
  279.8 1.9 triple_out.1
  281.7 5.2 %collective-permute-done.39.got = bf16[64,2304]{1,0:T(8,128)(2,1)S(1)} collective-permute-done((bf16[64,2304]{1,0:T(8,128)(2,1)}, bf16[64,2304]{1,0:T(8,128)(2,1)S(1)}, u32[]{:S(2)}, u32[]{:S(2)}) %collective-permute-start.39) | collective-permute-done | bytes 294944 | tf_op jit(solution)/shard_map/ppermute | solution.py:41
  287.6 2.2 columns.1
  289.9 4.0 %all-gather.12.cloned.1.call-done = bf16[5376,128]{1,0:T(8,128)(2,1)} async-done(((bf16[336,128]{1,0:T(8,128)(2,1)}), bf16[5376,128]{1,0:T(8,128)(2,1)}) %all-gather.12.cloned.1.call-update) | async-done | bytes 1376272 | tf_op jit(solution)/shard_map/all_gather | solution.py:1257
  293.8 2.9 spread.1
  (176 shorter events, 51.1 us)
Async XLA Ops:
  7.2 107.9 %all-gather.6.cloned.1.call-start = ((), (), s32[]{:S(2)}) async-start(), calls=%async_computation.5 | async-start | bytes 8912896 | tf_op jit(solution)/shard_map/all_gather | solution.py:955
  8.2 10.3 %collective-permute-start.28 = (bf16[64,1024]{1,0:T(8,128)(2,1)S(1)}, bf16[64,1024]{1,0:T(8,128)(2,1)S(1)}, u32[]{:S(2)}, u32[]{:S(2)}) collective-permute-start(bf16[64,1024]{1,0:T(8,128)(2,1)S(1)} %constant_dynamic-slice_fusion), channel_id=1, source_target_pairs={{0,8},{8,0},{16,24},{24,16},{1,9},{9,1},{17,25},{25,17},{2,10},{10... | collective-permute-start | bytes 393224 | tf_op jit(solution)/shard_map/ppermute | solution.py:33
  11.2 12.9 %collective-permute-start.29 = (bf16[64,1024]{1,0:T(8,128)(2,1)S(1)}, bf16[64,1024]{1,0:T(8,128)(2,1)S(1)}, u32[]{:S(2)}, u32[]{:S(2)}) collective-permute-start(bf16[64,1024]{1,0:T(8,128)(2,1)S(1)} %constant_dynamic-slice_fusion), channel_id=1, source_target_pairs={{0,16},{8,24},{16,0},{24,8},{1,17},{9,25},{17,1},{25,9},{2,18},{10... | collective-permute-start | bytes 393224 | tf_op jit(solution)/shard_map/ppermute | solution.py:33
  13.8 10.3 %collective-permute-start.30 = (bf16[64,1024]{1,0:T(8,128)(2,1)S(1)}, bf16[64,1024]{1,0:T(8,128)(2,1)S(1)}, u32[]{:S(2)}, u32[]{:S(2)}) collective-permute-start(bf16[64,1024]{1,0:T(8,128)(2,1)S(1)} %constant_dynamic-slice_fusion), channel_id=1, source_target_pairs={{0,24},{8,16},{16,8},{24,0},{1,25},{9,17},{17,9},{25,1},{2,26},{10... | collective-permute-start | bytes 393224 | tf_op jit(solution)/shard_map/ppermute | solution.py:33
  13.8 10.3 %collective-permute-start.27 = (bf16[128,1024]{1,0:T(8,128)(2,1)}, bf16[128,1024]{1,0:T(8,128)(2,1)S(1)}, u32[]{:S(2)}, u32[]{:S(2)}) collective-permute-start(bf16[128,1024]{1,0:T(8,128)(2,1)} %tokens.3), channel_id=1, source_target_pairs={{0,4},{4,0},{1,5},{5,1},{2,6},{6,2},{3,7},{7,3},{8,12},{12,8},{9,1... | collective-permute-start | bytes 786440 | tf_op jit(solution)/shard_map/ppermute | solution.py:41
  15.6 108.0 %copy-start.14 = (s32[5]{0:T(128)}, s32[5]{0:T(128)S(1)}, u32[]{:S(2)}) copy-start(s32[5]{0:T(128)S(1)} %stack.47.idx) | copy-start | bytes 64
  15.6 8.6 %copy-start.36 = (s32[4]{0:T(128)S(1)}, s32[4]{0:T(128)}, u32[]{:S(2)}) copy-start(s32[4]{0:T(128)} %param.44) | copy-start | bytes 52
  15.6 9.3 %copy-start.13 = (s32[128]{0:T(128)S(1)}, s32[128]{0:T(128)}, u32[]{:S(2)}) copy-start(s32[128]{0:T(128)} %param.46) | copy-start | bytes 1540
  15.6 9.3 %copy-start.18 = (bf16[4096,128]{1,0:T(8,128)(2,1)S(1)}, bf16[4096,128]{1,0:T(8,128)(2,1)}, u32[]{:S(2)}) copy-start(bf16[4096,128]{1,0:T(8,128)(2,1)} %param.42) | copy-start | bytes 3145732
  24.2 142.7 %all-gather.8.cloned.1.call-start = ((), (), s32[]{:S(2)}) async-start(), calls=%async_computation.6 | async-start | bytes 3342336 | tf_op jit(solution)/shard_map/all_gather | solution.py:1028
  24.9 49.8 %copy-start.6 = (bf16[128,1024]{1,0:T(8,128)(2,1)S(1)}, bf16[128,1024]{1,0:T(8,128)(2,1)}, u32[]{:S(2)}) copy-start(bf16[128,1024]{1,0:T(8,128)(2,1)} %tokens.3) | copy-start | bytes 786436
  24.9 49.8 %copy-start.34 = (f32[3,512]{1,0:T(4,128)S(1)}, f32[3,512]{1,0:T(4,128)}, u32[]{:S(2)}) copy-start(f32[3,512]{1,0:T(4,128)} %param.48) | copy-start | bytes 18436
  24.9 9.5 %collective-permute-start.14 = (bf16[64,1024]{1,0:T(8,128)(2,1)S(1)}, bf16[64,1024]{1,0:T(8,128)(2,1)S(1)}, u32[]{:S(2)}, u32[]{:S(2)}) collective-permute-start(bf16[64,1024]{1,0:T(8,128)(2,1)S(1)} %get-tuple-element.258), channel_id=1, source_target_pairs={{0,4},{4,0},{1,5},{5,1},{2,6},{6,2},{3,7},{7,3},{8,12},{12,8},{9,1... | collective-permute-start | bytes 393224 | tf_op jit(solution)/shard_map/cond/branch_1_fun/ppermute | solution.py:41
  26.5 10.1 %collective-permute-start.16 = (bf16[64,1024]{1,0:T(8,128)(2,1)S(1)}, bf16[64,1024]{1,0:T(8,128)(2,1)S(1)}, u32[]{:S(2)}, u32[]{:S(2)}) collective-permute-start(bf16[64,1024]{1,0:T(8,128)(2,1)S(1)} %get-tuple-element.259), channel_id=1, source_target_pairs={{0,4},{4,0},{1,5},{5,1},{2,6},{6,2},{3,7},{7,3},{8,12},{12,8},{9,1... | collective-permute-start | bytes 393224 | tf_op jit(solution)/shard_map/cond/branch_1_fun/ppermute | solution.py:41
  27.0 10.8 %collective-permute-start.18 = (bf16[64,1024]{1,0:T(8,128)(2,1)S(1)}, bf16[64,1024]{1,0:T(8,128)(2,1)S(1)}, u32[]{:S(2)}, u32[]{:S(2)}) collective-permute-start(bf16[64,1024]{1,0:T(8,128)(2,1)S(1)} %get-tuple-element.260), channel_id=1, source_target_pairs={{0,4},{4,0},{1,5},{5,1},{2,6},{6,2},{3,7},{7,3},{8,12},{12,8},{9,1... | collective-permute-start | bytes 393224 | tf_op jit(solution)/shard_map/cond/branch_1_fun/ppermute | solution.py:41
  28.5 40.1 %all-to-all-start.3 = ((bf16[8,192,256]{2,1,0:T(8,128)(2,1)}), bf16[8,192,256]{2,1,0:T(8,128)(2,1)}, u32[]{:S(2)}, u32[]{:S(2)}) async-start(bf16[8,192,256]{2,1,0:T(8,128)(2,1)} %get-tuple-element.257), calls=%async_computation.3 | async-start | bytes 1572864 | tf_op jit(solution)/shard_map/cond/branch_1_fun/all_to_all | solution.py:958
  35.1 9.6 %collective-permute-start.15 = (bf16[2,64,1024]{2,1,0:T(8,128)(2,1)}, bf16[2,64,1024]{2,1,0:T(8,128)(2,1)}, u32[]{:S(2)}, u32[]{:S(2)}) collective-permute-start(bf16[2,64,1024]{2,1,0:T(8,128)(2,1)} %pad_maximum_fusion), channel_id=1, source_target_pairs={{0,1},{1,0},{2,3},{3,2},{4,5},{5,4},{6,7},{7,6},{8,9},{9,8},{10,11... | collective-permute-start | bytes 786440 | tf_op jit(solution)/shard_map/cond/branch_1_fun/ppermute | solution.py:41
  37.4 12.5 %collective-permute-start.17 = (bf16[2,64,1024]{2,1,0:T(8,128)(2,1)}, bf16[2,64,1024]{2,1,0:T(8,128)(2,1)}, u32[]{:S(2)}, u32[]{:S(2)}) collective-permute-start(bf16[2,64,1024]{2,1,0:T(8,128)(2,1)} %pad_maximum_fusion.1), channel_id=1, source_target_pairs={{0,1},{1,0},{2,3},{3,2},{4,5},{5,4},{6,7},{7,6},{8,9},{9,8},{10,11... | collective-permute-start | bytes 786440 | tf_op jit(solution)/shard_map/cond/branch_1_fun/ppermute | solution.py:41
  38.6 14.0 %collective-permute-start.19 = (bf16[2,64,1024]{2,1,0:T(8,128)(2,1)}, bf16[2,64,1024]{2,1,0:T(8,128)(2,1)}, u32[]{:S(2)}, u32[]{:S(2)}) collective-permute-start(bf16[2,64,1024]{2,1,0:T(8,128)(2,1)} %pad_maximum_fusion.2), channel_id=1, source_target_pairs={{0,1},{1,0},{2,3},{3,2},{4,5},{5,4},{6,7},{7,6},{8,9},{9,8},{10,11... | collective-permute-start | bytes 786440 | tf_op jit(solution)/shard_map/cond/branch_1_fun/ppermute | solution.py:41
  68.6 2.6 collective-permute-start.20
  74.7 48.9 %copy-start.7 = (s32[8,128]{1,0:T(8,128)}, s32[8,128]{1,0:T(8,128)S(1)}, u32[]{:S(2)}) copy-start(s32[8,128]{1,0:T(8,128)S(1)} %get-tuple-element.556) | copy-start | bytes 12292
  78.8 1.9 collective-permute-start
  101.1 14.1 %copy-start.35 = (f32[1024]{0:T(1024)S(1)}, f32[1024]{0:T(1024)}, u32[]{:S(2)}) copy-start(f32[1024]{0:T(1024)} %param.51) | copy-start | bytes 12292
  104.3 8.1 %collective-permute-start.1 = (bf16[128,1024]{1,0:T(8,128)(2,1)}, bf16[128,1024]{1,0:T(8,128)(2,1)}, u32[]{:S(2)}, u32[]{:S(2)}) collective-permute-start(bf16[128,1024]{1,0:T(8,128)(2,1)} %get-tuple-element.729), channel_id=1, source_target_pairs={{0,1},{1,0},{2,3},{3,2},{4,5},{5,4},{6,7},{7,6},{8,9},{9,8},{10,11... | collective-permute-start | bytes 786440 | tf_op jit(solution)/shard_map/cond/branch_1_fun/ppermute | solution.py:41
  112.4 111.0 %all-gather.10.cloned.1.call-start = ((), (), s32[]{:S(2)}) async-start(), calls=%async_computation.7 | async-start | bytes 1114112 | tf_op jit(solution)/shard_map/all_gather | solution.py:1106
  122.3 14.0 %collective-permute-start.31 = (bf16[288,1024]{1,0:T(8,128)(2,1)}, bf16[288,1024]{1,0:T(8,128)(2,1)}, u32[]{:S(2)}, u32[]{:S(2)}) collective-permute-start(bf16[288,1024]{1,0:T(8,128)(2,1)} %get-tuple-element.572), channel_id=1, source_target_pairs={{0,2},{2,0},{1,3},{3,1},{4,6},{6,4},{5,7},{7,5},{8,10},{10,8},{9,1... | collective-permute-start | bytes 1769480 | tf_op jit(solution)/shard_map/ppermute | solution.py:41
  122.6 44.3 %collective-permute-start.32 = (bf16[288,1024]{1,0:T(8,128)(2,1)}, bf16[288,1024]{1,0:T(8,128)(2,1)}, u32[]{:S(2)}, u32[]{:S(2)}) collective-permute-start(bf16[288,1024]{1,0:T(8,128)(2,1)} %get-tuple-element.585), channel_id=1, source_target_pairs={{0,4},{4,0},{1,5},{5,1},{2,6},{6,2},{3,7},{7,3},{8,12},{12,8},{9,1... | collective-permute-start | bytes 1769480 | tf_op jit(solution)/shard_map/ppermute | solution.py:41
  123.6 8.5 %collective-permute-start.2 = (bf16[128,1024]{1,0:T(8,128)(2,1)}, bf16[128,1024]{1,0:T(8,128)(2,1)S(1)}, u32[]{:S(2)}, u32[]{:S(2)}) collective-permute-start(bf16[128,1024]{1,0:T(8,128)(2,1)} %get-tuple-element.307.own), channel_id=1, source_target_pairs={{0,1},{1,0},{2,3},{3,2},{4,5},{5,4},{6,7},{7,6},{8,9},{9,8},{10,11... | collective-permute-start | bytes 786440 | tf_op jit(solution)/shard_map/cond/branch_1_fun/ppermute | solution.py:41
  136.5 1.9 collective-permute-start.21
  136.5 6.0 %collective-permute-start.22 = (f32[4,4096]{1,0:T(4,128)S(1)}, f32[4,4096]{1,0:T(4,128)S(1)}, u32[]{:S(2)}, u32[]{:S(2)}) collective-permute-start(f32[4,4096]{1,0:T(4,128)S(1)} %get-tuple-element.316), channel_id=1, source_target_pairs={{0,4},{2,6},{4,0},{6,2},{1,5},{3,7},{5,1},{7,3},{8,12},{10,14},{12... | collective-permute-start | bytes 196616 | tf_op jit(solution)/shard_map/cond/branch_1_fun/ppermute | solution.py:37
  137.6 4.9 %collective-permute-start.23 = (f32[4,4096]{1,0:T(4,128)S(1)}, f32[4,4096]{1,0:T(4,128)S(1)}, u32[]{:S(2)}, u32[]{:S(2)}) collective-permute-start(f32[4,4096]{1,0:T(4,128)S(1)} %get-tuple-element.316), channel_id=1, source_target_pairs={{0,6},{2,4},{4,2},{6,0},{1,7},{3,5},{5,3},{7,1},{8,14},{10,12},{12... | collective-permute-start | bytes 196616 | tf_op jit(solution)/shard_map/cond/branch_1_fun/ppermute | solution.py:37
  142.6 13.0 %copy-start.5 = (f32[4,4096]{1,0:T(4,128)}, f32[4,4096]{1,0:T(4,128)S(1)}, u32[]{:S(2)}) copy-start(f32[4,4096]{1,0:T(4,128)S(1)} %add_add_fusion.t0) | copy-start | bytes 196612 | tf_op jit(solution)/shard_map/cond
  142.6 8.0 %collective-permute-start.24 = (f32[4,4096]{1,0:T(4,128)S(1)}, f32[4,4096]{1,0:T(4,128)S(1)}, u32[]{:S(2)}, u32[]{:S(2)}) collective-permute-start(f32[4,4096]{1,0:T(4,128)S(1)} %add_add_fusion.t0), channel_id=1, source_target_pairs={{0,8},{8,0},{16,24},{24,16},{1,9},{9,1},{17,25},{25,17},{2,10},{10... | collective-permute-start | bytes 196616 | tf_op jit(solution)/shard_map/cond/branch_1_fun/ppermute | solution.py:33
  143.9 11.6 %collective-permute-start.25 = (f32[4,4096]{1,0:T(4,128)S(1)}, f32[4,4096]{1,0:T(4,128)S(1)}, u32[]{:S(2)}, u32[]{:S(2)}) collective-permute-start(f32[4,4096]{1,0:T(4,128)S(1)} %add_add_fusion.t0), channel_id=1, source_target_pairs={{0,16},{8,24},{16,0},{24,8},{1,17},{9,25},{17,1},{25,9},{2,18},{10... | collective-permute-start | bytes 196616 | tf_op jit(solution)/shard_map/cond/branch_1_fun/ppermute | solution.py:33
  145.0 10.5 %collective-permute-start.26 = (f32[4,4096]{1,0:T(4,128)S(1)}, f32[4,4096]{1,0:T(4,128)S(1)}, u32[]{:S(2)}, u32[]{:S(2)}) collective-permute-start(f32[4,4096]{1,0:T(4,128)S(1)} %add_add_fusion.t0), channel_id=1, source_target_pairs={{0,24},{8,16},{16,8},{24,0},{1,25},{9,17},{17,9},{25,1},{2,26},{10... | collective-permute-start | bytes 196616 | tf_op jit(solution)/shard_map/cond/branch_1_fun/ppermute | solution.py:33
  166.9 126.9 %all-gather.12.cloned.1.call-start = ((), (), s32[]{:S(2)}) async-start(), calls=%async_computation.8 | async-start | bytes 1462272 | tf_op jit(solution)/shard_map/all_gather | solution.py:1257
  167.0 15.1 %collective-permute-start.33 = (bf16[256,1024]{1,0:T(8,128)(2,1)}, bf16[256,1024]{1,0:T(8,128)(2,1)S(1)}, u32[]{:S(2)}, u32[]{:S(2)}) collective-permute-start(bf16[256,1024]{1,0:T(8,128)(2,1)} %get-tuple-element.595), channel_id=1, source_target_pairs={{0,4},{4,0},{1,5},{5,1},{2,6},{6,2},{3,7},{7,3},{8,12},{12,8},{9,1... | collective-permute-start | bytes 1572872 | tf_op jit(solution)/shard_map/ppermute | solution.py:41
  167.9 14.1 %collective-permute-start.34 = (bf16[256,1024]{1,0:T(8,128)(2,1)}, bf16[256,1024]{1,0:T(8,128)(2,1)S(1)}, u32[]{:S(2)}, u32[]{:S(2)}) collective-permute-start(bf16[256,1024]{1,0:T(8,128)(2,1)} %get-tuple-element.597), channel_id=1, source_target_pairs={{0,2},{2,0},{1,3},{3,1},{4,6},{6,4},{5,7},{7,5},{8,10},{10,8},{9,1... | collective-permute-start | bytes 1572872 | tf_op jit(solution)/shard_map/ppermute | solution.py:41
  167.9 8.9 %collective-permute-start.3 = (bf16[128,1024]{1,0:T(8,128)(2,1)}, bf16[128,1024]{1,0:T(8,128)(2,1)S(1)}, u32[]{:S(2)}, u32[]{:S(2)}) collective-permute-start(bf16[128,1024]{1,0:T(8,128)(2,1)} %get-tuple-element.333.own), channel_id=1, source_target_pairs={{0,1},{1,0},{2,3},{3,2},{4,5},{5,4},{6,7},{7,6},{8,9},{9,8},{10,11... | collective-permute-start | bytes 786440 | tf_op jit(solution)/shard_map/cond/branch_1_fun/ppermute | solution.py:41
  169.4 1.6 collective-permute-start.4
  182.0 23.3 %copy-start.8 = (s32[8,128]{1,0:T(8,128)S(1)}, s32[8,128]{1,0:T(8,128)}, u32[]{:S(2)}) copy-start(s32[8,128]{1,0:T(8,128)} %copy-done.7) | copy-start | bytes 12292
  182.0 23.3 %copy-start.11 = (s32[8,128]{1,0:T(8,128)S(1)}, s32[8,128]{1,0:T(8,128)}, u32[]{:S(2)}) copy-start(s32[8,128]{1,0:T(8,128)} %copy-done.10) | copy-start | bytes 12292
  182.0 23.3 %copy-start.12 = (f32[4,1,1,256]{3,2,1,0:T(1,128)S(1)}, f32[4,1,1,256]{3,2,1,0:T(1,128)}, u32[]{:S(2)}) copy-start(f32[4,1,1,256]{3,2,1,0:T(1,128)} %get-tuple-element.600) | copy-start | bytes 12292
  182.0 23.3 %copy-start.37 = (s32[4]{0:T(128)S(1)}, s32[4]{0:T(128)}, u32[]{:S(2)}) copy-start(s32[4]{0:T(128)} %param.44) | copy-start | bytes 52
  182.1 9.0 %copy-start.20 = (bf16[256,1024]{1,0:T(8,128)(2,1)}, bf16[256,1024]{1,0:T(8,128)(2,1)S(1)}, u32[]{:S(2)}) copy-start(bf16[256,1024]{1,0:T(8,128)(2,1)S(1)} %get-tuple-element.349.g1) | copy-start | bytes 1572868 | tf_op jit(solution)/shard_map/cond
  182.1 9.0 %copy-start.21 = (bf16[256,1024]{1,0:T(8,128)(2,1)}, bf16[256,1024]{1,0:T(8,128)(2,1)S(1)}, u32[]{:S(2)}) copy-start(bf16[256,1024]{1,0:T(8,128)(2,1)S(1)} %get-tuple-element.350.g2) | copy-start | bytes 1572868 | tf_op jit(solution)/shard_map/cond
  182.1 9.0 %collective-permute-start.8 = (bf16[288,1024]{1,0:T(8,128)(2,1)}, bf16[288,1024]{1,0:T(8,128)(2,1)}, u32[]{:S(2)}, u32[]{:S(2)}) collective-permute-start(bf16[288,1024]{1,0:T(8,128)(2,1)} %get-tuple-element.344.f1), channel_id=1, source_target_pairs={{0,2},{2,0},{1,3},{3,1},{4,6},{6,4},{5,7},{7,5},{8,10},{10,8},{9,1... | collective-permute-start | bytes 1769480 | tf_op jit(solution)/shard_map/cond/branch_1_fun/ppermute | solution.py:41
  182.2 8.9 %collective-permute-start.9 = (bf16[256,1024]{1,0:T(8,128)(2,1)S(1)}, bf16[256,1024]{1,0:T(8,128)(2,1)S(1)}, u32[]{:S(2)}, u32[]{:S(2)}) collective-permute-start(bf16[256,1024]{1,0:T(8,128)(2,1)S(1)} %get-tuple-element.349.g1), channel_id=1, source_target_pairs={{0,2},{2,0},{1,3},{3,1},{4,6},{6,4},{5,7},{7,5},{8,10},{10,8},{9,1... | collective-permute-start | bytes 1572872 | tf_op jit(solution)/shard_map/cond/branch_1_fun/ppermute | solution.py:41
  182.7 8.4 %collective-permute-start.5 = (bf16[128,1024]{1,0:T(8,128)(2,1)S(1)}, bf16[128,1024]{1,0:T(8,128)(2,1)}, u32[]{:S(2)}, u32[]{:S(2)}) collective-permute-start(bf16[128,1024]{1,0:T(8,128)(2,1)S(1)} %get-tuple-element.343), channel_id=1, source_target_pairs={{0,4},{4,0},{1,5},{5,1},{2,6},{6,2},{3,7},{7,3},{8,12},{12,8},{9,1... | collective-permute-start | bytes 786440 | tf_op jit(solution)/shard_map/cond/branch_1_fun/ppermute | solution.py:41
  183.5 13.7 %collective-permute-start.6 = (bf16[128,1024]{1,0:T(8,128)(2,1)S(1)}, bf16[128,1024]{1,0:T(8,128)(2,1)}, u32[]{:S(2)}, u32[]{:S(2)}) collective-permute-start(bf16[128,1024]{1,0:T(8,128)(2,1)S(1)} %get-tuple-element.343), channel_id=1, source_target_pairs={{0,2},{2,0},{1,3},{3,1},{4,6},{6,4},{5,7},{7,5},{8,10},{10,8},{9,1... | collective-permute-start | bytes 786440 | tf_op jit(solution)/shard_map/cond/branch_1_fun/ppermute | solution.py:41
  183.6 19.8 %all-to-all-start.1 = ((bf16[8,144,128]{2,1,0:T(8,128)(2,1)}), bf16[8,144,128]{2,1,0:T(8,128)(2,1)}, u32[]{:S(2)}, u32[]{:S(2)}) async-start(bf16[8,144,128]{2,1,0:T(8,128)(2,1)} %get-tuple-element.342), calls=%async_computation.1 | async-start | bytes 589824 | tf_op jit(solution)/shard_map/cond/branch_1_fun/all_to_all | solution.py:1005
  191.1 12.2 %collective-permute-start.7 = (bf16[128,1024]{1,0:T(8,128)(2,1)}, bf16[128,1024]{1,0:T(8,128)(2,1)}, u32[]{:S(2)}, u32[]{:S(2)}) collective-permute-start(bf16[128,1024]{1,0:T(8,128)(2,1)} %collective-permute-done.5), channel_id=1, source_target_pairs={{0,2},{2,0},{1,3},{3,1},{4,6},{6,4},{5,7},{7,5},{8,10},{10,8},{9,1... | collective-permute-start | bytes 786440 | tf_op jit(solution)/shard_map/cond/branch_1_fun/ppermute | solution.py:41
  203.3 18.0 %collective-permute-start.35 = (bf16[2,2,64,1024]{3,2,1,0:T(8,128)(2,1)S(1)}, bf16[2,2,64,1024]{3,2,1,0:T(8,128)(2,1)}, u32[]{:S(2)}, u32[]{:S(2)}) collective-permute-start(bf16[2,2,64,1024]{3,2,1,0:T(8,128)(2,1)S(1)} %get-tuple-element.603), channel_id=1, source_target_pairs={{0,8},{8,0},{16,24},{24,16},{1,9},{9,1},{17,25},{25,17},{2,10},{10... | collective-permute-start | bytes 1572872 | tf_op jit(solution)/shard_map/ppermute | solution.py:33
  204.3 43.7 %collective-permute-start.37 = (bf16[2,2,64,1024]{3,2,1,0:T(8,128)(2,1)S(1)}, bf16[2,2,64,1024]{3,2,1,0:T(8,128)(2,1)}, u32[]{:S(2)}, u32[]{:S(2)}) collective-permute-start(bf16[2,2,64,1024]{3,2,1,0:T(8,128)(2,1)S(1)} %get-tuple-element.621), channel_id=1, source_target_pairs={{0,8},{8,0},{16,24},{24,16},{1,9},{9,1},{17,25},{25,17},{2,10},{10... | collective-permute-start | bytes 1572872 | tf_op jit(solution)/shard_map/ppermute | solution.py:33
  205.6 12.7 %copy-start.17 = (s32[5]{0:T(128)S(1)}, s32[5]{0:T(128)}, u32[]{:S(2)}) copy-start(s32[5]{0:T(128)} %get-tuple-element.355.idx) | copy-start | bytes 64 | tf_op jit(solution)/shard_map/cond
  215.3 2.2 collective-permute-start.10
  223.4 24.5 %collective-permute-start.36 = (bf16[2,64,1024]{2,1,0:T(8,128)(2,1)}, bf16[2,64,1024]{2,1,0:T(8,128)(2,1)}, u32[]{:S(2)}, u32[]{:S(2)}) collective-permute-start(bf16[2,64,1024]{2,1,0:T(8,128)(2,1)} %get-tuple-element.620), channel_id=1, source_target_pairs={{0,16},{8,24},{16,0},{24,8},{1,17},{9,25},{17,1},{25,9},{2,18},{10... | collective-permute-start | bytes 786440 | tf_op jit(solution)/shard_map/ppermute | solution.py:33
  228.1 15.3 %collective-permute-start.11 = (bf16[8,64,256]{2,1,0:T(8,128)(2,1)}, bf16[8,64,256]{2,1,0:T(8,128)(2,1)}, u32[]{:S(2)}, u32[]{:S(2)}) collective-permute-start(bf16[8,64,256]{2,1,0:T(8,128)(2,1)} %get-tuple-element.383), channel_id=1, source_target_pairs={{0,2},{2,0},{1,3},{3,1},{4,6},{6,4},{5,7},{7,5},{8,10},{10,8},{9,1... | collective-permute-start | bytes 786440 | tf_op jit(solution)/shard_map/cond/branch_1_fun/ppermute | solution.py:41
  228.2 19.8 %all-to-all-start.2 = ((bf16[8,96,256]{2,1,0:T(8,128)(2,1)}), bf16[8,96,256]{2,1,0:T(8,128)(2,1)}, u32[]{:S(2)}, u32[]{:S(2)}) async-start(bf16[8,96,256]{2,1,0:T(8,128)(2,1)} %get-tuple-element.370), calls=%async_computation.2 | async-start | bytes 786432 | tf_op jit(solution)/shard_map/cond/branch_1_fun/all_to_all | solution.py:1005
  239.0 9.0 %collective-permute-start.12 = (bf16[2,2,64,256]{3,2,1,0:T(8,128)(2,1)}, bf16[2,2,64,256]{3,2,1,0:T(8,128)(2,1)}, u32[]{:S(2)}, u32[]{:S(2)}) collective-permute-start(bf16[2,2,64,256]{3,2,1,0:T(8,128)(2,1)} %get-tuple-element.393), channel_id=1, source_target_pairs={{0,8},{8,0},{16,24},{24,16},{1,9},{9,1},{17,25},{25,17},{2,10},{10... | collective-permute-start | bytes 393224 | tf_op jit(solution)/shard_map/cond/branch_1_fun/ppermute | solution.py:33
  250.2 20.6 %collective-permute-start.38 = (bf16[2,64,1280]{2,1,0:T(8,128)(2,1)}, bf16[2,64,1280]{2,1,0:T(8,128)(2,1)S(1)}, u32[]{:S(2)}, u32[]{:S(2)}) collective-permute-start(bf16[2,64,1280]{2,1,0:T(8,128)(2,1)} %get-tuple-element.638), channel_id=1, source_target_pairs={{0,16},{8,24},{16,0},{24,8},{1,17},{9,25},{17,1},{25,9},{2,18},{10... | collective-permute-start | bytes 983048 | tf_op jit(solution)/shard_map/ppermute | solution.py:33
  256.7 7.8 %collective-permute-start.13 = (bf16[128,1024]{1,0:T(8,128)(2,1)}, bf16[128,1024]{1,0:T(8,128)(2,1)S(1)}, u32[]{:S(2)}, u32[]{:S(2)}) collective-permute-start(bf16[128,1024]{1,0:T(8,128)(2,1)} %tokens.2.own), channel_id=1, source_target_pairs={{0,1},{1,0},{2,3},{3,2},{4,5},{5,4},{6,7},{7,6},{8,9},{9,8},{10,11... | collective-permute-start | bytes 786440 | tf_op jit(solution)/shard_map/cond/branch_1_fun/ppermute | solution.py:41
  266.3 12.8 %all-to-all-start.4 = ((bf16[8,64,256]{2,1,0:T(8,128)(2,1)}), bf16[8,64,256]{2,1,0:T(8,128)(2,1)S(1)}, u32[]{:S(2)}, u32[]{:S(2)}) async-start(bf16[8,64,256]{2,1,0:T(8,128)(2,1)} %get-tuple-element.646), calls=%async_computation.4 | async-start | bytes 524288 | tf_op jit(solution)/shard_map/all_to_all | solution.py:1275
  274.0 12.9 %collective-permute-start.39 = (bf16[64,2304]{1,0:T(8,128)(2,1)}, bf16[64,2304]{1,0:T(8,128)(2,1)S(1)}, u32[]{:S(2)}, u32[]{:S(2)}) collective-permute-start(bf16[64,2304]{1,0:T(8,128)(2,1)} %get-tuple-element.641), channel_id=1, source_target_pairs={{0,4},{4,0},{1,5},{5,1},{2,6},{6,2},{3,7},{7,3},{8,12},{12,8},{9,1... | collective-permute-start | bytes 884744 | tf_op jit(solution)/shard_map/ppermute | solution.py:41
  (22 other events, 65.5 us)
Sparse Core Ops, SparseCore 0:
  24.3 90.7 all-gather.5
  117.4 49.4 all-gather.7
  169.1 39.2 all-gather.9
  250.3 43.4 all-gather.11

commit v4 on v3

--- a/solution.py
+++ b/solution.py
@@ -95,9 +95,9 @@
 PARAMS = pltpu.CompilerParams(vmem_limit_bytes=VMEM_BYTES)
 
 TAKES = dict(
-    prep=2.5, heads=2.0, project=3.8, attend=7.5, branch=3.5, forward=7.7, second=3.6, middle=12.0, first_back=3.8, attend_back=9.8, triple=2.9, triple_weight=3.8, tokens=3.9,
-    tokens_sum=2.1, weights=5.2, output=2.3, core_sum=3.9, line_sum=2.7, pair=2.0, columns=2.2, pair_sum=1.8,
-    triple_out=1.9, query_units=2.8, query_back=3.5, spread=3.5,
+    prep=2.5, heads=2.0, project=3.8, attend=7.5, branch=3.5, forward=7.7, second=3.6, middle=12.0, first_back=3.8, attend_back=9.8, triple=2.9, triple_weight=2.0, tokens=3.9,
+    tokens_sum=2.1, weights=5.2, output=1.5, core_sum=3.9, line_sum=2.7, pair=2.0, columns=2.2, pair_sum=0.8,
+    triple_out=1.9, query_units=2.8, query_back=1.0, spread=3.5,
 )
 
 
@@ -134,17 +134,16 @@
 def piece_copies(idx, pieces, weight, sems):
     if len(pieces) == 1:
         return [pltpu.make_async_copy(pieces[0], weight, sems.at[0])]
-    count, rows, cols = pieces[0].shape
-    slab = HEAD_DIM
-    behind = slab + extra_count(slab)
-    copies = []
+    count, half, _ = pieces[0].shape
+    span, copies = weight.shape[1], []
     for c, piece in enumerate(pieces):
         for spot in range(count):
-            row = (spot * 2 + (idx[3] ^ c)) * slab
+            there = (idx[1] ^ (spot // 2)) * 2 + (idx[2] ^ (spot % 2))
+            row = (there * 2 + (idx[3] ^ c)) * 2 * half
             for i in range(2):
-                here = piece.at[spot, pl.ds(behind + i * slab, slab), :]
-                there = weight.at[pl.ds(pl.multiple_of(row, slab), slab), pl.ds(i * cols, cols)]
-                copies.append(pltpu.make_async_copy(here, there, sems.at[len(copies)]))
+                rows = pl.ds(pl.multiple_of(row + i * half, half), half)
+                here = piece.at[spot, :, pl.ds(i * span, span)]
+                copies.append(pltpu.make_async_copy(here, weight.at[rows, :], sems.at[len(copies)]))
     return copies
 
 
@@ -188,19 +187,26 @@
     return jnp.concatenate([message[i * 16 : (i + 1) * 16, lanes] for i in range(4)], axis=1)
 
 
-def prep_kernel(idx, tw, ow, ew, cw, live, heads, low, tri):
+def prep_kernel(idx, tw, ow, ew, cw, live, tokens, heads, low, tri, mine, own):
     slab, span = ew.shape
     alive = jnp.broadcast_to(live[...], (16, live.shape[1])).astype(WIDE).astype(LOW)
     alive = jnp.concatenate([alive, jnp.zeros((16, QUAD - live.shape[1]), LOW)], axis=1)
-    behind = slab + extra_count(slab)
+    rows, span = tokens.shape[0], ow.shape[1]
+    half = rows // 2
+    mine[:half, :] = tokens[pl.ds(pl.multiple_of(idx[4] * half, half), half), :]
+    own[:rows, :] = tokens[...]
+    if own.shape[0] > rows:
+        for i in range(2):
+            part = ow[i * slab // 2 : (i + 1) * slab // 2, :].astype(LOW)
+            mine[half:, i * span : (i + 1) * span] = part
+            own[rows:, i * span : (i + 1) * span] = part
+    span = ew.shape[1]
     for spot in range(NZ * 2):
         at = spot * HEAD_DIM
         for part, lane in enumerate(LANES):
             heads[spot, :slab, lane : lane + HEAD_DIM] = tw[part, :, at : at + HEAD_DIM].astype(LOW)
         heads[spot, :slab, PAIR : PAIR + HEAD_DIM] = jnp.zeros((slab, HEAD_DIM), LOW)
         put_extra(heads.at[spot], slab, alive)
-        heads[spot, behind : behind + slab, :] = ow[:, :QUAD].astype(LOW)
-        heads[spot, behind + slab :, :] = ow[:, QUAD:].astype(LOW)
     low[:, :span] = ew[...].astype(LOW)
     low[:, span:] = cw[...].astype(LOW)
     for part in range(3):
@@ -236,7 +242,7 @@
     parts = []
     for x in range(2):
         spot = idx[1] * 2 + (idx[2] ^ x)
-        parts.append((sheets[x][...], pl.ds(pl.multiple_of(spot * rows, rows), rows)))
+        parts.append((sheets[x][:rows, :], pl.ds(pl.multiple_of(spot * rows, rows), rows)))
     for at, sheet in enumerate(sheets[2:]):
         z, y = at // 2 + 1, at % 2
         for x in range(2):
@@ -247,8 +253,9 @@
 
 
 def project_kernel(idx, *refs):
-    sheets, (weight, cosine, sine, bias, query, kv) = refs[:8], refs[8:]
-    parts = sheet_rows(idx, sheets)
+    sheets, (weight, cosine, sine, bias, query, kv, held) = refs[:8], refs[8:]
+    for value, at in sheet_rows(idx, sheets):
+        held[at, :] = value
     mz, mx = idx[1], idx[2]
     mine = mz * 2 + mx
     biases = []
@@ -261,9 +268,11 @@
     empty = jnp.zeros((1, HEAD_DIM), WIDE)
     offset = jnp.concatenate([biases[0], biases[1], empty, biases[2]], axis=1)
     weights = weight[...]
-    for value, at in parts:
-        low_lanes = lax.broadcasted_iota(jnp.int32, (value.shape[0], PAIR), 1) < HEAD_DIM
-        triple = dot_nn(value, weights) + offset
+    rows = sheets[0].shape[0]
+    low_lanes = lax.broadcasted_iota(jnp.int32, (rows, PAIR), 1) < HEAD_DIM
+    for i in range(NZ * 2):
+        at = slice(i * rows, (i + 1) * rows)
+        triple = dot_nn(held[at, :], weights) + offset
         turned = turn(triple[:, :PAIR], cosine[at, :], sine[at, :])
         query[at, :] = jnp.where(low_lanes, turned * HEAD_DIM ** (-0.5), 0.0).astype(LOW)
         kv[at, :] = jnp.where(
@@ -789,15 +798,12 @@
 
 
 def triple_weight_kernel(idx, *refs):
-    sheets, (grad, vectors, keep, send, total) = refs[:8], refs[8:]
+    sheets, (grad, vectors, keep, send, total, held) = refs[:8], refs[8:]
     mc = idx[3]
     slab = HEAD_DIM
-    for i, (value, at) in enumerate(sheet_rows(idx, sheets)):
-        part = dot_tn(value, grad[at, :])
-        if i == 0:
-            total[...] = part
-        else:
-            total[...] += part
+    for value, at in sheet_rows(idx, sheets):
+        held[at, :] = value
+    total[...] = dot_tn(held[...], grad[...])
     extra = extra_rows(column_sum(grad[...].astype(WIDE)), vectors).astype(LOW)
     for spot in range(NZ * 2):
         for out, c in ((keep, mc), (send, 1 - mc)):
@@ -912,14 +918,11 @@
         if outer > 1:
             pack = widen(both(heads, heads_other, mc)).transpose(0, 2, 1, 3, 4)
             head_triple = pack[..., :slab, :].reshape(width, QUAD)
-            outs = pack[..., slab + 16 :, :].reshape(-1, 2, slab, QUAD).transpose(0, 2, 1, 3)
-            outs = (outs.reshape(width, 2 * QUAD),)
             live0, live1 = [
                 pick(pack, c, 2)[..., slab, :rows].astype(WIDE).reshape(-1, rows)
                 for c in (mc, 1 - mc)
             ]
         else:
-            outs = (heads, heads_other)
             head_triple, live0, live1 = whole(
                 heads_kernel,
                 "heads",
@@ -927,13 +930,10 @@
                 (heads, heads_other),
                 [shape((width, QUAD), LOW)] + [shape((NZ * 2, rows), WIDE)] * 2,
             )
-        return head_triple, key_doc(live0, mc), key_doc(live1, 1 - mc), outs
-
-    half_tokens = lax.dynamic_slice_in_dim(tokens, my * half, half, 0)
-    by_z = [half_tokens] + [xor_z(half_tokens, m) for m in (1, 2, 3)]
-    own_other = flip(tokens, "x")
-
-    heads, low_slab, triple_slab = whole(
+        return head_triple, key_doc(live0, mc), key_doc(live1, 1 - mc)
+
+    few_out = slab // 2 if outer == 1 else 0
+    heads, low_slab, triple_slab, mine, own = whole(
         prep_kernel,
         "prep",
         index,
@@ -943,10 +943,14 @@
             expand_weight,
             contract_weight.T,
             line(live_mask),
+            tokens,
         ),
-        [shape((NZ * 2, 3 * slab + extra_count(slab), QUAD), LOW)]
-        + [shape((slab, n), LOW) for n in (2 * span, 6 * QUAD)],
-    )
+        [shape((NZ * 2, slab + extra_count(slab), QUAD), LOW)]
+        + [shape((slab, n), LOW) for n in (2 * span, 6 * QUAD)]
+        + [shape((half + few_out, width), LOW), shape((rows + few_out, width), LOW)],
+    )
+    by_z = [mine] + [xor_z(mine, m) for m in (1, 2, 3)]
+    own_other = flip(own, "x")
 
     where = jnp.arange(rows, dtype=jnp.int32) * blocks
     rank = jnp.arange(NZ * 2, dtype=jnp.int32) * 2
@@ -956,10 +960,18 @@
 
     def heads_stage():
         got = lax.all_to_all(heads, ("z", "x"), 0, 0)
-        sheets = [tokens, own_other]
+        sheets, outs = [tokens, own_other], [own[rows:], own_other[rows:]]
         for piece in by_z[1:]:
-            two = jnp.stack([piece, flip(piece, "x")])
+            turned = flip(piece, "x")
+            outs += [piece[half:], turned[half:]]
+            two = jnp.stack([piece[:half], turned[:half]])
             sheets += [two, flip(two, "y")]
+        if outer > 1:
+            out_low = output_weight.T.astype(LOW)
+            outs = [lax.all_gather(out_low, BLK, axis=0, tiled=True)]
+        else:
+            outs = [jnp.stack(outs)]
+            outs.append(flip(outs[0], "c"))
         own_places = (mo * NZ * 4 + rank + mc)[:, None] + where[None, :]
         own_position = doc_layout(doc_lengths, own_places.reshape(-1))[1]
         lane = jnp.arange(PAIR) % (HEAD_DIM // 2)
@@ -977,10 +989,11 @@
         positive = line(jnp.repeat(positives, query_vecs.shape[0] // queries_count))
         got = after(got, sheets[3], sheets[5], sheets[7], tables[0], units[0])
         head = head_weights(got, flip(got, "c"))
-        return head, sheets[2:], tables, list(units), positive
-
-    head, sheets, (cosine, sine), (query_unit, own_queries), positive = stage(heads_stage)
-    head_triple, kdoc0, kdoc1, outs = head
+        return head, outs, sheets[2:], tables, list(units), positive
+
+    head, outs, sheets, (cosine, sine), (query_unit, own_queries), positive = stage(heads_stage)
+    outs = tuple(outs)
+    head_triple, kdoc0, kdoc1 = head
     pieces = len(outs)
     sheets = [tokens, own_other] + sheets
     positive = lax.optimization_barrier(positive)
@@ -993,6 +1006,7 @@
             index,
             (*sheets, head_triple, cosine, sine, triple_bias),
             [shape((count, PAIR), LOW)] * 2,
+            [pltpu.VMEM((count, width), LOW)],
         )
         return queries, kv, flip(kv, "c")
 
@@ -1196,7 +1210,7 @@
                 index,
                 (*sheets, grad_triple, vectors1),
                 [shape(dims_triple, LOW)] * 2,
-                [pltpu.VMEM((width, QUAD), WIDE)],
+                [pltpu.VMEM((width, QUAD), WIDE), pltpu.VMEM((count, width), LOW)],
             )
         ordered = [(mz * 2 + (mx ^ x), sheets[x]) for x in range(2)]
         for m in (1, 2, 3):
@@ -1229,9 +1243,6 @@
         block_triple = to_blocks(dense_triple)
         keep, send = triple_parts()
         output_parts = output_parts_of()
-        packed = whole(
-            pair_sum_kernel, "pair_sum", index, (keep, flip(send, "c")), [shape(dims_triple, LOW)]
-        )[0]
         mine = whole(
             partial(query_back_kernel, half),
             "query_back",
@@ -1239,9 +1250,9 @@
             (kdoc0, kdoc1, coefficients, own_queries, units, sum_outer(grad_out)),
             [shape((shares + chunk + 16, proj), LOW)],
         )[0]
-        return block_triple, packed, output_parts[0], xor_z(output_parts[1], 1), mine
-
-    block_triple, packed, output_keep, output_got, mine = stage(triple_stage)
+        return block_triple, keep, send, output_parts[0], xor_z(output_parts[1], 1), mine
+
+    block_triple, packed_keep, packed_send, output_keep, output_got, mine = stage(triple_stage)
     block_triple, contract_got, expand_got = lax.optimization_barrier(
         (block_triple, contract_got, expand_got)
     )
@@ -1266,12 +1277,20 @@
             [pltpu.VMEM((rows, 6 * QUAD), LOW)] + slab_scratch(width, 6 * QUAD),
             (triple_low,),
         )[0]
+        part_other = flip(part, "y")
+        packed = whole(
+            pair_sum_kernel,
+            "pair_sum",
+            index,
+            (packed_keep, flip(packed_send, "c")),
+            [shape(dims_triple, LOW)],
+        )[0]
         tokens_grad = whole(
-            tokens_sum_kernel, "tokens_sum", index, (part, flip(part, "y"), grad_first_in), [wide_rows]
+            tokens_sum_kernel, "tokens_sum", index, (after(part, packed), part_other, grad_first_in), [wide_rows]
         )[0]
-        return tokens_grad
-
-    tokens_grad = stage(tokens_stage)
+        return tokens_grad, packed
+
+    tokens_grad, packed = stage(tokens_stage)
     packed = lax.all_to_all(after(packed, tokens_grad), ("z", "x"), 0, 0)
     contract_own, spread = after(contract_own, tokens_grad), after(spread, tokens_grad)
     keep, keep_out, send = whole(

time: 305 us -> 301 us (0.987)
  waiting for transfers between devices: 102 us -> 90.9 us
  local copies, waits for them, and re-layouts: 9.52 us -> 15.6 us
    all_to_all x1, waiting for transfers between devices: 16 us -> 0.01 us  [heads_stage(): got = lax.all_to_all(heads, ('z', 'x'), 0, 0)]
    ppermute x11, waiting for transfers between devices: 17.1 us -> 26.4 us  [xor_z(): return lax.ppermute(value, 'z', [(i, i ^ mask) for i in FOUR])]
    cond x32 -> x51, local copies, waits for them, and re-layouts: 4.35 us -> 11.3 us
    ppermute x26 -> x27, waiting for transfers between devices: 48.8 us -> 44.8 us  [flip(): return lax.ppermute(value, axis, [(0, 1), (1, 0)])]
    ppermute x26 -> x27, starting transfers between devices: 21.7 us -> 23.3 us  [flip(): return lax.ppermute(value, axis, [(0, 1), (1, 0)])]
  transfers between devices with their start and end apart: 48 -> 49, of which waited for: 25 -> 25; matrix products, arithmetic and copies ran while one was open for 3% -> 5% of each run, Pallas kernels for 30% -> 28%
where the time goes in v4:
time: 301 us; the launch traced here: 299 us
  Pallas kernels  92.5 us (31%)
  waiting for transfers between devices  90.9 us (30%)
  starting transfers between devices  64.2 us (21%)
  local copies, waits for them, and re-layouts  15.6 us (5%)
  between operations  14.1 us (5%)
  blocking collectives  13.9 us (5%)
  other arithmetic  7.34 us (2%)
    pallas_call x23, Pallas kernels, whole(): pl.pallas_call(kernel, in_specs=[pl.BlockSpec(memory_space=pltpu.SMEM)] +...  76.3 us
    ppermute x27, waiting for transfers between devices, flip(): return lax.ppermute(value, axis, [(0, 1), (1, 0)])  44.8 us
    ppermute x11, waiting for transfers between devices, xor_z(): return lax.ppermute(value, 'z', [(i, i ^ mask) for i in FOUR])  26.4 us
    ppermute x27, starting transfers between devices, flip(): return lax.ppermute(value, axis, [(0, 1), (1, 0)])  23.3 us
    ppermute x11, starting transfers between devices, xor_z(): return lax.ppermute(value, 'z', [(i, i ^ mask) for i in FOUR])  15.7 us
    all_to_all x1, blocking collectives, to_blocks(): lax.all_to_all(value.reshape((NZ * 2,) + value.shape[-2:]), ('z', 'x'), 0...  13.9 us
    all_to_all x2, starting transfers between devices, to_blocks(): lax.all_to_all(value.reshape((NZ * 2,) + value.shape[-2:]), ('z', 'x'), 0...  12.8 us
    cond x51, local copies, waits for them, and re-layouts  11.3 us
  transfers between devices with their start and end apart: 49, of which 25 were waited for; matrix products, arithmetic and copies ran while one was open for 5% of the time, Pallas kernels for 28%

profile of v4, /device:TPU:0, one launch (start us, length us, event | category | flops | bytes accessed | tf_op | source)
XLA Modules:
  0.0 299.3 jit_solution(15150541714326692439)
XLA Ops:
  7.3 2.7 prep.1
  10.0 2.9 collective-permute-start.28
  14.5 2.6 collective-permute-start.30
  17.3 5.3 %collective-permute-done.29 = bf16[96,1024]{1,0:T(8,128)(2,1)S(1)} collective-permute-done((bf16[96,1024]{1,0:T(8,128)(2,1)}, bf16[96,1024]{1,0:T(8,128)(2,1)S(1)}, u32[]{:S(2)}, u32[]{:S(2)}) %collective-permute-start.29) | collective-permute-done | bytes 196640 | tf_op jit(solution)/shard_map/ppermute | solution.py:33
  22.7 9.2 %collective-permute-done.30 = bf16[96,1024]{1,0:T(8,128)(2,1)S(1)} collective-permute-done((bf16[96,1024]{1,0:T(8,128)(2,1)}, bf16[96,1024]{1,0:T(8,128)(2,1)S(1)}, u32[]{:S(2)}, u32[]{:S(2)}) %collective-permute-start.30) | collective-permute-done | bytes 196640 | tf_op jit(solution)/shard_map/ppermute | solution.py:33
  32.1 41.3 %conditional.11 = (bf16[1024,256]{1,0:T(8,128)(2,1)S(1)}, s32[8,128]{1,0:T(8,128)S(1)}, s32[8,128]{1,0:T(8,128)S(1)}, bf16[8,32,1024]{2,1,0:T(8,128)(2,1)}, bf16...) conditional(s32[]{:T(128)} %bitcast.27, () %tuple.119, ...), branch_computations={%region_0.0_spmd, %region_1.6_spmd} | conditional | flops 5520703488 | bytes 35979452 | solution.py:910
  34.8 6.2 %all-to-all-start.3 = ((bf16[8,64,256]{2,1,0:T(8,128)(2,1)}), bf16[8,64,256]{2,1,0:T(8,128)(2,1)S(1)}, u32[]{:S(2)}, u32[]{:S(2)}) async-start(bf16[8,64,256]{2,1,0:T(8,128)(2,1)} %get-tuple-element.262), calls=%async_computation.3 | async-start | bytes 524288 | tf_op jit(solution)/shard_map/cond/branch_1_fun/all_to_all | solution.py:962
  45.9 3.0 %fusion = (f32[1024,128]{1,0:T(8,128)}, f32[1024,128]{1,0:T(8,128)}) fusion(f32[128]{0:T(128)S(1)} %get-tuple-element.699, f32[128]{0:T(128)S(1)} %get-tuple-element.700, f32[1024]{0:T(1024)S(1)} %subtract_convert_fusion), kind=kLoop, calls=%fused_computation.2 | loop fusion | flops 262144 | bytes 1053696 | tf_op jit(solution)/shard_map/cond/branch_1_fun/mul | solution.py:981
  57.3 2.6 collective-permute-done.15
  59.9 4.9 %collective-permute-done.17 = bf16[2,64,1024]{2,1,0:T(8,128)(2,1)} collective-permute-done((bf16[2,64,1024]{2,1,0:T(8,128)(2,1)}, bf16[2,64,1024]{2,1,0:T(8,128)(2,1)}, u32[]{:S(2)}, u32[]{:S(2)}) %collective-permute-start.17) | collective-permute-done | bytes 262176 | tf_op jit(solution)/shard_map/cond/branch_1_fun/ppermute | solution.py:41
  64.8 2.8 collective-permute-done.19
  70.1 1.9 heads.1
  73.4 5.6 %conditional.12 = (bf16[1024,128]{1,0:T(8,128)(2,1)}, bf16[1024,128]{1,0:T(8,128)(2,1)}, bf16[1024,128]{1,0:T(8,128)(2,1)}) conditional(s32[]{:T(128)} %bitcast.27, () %tuple.118, (s32[5]{0:T(128)S(1)}, bf16[128,1024]{1,0:T(8,128)(2,1)}, bf16[160,1024]{1,0:T(8,128)(2,1)S(1)}, bf16[2,64,1024]{2,1,0:T(8,128)(2,1)}, bf16[2,64,1024]{2,1,0:T(8,128)(2,1)}, ...), branch_computations={%region_6.7_spmd, %region_7.8_spmd} | conditional | flops 4369999872 | bytes 15108640 | solution.py:910
  73.4 3.7 %project.1 = (bf16[1024,128]{1,0:T(8,128)(2,1)}, bf16[1024,128]{1,0:T(8,128)(2,1)}) custom-call(s32[5]{0:T(128)S(1)} %get-tuple-element.282.idx, bf16[128,1024]{1,0:T(8,128)(2,1)} %get-tuple-element.283.refs_0_, bf16[160,1024]{1,0:T(8,128)(2,1)S(1)} %get-tuple-element.284.refs_1_, bf16[2,64,1024]{2,1,0:T(8,128)(2,1)} %get-tuple-element.285.refs_2_, ...), custom_call_target="tpu_custom_call" | custom-call | flops 4369999872 | bytes 14060000 | tf_op jit(solution)/shard_map/cond/branch_1_fun/project/pallas_call | solution.py:115
  79.0 20.4 %conditional.13 = (f32[4,2,2,64,128]{4,3,2,1,0:T(8,128)}, f32[4,1,1,256]{3,2,1,0:T(1,128)}, bf16[8,64,128]{2,1,0:T(8,128)(2,1)S(1)}) conditional(s32[]{:T(128)} %bitcast.27, () %tuple.117, (bf16[1024,128]{1,0:T(8,128)(2,1)}, s32[5]{0:T(128)S(1)}, s32[4]{0:T(128)S(1)}, bf16[1024,128]{1,0:T(8,128)(2,1)}, bf16[1024,128]{1,0:T(8,128)(2,1)}, ...), branch_computations={%region_8.9_spmd, %region_9.10_spmd} | conditional | flops 8625000448 | bytes 28012168 | solution.py:910
  79.0 6.5 %attend.1 = (f32[4,2,2,64,128]{4,3,2,1,0:T(8,128)}, f32[4,1,1,256]{3,2,1,0:T(1,128)}, bf16[4,2,64,128]{3,2,1,0:T(8,128)(2,1)}) custom-call(s32[5]{0:T(128)S(1)} %get-tuple-element.297.idx, s32[4]{0:T(128)S(1)} %get-tuple-element.298.lens, bf16[4,2,2,64,128]{4,3,2,1,0:T(8,128)(2,1)} %bitcast.17.q_ref, bf16[1024,128]{1,0:T(8,128)(2,1)} %get-tuple-element.300.kv0_ref, ...), custom_call_target="tpu_custom_call" | custom-call | flops 8625000448 | bytes 27750000 | tf_op jit(solution)/shard_map/cond/branch_1_fun/attend/pallas_call | solution.py:353
  85.5 13.9 %all_to_all.21 = bf16[8,64,128]{2,1,0:T(8,128)(2,1)S(1)} all-to-all(bf16[8,64,128]{2,1,0:T(8,128)(2,1)} %bitcast.77), channel_id=1, replica_groups=mesh['o'=1,'z'=4,'x'=2,'c'=2,'y'=2] {'z','x'}, dimensions={0} | all-to-all | bytes 262144 | tf_op jit(solution)/shard_map/cond/branch_1_fun/all_to_all | solution.py:1019
  99.4 11.1 %conditional.14 = (bf16[128,512]{1,0:T(8,128)(2,1)S(1)}, bf16[128,1024]{1,0:T(8,128)(2,1)}, bf16[128,1024]{1,0:T(8,128)(2,1)}) conditional(s32[]{:T(128)} %bitcast.27, () %tuple.116, (s32[5]{0:T(128)S(1)}, bf16[8,64,128]{2,1,0:T(8,128)(2,1)S(1)}, bf16[8,32,1024]{2,1,0:T(8,128)(2,1)}, bf16[8,32,1024]{2,1,0:T(8,128)(2,1)}) %tuple.124), branch_computations={%region_10.11_spmd, %region_11.12_spmd} | conditional | flops 4024999936 | bytes 13998640 | solution.py:910
  99.4 3.2 %branch.1 = (bf16[128,512]{1,0:T(8,128)(2,1)S(1)}, bf16[128,1024]{1,0:T(8,128)(2,1)}) custom-call(s32[5]{0:T(128)S(1)} %get-tuple-element.307.idx, bf16[8,64,128]{2,1,0:T(8,128)(2,1)S(1)} %get-tuple-element.308.got, bf16[8,32,1024]{2,1,0:T(8,128)(2,1)} %get-tuple-element.309.refs_0_, bf16[8,32,1024]{2,1,0:T(8,128)(2,1)} %get-tuple-element.310.refs_1_), custom_call_target="tpu_custom_call" | custom-call | flops 4024999936 | bytes 12950000 | tf_op jit(solution)/shard_map/cond/branch_1_fun/branch/pallas_call | solution.py:115
  104.2 6.3 %collective-permute-done.1 = bf16[128,1024]{1,0:T(8,128)(2,1)} collective-permute-done((bf16[128,1024]{1,0:T(8,128)(2,1)}, bf16[128,1024]{1,0:T(8,128)(2,1)}, u32[]{:S(2)}, u32[]{:S(2)}) %collective-permute-start.1) | collective-permute-done | bytes 262176 | tf_op jit(solution)/shard_map/cond/branch_1_fun/ppermute | solution.py:41
  111.2 7.2 %forward.1 = (f32[128,1024]{1,0:T(8,128)}, f32[128,1024]{1,0:T(8,128)}, f32[128,1]{1,0:T(8,128)}, f32[128,2048]{1,0:T(8,128)}, bf16[288,1024]{1,0:T(8,128)(2,1)}...) custom-call(s32[5]{0:T(128)S(1)} %stack.74.idx, bf16[128,1024]{1,0:T(8,128)(2,1)} %get-tuple-element.578.own, ...), custom_call_target="tpu_custom_call" | custom-call | flops 8855000064 | bytes 28490000 | tf_op jit(solution)/shard_map/forward/pallas_call | solution.py:115
  118.7 2.0 collective-permute-start.33
  120.7 12.8 %conditional.15 = ((bf16[128,1024]{1,0:T(8,128)(2,1)}, f32[128,1024]{1,0:T(8,128)}, f32[128,1]{1,0:T(8,128)}, f32[128,128]{1,0:T(8,128)}, bf16[128,128]{1,0:T(8,...) conditional(s32[]{:T(128)} %bitcast.27, () %tuple.115, ...), branch_computations={%region_12.13_spmd, %region_13.14_spmd} | conditional | flops 4140000000 | bytes 15433748 | solution.py:910
  122.3 6.9 %collective-permute-done.2.other = bf16[128,1024]{1,0:T(8,128)(2,1)S(1)} collective-permute-done((bf16[128,1024]{1,0:T(8,128)(2,1)}, bf16[128,1024]{1,0:T(8,128)(2,1)S(1)}, u32[]{:S(2)}, u32[]{:S(2)}) %collective-permute-start.2) | collective-permute-done | bytes 262176 | tf_op jit(solution)/shard_map/cond/branch_1_fun/ppermute | solution.py:41
  129.9 3.4 %second.1 = (bf16[128,1024]{1,0:T(8,128)(2,1)}, f32[128,1024]{1,0:T(8,128)}, f32[128,1]{1,0:T(8,128)}, f32[128,128]{1,0:T(8,128)}, bf16[128,128]{1,0:T(8,128)(2,...) custom-call(s32[5]{0:T(128)} %copy-done.19, bf16[128,1024]{1,0:T(8,128)(2,1)} %get-tuple-element.314.own, ...), custom_call_target="tpu_custom_call" | custom-call | flops 4140000000 | bytes 13320000 | tf_op jit(solution)/shard_map/cond/branch_1_fun/second/pallas_call | solution.py:115
  133.5 28.8 %conditional.16 = ((f32[128,1024]{1,0:T(8,128)}, bf16[256,1024]{1,0:T(8,128)(2,1)}, bf16[256,1024]{1,0:T(8,128)(2,1)}, bf16[128,1024]{1,0:T(8,128)(2,1)}, f32[8,...) conditional(s32[]{:T(128)} %bitcast.27, () %tuple.128, ...), branch_computations={%region_14.15_spmd, %region_15.16_spmd} | conditional | flops 13800048640 | bytes 47349480 | solution.py:910
  135.5 3.1 %collective-permute-done.23 = f32[4,4096]{1,0:T(4,128)S(1)} collective-permute-done((f32[4,4096]{1,0:T(4,128)S(1)}, f32[4,4096]{1,0:T(4,128)S(1)}, u32[]{:S(2)}, u32[]{:S(2)}) %collective-permute-start.23) | collective-permute-done | bytes 65568 | tf_op jit(solution)/shard_map/cond/branch_1_fun/ppermute | solution.py:37
  140.2 1.9 collective-permute-start.26
  143.6 2.7 collective-permute-done.25.t1
  146.4 5.4 %collective-permute-done.26.t2 = f32[4,4096]{1,0:T(4,128)S(1)} collective-permute-done((f32[4,4096]{1,0:T(4,128)S(1)}, f32[4,4096]{1,0:T(4,128)S(1)}, u32[]{:S(2)}, u32[]{:S(2)}) %collective-permute-start.26) | collective-permute-done | bytes 65568 | tf_op jit(solution)/shard_map/cond/branch_1_fun/ppermute | solution.py:33
  152.5 9.9 %middle.1 = (f32[128,1024]{1,0:T(8,128)}, bf16[256,1024]{1,0:T(8,128)(2,1)}, bf16[256,1024]{1,0:T(8,128)(2,1)}, bf16[128,1024]{1,0:T(8,128)(2,1)}, f32[8,128]{1,...) custom-call(s32[5]{0:T(128)} %get-tuple-element.322.idx, ...), custom_call_target="tpu_custom_call" | custom-call | flops 13799999488 | bytes 44400000 | tf_op jit(solution)/shard_map/cond/branch_1_fun/middle/pallas_call | solution.py:115
  165.1 13.9 %conditional.17 = ((f32[128,1024]{1,0:T(8,128)}, bf16[128,1024]{1,0:T(8,128)(2,1)S(1)}, f32[8,1024]{1,0:T(8,128)S(1)}, bf16[8,144,128]{2,1,0:T(8,128)(2,1)})) conditional(s32[]{:T(128)} %bitcast.27, () %tuple.135, (bf16[128,1024]{1,0:T(8,128)(2,1)}, f32[1024]{0:T(1024)}, bf16[8,80,128]{2,1,0:T(8,128)(2,1)}, s32[5]{0:T(128)}, ...), branch_computations={%region_16.17_spmd, %region_17.18_spmd} | conditional | flops 4369999872 | bytes 17468016 | solution.py:910
  168.1 5.9 %collective-permute-done.3.other = bf16[128,1024]{1,0:T(8,128)(2,1)S(1)} collective-permute-done((bf16[128,1024]{1,0:T(8,128)(2,1)}, bf16[128,1024]{1,0:T(8,128)(2,1)S(1)}, u32[]{:S(2)}, u32[]{:S(2)}) %collective-permute-start.3) | collective-permute-done | bytes 262176 | tf_op jit(solution)/shard_map/cond/branch_1_fun/ppermute | solution.py:41
  174.8 4.2 %first_back.1 = (f32[128,1024]{1,0:T(8,128)}, bf16[128,1024]{1,0:T(8,128)(2,1)S(1)}, f32[8,1024]{1,0:T(8,128)S(1)}, bf16[8,144,128]{2,1,0:T(8,128)(2,1)}) custom-call(s32[5]{0:T(128)} %get-tuple-element.339.idx, bf16[128,1024]{1,0:T(8,128)(2,1)} %get-tuple-element.340.own, bf16[128,1024]{1,0:T(8,128)(2,1)} %copy-done.31, ...), custom_call_target="tpu_custom_call" | custom-call | flops 4369999872 | bytes 14060000 | tf_op jit(solution)/shard_map/cond/branch_1_fun/first_back/pallas_call | solution.py:115
  179.1 20.4 %conditional.18 = (bf16[8,144,128]{2,1,0:T(8,128)(2,1)}, bf16[128,1024]{1,0:T(8,128)(2,1)}, bf16[128,1024]{1,0:T(8,128)(2,1)}, bf16[128,1024]{1,0:T(8,128)(2,1)}...) conditional(s32[]{:T(128)} %bitcast.27, () %tuple.134, ...), branch_computations={%region_18.19_spmd, %region_19.20_spmd} | conditional | flops 5980000256 | bytes 34018756 | solution.py:910
  180.8 5.6 %all-to-all-start.1 = ((bf16[8,144,128]{2,1,0:T(8,128)(2,1)}), bf16[8,144,128]{2,1,0:T(8,128)(2,1)}, u32[]{:S(2)}, u32[]{:S(2)}) async-start(bf16[8,144,128]{2,1,0:T(8,128)(2,1)} %get-tuple-element.349), calls=%async_computation.1 | async-start | bytes 589824 | tf_op jit(solution)/shard_map/cond/branch_1_fun/all_to_all | solution.py:1019
  188.9 5.3 %weights.1 = (f32[2,2,64,1024]{3,2,1,0:T(8,128)S(1)}, bf16[2,2,64,1024]{3,2,1,0:T(8,128)(2,1)S(1)}, f32[2,2,64,1024]{3,2,1,0:T(8,128)S(1)}, bf16[2,2,64,1024]{3,2,1,0:T(8,128)(2,1)S(1)}) custom-call(s32[5]{0:T(128)} %get-tuple-element.352.idx, bf16[288,1024]{1,0:T(8,128)(2,1)} %get-tuple-element.353.f0, bf16[288,1024]{1,0:T(8,128)(2,1)} %get-tuple-element.351.f1, ...), custom_call_target="tpu_custom_call" | custom-call | flops 5980000256 | bytes 19240000 | tf_op jit(solution)/shard_map/cond/branch_1_fun/weights/pallas_call | solution.py:115
  194.2 5.3 %all-to-all-done.1 = bf16[8,144,128]{2,1,0:T(8,128)(2,1)} async-done(((bf16[8,144,128]{2,1,0:T(8,128)(2,1)}), bf16[8,144,128]{2,1,0:T(8,128)(2,1)}, u32[]{:S(2)}, u32[]{:S(2)}) %all-to-all-start.1) | async-done | bytes 294944 | tf_op jit(solution)/shard_map/cond/branch_1_fun/all_to_all | solution.py:1019
  201.5 16.0 %conditional.19 = ((bf16[1024,256]{1,0:T(8,128)(2,1)}, bf16[8,96,256]{2,1,0:T(8,128)(2,1)})) conditional(s32[]{:T(128)} %bitcast.27, () %tuple.133, (bf16[1024,128]{1,0:T(8,128)(2,1)}, bf16[8,144,128]{2,1,0:T(8,128)(2,1)}, s32[5]{0:T(128)}, s32[4]{0:T(128)S(1)}, f32[4,2,2,64,128]{4,3,2,1,0:T(8,128)}, /*index=5*/f32[4,1,1,256]{3,2,1,0:T(1,128)S(1)}, ...), branch_computations={%region_20.21_spmd, %region_21.22_spmd} | conditional | flops 14604999680 | bytes 51184488 | solution.py:910
  201.7 9.7 %attend_back.1 = (f32[4,2,2,64,128]{4,3,2,1,0:T(8,128)}, f32[1024,128]{1,0:T(8,128)}, f32[1024,128]{1,0:T(8,128)}) custom-call(s32[5]{0:T(128)} %get-tuple-element.362.idx, s32[4]{0:T(128)S(1)} %get-tuple-element.363.lens, bf16[4,2,2,64,128]{4,3,2,1,0:T(8,128)(2,1)} %bitcast.24.q_ref, bf16[4,2,144,128]{3,2,1,0:T(8,128)(2,1)} %bitcast.25.g_ref, ...), custom_call_target="tpu_custom_call" | custom-call | flops 11269999616 | bytes 36260000 | tf_op jit(solution)/shard_map/cond/branch_1_fun/attend_back/pallas_call | solution.py:414
  211.5 2.1 collective-permute-done.10.got
  214.4 3.1 %triple.1 = (bf16[1024,256]{1,0:T(8,128)(2,1)}, bf16[8,96,256]{2,1,0:T(8,128)(2,1)}) custom-call(s32[5]{0:T(128)S(1)} %copy-done.20, f32[1024,128]{1,0:T(8,128)} %bitcast.95, f32[1024,128]{1,0:T(8,128)} %get-tuple-element.373.dkv, f32[1024,128]{1,0:T(8,128)} %copy-done.25, f32[1024,128]{1,0:T(8,128)} %get-tuple-element.375.cosine, ...), custom_call_target="tpu_custom_call" | custom-call | flops 3335000064 | bytes 10730000 | tf_op jit(solution)/shard_map/cond/branch_1_fun/triple/pallas_call | solution.py:115
  217.5 2.1 pair.2
  220.0 23.2 %conditional.20 = (bf16[8,96,256]{2,1,0:T(8,128)(2,1)}, bf16[8,64,256]{2,1,0:T(8,128)(2,1)S(1)}, bf16[8,64,256]{2,1,0:T(8,128)(2,1)S(1)}, f32[2,2,64,256]{3,2,1,...) conditional(s32[]{:T(128)} %bitcast.27, () %tuple.132, ...), branch_computations={%region_22.23_spmd, %region_23.24_spmd} | conditional | flops 5175000064 | bytes 24907740 | solution.py:910
  220.0 7.2 %all-to-all-start.2 = ((bf16[8,96,256]{2,1,0:T(8,128)(2,1)}), bf16[8,96,256]{2,1,0:T(8,128)(2,1)}, u32[]{:S(2)}, u32[]{:S(2)}) async-start(bf16[8,96,256]{2,1,0:T(8,128)(2,1)} %get-tuple-element.377), calls=%async_computation.2 | async-start | bytes 786432 | tf_op jit(solution)/shard_map/cond/branch_1_fun/all_to_all | solution.py:1019
  227.3 3.9 %output.1 = (f32[2,2,64,256]{3,2,1,0:T(8,128)S(1)}, bf16[2,2,64,256]{3,2,1,0:T(8,128)(2,1)}) custom-call(s32[5]{0:T(128)S(1)} %get-tuple-element.378.idx, bf16[288,1024]{1,0:T(8,128)(2,1)} %get-tuple-element.391.f0, bf16[288,1024]{1,0:T(8,128)(2,1)} %get-tuple-element.392.f1, bf16[288,1024]{1,0:T(8,128)(2,1)} %get-tuple-element.393.f2, ...), custom_call_target="tpu_custom_call" | custom-call | flops 1724999936 | bytes 5550000 | tf_op jit(solution)/shard_map/cond/branch_1_fun/output/pallas_call | solution.py:115
  231.2 2.0 collective-permute-start.11
  233.2 2.4 triple_weight.1
  235.7 2.3 query_back.1
  238.0 3.6 %collective-permute-done.11 = bf16[2,2,64,256]{3,2,1,0:T(8,128)(2,1)} collective-permute-done((bf16[2,2,64,256]{3,2,1,0:T(8,128)(2,1)}, bf16[2,2,64,256]{3,2,1,0:T(8,128)(2,1)}, u32[]{:S(2)}, u32[]{:S(2)}) %collective-permute-start.11) | collective-permute-done | bytes 131104 | tf_op jit(solution)/shard_map/cond/branch_1_fun/ppermute | solution.py:33
  243.3 2.2 pair.3
  245.5 2.3 collective-permute-start.39
  247.8 15.6 %conditional.21 = (f32[128,1024]{1,0:T(8,128)S(1)}, bf16[8,64,256]{2,1,0:T(8,128)(2,1)}) conditional(s32[]{:T(128)} %bitcast.27, () %tuple.131, (s32[5]{0:T(128)S(1)}, bf16[8,96,256]{2,1,0:T(8,128)(2,1)}, bf16[1024,1536]{1,0:T(8,128)(2,1)}, bf16[8,64,256]{2,1,0:T(8,128)(2,1)S(1)}, bf16[8,64,256]{2,1,0:T(8,128)(2,1)S(1)}, ...), branch_computations={%region_24.25_spmd, %region_25.26_spmd} | conditional | flops 7820000256 | bytes 29354456 | solution.py:910
  247.8 4.8 %tokens.3.own = bf16[128,1024]{1,0:T(8,128)(2,1)} custom-call(s32[5]{0:T(128)S(1)} %get-tuple-element.407.idx, bf16[8,96,256]{2,1,0:T(8,128)(2,1)} %get-tuple-element.408.got, bf16[1024,1536]{1,0:T(8,128)(2,1)} %get-tuple-element.409.message), custom_call_target="tpu_custom_call" | custom-call | flops 4485000192 | bytes 14430000 | tf_op jit(solution)/shard_map/cond/branch_1_fun/tokens/pallas_call | solution.py:115
  256.5 5.1 %collective-permute-done.13.other = bf16[128,1024]{1,0:T(8,128)(2,1)S(1)} collective-permute-done((bf16[128,1024]{1,0:T(8,128)(2,1)}, bf16[128,1024]{1,0:T(8,128)(2,1)S(1)}, u32[]{:S(2)}, u32[]{:S(2)}) %collective-permute-start.13) | collective-permute-done | bytes 262176 | tf_op jit(solution)/shard_map/cond/branch_1_fun/ppermute | solution.py:41
  263.4 4.2 %all-to-all-start.4 = ((bf16[8,64,256]{2,1,0:T(8,128)(2,1)}), bf16[8,64,256]{2,1,0:T(8,128)(2,1)S(1)}, u32[]{:S(2)}, u32[]{:S(2)}) async-start(bf16[8,64,256]{2,1,0:T(8,128)(2,1)} %get-tuple-element.666), calls=%async_computation.4 | async-start | bytes 524288 | tf_op jit(solution)/shard_map/all_to_all | solution.py:1294
  268.3 2.5 line_sum.1
  270.8 2.0 collective-permute-start.40
  274.0 4.4 %all-to-all-done.4.got = bf16[8,64,256]{2,1,0:T(8,128)(2,1)S(1)} async-done(((bf16[8,64,256]{2,1,0:T(8,128)(2,1)}), bf16[8,64,256]{2,1,0:T(8,128)(2,1)S(1)}, u32[]{:S(2)}, u32[]{:S(2)}) %all-to-all-start.4) | async-done | bytes 262176 | tf_op jit(solution)/shard_map/all_to_all | solution.py:1294
  279.1 1.9 triple_out.1
  281.0 3.1 %collective-permute-done.40.got = bf16[64,2304]{1,0:T(8,128)(2,1)S(1)} collective-permute-done((bf16[64,2304]{1,0:T(8,128)(2,1)}, bf16[64,2304]{1,0:T(8,128)(2,1)S(1)}, u32[]{:S(2)}, u32[]{:S(2)}) %collective-permute-start.40) | collective-permute-done | bytes 294944 | tf_op jit(solution)/shard_map/ppermute | solution.py:41
  284.9 2.2 columns.1
  287.1 2.7 all-gather.12.cloned.1.call-done
  289.9 2.9 spread.1
  (201 shorter events, 59.2 us)
Async XLA Ops:
  7.2 104.0 %all-gather.6.cloned.1.call-start = ((), (), s32[]{:S(2)}) async-start(), calls=%async_computation.5 | async-start | bytes 8912896 | tf_op jit(solution)/shard_map/all_gather | solution.py:959
  7.3 113.4 %copy-start.17 = (s32[5]{0:T(128)}, s32[5]{0:T(128)S(1)}, u32[]{:S(2)}) copy-start(s32[5]{0:T(128)S(1)} %stack.74.idx) | copy-start | bytes 64
  7.3 24.6 %copy-start.41 = (s32[4]{0:T(128)S(1)}, s32[4]{0:T(128)}, u32[]{:S(2)}) copy-start(s32[4]{0:T(128)} %param.44) | copy-start | bytes 52
  7.3 24.7 %copy-start.16 = (s32[128]{0:T(128)S(1)}, s32[128]{0:T(128)}, u32[]{:S(2)}) copy-start(s32[128]{0:T(128)} %param.46) | copy-start | bytes 1540
  10.0 21.9 %collective-permute-start.28 = (bf16[160,1024]{1,0:T(8,128)(2,1)S(1)}, bf16[160,1024]{1,0:T(8,128)(2,1)S(1)}, u32[]{:S(2)}, u32[]{:S(2)}) collective-permute-start(bf16[160,1024]{1,0:T(8,128)(2,1)S(1)} %get-tuple-element.555), channel_id=1, source_target_pairs={{0,4},{4,0},{1,5},{5,1},{2,6},{6,2},{3,7},{7,3},{8,12},{12,8},{9,1... | collective-permute-start | bytes 983048 | tf_op jit(solution)/shard_map/ppermute | solution.py:41
  12.9 9.7 %collective-permute-start.29 = (bf16[96,1024]{1,0:T(8,128)(2,1)}, bf16[96,1024]{1,0:T(8,128)(2,1)S(1)}, u32[]{:S(2)}, u32[]{:S(2)}) collective-permute-start(bf16[96,1024]{1,0:T(8,128)(2,1)} %get-tuple-element.557), channel_id=1, source_target_pairs={{0,8},{8,0},{16,24},{24,16},{1,9},{9,1},{17,25},{25,17},{2,10},{10... | collective-permute-start | bytes 589832 | tf_op jit(solution)/shard_map/ppermute | solution.py:33
  14.5 17.4 %collective-permute-start.30 = (bf16[96,1024]{1,0:T(8,128)(2,1)}, bf16[96,1024]{1,0:T(8,128)(2,1)S(1)}, u32[]{:S(2)}, u32[]{:S(2)}) collective-permute-start(bf16[96,1024]{1,0:T(8,128)(2,1)} %get-tuple-element.557), channel_id=1, source_target_pairs={{0,16},{8,24},{16,0},{24,8},{1,17},{9,25},{17,1},{25,9},{2,18},{10... | collective-permute-start | bytes 589832 | tf_op jit(solution)/shard_map/ppermute | solution.py:33
  17.1 14.8 %collective-permute-start.31 = (bf16[96,1024]{1,0:T(8,128)(2,1)}, bf16[96,1024]{1,0:T(8,128)(2,1)S(1)}, u32[]{:S(2)}, u32[]{:S(2)}) collective-permute-start(bf16[96,1024]{1,0:T(8,128)(2,1)} %get-tuple-element.557), channel_id=1, source_target_pairs={{0,24},{8,16},{16,8},{24,0},{1,25},{9,17},{17,9},{25,1},{2,26},{10... | collective-permute-start | bytes 589832 | tf_op jit(solution)/shard_map/ppermute | solution.py:33
  31.9 41.5 %copy-start.7 = (bf16[160,1024]{1,0:T(8,128)(2,1)}, bf16[160,1024]{1,0:T(8,128)(2,1)S(1)}, u32[]{:S(2)}) copy-start(bf16[160,1024]{1,0:T(8,128)(2,1)S(1)} %collective-permute-done.28) | copy-start | bytes 983044
  31.9 131.7 %all-gather.8.cloned.1.call-start = ((), (), s32[]{:S(2)}) async-start(), calls=%async_computation.6 | async-start | bytes 3342336 | tf_op jit(solution)/shard_map/all_gather | solution.py:1042
  32.1 41.3 %copy-start.39 = (f32[3,512]{1,0:T(4,128)S(1)}, f32[3,512]{1,0:T(4,128)}, u32[]{:S(2)}) copy-start(f32[3,512]{1,0:T(4,128)} %param.48) | copy-start | bytes 18436
  32.1 17.5 %collective-permute-start.14 = (bf16[96,1024]{1,0:T(8,128)(2,1)S(1)}, bf16[96,1024]{1,0:T(8,128)(2,1)S(1)}, u32[]{:S(2)}, u32[]{:S(2)}) collective-permute-start(bf16[96,1024]{1,0:T(8,128)(2,1)S(1)} %get-tuple-element.263), channel_id=1, source_target_pairs={{0,4},{4,0},{1,5},{5,1},{2,6},{6,2},{3,7},{7,3},{8,12},{12,8},{9,1... | collective-permute-start | bytes 589832 | tf_op jit(solution)/shard_map/cond/branch_1_fun/ppermute | solution.py:41
  32.8 19.1 %collective-permute-start.16 = (bf16[96,1024]{1,0:T(8,128)(2,1)S(1)}, bf16[96,1024]{1,0:T(8,128)(2,1)S(1)}, u32[]{:S(2)}, u32[]{:S(2)}) collective-permute-start(bf16[96,1024]{1,0:T(8,128)(2,1)S(1)} %get-tuple-element.264), channel_id=1, source_target_pairs={{0,4},{4,0},{1,5},{5,1},{2,6},{6,2},{3,7},{7,3},{8,12},{12,8},{9,1... | collective-permute-start | bytes 589832 | tf_op jit(solution)/shard_map/cond/branch_1_fun/ppermute | solution.py:41
  34.2 19.0 %collective-permute-start.18 = (bf16[96,1024]{1,0:T(8,128)(2,1)S(1)}, bf16[96,1024]{1,0:T(8,128)(2,1)S(1)}, u32[]{:S(2)}, u32[]{:S(2)}) collective-permute-start(bf16[96,1024]{1,0:T(8,128)(2,1)S(1)} %get-tuple-element.265), channel_id=1, source_target_pairs={{0,4},{4,0},{1,5},{5,1},{2,6},{6,2},{3,7},{7,3},{8,12},{12,8},{9,1... | collective-permute-start | bytes 589832 | tf_op jit(solution)/shard_map/cond/branch_1_fun/ppermute | solution.py:41
  34.8 32.8 %all-to-all-start.3 = ((bf16[8,64,256]{2,1,0:T(8,128)(2,1)}), bf16[8,64,256]{2,1,0:T(8,128)(2,1)S(1)}, u32[]{:S(2)}, u32[]{:S(2)}) async-start(bf16[8,64,256]{2,1,0:T(8,128)(2,1)} %get-tuple-element.262), calls=%async_computation.3 | async-start | bytes 524288 | tf_op jit(solution)/shard_map/cond/branch_1_fun/all_to_all | solution.py:962
  50.4 9.6 %collective-permute-start.15 = (bf16[2,64,1024]{2,1,0:T(8,128)(2,1)}, bf16[2,64,1024]{2,1,0:T(8,128)(2,1)}, u32[]{:S(2)}, u32[]{:S(2)}) collective-permute-start(bf16[2,64,1024]{2,1,0:T(8,128)(2,1)} %pad_maximum_fusion), channel_id=1, source_target_pairs={{0,1},{1,0},{2,3},{3,2},{4,5},{5,4},{6,7},{7,6},{8,9},{9,8},{10,11... | collective-permute-start | bytes 786440 | tf_op jit(solution)/shard_map/cond/branch_1_fun/ppermute | solution.py:41
  52.6 12.2 %collective-permute-start.17 = (bf16[2,64,1024]{2,1,0:T(8,128)(2,1)}, bf16[2,64,1024]{2,1,0:T(8,128)(2,1)}, u32[]{:S(2)}, u32[]{:S(2)}) collective-permute-start(bf16[2,64,1024]{2,1,0:T(8,128)(2,1)} %pad_maximum_fusion.1), channel_id=1, source_target_pairs={{0,1},{1,0},{2,3},{3,2},{4,5},{5,4},{6,7},{7,6},{8,9},{9,8},{10,11... | collective-permute-start | bytes 786440 | tf_op jit(solution)/shard_map/cond/branch_1_fun/ppermute | solution.py:41
  53.9 13.7 %collective-permute-start.19 = (bf16[2,64,1024]{2,1,0:T(8,128)(2,1)}, bf16[2,64,1024]{2,1,0:T(8,128)(2,1)}, u32[]{:S(2)}, u32[]{:S(2)}) collective-permute-start(bf16[2,64,1024]{2,1,0:T(8,128)(2,1)} %pad_maximum_fusion.2), channel_id=1, source_target_pairs={{0,1},{1,0},{2,3},{3,2},{4,5},{5,4},{6,7},{7,6},{8,9},{9,8},{10,11... | collective-permute-start | bytes 786440 | tf_op jit(solution)/shard_map/cond/branch_1_fun/ppermute | solution.py:41
  67.6 1.8 collective-permute-start.20
  68.9 4.4 %collective-permute-start.21 = (bf16[8,32,1024]{2,1,0:T(8,128)(2,1)}, bf16[8,32,1024]{2,1,0:T(8,128)(2,1)}, u32[]{:S(2)}, u32[]{:S(2)}) collective-permute-start(bf16[8,32,1024]{2,1,0:T(8,128)(2,1)} %fusion.1), channel_id=1, source_target_pairs={{0,2},{2,0},{1,3},{3,1},{4,6},{6,4},{5,7},{7,5},{8,10},{10,8},{9,1... | collective-permute-start | bytes 1572872 | tf_op jit(solution)/shard_map/cond/branch_1_fun/ppermute | solution.py:41
  73.4 47.3 %copy-start.10 = (s32[8,128]{1,0:T(8,128)}, s32[8,128]{1,0:T(8,128)S(1)}, u32[]{:S(2)}) copy-start(s32[8,128]{1,0:T(8,128)S(1)} %get-tuple-element.573) | copy-start | bytes 12292
  77.1 1.9 collective-permute-start
  99.4 11.8 %copy-start.28 = (bf16[128,1024]{1,0:T(8,128)(2,1)S(1)}, bf16[128,1024]{1,0:T(8,128)(2,1)}, u32[]{:S(2)}) copy-start(bf16[128,1024]{1,0:T(8,128)(2,1)} %tokens.5) | copy-start | bytes 786436
  99.4 11.8 %copy-start.40 = (f32[1024]{0:T(1024)S(1)}, f32[1024]{0:T(1024)}, u32[]{:S(2)}) copy-start(f32[1024]{0:T(1024)} %param.51) | copy-start | bytes 12292
  102.6 7.9 %collective-permute-start.1 = (bf16[128,1024]{1,0:T(8,128)(2,1)}, bf16[128,1024]{1,0:T(8,128)(2,1)}, u32[]{:S(2)}, u32[]{:S(2)}) collective-permute-start(bf16[128,1024]{1,0:T(8,128)(2,1)} %get-tuple-element.749), channel_id=1, source_target_pairs={{0,1},{1,0},{2,3},{3,2},{4,5},{5,4},{6,7},{7,6},{8,9},{9,8},{10,11... | collective-permute-start | bytes 786440 | tf_op jit(solution)/shard_map/cond/branch_1_fun/ppermute | solution.py:41
  110.5 109.5 %all-gather.10.cloned.1.call-start = ((), (), s32[]{:S(2)}) async-start(), calls=%async_computation.7 | async-start | bytes 1114112 | tf_op jit(solution)/shard_map/all_gather | solution.py:1120
  118.4 15.2 %collective-permute-start.32 = (bf16[288,1024]{1,0:T(8,128)(2,1)}, bf16[288,1024]{1,0:T(8,128)(2,1)}, u32[]{:S(2)}, u32[]{:S(2)}) collective-permute-start(bf16[288,1024]{1,0:T(8,128)(2,1)} %get-tuple-element.589), channel_id=1, source_target_pairs={{0,2},{2,0},{1,3},{3,1},{4,6},{6,4},{5,7},{7,5},{8,10},{10,8},{9,1... | collective-permute-start | bytes 1769480 | tf_op jit(solution)/shard_map/ppermute | solution.py:41
  118.7 44.9 %collective-permute-start.33 = (bf16[288,1024]{1,0:T(8,128)(2,1)}, bf16[288,1024]{1,0:T(8,128)(2,1)}, u32[]{:S(2)}, u32[]{:S(2)}) collective-permute-start(bf16[288,1024]{1,0:T(8,128)(2,1)} %get-tuple-element.602), channel_id=1, source_target_pairs={{0,4},{4,0},{1,5},{5,1},{2,6},{6,2},{3,7},{7,3},{8,12},{12,8},{9,1... | collective-permute-start | bytes 1769480 | tf_op jit(solution)/shard_map/ppermute | solution.py:41
  120.7 8.5 %collective-permute-start.2 = (bf16[128,1024]{1,0:T(8,128)(2,1)}, bf16[128,1024]{1,0:T(8,128)(2,1)S(1)}, u32[]{:S(2)}, u32[]{:S(2)}) collective-permute-start(bf16[128,1024]{1,0:T(8,128)(2,1)} %get-tuple-element.314.own), channel_id=1, source_target_pairs={{0,1},{1,0},{2,3},{3,2},{4,5},{5,4},{6,7},{7,6},{8,9},{9,8},{10,11... | collective-permute-start | bytes 786440 | tf_op jit(solution)/shard_map/cond/branch_1_fun/ppermute | solution.py:41
  133.5 1.9 collective-permute-start.22
  133.6 5.0 %collective-permute-start.23 = (f32[4,4096]{1,0:T(4,128)S(1)}, f32[4,4096]{1,0:T(4,128)S(1)}, u32[]{:S(2)}, u32[]{:S(2)}) collective-permute-start(f32[4,4096]{1,0:T(4,128)S(1)} %get-tuple-element.323), channel_id=1, source_target_pairs={{0,4},{2,6},{4,0},{6,2},{1,5},{3,7},{5,1},{7,3},{8,12},{10,14},{12... | collective-permute-start | bytes 196616 | tf_op jit(solution)/shard_map/cond/branch_1_fun/ppermute | solution.py:37
  134.0 5.1 %collective-permute-start.24 = (f32[4,4096]{1,0:T(4,128)S(1)}, f32[4,4096]{1,0:T(4,128)S(1)}, u32[]{:S(2)}, u32[]{:S(2)}) collective-permute-start(f32[4,4096]{1,0:T(4,128)S(1)} %get-tuple-element.323), channel_id=1, source_target_pairs={{0,6},{2,4},{4,2},{6,0},{1,7},{3,5},{5,3},{7,1},{8,14},{10,12},{12... | collective-permute-start | bytes 196616 | tf_op jit(solution)/shard_map/cond/branch_1_fun/ppermute | solution.py:37
  139.2 12.7 %copy-start.6 = (f32[4,4096]{1,0:T(4,128)}, f32[4,4096]{1,0:T(4,128)S(1)}, u32[]{:S(2)}) copy-start(f32[4,4096]{1,0:T(4,128)S(1)} %add_add_fusion.t0) | copy-start | bytes 196612 | tf_op jit(solution)/shard_map/cond
  139.2 7.2 %collective-permute-start.25 = (f32[4,4096]{1,0:T(4,128)S(1)}, f32[4,4096]{1,0:T(4,128)S(1)}, u32[]{:S(2)}, u32[]{:S(2)}) collective-permute-start(f32[4,4096]{1,0:T(4,128)S(1)} %add_add_fusion.t0), channel_id=1, source_target_pairs={{0,8},{8,0},{16,24},{24,16},{1,9},{9,1},{17,25},{25,17},{2,10},{10... | collective-permute-start | bytes 196616 | tf_op jit(solution)/shard_map/cond/branch_1_fun/ppermute | solution.py:33
  140.2 11.6 %collective-permute-start.26 = (f32[4,4096]{1,0:T(4,128)S(1)}, f32[4,4096]{1,0:T(4,128)S(1)}, u32[]{:S(2)}, u32[]{:S(2)}) collective-permute-start(f32[4,4096]{1,0:T(4,128)S(1)} %add_add_fusion.t0), channel_id=1, source_target_pairs={{0,16},{8,24},{16,0},{24,8},{1,17},{9,25},{17,1},{25,9},{2,18},{10... | collective-permute-start | bytes 196616 | tf_op jit(solution)/shard_map/cond/branch_1_fun/ppermute | solution.py:33
  142.1 9.7 %collective-permute-start.27 = (f32[4,4096]{1,0:T(4,128)S(1)}, f32[4,4096]{1,0:T(4,128)S(1)}, u32[]{:S(2)}, u32[]{:S(2)}) collective-permute-start(f32[4,4096]{1,0:T(4,128)S(1)} %add_add_fusion.t0), channel_id=1, source_target_pairs={{0,24},{8,16},{16,8},{24,0},{1,25},{9,17},{17,9},{25,1},{2,26},{10... | collective-permute-start | bytes 196616 | tf_op jit(solution)/shard_map/cond/branch_1_fun/ppermute | solution.py:33
  163.7 126.2 %all-gather.12.cloned.1.call-start = ((), (), s32[]{:S(2)}) async-start(), calls=%async_computation.8 | async-start | bytes 1462272 | tf_op jit(solution)/shard_map/all_gather | solution.py:1268
  163.7 15.3 %collective-permute-start.34 = (bf16[256,1024]{1,0:T(8,128)(2,1)}, bf16[256,1024]{1,0:T(8,128)(2,1)S(1)}, u32[]{:S(2)}, u32[]{:S(2)}) collective-permute-start(bf16[256,1024]{1,0:T(8,128)(2,1)} %get-tuple-element.612), channel_id=1, source_target_pairs={{0,4},{4,0},{1,5},{5,1},{2,6},{6,2},{3,7},{7,3},{8,12},{12,8},{9,1... | collective-permute-start | bytes 1572872 | tf_op jit(solution)/shard_map/ppermute | solution.py:41
  165.1 13.9 %collective-permute-start.35 = (bf16[256,1024]{1,0:T(8,128)(2,1)}, bf16[256,1024]{1,0:T(8,128)(2,1)S(1)}, u32[]{:S(2)}, u32[]{:S(2)}) collective-permute-start(bf16[256,1024]{1,0:T(8,128)(2,1)} %get-tuple-element.614), channel_id=1, source_target_pairs={{0,2},{2,0},{1,3},{3,1},{4,6},{6,4},{5,7},{7,5},{8,10},{10,8},{9,1... | collective-permute-start | bytes 1572872 | tf_op jit(solution)/shard_map/ppermute | solution.py:41
  165.1 8.9 %collective-permute-start.3 = (bf16[128,1024]{1,0:T(8,128)(2,1)}, bf16[128,1024]{1,0:T(8,128)(2,1)S(1)}, u32[]{:S(2)}, u32[]{:S(2)}) collective-permute-start(bf16[128,1024]{1,0:T(8,128)(2,1)} %get-tuple-element.340.own), channel_id=1, source_target_pairs={{0,1},{1,0},{2,3},{3,2},{4,5},{5,4},{6,7},{7,6},{8,9},{9,8},{10,11... | collective-permute-start | bytes 786440 | tf_op jit(solution)/shard_map/cond/branch_1_fun/ppermute | solution.py:41
  166.5 1.6 collective-permute-start.4
  179.0 22.4 %copy-start.11 = (s32[8,128]{1,0:T(8,128)S(1)}, s32[8,128]{1,0:T(8,128)}, u32[]{:S(2)}) copy-start(s32[8,128]{1,0:T(8,128)} %copy-done.10) | copy-start | bytes 12292
  179.0 22.4 %copy-start.14 = (s32[8,128]{1,0:T(8,128)S(1)}, s32[8,128]{1,0:T(8,128)}, u32[]{:S(2)}) copy-start(s32[8,128]{1,0:T(8,128)} %copy-done.13) | copy-start | bytes 12292
  179.0 22.4 %copy-start.15 = (f32[4,1,1,256]{3,2,1,0:T(1,128)S(1)}, f32[4,1,1,256]{3,2,1,0:T(1,128)}, u32[]{:S(2)}) copy-start(f32[4,1,1,256]{3,2,1,0:T(1,128)} %get-tuple-element.617) | copy-start | bytes 12292
  179.1 22.4 %copy-start.42 = (s32[4]{0:T(128)S(1)}, s32[4]{0:T(128)}, u32[]{:S(2)}) copy-start(s32[4]{0:T(128)} %param.44) | copy-start | bytes 52
  179.1 9.0 %copy-start.22 = (bf16[256,1024]{1,0:T(8,128)(2,1)}, bf16[256,1024]{1,0:T(8,128)(2,1)S(1)}, u32[]{:S(2)}) copy-start(bf16[256,1024]{1,0:T(8,128)(2,1)S(1)} %get-tuple-element.356.g1) | copy-start | bytes 1572868 | tf_op jit(solution)/shard_map/cond
  179.1 9.0 %collective-permute-start.8 = (bf16[288,1024]{1,0:T(8,128)(2,1)}, bf16[288,1024]{1,0:T(8,128)(2,1)}, u32[]{:S(2)}, u32[]{:S(2)}) collective-permute-start(bf16[288,1024]{1,0:T(8,128)(2,1)} %get-tuple-element.351.f1), channel_id=1, source_target_pairs={{0,2},{2,0},{1,3},{3,1},{4,6},{6,4},{5,7},{7,5},{8,10},{10,8},{9,1... | collective-permute-start | bytes 1769480 | tf_op jit(solution)/shard_map/cond/branch_1_fun/ppermute | solution.py:41
  179.2 8.9 %collective-permute-start.9 = (bf16[256,1024]{1,0:T(8,128)(2,1)S(1)}, bf16[256,1024]{1,0:T(8,128)(2,1)S(1)}, u32[]{:S(2)}, u32[]{:S(2)}) collective-permute-start(bf16[256,1024]{1,0:T(8,128)(2,1)S(1)} %get-tuple-element.356.g1), channel_id=1, source_target_pairs={{0,2},{2,0},{1,3},{3,1},{4,6},{6,4},{5,7},{7,5},{8,10},{10,8},{9,1... | collective-permute-start | bytes 1572872 | tf_op jit(solution)/shard_map/cond/branch_1_fun/ppermute | solution.py:41
  179.7 8.4 %collective-permute-start.5 = (bf16[128,1024]{1,0:T(8,128)(2,1)S(1)}, bf16[128,1024]{1,0:T(8,128)(2,1)}, u32[]{:S(2)}, u32[]{:S(2)}) collective-permute-start(bf16[128,1024]{1,0:T(8,128)(2,1)S(1)} %get-tuple-element.350), channel_id=1, source_target_pairs={{0,4},{4,0},{1,5},{5,1},{2,6},{6,2},{3,7},{7,3},{8,12},{12,8},{9,1... | collective-permute-start | bytes 786440 | tf_op jit(solution)/shard_map/cond/branch_1_fun/ppermute | solution.py:41
  180.8 13.4 %collective-permute-start.6 = (bf16[128,1024]{1,0:T(8,128)(2,1)S(1)}, bf16[128,1024]{1,0:T(8,128)(2,1)}, u32[]{:S(2)}, u32[]{:S(2)}) collective-permute-start(bf16[128,1024]{1,0:T(8,128)(2,1)S(1)} %get-tuple-element.350), channel_id=1, source_target_pairs={{0,2},{2,0},{1,3},{3,1},{4,6},{6,4},{5,7},{7,5},{8,10},{10,8},{9,1... | collective-permute-start | bytes 786440 | tf_op jit(solution)/shard_map/cond/branch_1_fun/ppermute | solution.py:41
  180.8 18.7 %all-to-all-start.1 = ((bf16[8,144,128]{2,1,0:T(8,128)(2,1)}), bf16[8,144,128]{2,1,0:T(8,128)(2,1)}, u32[]{:S(2)}, u32[]{:S(2)}) async-start(bf16[8,144,128]{2,1,0:T(8,128)(2,1)} %get-tuple-element.349), calls=%async_computation.1 | async-start | bytes 589824 | tf_op jit(solution)/shard_map/cond/branch_1_fun/all_to_all | solution.py:1019
  188.1 11.3 %collective-permute-start.7 = (bf16[128,1024]{1,0:T(8,128)(2,1)}, bf16[128,1024]{1,0:T(8,128)(2,1)}, u32[]{:S(2)}, u32[]{:S(2)}) collective-permute-start(bf16[128,1024]{1,0:T(8,128)(2,1)} %collective-permute-done.5), channel_id=1, source_target_pairs={{0,2},{2,0},{1,3},{3,1},{4,6},{6,4},{5,7},{7,5},{8,10},{10,8},{9,1... | collective-permute-start | bytes 786440 | tf_op jit(solution)/shard_map/cond/branch_1_fun/ppermute | solution.py:41
  199.4 18.1 %collective-permute-start.36 = (bf16[2,2,64,1024]{3,2,1,0:T(8,128)(2,1)S(1)}, bf16[2,2,64,1024]{3,2,1,0:T(8,128)(2,1)}, u32[]{:S(2)}, u32[]{:S(2)}) collective-permute-start(bf16[2,2,64,1024]{3,2,1,0:T(8,128)(2,1)S(1)} %get-tuple-element.620), channel_id=1, source_target_pairs={{0,8},{8,0},{16,24},{24,16},{1,9},{9,1},{17,25},{25,17},{2,10},{10... | collective-permute-start | bytes 1572872 | tf_op jit(solution)/shard_map/ppermute | solution.py:33
  201.0 42.2 %collective-permute-start.38 = (bf16[2,2,64,1024]{3,2,1,0:T(8,128)(2,1)S(1)}, bf16[2,2,64,1024]{3,2,1,0:T(8,128)(2,1)}, u32[]{:S(2)}, u32[]{:S(2)}) collective-permute-start(bf16[2,2,64,1024]{3,2,1,0:T(8,128)(2,1)S(1)} %get-tuple-element.638), channel_id=1, source_target_pairs={{0,8},{8,0},{16,24},{24,16},{1,9},{9,1},{17,25},{25,17},{2,10},{10... | collective-permute-start | bytes 1572872 | tf_op jit(solution)/shard_map/ppermute | solution.py:33
  201.7 12.7 %copy-start.20 = (s32[5]{0:T(128)S(1)}, s32[5]{0:T(128)}, u32[]{:S(2)}) copy-start(s32[5]{0:T(128)} %get-tuple-element.362.idx) | copy-start | bytes 64 | tf_op jit(solution)/shard_map/cond
  211.4 2.2 collective-permute-start.10
  219.6 23.7 %collective-permute-start.37 = (bf16[2,64,1024]{2,1,0:T(8,128)(2,1)}, bf16[2,64,1024]{2,1,0:T(8,128)(2,1)}, u32[]{:S(2)}, u32[]{:S(2)}) collective-permute-start(bf16[2,64,1024]{2,1,0:T(8,128)(2,1)} %get-tuple-element.637), channel_id=1, source_target_pairs={{0,16},{8,24},{16,0},{24,8},{1,17},{9,25},{17,1},{25,9},{2,18},{10... | collective-permute-start | bytes 786440 | tf_op jit(solution)/shard_map/ppermute | solution.py:33
  220.0 23.2 %all-to-all-start.2 = ((bf16[8,96,256]{2,1,0:T(8,128)(2,1)}), bf16[8,96,256]{2,1,0:T(8,128)(2,1)}, u32[]{:S(2)}, u32[]{:S(2)}) async-start(bf16[8,96,256]{2,1,0:T(8,128)(2,1)} %get-tuple-element.377), calls=%async_computation.2 | async-start | bytes 786432 | tf_op jit(solution)/shard_map/cond/branch_1_fun/all_to_all | solution.py:1019
  231.2 10.4 %collective-permute-start.11 = (bf16[2,2,64,256]{3,2,1,0:T(8,128)(2,1)}, bf16[2,2,64,256]{3,2,1,0:T(8,128)(2,1)}, u32[]{:S(2)}, u32[]{:S(2)}) collective-permute-start(bf16[2,2,64,256]{3,2,1,0:T(8,128)(2,1)} %get-tuple-element.400), channel_id=1, source_target_pairs={{0,8},{8,0},{16,24},{24,16},{1,9},{9,1},{17,25},{25,17},{2,10},{10... | collective-permute-start | bytes 393224 | tf_op jit(solution)/shard_map/cond/branch_1_fun/ppermute | solution.py:33
  245.5 22.1 %collective-permute-start.39 = (bf16[2,64,1280]{2,1,0:T(8,128)(2,1)}, bf16[2,64,1280]{2,1,0:T(8,128)(2,1)S(1)}, u32[]{:S(2)}, u32[]{:S(2)}) collective-permute-start(bf16[2,64,1280]{2,1,0:T(8,128)(2,1)} %get-tuple-element.658), channel_id=1, source_target_pairs={{0,16},{8,24},{16,0},{24,8},{1,17},{9,25},{17,1},{25,9},{2,18},{10... | collective-permute-start | bytes 983048 | tf_op jit(solution)/shard_map/ppermute | solution.py:33
  247.8 6.3 %collective-permute-start.12 = (bf16[8,64,256]{2,1,0:T(8,128)(2,1)S(1)}, bf16[8,64,256]{2,1,0:T(8,128)(2,1)S(1)}, u32[]{:S(2)}, u32[]{:S(2)}) collective-permute-start(bf16[8,64,256]{2,1,0:T(8,128)(2,1)S(1)} %get-tuple-element.411), channel_id=1, source_target_pairs={{0,2},{2,0},{1,3},{3,1},{4,6},{6,4},{5,7},{7,5},{8,10},{10,8},{9,1... | collective-permute-start | bytes 786440 | tf_op jit(solution)/shard_map/cond/branch_1_fun/ppermute | solution.py:41
  252.6 9.0 %collective-permute-start.13 = (bf16[128,1024]{1,0:T(8,128)(2,1)}, bf16[128,1024]{1,0:T(8,128)(2,1)S(1)}, u32[]{:S(2)}, u32[]{:S(2)}) collective-permute-start(bf16[128,1024]{1,0:T(8,128)(2,1)} %tokens.3.own), channel_id=1, source_target_pairs={{0,1},{1,0},{2,3},{3,2},{4,5},{5,4},{6,7},{7,6},{8,9},{9,8},{10,11... | collective-permute-start | bytes 786440 | tf_op jit(solution)/shard_map/cond/branch_1_fun/ppermute | solution.py:41
  263.4 15.0 %all-to-all-start.4 = ((bf16[8,64,256]{2,1,0:T(8,128)(2,1)}), bf16[8,64,256]{2,1,0:T(8,128)(2,1)S(1)}, u32[]{:S(2)}, u32[]{:S(2)}) async-start(bf16[8,64,256]{2,1,0:T(8,128)(2,1)} %get-tuple-element.666), calls=%async_computation.4 | async-start | bytes 524288 | tf_op jit(solution)/shard_map/all_to_all | solution.py:1294
  270.8 13.4 %collective-permute-start.40 = (bf16[64,2304]{1,0:T(8,128)(2,1)}, bf16[64,2304]{1,0:T(8,128)(2,1)S(1)}, u32[]{:S(2)}, u32[]{:S(2)}) collective-permute-start(bf16[64,2304]{1,0:T(8,128)(2,1)} %get-tuple-element.661), channel_id=1, source_target_pairs={{0,4},{4,0},{1,5},{5,1},{2,6},{6,2},{3,7},{7,3},{8,12},{12,8},{9,1... | collective-permute-start | bytes 884744 | tf_op jit(solution)/shard_map/ppermute | solution.py:41
  (28 other events, 87.6 us)
Sparse Core Ops, SparseCore 0:
  32.0 79.1 all-gather.5
  113.5 50.1 all-gather.7
  165.8 39.0 all-gather.9
  245.6 44.2 all-gather.11

commit v5 on v4

--- a/solution.py
+++ b/solution.py
@@ -500,7 +500,7 @@
     unit[...] = (embed[...] * unit_scale(embed[...])).astype(LOW)
     message[...] = unit[...].astype(WIDE)
     expo[...] = jnp.exp(dot_nt(unit[...], query[...]) / SOFTMAX_TEMPER)
-    totals[...] = dot_nn(member(idx, kdoc, totals.shape[0]), expo[...], PRECISE)
+    totals[...] = dot_nn(member(idx, kdoc, totals.shape[0]), expo[...], PRECISE).astype(LOW)
 
 
 def query_kernel(idx, vecs, out, own):
@@ -631,7 +631,7 @@
     copy1 = [slab_copy(slabs, 0, expand, sems1)]
     copy2 = [slab_copy(slabs, expand.shape[1], contract, sems2)]
     start(copy2 + copy1)
-    totals = (t0[...] + t1[...]) + (t2[...] + t3[...])
+    totals = pair(t0, t1) + pair(t2, t3)
     value, coefficient = loss_of(count, totals, (kdoc0, kdoc1), positive[...])
     loss[...] = jnp.broadcast_to(value, loss.shape)
     coefficients[...] = coefficient
@@ -1076,7 +1076,7 @@
                 line(second_shift), head_weight, query_unit, kdoc0,
             ),
             [low_rows, wide_rows, thin_rows] + [shape((rows, proj), t) for t in (WIDE, LOW)]
-            + [shape((rows, my_tokens), WIDE), shape((docs, my_tokens), WIDE)]
+            + [shape((rows, my_tokens), WIDE), shape((docs, my_tokens), LOW)]
             + [shape((rows, proj), WIDE)],
         )
 
@@ -1084,7 +1084,8 @@
     totals = after(totals, first_across)
 
     def tree(own, one, two, three):
-        return (own + one) + (two + three)
+        one, two, three = [part.astype(WIDE) for part in (one, two, three)]
+        return ((own.astype(WIDE) + one) + (two + three)).astype(LOW)
 
     chunk = width // (NZ * 4)
     sums_dims = (NZ * 2, chunk + 16, proj)
@@ -1116,7 +1117,7 @@
 
     grad_second_in, keep, send, part, loss, coefficients, sums_own, sums_send = stage(middle_stage)
 
-    triple_low, part, first_other = lax.optimization_barrier((triple_low, part, first_other))
+    part, first_other = lax.optimization_barrier((part, first_other))
     units = lax.all_gather(after(message, part), BLK, axis=0, tiled=True)
     keep_other, keep_across = flip(send, "x"), flip(keep, "c")
 
@@ -1136,7 +1137,7 @@
         )
 
     grad_first_in, grad_branch, vectors1, pack = stage(first_stage)
-    keep_other = after(keep_other, grad_branch)
+    keep_other, triple_low, grad_branch = lax.optimization_barrier((keep_other, triple_low, grad_branch))
     dims, dims_out = (2, slab, quarter), (2, slab, QUAD)
     dims_both = (2, slab, quarter + QUAD)
     left_right = [pltpu.VMEM((4 * rows, width), LOW)]

time: 301 us -> 292 us (0.970)
  starting transfers between devices: 64.2 us -> 58.9 us
  waiting for transfers between devices: 90.9 us -> 87.1 us
    ppermute x11, waiting for transfers between devices: 26.4 us -> 21.7 us  [xor_z(): return lax.ppermute(value, 'z', [(i, i ^ mask) for i in FOUR])]
    all_to_all x2, starting transfers between devices: 12.8 us -> 9.44 us  [to_blocks(): lax.all_to_all(value.reshape((NZ * 2,) + value.shape[-2:]), ('z', 'x'), 0...]
  transfers between devices with their start and end apart: 49 -> 49, of which waited for: 25 -> 24; matrix products, arithmetic and copies ran while one was open for 5% -> 5% of each run, Pallas kernels for 28% -> 29%
where the time goes in v5:
time: 292 us; the launch traced here: 291 us
  Pallas kernels  93.4 us (32%)
  waiting for transfers between devices  87.1 us (30%)
  starting transfers between devices  58.9 us (20%)
  local copies, waits for them, and re-layouts  15.6 us (5%)
  between operations  14.1 us (5%)
  blocking collectives  13.5 us (5%)
  other arithmetic  7.33 us (3%)
    pallas_call x23, Pallas kernels, whole(): pl.pallas_call(kernel, in_specs=[pl.BlockSpec(memory_space=pltpu.SMEM)] +...  77.2 us
    ppermute x27, waiting for transfers between devices, flip(): return lax.ppermute(value, axis, [(0, 1), (1, 0)])  45.9 us
    ppermute x27, starting transfers between devices, flip(): return lax.ppermute(value, axis, [(0, 1), (1, 0)])  22.5 us
    ppermute x11, waiting for transfers between devices, xor_z(): return lax.ppermute(value, 'z', [(i, i ^ mask) for i in FOUR])  21.7 us
    ppermute x11, starting transfers between devices, xor_z(): return lax.ppermute(value, 'z', [(i, i ^ mask) for i in FOUR])  14.4 us
    all_to_all x1, blocking collectives, to_blocks(): lax.all_to_all(value.reshape((NZ * 2,) + value.shape[-2:]), ('z', 'x'), 0...  13.5 us
    cond x51, local copies, waits for them, and re-layouts  11.2 us
    pallas_call x1, Pallas kernels, attend_back(): pl.pallas_call(partial(attend_back_kernel, blocks), grid=grid, in_specs=S...  9.66 us
  transfers between devices with their start and end apart: 49, of which 24 were waited for; matrix products, arithmetic and copies ran while one was open for 5% of the time, Pallas kernels for 29%

profile of v5, /device:TPU:0, one launch (start us, length us, event | category | flops | bytes accessed | tf_op | source)
XLA Modules:
  0.0 290.7 jit_solution(431553668764937224)
XLA Ops:
  7.3 2.7 prep.1
  10.0 2.9 %collective-permute-start.28 = (bf16[160,1024]{1,0:T(8,128)(2,1)S(1)}, bf16[160,1024]{1,0:T(8,128)(2,1)S(1)}, u32[]{:S(2)}, u32[]{:S(2)}) collective-permute-start(bf16[160,1024]{1,0:T(8,128)(2,1)S(1)} %get-tuple-element.556), channel_id=1, source_target_pairs={{0,4},{4,0},{1,5},{5,1},{2,6},{6,2},{3,7},{7,3},{8,12},{12,8},{9,1... | collective-permute-start | bytes 983048 | tf_op jit(solution)/shard_map/ppermute | solution.py:41
  14.5 2.6 collective-permute-start.30
  17.3 5.3 %collective-permute-done.29 = bf16[96,1024]{1,0:T(8,128)(2,1)S(1)} collective-permute-done((bf16[96,1024]{1,0:T(8,128)(2,1)}, bf16[96,1024]{1,0:T(8,128)(2,1)S(1)}, u32[]{:S(2)}, u32[]{:S(2)}) %collective-permute-start.29) | collective-permute-done | bytes 196640 | tf_op jit(solution)/shard_map/ppermute | solution.py:33
  22.7 9.2 %collective-permute-done.30 = bf16[96,1024]{1,0:T(8,128)(2,1)S(1)} collective-permute-done((bf16[96,1024]{1,0:T(8,128)(2,1)}, bf16[96,1024]{1,0:T(8,128)(2,1)S(1)}, u32[]{:S(2)}, u32[]{:S(2)}) %collective-permute-start.30) | collective-permute-done | bytes 196640 | tf_op jit(solution)/shard_map/ppermute | solution.py:33
  32.1 41.7 %conditional.11 = (bf16[1024,256]{1,0:T(8,128)(2,1)S(1)}, s32[8,128]{1,0:T(8,128)S(1)}, s32[8,128]{1,0:T(8,128)S(1)}, bf16[8,32,1024]{2,1,0:T(8,128)(2,1)}, bf16...) conditional(s32[]{:T(128)} %bitcast.27, () %tuple.119, ...), branch_computations={%region_0.0_spmd, %region_1.6_spmd} | conditional | flops 5520703488 | bytes 35979452 | solution.py:910
  34.8 6.2 %all-to-all-start.3 = ((bf16[8,64,256]{2,1,0:T(8,128)(2,1)}), bf16[8,64,256]{2,1,0:T(8,128)(2,1)S(1)}, u32[]{:S(2)}, u32[]{:S(2)}) async-start(bf16[8,64,256]{2,1,0:T(8,128)(2,1)} %get-tuple-element.262), calls=%async_computation.3 | async-start | bytes 524288 | tf_op jit(solution)/shard_map/cond/branch_1_fun/all_to_all | solution.py:962
  43.2 2.4 query_units.1
  46.5 3.0 %fusion = (f32[1024,128]{1,0:T(8,128)}, f32[1024,128]{1,0:T(8,128)}) fusion(f32[128]{0:T(128)S(1)} %get-tuple-element.701, f32[128]{0:T(128)S(1)} %get-tuple-element.702, f32[1024]{0:T(1024)S(1)} %subtract_convert_fusion), kind=kLoop, calls=%fused_computation.2 | loop fusion | flops 262144 | bytes 1053696 | tf_op jit(solution)/shard_map/cond/branch_1_fun/mul | solution.py:981
  57.8 2.6 collective-permute-done.15
  60.5 4.9 %collective-permute-done.17 = bf16[2,64,1024]{2,1,0:T(8,128)(2,1)} collective-permute-done((bf16[2,64,1024]{2,1,0:T(8,128)(2,1)}, bf16[2,64,1024]{2,1,0:T(8,128)(2,1)}, u32[]{:S(2)}, u32[]{:S(2)}) %collective-permute-start.17) | collective-permute-done | bytes 262176 | tf_op jit(solution)/shard_map/cond/branch_1_fun/ppermute | solution.py:41
  65.3 2.8 collective-permute-done.19
  73.8 5.6 %conditional.12 = (bf16[1024,128]{1,0:T(8,128)(2,1)}, bf16[1024,128]{1,0:T(8,128)(2,1)}, bf16[1024,128]{1,0:T(8,128)(2,1)}) conditional(s32[]{:T(128)} %bitcast.27, () %tuple.118, (s32[5]{0:T(128)S(1)}, bf16[128,1024]{1,0:T(8,128)(2,1)}, bf16[160,1024]{1,0:T(8,128)(2,1)S(1)}, bf16[2,64,1024]{2,1,0:T(8,128)(2,1)}, bf16[2,64,1024]{2,1,0:T(8,128)(2,1)}, ...), branch_computations={%region_6.7_spmd, %region_7.8_spmd} | conditional | flops 4369999872 | bytes 15108640 | solution.py:910
  73.8 3.7 %project.1 = (bf16[1024,128]{1,0:T(8,128)(2,1)}, bf16[1024,128]{1,0:T(8,128)(2,1)}) custom-call(s32[5]{0:T(128)S(1)} %get-tuple-element.282.idx, bf16[128,1024]{1,0:T(8,128)(2,1)} %get-tuple-element.283.refs_0_, bf16[160,1024]{1,0:T(8,128)(2,1)S(1)} %get-tuple-element.284.refs_1_, bf16[2,64,1024]{2,1,0:T(8,128)(2,1)} %get-tuple-element.285.refs_2_, ...), custom_call_target="tpu_custom_call" | custom-call | flops 4369999872 | bytes 14060000 | tf_op jit(solution)/shard_map/cond/branch_1_fun/project/pallas_call | solution.py:115
  77.6 1.8 collective-permute-done
  79.4 20.0 %conditional.13 = (f32[4,2,2,64,128]{4,3,2,1,0:T(8,128)}, f32[4,1,1,256]{3,2,1,0:T(1,128)}, bf16[8,64,128]{2,1,0:T(8,128)(2,1)S(1)}) conditional(s32[]{:T(128)} %bitcast.27, () %tuple.117, (bf16[1024,128]{1,0:T(8,128)(2,1)}, s32[5]{0:T(128)S(1)}, s32[4]{0:T(128)S(1)}, bf16[1024,128]{1,0:T(8,128)(2,1)}, bf16[1024,128]{1,0:T(8,128)(2,1)}, ...), branch_computations={%region_8.9_spmd, %region_9.10_spmd} | conditional | flops 8625000448 | bytes 28012168 | solution.py:910
  79.4 6.5 %attend.1 = (f32[4,2,2,64,128]{4,3,2,1,0:T(8,128)}, f32[4,1,1,256]{3,2,1,0:T(1,128)}, bf16[4,2,64,128]{3,2,1,0:T(8,128)(2,1)}) custom-call(s32[5]{0:T(128)S(1)} %get-tuple-element.297.idx, s32[4]{0:T(128)S(1)} %get-tuple-element.298.lens, bf16[4,2,2,64,128]{4,3,2,1,0:T(8,128)(2,1)} %bitcast.17.q_ref, bf16[1024,128]{1,0:T(8,128)(2,1)} %get-tuple-element.300.kv0_ref, ...), custom_call_target="tpu_custom_call" | custom-call | flops 8625000448 | bytes 27750000 | tf_op jit(solution)/shard_map/cond/branch_1_fun/attend/pallas_call | solution.py:353
  86.0 13.5 %all_to_all.21 = bf16[8,64,128]{2,1,0:T(8,128)(2,1)S(1)} all-to-all(bf16[8,64,128]{2,1,0:T(8,128)(2,1)} %bitcast.77), channel_id=1, replica_groups=mesh['o'=1,'z'=4,'x'=2,'c'=2,'y'=2] {'z','x'}, dimensions={0} | all-to-all | bytes 262144 | tf_op jit(solution)/shard_map/cond/branch_1_fun/all_to_all | solution.py:1019
  99.4 10.7 %conditional.14 = (bf16[128,512]{1,0:T(8,128)(2,1)S(1)}, bf16[128,1024]{1,0:T(8,128)(2,1)}, bf16[128,1024]{1,0:T(8,128)(2,1)}) conditional(s32[]{:T(128)} %bitcast.27, () %tuple.116, (s32[5]{0:T(128)S(1)}, bf16[8,64,128]{2,1,0:T(8,128)(2,1)S(1)}, bf16[8,32,1024]{2,1,0:T(8,128)(2,1)}, bf16[8,32,1024]{2,1,0:T(8,128)(2,1)}) %tuple.124), branch_computations={%region_10.11_spmd, %region_11.12_spmd} | conditional | flops 4024999936 | bytes 13998640 | solution.py:910
  99.4 3.2 %branch.1 = (bf16[128,512]{1,0:T(8,128)(2,1)S(1)}, bf16[128,1024]{1,0:T(8,128)(2,1)}) custom-call(s32[5]{0:T(128)S(1)} %get-tuple-element.307.idx, bf16[8,64,128]{2,1,0:T(8,128)(2,1)S(1)} %get-tuple-element.308.got, bf16[8,32,1024]{2,1,0:T(8,128)(2,1)} %get-tuple-element.309.refs_0_, bf16[8,32,1024]{2,1,0:T(8,128)(2,1)} %get-tuple-element.310.refs_1_), custom_call_target="tpu_custom_call" | custom-call | flops 4024999936 | bytes 12950000 | tf_op jit(solution)/shard_map/cond/branch_1_fun/branch/pallas_call | solution.py:115
  104.2 5.9 %collective-permute-done.1 = bf16[128,1024]{1,0:T(8,128)(2,1)} collective-permute-done((bf16[128,1024]{1,0:T(8,128)(2,1)}, bf16[128,1024]{1,0:T(8,128)(2,1)}, u32[]{:S(2)}, u32[]{:S(2)}) %collective-permute-start.1) | collective-permute-done | bytes 262176 | tf_op jit(solution)/shard_map/cond/branch_1_fun/ppermute | solution.py:41
  111.8 7.2 %forward.1 = (f32[128,1024]{1,0:T(8,128)}, f32[128,1024]{1,0:T(8,128)}, f32[128,1]{1,0:T(8,128)}, f32[128,2048]{1,0:T(8,128)}, bf16[288,1024]{1,0:T(8,128)(2,1)}...) custom-call(s32[5]{0:T(128)S(1)} %stack.74.idx, bf16[128,1024]{1,0:T(8,128)(2,1)} %get-tuple-element.579.own, ...), custom_call_target="tpu_custom_call" | custom-call | flops 8855000064 | bytes 28490000 | tf_op jit(solution)/shard_map/forward/pallas_call | solution.py:115
  120.7 13.0 %conditional.15 = ((bf16[128,1024]{1,0:T(8,128)(2,1)}, f32[128,1024]{1,0:T(8,128)}, f32[128,1]{1,0:T(8,128)}, f32[128,128]{1,0:T(8,128)}, bf16[128,128]{1,0:T(8,...) conditional(s32[]{:T(128)} %bitcast.27, () %tuple.115, ...), branch_computations={%region_12.13_spmd, %region_13.14_spmd} | conditional | flops 4140000000 | bytes 15433748 | solution.py:910
  122.3 6.9 %collective-permute-done.2.other = bf16[128,1024]{1,0:T(8,128)(2,1)S(1)} collective-permute-done((bf16[128,1024]{1,0:T(8,128)(2,1)}, bf16[128,1024]{1,0:T(8,128)(2,1)S(1)}, u32[]{:S(2)}, u32[]{:S(2)}) %collective-permute-start.2) | collective-permute-done | bytes 262176 | tf_op jit(solution)/shard_map/cond/branch_1_fun/ppermute | solution.py:41
  129.9 3.8 %second.1 = (bf16[128,1024]{1,0:T(8,128)(2,1)}, f32[128,1024]{1,0:T(8,128)}, f32[128,1]{1,0:T(8,128)}, f32[128,128]{1,0:T(8,128)}, bf16[128,128]{1,0:T(8,128)(2,...) custom-call(s32[5]{0:T(128)} %copy-done.20, ...), custom_call_target="tpu_custom_call" | custom-call | flops 4140000000 | bytes 13320000 | tf_op jit(solution)/shard_map/cond/branch_1_fun/second/pallas_call | solution.py:115
  133.7 24.3 %conditional.16 = ((f32[128,1024]{1,0:T(8,128)}, bf16[256,1024]{1,0:T(8,128)(2,1)}, bf16[256,1024]{1,0:T(8,128)(2,1)}, bf16[128,1024]{1,0:T(8,128)(2,1)}, f32[8,...) conditional(s32[]{:T(128)} %bitcast.27, () %tuple.128, ...), branch_computations={%region_14.15_spmd, %region_15.16_spmd} | conditional | flops 13800130560 | bytes 45874920 | solution.py:910
  135.8 2.4 collective-permute-done.23
  139.1 2.2 collective-permute-start.26
  142.9 4.0 %collective-permute-done.26.t2 = bf16[4,4096]{1,0:T(4,128)(2,1)S(1)} collective-permute-done((bf16[4,4096]{1,0:T(4,128)(2,1)S(1)}, bf16[4,4096]{1,0:T(4,128)(2,1)S(1)}, u32[]{:S(2)}, u32[]{:S(2)}) %collective-permute-start.26) | collective-permute-done | bytes 32800 | tf_op jit(solution)/shard_map/cond/branch_1_fun/ppermute | solution.py:33
  148.2 9.8 %middle.1 = (f32[128,1024]{1,0:T(8,128)}, bf16[256,1024]{1,0:T(8,128)(2,1)}, bf16[256,1024]{1,0:T(8,128)(2,1)}, bf16[128,1024]{1,0:T(8,128)(2,1)}, f32[8,128]{1,...) custom-call(s32[5]{0:T(128)} %get-tuple-element.322.idx, ...), custom_call_target="tpu_custom_call" | custom-call | flops 13799999488 | bytes 44400000 | tf_op jit(solution)/shard_map/cond/branch_1_fun/middle/pallas_call | solution.py:115
  159.8 13.9 %conditional.17 = ((f32[128,1024]{1,0:T(8,128)}, bf16[128,1024]{1,0:T(8,128)(2,1)S(1)}, f32[8,1024]{1,0:T(8,128)S(1)}, bf16[8,144,128]{2,1,0:T(8,128)(2,1)})) conditional(s32[]{:T(128)} %bitcast.27, () %tuple.135, (bf16[128,1024]{1,0:T(8,128)(2,1)}, f32[1024]{0:T(1024)}, bf16[8,80,128]{2,1,0:T(8,128)(2,1)}, s32[5]{0:T(128)}, ...), branch_computations={%region_16.17_spmd, %region_17.18_spmd} | conditional | flops 4369999872 | bytes 17468016 | solution.py:910
  162.9 5.8 %collective-permute-done.3.other = bf16[128,1024]{1,0:T(8,128)(2,1)S(1)} collective-permute-done((bf16[128,1024]{1,0:T(8,128)(2,1)}, bf16[128,1024]{1,0:T(8,128)(2,1)S(1)}, u32[]{:S(2)}, u32[]{:S(2)}) %collective-permute-start.3) | collective-permute-done | bytes 262176 | tf_op jit(solution)/shard_map/cond/branch_1_fun/ppermute | solution.py:41
  169.4 4.2 %first_back.1 = (f32[128,1024]{1,0:T(8,128)}, bf16[128,1024]{1,0:T(8,128)(2,1)S(1)}, f32[8,1024]{1,0:T(8,128)S(1)}, bf16[8,144,128]{2,1,0:T(8,128)(2,1)}) custom-call(s32[5]{0:T(128)} %get-tuple-element.339.idx, bf16[128,1024]{1,0:T(8,128)(2,1)} %get-tuple-element.340.own, bf16[128,1024]{1,0:T(8,128)(2,1)} %copy-done.32, ...), custom_call_target="tpu_custom_call" | custom-call | flops 4369999872 | bytes 14060000 | tf_op jit(solution)/shard_map/cond/branch_1_fun/first_back/pallas_call | solution.py:115
  173.7 17.9 %conditional.18 = (bf16[8,144,128]{2,1,0:T(8,128)(2,1)}, bf16[128,1024]{1,0:T(8,128)(2,1)}, bf16[128,1024]{1,0:T(8,128)(2,1)}, bf16[128,1024]{1,0:T(8,128)(2,1)}...) conditional(s32[]{:T(128)} %bitcast.27, () %tuple.134, ...), branch_computations={%region_18.19_spmd, %region_19.20_spmd} | conditional | flops 5980000256 | bytes 34018756 | solution.py:910
  174.8 4.9 %all-to-all-start.1 = ((bf16[8,144,128]{2,1,0:T(8,128)(2,1)}), bf16[8,144,128]{2,1,0:T(8,128)(2,1)}, u32[]{:S(2)}, u32[]{:S(2)}) async-start(bf16[8,144,128]{2,1,0:T(8,128)(2,1)} %get-tuple-element.349), calls=%async_computation.1 | async-start | bytes 589824 | tf_op jit(solution)/shard_map/cond/branch_1_fun/all_to_all | solution.py:1019
  179.8 3.0 %collective-permute-done.5 = bf16[128,1024]{1,0:T(8,128)(2,1)} collective-permute-done((bf16[128,1024]{1,0:T(8,128)(2,1)S(1)}, bf16[128,1024]{1,0:T(8,128)(2,1)}, u32[]{:S(2)}, u32[]{:S(2)}) %collective-permute-start.5) | collective-permute-done | bytes 262176 | tf_op jit(solution)/shard_map/cond/branch_1_fun/ppermute | solution.py:41
  183.6 5.3 %weights.1 = (f32[2,2,64,1024]{3,2,1,0:T(8,128)S(1)}, bf16[2,2,64,1024]{3,2,1,0:T(8,128)(2,1)S(1)}, f32[2,2,64,1024]{3,2,1,0:T(8,128)S(1)}, bf16[2,2,64,1024]{3,2,1,0:T(8,128)(2,1)S(1)}) custom-call(s32[5]{0:T(128)} %get-tuple-element.352.idx, bf16[288,1024]{1,0:T(8,128)(2,1)} %get-tuple-element.353.f0, bf16[288,1024]{1,0:T(8,128)(2,1)} %get-tuple-element.351.f1, ...), custom_call_target="tpu_custom_call" | custom-call | flops 5980000256 | bytes 19240000 | tf_op jit(solution)/shard_map/cond/branch_1_fun/weights/pallas_call | solution.py:115
  188.9 2.7 all-to-all-done.1
  193.6 16.0 %conditional.19 = ((bf16[1024,256]{1,0:T(8,128)(2,1)}, bf16[8,96,256]{2,1,0:T(8,128)(2,1)})) conditional(s32[]{:T(128)} %bitcast.27, () %tuple.133, (bf16[1024,128]{1,0:T(8,128)(2,1)}, bf16[8,144,128]{2,1,0:T(8,128)(2,1)}, s32[5]{0:T(128)}, s32[4]{0:T(128)S(1)}, f32[4,2,2,64,128]{4,3,2,1,0:T(8,128)}, /*index=5*/f32[4,1,1,256]{3,2,1,0:T(1,128)S(1)}, ...), branch_computations={%region_20.21_spmd, %region_21.22_spmd} | conditional | flops 14604999680 | bytes 51184488 | solution.py:910
  193.9 9.7 %attend_back.1 = (f32[4,2,2,64,128]{4,3,2,1,0:T(8,128)}, f32[1024,128]{1,0:T(8,128)}, f32[1024,128]{1,0:T(8,128)}) custom-call(s32[5]{0:T(128)} %get-tuple-element.362.idx, s32[4]{0:T(128)S(1)} %get-tuple-element.363.lens, bf16[4,2,2,64,128]{4,3,2,1,0:T(8,128)(2,1)} %bitcast.24.q_ref, bf16[4,2,144,128]{3,2,1,0:T(8,128)(2,1)} %bitcast.25.g_ref, ...), custom_call_target="tpu_custom_call" | custom-call | flops 11269999616 | bytes 36260000 | tf_op jit(solution)/shard_map/cond/branch_1_fun/attend_back/pallas_call | solution.py:414
  203.6 2.1 collective-permute-done.10.got
  206.6 3.1 %triple.1 = (bf16[1024,256]{1,0:T(8,128)(2,1)}, bf16[8,96,256]{2,1,0:T(8,128)(2,1)}) custom-call(s32[5]{0:T(128)S(1)} %copy-done.21, f32[1024,128]{1,0:T(8,128)} %bitcast.95, f32[1024,128]{1,0:T(8,128)} %get-tuple-element.373.dkv, f32[1024,128]{1,0:T(8,128)} %copy-done.26, f32[1024,128]{1,0:T(8,128)} %get-tuple-element.375.cosine, ...), custom_call_target="tpu_custom_call" | custom-call | flops 3335000064 | bytes 10730000 | tf_op jit(solution)/shard_map/cond/branch_1_fun/triple/pallas_call | solution.py:115
  209.7 2.1 pair.2
  212.4 23.0 %conditional.20 = (bf16[8,96,256]{2,1,0:T(8,128)(2,1)}, bf16[8,64,256]{2,1,0:T(8,128)(2,1)S(1)}, bf16[8,64,256]{2,1,0:T(8,128)(2,1)S(1)}, f32[2,2,64,256]{3,2,1,...) conditional(s32[]{:T(128)} %bitcast.27, () %tuple.132, ...), branch_computations={%region_22.23_spmd, %region_23.24_spmd} | conditional | flops 5175000064 | bytes 24907740 | solution.py:910
  212.4 4.5 %all-to-all-start.2 = ((bf16[8,96,256]{2,1,0:T(8,128)(2,1)}), bf16[8,96,256]{2,1,0:T(8,128)(2,1)}, u32[]{:S(2)}, u32[]{:S(2)}) async-start(bf16[8,96,256]{2,1,0:T(8,128)(2,1)} %get-tuple-element.377), calls=%async_computation.2 | async-start | bytes 786432 | tf_op jit(solution)/shard_map/cond/branch_1_fun/all_to_all | solution.py:1019
  216.9 3.9 %output.1 = (f32[2,2,64,256]{3,2,1,0:T(8,128)S(1)}, bf16[2,2,64,256]{3,2,1,0:T(8,128)(2,1)}) custom-call(s32[5]{0:T(128)S(1)} %get-tuple-element.378.idx, bf16[288,1024]{1,0:T(8,128)(2,1)} %get-tuple-element.391.f0, bf16[288,1024]{1,0:T(8,128)(2,1)} %get-tuple-element.392.f1, bf16[288,1024]{1,0:T(8,128)(2,1)} %get-tuple-element.393.f2, ...), custom_call_target="tpu_custom_call" | custom-call | flops 1724999936 | bytes 5550000 | tf_op jit(solution)/shard_map/cond/branch_1_fun/output/pallas_call | solution.py:115
  220.8 2.0 collective-permute-start.11
  222.9 2.4 triple_weight.1
  225.3 2.3 query_back.1
  227.6 2.5 collective-permute-done.11
  230.1 5.4 %all-to-all-done.2 = bf16[8,96,256]{2,1,0:T(8,128)(2,1)} async-done(((bf16[8,96,256]{2,1,0:T(8,128)(2,1)}), bf16[8,96,256]{2,1,0:T(8,128)(2,1)}, u32[]{:S(2)}, u32[]{:S(2)}) %all-to-all-start.2) | async-done | bytes 393248 | tf_op jit(solution)/shard_map/cond/branch_1_fun/all_to_all | solution.py:1019
  235.5 2.2 pair.3
  238.6 15.6 %conditional.21 = (f32[128,1024]{1,0:T(8,128)S(1)}, bf16[8,64,256]{2,1,0:T(8,128)(2,1)}) conditional(s32[]{:T(128)} %bitcast.27, () %tuple.131, (s32[5]{0:T(128)S(1)}, bf16[8,96,256]{2,1,0:T(8,128)(2,1)}, bf16[1024,1536]{1,0:T(8,128)(2,1)}, bf16[8,64,256]{2,1,0:T(8,128)(2,1)S(1)}, bf16[8,64,256]{2,1,0:T(8,128)(2,1)S(1)}, ...), branch_computations={%region_24.25_spmd, %region_25.26_spmd} | conditional | flops 7820000256 | bytes 29354456 | solution.py:910
  238.6 4.8 %tokens.3.own = bf16[128,1024]{1,0:T(8,128)(2,1)} custom-call(s32[5]{0:T(128)S(1)} %get-tuple-element.407.idx, bf16[8,96,256]{2,1,0:T(8,128)(2,1)} %get-tuple-element.408.got, bf16[1024,1536]{1,0:T(8,128)(2,1)} %get-tuple-element.409.message), custom_call_target="tpu_custom_call" | custom-call | flops 4485000192 | bytes 14430000 | tf_op jit(solution)/shard_map/cond/branch_1_fun/tokens/pallas_call | solution.py:115
  247.4 5.0 %collective-permute-done.13.other = bf16[128,1024]{1,0:T(8,128)(2,1)S(1)} collective-permute-done((bf16[128,1024]{1,0:T(8,128)(2,1)}, bf16[128,1024]{1,0:T(8,128)(2,1)S(1)}, u32[]{:S(2)}, u32[]{:S(2)}) %collective-permute-start.13) | collective-permute-done | bytes 262176 | tf_op jit(solution)/shard_map/cond/branch_1_fun/ppermute | solution.py:41
  254.2 4.3 %all-to-all-start.4 = ((bf16[8,64,256]{2,1,0:T(8,128)(2,1)}), bf16[8,64,256]{2,1,0:T(8,128)(2,1)S(1)}, u32[]{:S(2)}, u32[]{:S(2)}) async-start(bf16[8,64,256]{2,1,0:T(8,128)(2,1)} %get-tuple-element.668), calls=%async_computation.4 | async-start | bytes 524288 | tf_op jit(solution)/shard_map/all_to_all | solution.py:1295
  259.2 2.5 line_sum.1
  261.7 2.0 collective-permute-start.40
  265.0 3.9 %all-to-all-done.4.got = bf16[8,64,256]{2,1,0:T(8,128)(2,1)S(1)} async-done(((bf16[8,64,256]{2,1,0:T(8,128)(2,1)}), bf16[8,64,256]{2,1,0:T(8,128)(2,1)S(1)}, u32[]{:S(2)}, u32[]{:S(2)}) %all-to-all-start.4) | async-done | bytes 262176 | tf_op jit(solution)/shard_map/all_to_all | solution.py:1295
  269.6 1.9 triple_out.1
  271.5 3.7 %collective-permute-done.40.got = bf16[64,2304]{1,0:T(8,128)(2,1)S(1)} collective-permute-done((bf16[64,2304]{1,0:T(8,128)(2,1)}, bf16[64,2304]{1,0:T(8,128)(2,1)S(1)}, u32[]{:S(2)}, u32[]{:S(2)}) %collective-permute-start.40) | collective-permute-done | bytes 294944 | tf_op jit(solution)/shard_map/ppermute | solution.py:41
  275.9 2.2 columns.1
  278.1 3.2 %all-gather.12.cloned.1.call-done = bf16[5376,128]{1,0:T(8,128)(2,1)} async-done(((bf16[336,128]{1,0:T(8,128)(2,1)}), bf16[5376,128]{1,0:T(8,128)(2,1)}) %all-gather.12.cloned.1.call-update) | async-done | bytes 1376272 | tf_op jit(solution)/shard_map/all_gather | solution.py:1269
  281.3 2.9 spread.1
  (203 shorter events, 56.0 us)
Async XLA Ops:
  7.2 104.7 %all-gather.6.cloned.1.call-start = ((), (), s32[]{:S(2)}) async-start(), calls=%async_computation.5 | async-start | bytes 8912896 | tf_op jit(solution)/shard_map/all_gather | solution.py:959
  7.3 113.4 %copy-start.18 = (s32[5]{0:T(128)}, s32[5]{0:T(128)S(1)}, u32[]{:S(2)}) copy-start(s32[5]{0:T(128)S(1)} %stack.74.idx) | copy-start | bytes 64
  7.3 24.6 %copy-start.42 = (s32[4]{0:T(128)S(1)}, s32[4]{0:T(128)}, u32[]{:S(2)}) copy-start(s32[4]{0:T(128)} %param.44) | copy-start | bytes 52
  7.3 24.7 %copy-start.17 = (s32[128]{0:T(128)S(1)}, s32[128]{0:T(128)}, u32[]{:S(2)}) copy-start(s32[128]{0:T(128)} %param.46) | copy-start | bytes 1540
  10.0 21.9 %collective-permute-start.28 = (bf16[160,1024]{1,0:T(8,128)(2,1)S(1)}, bf16[160,1024]{1,0:T(8,128)(2,1)S(1)}, u32[]{:S(2)}, u32[]{:S(2)}) collective-permute-start(bf16[160,1024]{1,0:T(8,128)(2,1)S(1)} %get-tuple-element.556), channel_id=1, source_target_pairs={{0,4},{4,0},{1,5},{5,1},{2,6},{6,2},{3,7},{7,3},{8,12},{12,8},{9,1... | collective-permute-start | bytes 983048 | tf_op jit(solution)/shard_map/ppermute | solution.py:41
  12.9 9.7 %collective-permute-start.29 = (bf16[96,1024]{1,0:T(8,128)(2,1)}, bf16[96,1024]{1,0:T(8,128)(2,1)S(1)}, u32[]{:S(2)}, u32[]{:S(2)}) collective-permute-start(bf16[96,1024]{1,0:T(8,128)(2,1)} %get-tuple-element.558), channel_id=1, source_target_pairs={{0,8},{8,0},{16,24},{24,16},{1,9},{9,1},{17,25},{25,17},{2,10},{10... | collective-permute-start | bytes 589832 | tf_op jit(solution)/shard_map/ppermute | solution.py:33
  14.5 17.4 %collective-permute-start.30 = (bf16[96,1024]{1,0:T(8,128)(2,1)}, bf16[96,1024]{1,0:T(8,128)(2,1)S(1)}, u32[]{:S(2)}, u32[]{:S(2)}) collective-permute-start(bf16[96,1024]{1,0:T(8,128)(2,1)} %get-tuple-element.558), channel_id=1, source_target_pairs={{0,16},{8,24},{16,0},{24,8},{1,17},{9,25},{17,1},{25,9},{2,18},{10... | collective-permute-start | bytes 589832 | tf_op jit(solution)/shard_map/ppermute | solution.py:33
  17.1 14.8 %collective-permute-start.31 = (bf16[96,1024]{1,0:T(8,128)(2,1)}, bf16[96,1024]{1,0:T(8,128)(2,1)S(1)}, u32[]{:S(2)}, u32[]{:S(2)}) collective-permute-start(bf16[96,1024]{1,0:T(8,128)(2,1)} %get-tuple-element.558), channel_id=1, source_target_pairs={{0,24},{8,16},{16,8},{24,0},{1,25},{9,17},{17,9},{25,1},{2,26},{10... | collective-permute-start | bytes 589832 | tf_op jit(solution)/shard_map/ppermute | solution.py:33
  31.9 41.9 %copy-start.8 = (bf16[160,1024]{1,0:T(8,128)(2,1)}, bf16[160,1024]{1,0:T(8,128)(2,1)S(1)}, u32[]{:S(2)}) copy-start(bf16[160,1024]{1,0:T(8,128)(2,1)S(1)} %collective-permute-done.28) | copy-start | bytes 983044
  31.9 141.7 %all-gather.8.cloned.1.call-start = ((), (), s32[]{:S(2)}) async-start(), calls=%async_computation.6 | async-start | bytes 3342336 | tf_op jit(solution)/shard_map/all_gather | solution.py:1042
  32.1 41.7 %copy-start.40 = (f32[3,512]{1,0:T(4,128)S(1)}, f32[3,512]{1,0:T(4,128)}, u32[]{:S(2)}) copy-start(f32[3,512]{1,0:T(4,128)} %param.48) | copy-start | bytes 18436
  32.1 18.0 %collective-permute-start.14 = (bf16[96,1024]{1,0:T(8,128)(2,1)S(1)}, bf16[96,1024]{1,0:T(8,128)(2,1)S(1)}, u32[]{:S(2)}, u32[]{:S(2)}) collective-permute-start(bf16[96,1024]{1,0:T(8,128)(2,1)S(1)} %get-tuple-element.263), channel_id=1, source_target_pairs={{0,4},{4,0},{1,5},{5,1},{2,6},{6,2},{3,7},{7,3},{8,12},{12,8},{9,1... | collective-permute-start | bytes 589832 | tf_op jit(solution)/shard_map/cond/branch_1_fun/ppermute | solution.py:41
  32.8 19.6 %collective-permute-start.16 = (bf16[96,1024]{1,0:T(8,128)(2,1)S(1)}, bf16[96,1024]{1,0:T(8,128)(2,1)S(1)}, u32[]{:S(2)}, u32[]{:S(2)}) collective-permute-start(bf16[96,1024]{1,0:T(8,128)(2,1)S(1)} %get-tuple-element.264), channel_id=1, source_target_pairs={{0,4},{4,0},{1,5},{5,1},{2,6},{6,2},{3,7},{7,3},{8,12},{12,8},{9,1... | collective-permute-start | bytes 589832 | tf_op jit(solution)/shard_map/cond/branch_1_fun/ppermute | solution.py:41
  34.2 19.5 %collective-permute-start.18 = (bf16[96,1024]{1,0:T(8,128)(2,1)S(1)}, bf16[96,1024]{1,0:T(8,128)(2,1)S(1)}, u32[]{:S(2)}, u32[]{:S(2)}) collective-permute-start(bf16[96,1024]{1,0:T(8,128)(2,1)S(1)} %get-tuple-element.265), channel_id=1, source_target_pairs={{0,4},{4,0},{1,5},{5,1},{2,6},{6,2},{3,7},{7,3},{8,12},{12,8},{9,1... | collective-permute-start | bytes 589832 | tf_op jit(solution)/shard_map/cond/branch_1_fun/ppermute | solution.py:41
  34.8 33.3 %all-to-all-start.3 = ((bf16[8,64,256]{2,1,0:T(8,128)(2,1)}), bf16[8,64,256]{2,1,0:T(8,128)(2,1)S(1)}, u32[]{:S(2)}, u32[]{:S(2)}) async-start(bf16[8,64,256]{2,1,0:T(8,128)(2,1)} %get-tuple-element.262), calls=%async_computation.3 | async-start | bytes 524288 | tf_op jit(solution)/shard_map/cond/branch_1_fun/all_to_all | solution.py:962
  50.9 9.6 %collective-permute-start.15 = (bf16[2,64,1024]{2,1,0:T(8,128)(2,1)}, bf16[2,64,1024]{2,1,0:T(8,128)(2,1)}, u32[]{:S(2)}, u32[]{:S(2)}) collective-permute-start(bf16[2,64,1024]{2,1,0:T(8,128)(2,1)} %pad_maximum_fusion), channel_id=1, source_target_pairs={{0,1},{1,0},{2,3},{3,2},{4,5},{5,4},{6,7},{7,6},{8,9},{9,8},{10,11... | collective-permute-start | bytes 786440 | tf_op jit(solution)/shard_map/cond/branch_1_fun/ppermute | solution.py:41
  53.2 12.2 %collective-permute-start.17 = (bf16[2,64,1024]{2,1,0:T(8,128)(2,1)}, bf16[2,64,1024]{2,1,0:T(8,128)(2,1)}, u32[]{:S(2)}, u32[]{:S(2)}) collective-permute-start(bf16[2,64,1024]{2,1,0:T(8,128)(2,1)} %pad_maximum_fusion.1), channel_id=1, source_target_pairs={{0,1},{1,0},{2,3},{3,2},{4,5},{5,4},{6,7},{7,6},{8,9},{9,8},{10,11... | collective-permute-start | bytes 786440 | tf_op jit(solution)/shard_map/cond/branch_1_fun/ppermute | solution.py:41
  54.4 13.7 %collective-permute-start.19 = (bf16[2,64,1024]{2,1,0:T(8,128)(2,1)}, bf16[2,64,1024]{2,1,0:T(8,128)(2,1)}, u32[]{:S(2)}, u32[]{:S(2)}) collective-permute-start(bf16[2,64,1024]{2,1,0:T(8,128)(2,1)} %pad_maximum_fusion.2), channel_id=1, source_target_pairs={{0,1},{1,0},{2,3},{3,2},{4,5},{5,4},{6,7},{7,6},{8,9},{9,8},{10,11... | collective-permute-start | bytes 786440 | tf_op jit(solution)/shard_map/cond/branch_1_fun/ppermute | solution.py:41
  68.1 1.8 collective-permute-start.20
  69.5 4.3 %collective-permute-start.21 = (bf16[8,32,1024]{2,1,0:T(8,128)(2,1)}, bf16[8,32,1024]{2,1,0:T(8,128)(2,1)}, u32[]{:S(2)}, u32[]{:S(2)}) collective-permute-start(bf16[8,32,1024]{2,1,0:T(8,128)(2,1)} %fusion.1), channel_id=1, source_target_pairs={{0,2},{2,0},{1,3},{3,1},{4,6},{6,4},{5,7},{7,5},{8,10},{10,8},{9,1... | collective-permute-start | bytes 1572872 | tf_op jit(solution)/shard_map/cond/branch_1_fun/ppermute | solution.py:41
  73.8 46.9 %copy-start.11 = (s32[8,128]{1,0:T(8,128)}, s32[8,128]{1,0:T(8,128)S(1)}, u32[]{:S(2)}) copy-start(s32[8,128]{1,0:T(8,128)S(1)} %get-tuple-element.574) | copy-start | bytes 12292
  77.5 1.9 collective-permute-start
  99.4 12.4 %copy-start.29 = (bf16[128,1024]{1,0:T(8,128)(2,1)S(1)}, bf16[128,1024]{1,0:T(8,128)(2,1)}, u32[]{:S(2)}) copy-start(bf16[128,1024]{1,0:T(8,128)(2,1)} %tokens.5) | copy-start | bytes 786436
  99.4 12.4 %copy-start.41 = (f32[1024]{0:T(1024)S(1)}, f32[1024]{0:T(1024)}, u32[]{:S(2)}) copy-start(f32[1024]{0:T(1024)} %param.51) | copy-start | bytes 12292
  102.6 7.4 %collective-permute-start.1 = (bf16[128,1024]{1,0:T(8,128)(2,1)}, bf16[128,1024]{1,0:T(8,128)(2,1)}, u32[]{:S(2)}, u32[]{:S(2)}) collective-permute-start(bf16[128,1024]{1,0:T(8,128)(2,1)} %get-tuple-element.751), channel_id=1, source_target_pairs={{0,1},{1,0},{2,3},{3,2},{4,5},{5,4},{6,7},{7,6},{8,9},{9,8},{10,11... | collective-permute-start | bytes 786440 | tf_op jit(solution)/shard_map/cond/branch_1_fun/ppermute | solution.py:41
  110.1 102.3 %all-gather.10.cloned.1.call-start = ((), (), s32[]{:S(2)}) async-start(), calls=%async_computation.7 | async-start | bytes 1114112 | tf_op jit(solution)/shard_map/all_gather | solution.py:1121
  119.0 14.7 %collective-permute-start.32 = (bf16[288,1024]{1,0:T(8,128)(2,1)}, bf16[288,1024]{1,0:T(8,128)(2,1)}, u32[]{:S(2)}, u32[]{:S(2)}) collective-permute-start(bf16[288,1024]{1,0:T(8,128)(2,1)} %get-tuple-element.590), channel_id=1, source_target_pairs={{0,2},{2,0},{1,3},{3,1},{4,6},{6,4},{5,7},{7,5},{8,10},{10,8},{9,1... | collective-permute-start | bytes 1769480 | tf_op jit(solution)/shard_map/ppermute | solution.py:41
  119.3 38.7 %collective-permute-start.33 = (bf16[288,1024]{1,0:T(8,128)(2,1)}, bf16[288,1024]{1,0:T(8,128)(2,1)}, u32[]{:S(2)}, u32[]{:S(2)}) collective-permute-start(bf16[288,1024]{1,0:T(8,128)(2,1)} %get-tuple-element.601), channel_id=1, source_target_pairs={{0,4},{4,0},{1,5},{5,1},{2,6},{6,2},{3,7},{7,3},{8,12},{12,8},{9,1... | collective-permute-start | bytes 1769480 | tf_op jit(solution)/shard_map/ppermute | solution.py:41
  120.7 8.5 %collective-permute-start.2 = (bf16[128,1024]{1,0:T(8,128)(2,1)}, bf16[128,1024]{1,0:T(8,128)(2,1)S(1)}, u32[]{:S(2)}, u32[]{:S(2)}) collective-permute-start(bf16[128,1024]{1,0:T(8,128)(2,1)} %get-tuple-element.314.own), channel_id=1, source_target_pairs={{0,1},{1,0},{2,3},{3,2},{4,5},{5,4},{6,7},{7,6},{8,9},{9,8},{10,11... | collective-permute-start | bytes 786440 | tf_op jit(solution)/shard_map/cond/branch_1_fun/ppermute | solution.py:41
  133.9 1.9 collective-permute-start.22
  134.0 4.2 %collective-permute-start.23 = (bf16[4,4096]{1,0:T(4,128)(2,1)S(1)}, bf16[4,4096]{1,0:T(4,128)(2,1)S(1)}, u32[]{:S(2)}, u32[]{:S(2)}) collective-permute-start(bf16[4,4096]{1,0:T(4,128)(2,1)S(1)} %get-tuple-element.323), channel_id=1, source_target_pairs={{0,4},{2,6},{4,0},{6,2},{1,5},{3,7},{5,1},{7,3},{8,12},{10,14},{12... | collective-permute-start | bytes 98312 | tf_op jit(solution)/shard_map/cond/branch_1_fun/ppermute | solution.py:37
  134.7 3.7 %collective-permute-start.24 = (bf16[4,4096]{1,0:T(4,128)(2,1)S(1)}, bf16[4,4096]{1,0:T(4,128)(2,1)S(1)}, u32[]{:S(2)}, u32[]{:S(2)}) collective-permute-start(bf16[4,4096]{1,0:T(4,128)(2,1)S(1)} %get-tuple-element.323), channel_id=1, source_target_pairs={{0,6},{2,4},{4,2},{6,0},{1,7},{3,5},{5,3},{7,1},{8,14},{10,12},{12... | collective-permute-start | bytes 98312 | tf_op jit(solution)/shard_map/cond/branch_1_fun/ppermute | solution.py:37
  138.4 9.2 %copy-start.7 = (bf16[4,4096]{1,0:T(4,128)(2,1)}, bf16[4,4096]{1,0:T(4,128)(2,1)S(1)}, u32[]{:S(2)}) copy-start(bf16[4,4096]{1,0:T(4,128)(2,1)S(1)} %add_convert_fusion.t0) | copy-start | bytes 98308 | tf_op jit(solution)/shard_map/cond
  138.4 4.5 %collective-permute-start.25 = (bf16[4,4096]{1,0:T(4,128)(2,1)S(1)}, bf16[4,4096]{1,0:T(4,128)(2,1)S(1)}, u32[]{:S(2)}, u32[]{:S(2)}) collective-permute-start(bf16[4,4096]{1,0:T(4,128)(2,1)S(1)} %add_convert_fusion.t0), channel_id=1, source_target_pairs={{0,8},{8,0},{16,24},{24,16},{1,9},{9,1},{17,25},{25,17},{2,10},{10... | collective-permute-start | bytes 98312 | tf_op jit(solution)/shard_map/cond/branch_1_fun/ppermute | solution.py:33
  139.1 7.8 %collective-permute-start.26 = (bf16[4,4096]{1,0:T(4,128)(2,1)S(1)}, bf16[4,4096]{1,0:T(4,128)(2,1)S(1)}, u32[]{:S(2)}, u32[]{:S(2)}) collective-permute-start(bf16[4,4096]{1,0:T(4,128)(2,1)S(1)} %add_convert_fusion.t0), channel_id=1, source_target_pairs={{0,16},{8,24},{16,0},{24,8},{1,17},{9,25},{17,1},{25,9},{2,18},{10... | collective-permute-start | bytes 98312 | tf_op jit(solution)/shard_map/cond/branch_1_fun/ppermute | solution.py:33
  141.2 6.4 %collective-permute-start.27 = (bf16[4,4096]{1,0:T(4,128)(2,1)S(1)}, bf16[4,4096]{1,0:T(4,128)(2,1)S(1)}, u32[]{:S(2)}, u32[]{:S(2)}) collective-permute-start(bf16[4,4096]{1,0:T(4,128)(2,1)S(1)} %add_convert_fusion.t0), channel_id=1, source_target_pairs={{0,24},{8,16},{16,8},{24,0},{1,25},{9,17},{17,9},{25,1},{2,26},{10... | collective-permute-start | bytes 98312 | tf_op jit(solution)/shard_map/cond/branch_1_fun/ppermute | solution.py:33
  158.1 123.3 %all-gather.12.cloned.1.call-start = ((), (), s32[]{:S(2)}) async-start(), calls=%async_computation.8 | async-start | bytes 1462272 | tf_op jit(solution)/shard_map/all_gather | solution.py:1269
  158.1 15.6 %collective-permute-start.34 = (bf16[256,1024]{1,0:T(8,128)(2,1)}, bf16[256,1024]{1,0:T(8,128)(2,1)S(1)}, u32[]{:S(2)}, u32[]{:S(2)}) collective-permute-start(bf16[256,1024]{1,0:T(8,128)(2,1)} %get-tuple-element.609), channel_id=1, source_target_pairs={{0,4},{4,0},{1,5},{5,1},{2,6},{6,2},{3,7},{7,3},{8,12},{12,8},{9,1... | collective-permute-start | bytes 1572872 | tf_op jit(solution)/shard_map/ppermute | solution.py:41
  159.8 13.9 %collective-permute-start.35 = (bf16[256,1024]{1,0:T(8,128)(2,1)}, bf16[256,1024]{1,0:T(8,128)(2,1)S(1)}, u32[]{:S(2)}, u32[]{:S(2)}) collective-permute-start(bf16[256,1024]{1,0:T(8,128)(2,1)} %get-tuple-element.616), channel_id=1, source_target_pairs={{0,2},{2,0},{1,3},{3,1},{4,6},{6,4},{5,7},{7,5},{8,10},{10,8},{9,1... | collective-permute-start | bytes 1572872 | tf_op jit(solution)/shard_map/ppermute | solution.py:41
  159.8 8.9 %collective-permute-start.3 = (bf16[128,1024]{1,0:T(8,128)(2,1)}, bf16[128,1024]{1,0:T(8,128)(2,1)S(1)}, u32[]{:S(2)}, u32[]{:S(2)}) collective-permute-start(bf16[128,1024]{1,0:T(8,128)(2,1)} %get-tuple-element.340.own), channel_id=1, source_target_pairs={{0,1},{1,0},{2,3},{3,2},{4,5},{5,4},{6,7},{7,6},{8,9},{9,8},{10,11... | collective-permute-start | bytes 786440 | tf_op jit(solution)/shard_map/cond/branch_1_fun/ppermute | solution.py:41
  161.3 1.6 collective-permute-start.4
  173.7 19.9 %copy-start.12 = (s32[8,128]{1,0:T(8,128)S(1)}, s32[8,128]{1,0:T(8,128)}, u32[]{:S(2)}) copy-start(s32[8,128]{1,0:T(8,128)} %copy-done.11) | copy-start | bytes 12292
  173.7 19.9 %copy-start.15 = (s32[8,128]{1,0:T(8,128)S(1)}, s32[8,128]{1,0:T(8,128)}, u32[]{:S(2)}) copy-start(s32[8,128]{1,0:T(8,128)} %copy-done.14) | copy-start | bytes 12292
  173.7 19.9 %copy-start.16 = (f32[4,1,1,256]{3,2,1,0:T(1,128)S(1)}, f32[4,1,1,256]{3,2,1,0:T(1,128)}, u32[]{:S(2)}) copy-start(f32[4,1,1,256]{3,2,1,0:T(1,128)} %get-tuple-element.619) | copy-start | bytes 12292
  173.7 19.9 %copy-start.43 = (s32[4]{0:T(128)S(1)}, s32[4]{0:T(128)}, u32[]{:S(2)}) copy-start(s32[4]{0:T(128)} %param.44) | copy-start | bytes 52
  173.7 9.0 %copy-start.23 = (bf16[256,1024]{1,0:T(8,128)(2,1)}, bf16[256,1024]{1,0:T(8,128)(2,1)S(1)}, u32[]{:S(2)}) copy-start(bf16[256,1024]{1,0:T(8,128)(2,1)S(1)} %get-tuple-element.356.g1) | copy-start | bytes 1572868 | tf_op jit(solution)/shard_map/cond
  173.8 9.0 %collective-permute-start.8 = (bf16[288,1024]{1,0:T(8,128)(2,1)}, bf16[288,1024]{1,0:T(8,128)(2,1)}, u32[]{:S(2)}, u32[]{:S(2)}) collective-permute-start(bf16[288,1024]{1,0:T(8,128)(2,1)} %get-tuple-element.351.f1), channel_id=1, source_target_pairs={{0,2},{2,0},{1,3},{3,1},{4,6},{6,4},{5,7},{7,5},{8,10},{10,8},{9,1... | collective-permute-start | bytes 1769480 | tf_op jit(solution)/shard_map/cond/branch_1_fun/ppermute | solution.py:41
  173.9 8.9 %collective-permute-start.9 = (bf16[256,1024]{1,0:T(8,128)(2,1)S(1)}, bf16[256,1024]{1,0:T(8,128)(2,1)S(1)}, u32[]{:S(2)}, u32[]{:S(2)}) collective-permute-start(bf16[256,1024]{1,0:T(8,128)(2,1)S(1)} %get-tuple-element.356.g1), channel_id=1, source_target_pairs={{0,2},{2,0},{1,3},{3,1},{4,6},{6,4},{5,7},{7,5},{8,10},{10,8},{9,1... | collective-permute-start | bytes 1572872 | tf_op jit(solution)/shard_map/cond/branch_1_fun/ppermute | solution.py:41
  174.3 8.4 %collective-permute-start.5 = (bf16[128,1024]{1,0:T(8,128)(2,1)S(1)}, bf16[128,1024]{1,0:T(8,128)(2,1)}, u32[]{:S(2)}, u32[]{:S(2)}) collective-permute-start(bf16[128,1024]{1,0:T(8,128)(2,1)S(1)} %get-tuple-element.350), channel_id=1, source_target_pairs={{0,4},{4,0},{1,5},{5,1},{2,6},{6,2},{3,7},{7,3},{8,12},{12,8},{9,1... | collective-permute-start | bytes 786440 | tf_op jit(solution)/shard_map/cond/branch_1_fun/ppermute | solution.py:41
  174.8 14.1 %collective-permute-start.6 = (bf16[128,1024]{1,0:T(8,128)(2,1)S(1)}, bf16[128,1024]{1,0:T(8,128)(2,1)}, u32[]{:S(2)}, u32[]{:S(2)}) collective-permute-start(bf16[128,1024]{1,0:T(8,128)(2,1)S(1)} %get-tuple-element.350), channel_id=1, source_target_pairs={{0,2},{2,0},{1,3},{3,1},{4,6},{6,4},{5,7},{7,5},{8,10},{10,8},{9,1... | collective-permute-start | bytes 786440 | tf_op jit(solution)/shard_map/cond/branch_1_fun/ppermute | solution.py:41
  174.8 16.8 %all-to-all-start.1 = ((bf16[8,144,128]{2,1,0:T(8,128)(2,1)}), bf16[8,144,128]{2,1,0:T(8,128)(2,1)}, u32[]{:S(2)}, u32[]{:S(2)}) async-start(bf16[8,144,128]{2,1,0:T(8,128)(2,1)} %get-tuple-element.349), calls=%async_computation.1 | async-start | bytes 589824 | tf_op jit(solution)/shard_map/cond/branch_1_fun/all_to_all | solution.py:1019
  182.7 8.9 %collective-permute-start.7 = (bf16[128,1024]{1,0:T(8,128)(2,1)}, bf16[128,1024]{1,0:T(8,128)(2,1)}, u32[]{:S(2)}, u32[]{:S(2)}) collective-permute-start(bf16[128,1024]{1,0:T(8,128)(2,1)} %collective-permute-done.5), channel_id=1, source_target_pairs={{0,2},{2,0},{1,3},{3,1},{4,6},{6,4},{5,7},{7,5},{8,10},{10,8},{9,1... | collective-permute-start | bytes 786440 | tf_op jit(solution)/shard_map/cond/branch_1_fun/ppermute | solution.py:41
  191.6 18.1 %collective-permute-start.36 = (bf16[2,2,64,1024]{3,2,1,0:T(8,128)(2,1)S(1)}, bf16[2,2,64,1024]{3,2,1,0:T(8,128)(2,1)}, u32[]{:S(2)}, u32[]{:S(2)}) collective-permute-start(bf16[2,2,64,1024]{3,2,1,0:T(8,128)(2,1)S(1)} %get-tuple-element.622), channel_id=1, source_target_pairs={{0,8},{8,0},{16,24},{24,16},{1,9},{9,1},{17,25},{25,17},{2,10},{10... | collective-permute-start | bytes 1572872 | tf_op jit(solution)/shard_map/ppermute | solution.py:33
  192.3 43.1 %collective-permute-start.38 = (bf16[2,2,64,1024]{3,2,1,0:T(8,128)(2,1)S(1)}, bf16[2,2,64,1024]{3,2,1,0:T(8,128)(2,1)}, u32[]{:S(2)}, u32[]{:S(2)}) collective-permute-start(bf16[2,2,64,1024]{3,2,1,0:T(8,128)(2,1)S(1)} %get-tuple-element.640), channel_id=1, source_target_pairs={{0,8},{8,0},{16,24},{24,16},{1,9},{9,1},{17,25},{25,17},{2,10},{10... | collective-permute-start | bytes 1572872 | tf_op jit(solution)/shard_map/ppermute | solution.py:33
  193.9 12.7 %copy-start.21 = (s32[5]{0:T(128)S(1)}, s32[5]{0:T(128)}, u32[]{:S(2)}) copy-start(s32[5]{0:T(128)} %get-tuple-element.362.idx) | copy-start | bytes 64 | tf_op jit(solution)/shard_map/cond
  203.6 2.2 collective-permute-start.10
  211.7 23.7 %collective-permute-start.37 = (bf16[2,64,1024]{2,1,0:T(8,128)(2,1)}, bf16[2,64,1024]{2,1,0:T(8,128)(2,1)}, u32[]{:S(2)}, u32[]{:S(2)}) collective-permute-start(bf16[2,64,1024]{2,1,0:T(8,128)(2,1)} %get-tuple-element.639), channel_id=1, source_target_pairs={{0,16},{8,24},{16,0},{24,8},{1,17},{9,25},{17,1},{25,9},{2,18},{10... | collective-permute-start | bytes 786440 | tf_op jit(solution)/shard_map/ppermute | solution.py:33
  212.4 23.0 %all-to-all-start.2 = ((bf16[8,96,256]{2,1,0:T(8,128)(2,1)}), bf16[8,96,256]{2,1,0:T(8,128)(2,1)}, u32[]{:S(2)}, u32[]{:S(2)}) async-start(bf16[8,96,256]{2,1,0:T(8,128)(2,1)} %get-tuple-element.377), calls=%async_computation.2 | async-start | bytes 786432 | tf_op jit(solution)/shard_map/cond/branch_1_fun/all_to_all | solution.py:1019
  220.8 9.2 %collective-permute-start.11 = (bf16[2,2,64,256]{3,2,1,0:T(8,128)(2,1)}, bf16[2,2,64,256]{3,2,1,0:T(8,128)(2,1)}, u32[]{:S(2)}, u32[]{:S(2)}) collective-permute-start(bf16[2,2,64,256]{3,2,1,0:T(8,128)(2,1)} %get-tuple-element.400), channel_id=1, source_target_pairs={{0,8},{8,0},{16,24},{24,16},{1,9},{9,1},{17,25},{25,17},{2,10},{10... | collective-permute-start | bytes 393224 | tf_op jit(solution)/shard_map/cond/branch_1_fun/ppermute | solution.py:33
  237.7 20.8 %collective-permute-start.39 = (bf16[2,64,1280]{2,1,0:T(8,128)(2,1)}, bf16[2,64,1280]{2,1,0:T(8,128)(2,1)S(1)}, u32[]{:S(2)}, u32[]{:S(2)}) collective-permute-start(bf16[2,64,1280]{2,1,0:T(8,128)(2,1)} %get-tuple-element.660), channel_id=1, source_target_pairs={{0,16},{8,24},{16,0},{24,8},{1,17},{9,25},{17,1},{25,9},{2,18},{10... | collective-permute-start | bytes 983048 | tf_op jit(solution)/shard_map/ppermute | solution.py:33
  238.6 6.4 %collective-permute-start.12 = (bf16[8,64,256]{2,1,0:T(8,128)(2,1)S(1)}, bf16[8,64,256]{2,1,0:T(8,128)(2,1)S(1)}, u32[]{:S(2)}, u32[]{:S(2)}) collective-permute-start(bf16[8,64,256]{2,1,0:T(8,128)(2,1)S(1)} %get-tuple-element.411), channel_id=1, source_target_pairs={{0,2},{2,0},{1,3},{3,1},{4,6},{6,4},{5,7},{7,5},{8,10},{10,8},{9,1... | collective-permute-start | bytes 786440 | tf_op jit(solution)/shard_map/cond/branch_1_fun/ppermute | solution.py:41
  243.4 9.0 %collective-permute-start.13 = (bf16[128,1024]{1,0:T(8,128)(2,1)}, bf16[128,1024]{1,0:T(8,128)(2,1)S(1)}, u32[]{:S(2)}, u32[]{:S(2)}) collective-permute-start(bf16[128,1024]{1,0:T(8,128)(2,1)} %tokens.3.own), channel_id=1, source_target_pairs={{0,1},{1,0},{2,3},{3,2},{4,5},{5,4},{6,7},{7,6},{8,9},{9,8},{10,11... | collective-permute-start | bytes 786440 | tf_op jit(solution)/shard_map/cond/branch_1_fun/ppermute | solution.py:41
  254.2 14.7 %all-to-all-start.4 = ((bf16[8,64,256]{2,1,0:T(8,128)(2,1)}), bf16[8,64,256]{2,1,0:T(8,128)(2,1)S(1)}, u32[]{:S(2)}, u32[]{:S(2)}) async-start(bf16[8,64,256]{2,1,0:T(8,128)(2,1)} %get-tuple-element.668), calls=%async_computation.4 | async-start | bytes 524288 | tf_op jit(solution)/shard_map/all_to_all | solution.py:1295
  261.7 13.4 %collective-permute-start.40 = (bf16[64,2304]{1,0:T(8,128)(2,1)}, bf16[64,2304]{1,0:T(8,128)(2,1)S(1)}, u32[]{:S(2)}, u32[]{:S(2)}) collective-permute-start(bf16[64,2304]{1,0:T(8,128)(2,1)} %get-tuple-element.663), channel_id=1, source_target_pairs={{0,4},{4,0},{1,5},{5,1},{2,6},{6,2},{3,7},{7,3},{8,12},{12,8},{9,1... | collective-permute-start | bytes 884744 | tf_op jit(solution)/shard_map/ppermute | solution.py:41
  (29 other events, 88.7 us)
Sparse Core Ops, SparseCore 0:
  32.0 79.7 all-gather.5
  114.1 45.7 all-gather.7
  162.1 37.8 all-gather.9
  237.8 43.4 all-gather.11

commit v6 on v5

--- a/solution.py
+++ b/solution.py
@@ -368,7 +368,7 @@
 
 def attend_back_kernel(
     blocks, idx, lens, q_ref, g_ref, o_ref, log_ref, kv0_ref, kv1_ref, kdoc0_ref, kdoc1_ref,
-    dq_ref, dkv0_ref, dkv1_ref, column0, column1,
+    dq_ref, dkv0_ref, dkv1_ref, column0, column1, held,
 ):
     rows, width = q_ref.shape[3], kdoc0_ref.shape[1]
     z, part = pl.program_id(0), pl.program_id(1)
@@ -376,7 +376,7 @@
     @pl.when((z == 0) & (part == 0))
     def _():
         dkv0_ref[...] = jnp.zeros_like(dkv0_ref)
-        dkv1_ref[...] = jnp.zeros_like(dkv1_ref)
+        held[...] = jnp.zeros_like(held)
         for ref, column in ((kdoc0_ref, column0), (kdoc1_ref, column1)):
             turned = jnp.transpose(ref[...].astype(WIDE))
             for i in range(ref.shape[0]):
@@ -396,7 +396,7 @@
     doc = docs_of(places_of(token, rows, width // 2, blocks, idx, z, part), lens).astype(WIDE)
     log_total = log_ref[0, 0]
     total = jnp.zeros((4 * rows, PAIR), WIDE)
-    for kv_ref, column, dkv_ref in ((kv0_ref, column0, dkv0_ref), (kv1_ref, column1, dkv1_ref)):
+    for kv_ref, column, dkv_ref in ((kv0_ref, column0, dkv0_ref), (kv1_ref, column1, held)):
         keys = kv_ref[...]
         raw = dot_nt(keys, queries)
         probs = jnp.where(column[...] == doc, jnp.exp(raw - log_total), 0.0)
@@ -405,6 +405,10 @@
         total = total + dot_tn(dscores, keys)
         dkv_ref[...] += dot_nn(dscores, queries) + dot_nn(probs.astype(LOW), grads)
     dq_ref[0] = (total * HEAD_DIM ** (-0.5)).reshape(2, 2, rows, PAIR)
+
+    @pl.when((z == pl.num_programs(0) - 1) & (part == pl.num_programs(1) - 1))
+    def _():
+        dkv1_ref[...] = held[...].astype(LOW)
 
 
 def attend_back(blocks, index, lens, queries, grads, out, log_total, kv0, kv1, kdoc0, kdoc1):
@@ -419,9 +423,9 @@
         out_shape=[
             shape((NZ, 2, 2, half, PAIR), WIDE),
             shape((keys, PAIR), WIDE),
-            shape((keys, PAIR), WIDE),
+            shape((keys, PAIR), LOW),
         ],
-        scratch_shapes=[pltpu.VMEM((keys, 1), WIDE)] * 2,
+        scratch_shapes=[pltpu.VMEM((keys, 1), WIDE)] * 2 + [pltpu.VMEM((keys, PAIR), WIDE)],
         compiler_params=PARAMS,
         cost_estimate=cost("attend_back"),
         name="attend_back",
@@ -770,7 +774,7 @@
 def triple_kernel(idx, dq, dkv, got, cosine, sine, out, dense):
     rows = dq.shape[0]
     low_lanes = lax.broadcasted_iota(jnp.int32, (rows, PAIR), 1) < HEAD_DIM
-    grads = dkv[...] + got[...]
+    grads = dkv[...] + got[...].astype(WIDE)
     both_parts = jnp.where(low_lanes, dq[...], pltpu.roll(grads, HEAD_DIM, 1))
     turned = turn(both_parts, cosine[...], -sine[...])
     turned, value = turned.astype(LOW), grads[:, HEAD_DIM:].astype(LOW)

time: 292 us -> 292 us (level)
  transfers between devices with their start and end apart: 49 -> 49, of which waited for: 24 -> 24; matrix products, arithmetic and copies ran while one was open for 5% -> 5% of each run, Pallas kernels for 29% -> 30%
where the time goes in v6:
time: 292 us; the launch traced here: 290 us
  Pallas kernels  93.5 us (32%)
  waiting for transfers between devices  86.8 us (30%)
  starting transfers between devices  59 us (20%)
  local copies, waits for them, and re-layouts  15.5 us (5%)
  between operations  14.1 us (5%)
  blocking collectives  13.5 us (5%)
  other arithmetic  7.33 us (3%)
    pallas_call x23, Pallas kernels, whole(): pl.pallas_call(kernel, in_specs=[pl.BlockSpec(memory_space=pltpu.SMEM)] +...  77.1 us
    ppermute x27, waiting for transfers between devices, flip(): return lax.ppermute(value, axis, [(0, 1), (1, 0)])  45.6 us
    ppermute x27, starting transfers between devices, flip(): return lax.ppermute(value, axis, [(0, 1), (1, 0)])  22.5 us
    ppermute x11, waiting for transfers between devices, xor_z(): return lax.ppermute(value, 'z', [(i, i ^ mask) for i in FOUR])  22 us
    ppermute x11, starting transfers between devices, xor_z(): return lax.ppermute(value, 'z', [(i, i ^ mask) for i in FOUR])  14.5 us
    all_to_all x1, blocking collectives, to_blocks(): lax.all_to_all(value.reshape((NZ * 2,) + value.shape[-2:]), ('z', 'x'), 0...  13.5 us
    cond x51, local copies, waits for them, and re-layouts  11.1 us
    pallas_call x1, Pallas kernels, attend_back(): pl.pallas_call(partial(attend_back_kernel, blocks), grid=grid, in_specs=S...  9.81 us
  transfers between devices with their start and end apart: 49, of which 24 were waited for; matrix products, arithmetic and copies ran while one was open for 5% of the time, Pallas kernels for 30%

profile of v6, /device:TPU:0, one launch (start us, length us, event | category | flops | bytes accessed | tf_op | source)
XLA Modules:
  0.0 290.3 jit_solution(12033988200837764025)
XLA Ops:
  7.3 2.7 prep.1
  10.0 2.9 %collective-permute-start.28 = (bf16[160,1024]{1,0:T(8,128)(2,1)S(1)}, bf16[160,1024]{1,0:T(8,128)(2,1)S(1)}, u32[]{:S(2)}, u32[]{:S(2)}) collective-permute-start(bf16[160,1024]{1,0:T(8,128)(2,1)S(1)} %get-tuple-element.556), channel_id=1, source_target_pairs={{0,4},{4,0},{1,5},{5,1},{2,6},{6,2},{3,7},{7,3},{8,12},{12,8},{9,1... | collective-permute-start | bytes 983048 | tf_op jit(solution)/shard_map/ppermute | solution.py:41
  14.5 2.6 collective-permute-start.30
  17.3 5.3 %collective-permute-done.29 = bf16[96,1024]{1,0:T(8,128)(2,1)S(1)} collective-permute-done((bf16[96,1024]{1,0:T(8,128)(2,1)}, bf16[96,1024]{1,0:T(8,128)(2,1)S(1)}, u32[]{:S(2)}, u32[]{:S(2)}) %collective-permute-start.29) | collective-permute-done | bytes 196640 | tf_op jit(solution)/shard_map/ppermute | solution.py:33
  22.7 9.2 %collective-permute-done.30 = bf16[96,1024]{1,0:T(8,128)(2,1)S(1)} collective-permute-done((bf16[96,1024]{1,0:T(8,128)(2,1)}, bf16[96,1024]{1,0:T(8,128)(2,1)S(1)}, u32[]{:S(2)}, u32[]{:S(2)}) %collective-permute-start.30) | collective-permute-done | bytes 196640 | tf_op jit(solution)/shard_map/ppermute | solution.py:33
  32.1 41.7 %conditional.11 = (bf16[1024,256]{1,0:T(8,128)(2,1)S(1)}, s32[8,128]{1,0:T(8,128)S(1)}, s32[8,128]{1,0:T(8,128)S(1)}, bf16[8,32,1024]{2,1,0:T(8,128)(2,1)}, bf16...) conditional(s32[]{:T(128)} %bitcast.27, () %tuple.119, ...), branch_computations={%region_0.0_spmd, %region_1.6_spmd} | conditional | flops 5520703488 | bytes 35979452 | solution.py:914
  34.8 6.2 %all-to-all-start.3 = ((bf16[8,64,256]{2,1,0:T(8,128)(2,1)}), bf16[8,64,256]{2,1,0:T(8,128)(2,1)S(1)}, u32[]{:S(2)}, u32[]{:S(2)}) async-start(bf16[8,64,256]{2,1,0:T(8,128)(2,1)} %get-tuple-element.262), calls=%async_computation.3 | async-start | bytes 524288 | tf_op jit(solution)/shard_map/cond/branch_1_fun/all_to_all | solution.py:966
  43.2 2.4 query_units.1
  46.5 3.0 %fusion = (f32[1024,128]{1,0:T(8,128)}, f32[1024,128]{1,0:T(8,128)}) fusion(f32[128]{0:T(128)S(1)} %get-tuple-element.701, f32[128]{0:T(128)S(1)} %get-tuple-element.702, f32[1024]{0:T(1024)S(1)} %subtract_convert_fusion), kind=kLoop, calls=%fused_computation.2 | loop fusion | flops 262144 | bytes 1053696 | tf_op jit(solution)/shard_map/cond/branch_1_fun/mul | solution.py:985
  57.8 2.6 collective-permute-done.15
  60.5 4.9 %collective-permute-done.17 = bf16[2,64,1024]{2,1,0:T(8,128)(2,1)} collective-permute-done((bf16[2,64,1024]{2,1,0:T(8,128)(2,1)}, bf16[2,64,1024]{2,1,0:T(8,128)(2,1)}, u32[]{:S(2)}, u32[]{:S(2)}) %collective-permute-start.17) | collective-permute-done | bytes 262176 | tf_op jit(solution)/shard_map/cond/branch_1_fun/ppermute | solution.py:41
  65.3 2.8 collective-permute-done.19
  70.6 1.8 heads.1
  73.8 5.6 %conditional.12 = (bf16[1024,128]{1,0:T(8,128)(2,1)}, bf16[1024,128]{1,0:T(8,128)(2,1)}, bf16[1024,128]{1,0:T(8,128)(2,1)}) conditional(s32[]{:T(128)} %bitcast.27, () %tuple.118, (s32[5]{0:T(128)S(1)}, bf16[128,1024]{1,0:T(8,128)(2,1)}, bf16[160,1024]{1,0:T(8,128)(2,1)S(1)}, bf16[2,64,1024]{2,1,0:T(8,128)(2,1)}, bf16[2,64,1024]{2,1,0:T(8,128)(2,1)}, ...), branch_computations={%region_6.7_spmd, %region_7.8_spmd} | conditional | flops 4369999872 | bytes 15108640 | solution.py:914
  73.8 3.7 %project.1 = (bf16[1024,128]{1,0:T(8,128)(2,1)}, bf16[1024,128]{1,0:T(8,128)(2,1)}) custom-call(s32[5]{0:T(128)S(1)} %get-tuple-element.282.idx, bf16[128,1024]{1,0:T(8,128)(2,1)} %get-tuple-element.283.refs_0_, bf16[160,1024]{1,0:T(8,128)(2,1)S(1)} %get-tuple-element.284.refs_1_, bf16[2,64,1024]{2,1,0:T(8,128)(2,1)} %get-tuple-element.285.refs_2_, ...), custom_call_target="tpu_custom_call" | custom-call | flops 4369999872 | bytes 14060000 | tf_op jit(solution)/shard_map/cond/branch_1_fun/project/pallas_call | solution.py:115
  77.6 1.8 collective-permute-done
  79.4 20.0 %conditional.13 = (f32[4,2,2,64,128]{4,3,2,1,0:T(8,128)}, f32[4,1,1,256]{3,2,1,0:T(1,128)}, bf16[8,64,128]{2,1,0:T(8,128)(2,1)S(1)}) conditional(s32[]{:T(128)} %bitcast.27, () %tuple.117, (bf16[1024,128]{1,0:T(8,128)(2,1)}, s32[5]{0:T(128)S(1)}, s32[4]{0:T(128)S(1)}, bf16[1024,128]{1,0:T(8,128)(2,1)}, bf16[1024,128]{1,0:T(8,128)(2,1)}, ...), branch_computations={%region_8.9_spmd, %region_9.10_spmd} | conditional | flops 8625000448 | bytes 28012168 | solution.py:914
  79.4 6.5 %attend.1 = (f32[4,2,2,64,128]{4,3,2,1,0:T(8,128)}, f32[4,1,1,256]{3,2,1,0:T(1,128)}, bf16[4,2,64,128]{3,2,1,0:T(8,128)(2,1)}) custom-call(s32[5]{0:T(128)S(1)} %get-tuple-element.297.idx, s32[4]{0:T(128)S(1)} %get-tuple-element.298.lens, bf16[4,2,2,64,128]{4,3,2,1,0:T(8,128)(2,1)} %bitcast.17.q_ref, bf16[1024,128]{1,0:T(8,128)(2,1)} %get-tuple-element.300.kv0_ref, ...), custom_call_target="tpu_custom_call" | custom-call | flops 8625000448 | bytes 27750000 | tf_op jit(solution)/shard_map/cond/branch_1_fun/attend/pallas_call | solution.py:353
  86.0 13.5 %all_to_all.21 = bf16[8,64,128]{2,1,0:T(8,128)(2,1)S(1)} all-to-all(bf16[8,64,128]{2,1,0:T(8,128)(2,1)} %bitcast.77), channel_id=1, replica_groups=mesh['o'=1,'z'=4,'x'=2,'c'=2,'y'=2] {'z','x'}, dimensions={0} | all-to-all | bytes 262144 | tf_op jit(solution)/shard_map/cond/branch_1_fun/all_to_all | solution.py:1023
  99.4 10.7 %conditional.14 = (bf16[128,512]{1,0:T(8,128)(2,1)S(1)}, bf16[128,1024]{1,0:T(8,128)(2,1)}, bf16[128,1024]{1,0:T(8,128)(2,1)}) conditional(s32[]{:T(128)} %bitcast.27, () %tuple.116, (s32[5]{0:T(128)S(1)}, bf16[8,64,128]{2,1,0:T(8,128)(2,1)S(1)}, bf16[8,32,1024]{2,1,0:T(8,128)(2,1)}, bf16[8,32,1024]{2,1,0:T(8,128)(2,1)}) %tuple.124), branch_computations={%region_10.11_spmd, %region_11.12_spmd} | conditional | flops 4024999936 | bytes 13998640 | solution.py:914
  99.4 3.2 %branch.1 = (bf16[128,512]{1,0:T(8,128)(2,1)S(1)}, bf16[128,1024]{1,0:T(8,128)(2,1)}) custom-call(s32[5]{0:T(128)S(1)} %get-tuple-element.307.idx, bf16[8,64,128]{2,1,0:T(8,128)(2,1)S(1)} %get-tuple-element.308.got, bf16[8,32,1024]{2,1,0:T(8,128)(2,1)} %get-tuple-element.309.refs_0_, bf16[8,32,1024]{2,1,0:T(8,128)(2,1)} %get-tuple-element.310.refs_1_), custom_call_target="tpu_custom_call" | custom-call | flops 4024999936 | bytes 12950000 | tf_op jit(solution)/shard_map/cond/branch_1_fun/branch/pallas_call | solution.py:115
  104.2 5.9 %collective-permute-done.1 = bf16[128,1024]{1,0:T(8,128)(2,1)} collective-permute-done((bf16[128,1024]{1,0:T(8,128)(2,1)}, bf16[128,1024]{1,0:T(8,128)(2,1)}, u32[]{:S(2)}, u32[]{:S(2)}) %collective-permute-start.1) | collective-permute-done | bytes 262176 | tf_op jit(solution)/shard_map/cond/branch_1_fun/ppermute | solution.py:41
  111.8 7.2 %forward.1 = (f32[128,1024]{1,0:T(8,128)}, f32[128,1024]{1,0:T(8,128)}, f32[128,1]{1,0:T(8,128)}, f32[128,2048]{1,0:T(8,128)}, bf16[288,1024]{1,0:T(8,128)(2,1)}...) custom-call(s32[5]{0:T(128)S(1)} %stack.74.idx, bf16[128,1024]{1,0:T(8,128)(2,1)} %get-tuple-element.579.own, ...), custom_call_target="tpu_custom_call" | custom-call | flops 8855000064 | bytes 28490000 | tf_op jit(solution)/shard_map/forward/pallas_call | solution.py:115
  120.7 13.0 %conditional.15 = ((bf16[128,1024]{1,0:T(8,128)(2,1)}, f32[128,1024]{1,0:T(8,128)}, f32[128,1]{1,0:T(8,128)}, f32[128,128]{1,0:T(8,128)}, bf16[128,128]{1,0:T(8,...) conditional(s32[]{:T(128)} %bitcast.27, () %tuple.115, ...), branch_computations={%region_12.13_spmd, %region_13.14_spmd} | conditional | flops 4140000000 | bytes 15433748 | solution.py:914
  122.3 6.9 %collective-permute-done.2.other = bf16[128,1024]{1,0:T(8,128)(2,1)S(1)} collective-permute-done((bf16[128,1024]{1,0:T(8,128)(2,1)}, bf16[128,1024]{1,0:T(8,128)(2,1)S(1)}, u32[]{:S(2)}, u32[]{:S(2)}) %collective-permute-start.2) | collective-permute-done | bytes 262176 | tf_op jit(solution)/shard_map/cond/branch_1_fun/ppermute | solution.py:41
  129.9 3.8 %second.1 = (bf16[128,1024]{1,0:T(8,128)(2,1)}, f32[128,1024]{1,0:T(8,128)}, f32[128,1]{1,0:T(8,128)}, f32[128,128]{1,0:T(8,128)}, bf16[128,128]{1,0:T(8,128)(2,...) custom-call(s32[5]{0:T(128)} %copy-done.20, ...), custom_call_target="tpu_custom_call" | custom-call | flops 4140000000 | bytes 13320000 | tf_op jit(solution)/shard_map/cond/branch_1_fun/second/pallas_call | solution.py:115
  133.7 24.3 %conditional.16 = ((f32[128,1024]{1,0:T(8,128)}, bf16[256,1024]{1,0:T(8,128)(2,1)}, bf16[256,1024]{1,0:T(8,128)(2,1)}, bf16[128,1024]{1,0:T(8,128)(2,1)}, f32[8,...) conditional(s32[]{:T(128)} %bitcast.27, () %tuple.128, ...), branch_computations={%region_14.15_spmd, %region_15.16_spmd} | conditional | flops 13800130560 | bytes 45874920 | solution.py:914
  135.8 2.4 collective-permute-done.23
  139.1 2.2 collective-permute-start.26
  142.9 4.0 %collective-permute-done.26.t2 = bf16[4,4096]{1,0:T(4,128)(2,1)S(1)} collective-permute-done((bf16[4,4096]{1,0:T(4,128)(2,1)S(1)}, bf16[4,4096]{1,0:T(4,128)(2,1)S(1)}, u32[]{:S(2)}, u32[]{:S(2)}) %collective-permute-start.26) | collective-permute-done | bytes 32800 | tf_op jit(solution)/shard_map/cond/branch_1_fun/ppermute | solution.py:33
  148.2 9.8 %middle.1 = (f32[128,1024]{1,0:T(8,128)}, bf16[256,1024]{1,0:T(8,128)(2,1)}, bf16[256,1024]{1,0:T(8,128)(2,1)}, bf16[128,1024]{1,0:T(8,128)(2,1)}, f32[8,128]{1,...) custom-call(s32[5]{0:T(128)} %get-tuple-element.322.idx, ...), custom_call_target="tpu_custom_call" | custom-call | flops 13799999488 | bytes 44400000 | tf_op jit(solution)/shard_map/cond/branch_1_fun/middle/pallas_call | solution.py:115
  159.8 13.9 %conditional.17 = ((f32[128,1024]{1,0:T(8,128)}, bf16[128,1024]{1,0:T(8,128)(2,1)S(1)}, f32[8,1024]{1,0:T(8,128)S(1)}, bf16[8,144,128]{2,1,0:T(8,128)(2,1)})) conditional(s32[]{:T(128)} %bitcast.27, () %tuple.135, (bf16[128,1024]{1,0:T(8,128)(2,1)}, f32[1024]{0:T(1024)}, bf16[8,80,128]{2,1,0:T(8,128)(2,1)}, s32[5]{0:T(128)}, ...), branch_computations={%region_16.17_spmd, %region_17.18_spmd} | conditional | flops 4369999872 | bytes 17468016 | solution.py:914
  162.9 5.8 %collective-permute-done.3.other = bf16[128,1024]{1,0:T(8,128)(2,1)S(1)} collective-permute-done((bf16[128,1024]{1,0:T(8,128)(2,1)}, bf16[128,1024]{1,0:T(8,128)(2,1)S(1)}, u32[]{:S(2)}, u32[]{:S(2)}) %collective-permute-start.3) | collective-permute-done | bytes 262176 | tf_op jit(solution)/shard_map/cond/branch_1_fun/ppermute | solution.py:41
  169.4 4.2 %first_back.1 = (f32[128,1024]{1,0:T(8,128)}, bf16[128,1024]{1,0:T(8,128)(2,1)S(1)}, f32[8,1024]{1,0:T(8,128)S(1)}, bf16[8,144,128]{2,1,0:T(8,128)(2,1)}) custom-call(s32[5]{0:T(128)} %get-tuple-element.339.idx, bf16[128,1024]{1,0:T(8,128)(2,1)} %get-tuple-element.340.own, bf16[128,1024]{1,0:T(8,128)(2,1)} %copy-done.31, ...), custom_call_target="tpu_custom_call" | custom-call | flops 4369999872 | bytes 14060000 | tf_op jit(solution)/shard_map/cond/branch_1_fun/first_back/pallas_call | solution.py:115
  173.7 17.9 %conditional.18 = (bf16[8,144,128]{2,1,0:T(8,128)(2,1)}, bf16[128,1024]{1,0:T(8,128)(2,1)}, bf16[128,1024]{1,0:T(8,128)(2,1)}, bf16[128,1024]{1,0:T(8,128)(2,1)}...) conditional(s32[]{:T(128)} %bitcast.27, () %tuple.134, ...), branch_computations={%region_18.19_spmd, %region_19.20_spmd} | conditional | flops 5980000256 | bytes 34018756 | solution.py:914
  174.8 4.9 %all-to-all-start.1 = ((bf16[8,144,128]{2,1,0:T(8,128)(2,1)}), bf16[8,144,128]{2,1,0:T(8,128)(2,1)}, u32[]{:S(2)}, u32[]{:S(2)}) async-start(bf16[8,144,128]{2,1,0:T(8,128)(2,1)} %get-tuple-element.349), calls=%async_computation.1 | async-start | bytes 589824 | tf_op jit(solution)/shard_map/cond/branch_1_fun/all_to_all | solution.py:1023
  179.8 3.0 %collective-permute-done.5 = bf16[128,1024]{1,0:T(8,128)(2,1)} collective-permute-done((bf16[128,1024]{1,0:T(8,128)(2,1)S(1)}, bf16[128,1024]{1,0:T(8,128)(2,1)}, u32[]{:S(2)}, u32[]{:S(2)}) %collective-permute-start.5) | collective-permute-done | bytes 262176 | tf_op jit(solution)/shard_map/cond/branch_1_fun/ppermute | solution.py:41
  183.6 5.3 %weights.1 = (f32[2,2,64,1024]{3,2,1,0:T(8,128)S(1)}, bf16[2,2,64,1024]{3,2,1,0:T(8,128)(2,1)S(1)}, f32[2,2,64,1024]{3,2,1,0:T(8,128)S(1)}, bf16[2,2,64,1024]{3,2,1,0:T(8,128)(2,1)S(1)}) custom-call(s32[5]{0:T(128)} %get-tuple-element.352.idx, bf16[288,1024]{1,0:T(8,128)(2,1)} %get-tuple-element.353.f0, bf16[288,1024]{1,0:T(8,128)(2,1)} %get-tuple-element.351.f1, ...), custom_call_target="tpu_custom_call" | custom-call | flops 5980000256 | bytes 19240000 | tf_op jit(solution)/shard_map/cond/branch_1_fun/weights/pallas_call | solution.py:115
  188.9 2.7 all-to-all-done.1
  193.6 15.6 %conditional.19 = ((bf16[1024,256]{1,0:T(8,128)(2,1)}, bf16[8,96,256]{2,1,0:T(8,128)(2,1)})) conditional(s32[]{:T(128)} %bitcast.27, () %tuple.133, (bf16[1024,128]{1,0:T(8,128)(2,1)}, bf16[8,144,128]{2,1,0:T(8,128)(2,1)}, s32[5]{0:T(128)}, s32[4]{0:T(128)S(1)}, f32[4,2,2,64,128]{4,3,2,1,0:T(8,128)}, /*index=5*/f32[4,1,1,256]{3,2,1,0:T(1,128)S(1)}, ...), branch_computations={%region_20.21_spmd, %region_21.22_spmd} | conditional | flops 14604999680 | bytes 49087336 | solution.py:914
  193.9 9.8 %attend_back.1 = (f32[4,2,2,64,128]{4,3,2,1,0:T(8,128)}, f32[1024,128]{1,0:T(8,128)}, bf16[1024,128]{1,0:T(8,128)(2,1)}) custom-call(s32[5]{0:T(128)} %get-tuple-element.362.idx, s32[4]{0:T(128)S(1)} %get-tuple-element.363.lens, bf16[4,2,2,64,128]{4,3,2,1,0:T(8,128)(2,1)} %bitcast.24.q_ref, bf16[4,2,144,128]{3,2,1,0:T(8,128)(2,1)} %bitcast.25.g_ref, ...), custom_call_target="tpu_custom_call" | custom-call | flops 11269999616 | bytes 36260000 | tf_op jit(solution)/shard_map/cond/branch_1_fun/attend_back/pallas_call | solution.py:418
  206.2 3.0 %triple.1 = (bf16[1024,256]{1,0:T(8,128)(2,1)}, bf16[8,96,256]{2,1,0:T(8,128)(2,1)}) custom-call(s32[5]{0:T(128)S(1)} %copy-done.21, f32[1024,128]{1,0:T(8,128)} %bitcast.95, f32[1024,128]{1,0:T(8,128)} %get-tuple-element.373.dkv, bf16[1024,128]{1,0:T(8,128)(2,1)} %copy-done.33, f32[1024,128]{1,0:T(8,128)} %get-tuple-element.375.cosine, ...), custom_call_target="tpu_custom_call" | custom-call | flops 3335000064 | bytes 10730000 | tf_op jit(solution)/shard_map/cond/branch_1_fun/triple/pallas_call | solution.py:115
  209.2 2.1 pair.2
  212.0 23.0 %conditional.20 = (bf16[8,96,256]{2,1,0:T(8,128)(2,1)}, bf16[8,64,256]{2,1,0:T(8,128)(2,1)S(1)}, bf16[8,64,256]{2,1,0:T(8,128)(2,1)S(1)}, f32[2,2,64,256]{3,2,1,...) conditional(s32[]{:T(128)} %bitcast.27, () %tuple.132, ...), branch_computations={%region_22.23_spmd, %region_23.24_spmd} | conditional | flops 5175000064 | bytes 24907740 | solution.py:914
  212.0 4.5 %all-to-all-start.2 = ((bf16[8,96,256]{2,1,0:T(8,128)(2,1)}), bf16[8,96,256]{2,1,0:T(8,128)(2,1)}, u32[]{:S(2)}, u32[]{:S(2)}) async-start(bf16[8,96,256]{2,1,0:T(8,128)(2,1)} %get-tuple-element.377), calls=%async_computation.2 | async-start | bytes 786432 | tf_op jit(solution)/shard_map/cond/branch_1_fun/all_to_all | solution.py:1023
  216.5 3.9 %output.1 = (f32[2,2,64,256]{3,2,1,0:T(8,128)S(1)}, bf16[2,2,64,256]{3,2,1,0:T(8,128)(2,1)}) custom-call(s32[5]{0:T(128)S(1)} %get-tuple-element.378.idx, bf16[288,1024]{1,0:T(8,128)(2,1)} %get-tuple-element.391.f0, bf16[288,1024]{1,0:T(8,128)(2,1)} %get-tuple-element.392.f1, bf16[288,1024]{1,0:T(8,128)(2,1)} %get-tuple-element.393.f2, ...), custom_call_target="tpu_custom_call" | custom-call | flops 1724999936 | bytes 5550000 | tf_op jit(solution)/shard_map/cond/branch_1_fun/output/pallas_call | solution.py:115
  220.4 2.0 collective-permute-start.11
  222.4 2.4 triple_weight.1
  224.9 2.3 query_back.1
  227.2 2.7 collective-permute-done.11
  229.9 5.1 %all-to-all-done.2 = bf16[8,96,256]{2,1,0:T(8,128)(2,1)} async-done(((bf16[8,96,256]{2,1,0:T(8,128)(2,1)}), bf16[8,96,256]{2,1,0:T(8,128)(2,1)}, u32[]{:S(2)}, u32[]{:S(2)}) %all-to-all-start.2) | async-done | bytes 393248 | tf_op jit(solution)/shard_map/cond/branch_1_fun/all_to_all | solution.py:1023
  235.0 2.2 pair.3
  238.1 15.6 %conditional.21 = (f32[128,1024]{1,0:T(8,128)S(1)}, bf16[8,64,256]{2,1,0:T(8,128)(2,1)}) conditional(s32[]{:T(128)} %bitcast.27, () %tuple.131, (s32[5]{0:T(128)S(1)}, bf16[8,96,256]{2,1,0:T(8,128)(2,1)}, bf16[1024,1536]{1,0:T(8,128)(2,1)}, bf16[8,64,256]{2,1,0:T(8,128)(2,1)S(1)}, bf16[8,64,256]{2,1,0:T(8,128)(2,1)S(1)}, ...), branch_computations={%region_24.25_spmd, %region_25.26_spmd} | conditional | flops 7820000256 | bytes 29354456 | solution.py:914
  238.2 4.8 %tokens.3.own = bf16[128,1024]{1,0:T(8,128)(2,1)} custom-call(s32[5]{0:T(128)S(1)} %get-tuple-element.407.idx, bf16[8,96,256]{2,1,0:T(8,128)(2,1)} %get-tuple-element.408.got, bf16[1024,1536]{1,0:T(8,128)(2,1)} %get-tuple-element.409.message), custom_call_target="tpu_custom_call" | custom-call | flops 4485000192 | bytes 14430000 | tf_op jit(solution)/shard_map/cond/branch_1_fun/tokens/pallas_call | solution.py:115
  246.9 5.0 %collective-permute-done.13.other = bf16[128,1024]{1,0:T(8,128)(2,1)S(1)} collective-permute-done((bf16[128,1024]{1,0:T(8,128)(2,1)}, bf16[128,1024]{1,0:T(8,128)(2,1)S(1)}, u32[]{:S(2)}, u32[]{:S(2)}) %collective-permute-start.13) | collective-permute-done | bytes 262176 | tf_op jit(solution)/shard_map/cond/branch_1_fun/ppermute | solution.py:41
  253.7 4.3 %all-to-all-start.4 = ((bf16[8,64,256]{2,1,0:T(8,128)(2,1)}), bf16[8,64,256]{2,1,0:T(8,128)(2,1)S(1)}, u32[]{:S(2)}, u32[]{:S(2)}) async-start(bf16[8,64,256]{2,1,0:T(8,128)(2,1)} %get-tuple-element.668), calls=%async_computation.4 | async-start | bytes 524288 | tf_op jit(solution)/shard_map/all_to_all | solution.py:1299
  258.8 2.5 line_sum.1
  261.3 2.0 collective-permute-start.40
  264.5 3.8 %all-to-all-done.4.got = bf16[8,64,256]{2,1,0:T(8,128)(2,1)S(1)} async-done(((bf16[8,64,256]{2,1,0:T(8,128)(2,1)}), bf16[8,64,256]{2,1,0:T(8,128)(2,1)S(1)}, u32[]{:S(2)}, u32[]{:S(2)}) %all-to-all-start.4) | async-done | bytes 262176 | tf_op jit(solution)/shard_map/all_to_all | solution.py:1299
  269.1 1.9 triple_out.1
  271.0 3.8 %collective-permute-done.40.got = bf16[64,2304]{1,0:T(8,128)(2,1)S(1)} collective-permute-done((bf16[64,2304]{1,0:T(8,128)(2,1)}, bf16[64,2304]{1,0:T(8,128)(2,1)S(1)}, u32[]{:S(2)}, u32[]{:S(2)}) %collective-permute-start.40) | collective-permute-done | bytes 294944 | tf_op jit(solution)/shard_map/ppermute | solution.py:41
  275.4 2.2 columns.1
  277.7 3.2 %all-gather.12.cloned.1.call-done = bf16[5376,128]{1,0:T(8,128)(2,1)} async-done(((bf16[336,128]{1,0:T(8,128)(2,1)}), bf16[5376,128]{1,0:T(8,128)(2,1)}) %all-gather.12.cloned.1.call-update) | async-done | bytes 1376272 | tf_op jit(solution)/shard_map/all_gather | solution.py:1273
  280.9 2.9 spread.1
  (203 shorter events, 55.8 us)
Async XLA Ops:
  7.2 104.7 %all-gather.6.cloned.1.call-start = ((), (), s32[]{:S(2)}) async-start(), calls=%async_computation.5 | async-start | bytes 8912896 | tf_op jit(solution)/shard_map/all_gather | solution.py:963
  7.3 113.4 %copy-start.18 = (s32[5]{0:T(128)}, s32[5]{0:T(128)S(1)}, u32[]{:S(2)}) copy-start(s32[5]{0:T(128)S(1)} %stack.74.idx) | copy-start | bytes 64
  7.3 24.6 %copy-start.42 = (s32[4]{0:T(128)S(1)}, s32[4]{0:T(128)}, u32[]{:S(2)}) copy-start(s32[4]{0:T(128)} %param.44) | copy-start | bytes 52
  7.3 24.7 %copy-start.17 = (s32[128]{0:T(128)S(1)}, s32[128]{0:T(128)}, u32[]{:S(2)}) copy-start(s32[128]{0:T(128)} %param.46) | copy-start | bytes 1540
  10.0 21.9 %collective-permute-start.28 = (bf16[160,1024]{1,0:T(8,128)(2,1)S(1)}, bf16[160,1024]{1,0:T(8,128)(2,1)S(1)}, u32[]{:S(2)}, u32[]{:S(2)}) collective-permute-start(bf16[160,1024]{1,0:T(8,128)(2,1)S(1)} %get-tuple-element.556), channel_id=1, source_target_pairs={{0,4},{4,0},{1,5},{5,1},{2,6},{6,2},{3,7},{7,3},{8,12},{12,8},{9,1... | collective-permute-start | bytes 983048 | tf_op jit(solution)/shard_map/ppermute | solution.py:41
  12.9 9.7 %collective-permute-start.29 = (bf16[96,1024]{1,0:T(8,128)(2,1)}, bf16[96,1024]{1,0:T(8,128)(2,1)S(1)}, u32[]{:S(2)}, u32[]{:S(2)}) collective-permute-start(bf16[96,1024]{1,0:T(8,128)(2,1)} %get-tuple-element.558), channel_id=1, source_target_pairs={{0,8},{8,0},{16,24},{24,16},{1,9},{9,1},{17,25},{25,17},{2,10},{10... | collective-permute-start | bytes 589832 | tf_op jit(solution)/shard_map/ppermute | solution.py:33
  14.5 17.4 %collective-permute-start.30 = (bf16[96,1024]{1,0:T(8,128)(2,1)}, bf16[96,1024]{1,0:T(8,128)(2,1)S(1)}, u32[]{:S(2)}, u32[]{:S(2)}) collective-permute-start(bf16[96,1024]{1,0:T(8,128)(2,1)} %get-tuple-element.558), channel_id=1, source_target_pairs={{0,16},{8,24},{16,0},{24,8},{1,17},{9,25},{17,1},{25,9},{2,18},{10... | collective-permute-start | bytes 589832 | tf_op jit(solution)/shard_map/ppermute | solution.py:33
  17.1 14.8 %collective-permute-start.31 = (bf16[96,1024]{1,0:T(8,128)(2,1)}, bf16[96,1024]{1,0:T(8,128)(2,1)S(1)}, u32[]{:S(2)}, u32[]{:S(2)}) collective-permute-start(bf16[96,1024]{1,0:T(8,128)(2,1)} %get-tuple-element.558), channel_id=1, source_target_pairs={{0,24},{8,16},{16,8},{24,0},{1,25},{9,17},{17,9},{25,1},{2,26},{10... | collective-permute-start | bytes 589832 | tf_op jit(solution)/shard_map/ppermute | solution.py:33
  31.9 41.9 %copy-start.8 = (bf16[160,1024]{1,0:T(8,128)(2,1)}, bf16[160,1024]{1,0:T(8,128)(2,1)S(1)}, u32[]{:S(2)}) copy-start(bf16[160,1024]{1,0:T(8,128)(2,1)S(1)} %collective-permute-done.28) | copy-start | bytes 983044
  31.9 141.7 %all-gather.8.cloned.1.call-start = ((), (), s32[]{:S(2)}) async-start(), calls=%async_computation.6 | async-start | bytes 3342336 | tf_op jit(solution)/shard_map/all_gather | solution.py:1046
  32.1 41.7 %copy-start.40 = (f32[3,512]{1,0:T(4,128)S(1)}, f32[3,512]{1,0:T(4,128)}, u32[]{:S(2)}) copy-start(f32[3,512]{1,0:T(4,128)} %param.48) | copy-start | bytes 18436
  32.1 18.0 %collective-permute-start.14 = (bf16[96,1024]{1,0:T(8,128)(2,1)S(1)}, bf16[96,1024]{1,0:T(8,128)(2,1)S(1)}, u32[]{:S(2)}, u32[]{:S(2)}) collective-permute-start(bf16[96,1024]{1,0:T(8,128)(2,1)S(1)} %get-tuple-element.263), channel_id=1, source_target_pairs={{0,4},{4,0},{1,5},{5,1},{2,6},{6,2},{3,7},{7,3},{8,12},{12,8},{9,1... | collective-permute-start | bytes 589832 | tf_op jit(solution)/shard_map/cond/branch_1_fun/ppermute | solution.py:41
  32.8 19.6 %collective-permute-start.16 = (bf16[96,1024]{1,0:T(8,128)(2,1)S(1)}, bf16[96,1024]{1,0:T(8,128)(2,1)S(1)}, u32[]{:S(2)}, u32[]{:S(2)}) collective-permute-start(bf16[96,1024]{1,0:T(8,128)(2,1)S(1)} %get-tuple-element.264), channel_id=1, source_target_pairs={{0,4},{4,0},{1,5},{5,1},{2,6},{6,2},{3,7},{7,3},{8,12},{12,8},{9,1... | collective-permute-start | bytes 589832 | tf_op jit(solution)/shard_map/cond/branch_1_fun/ppermute | solution.py:41
  34.2 19.5 %collective-permute-start.18 = (bf16[96,1024]{1,0:T(8,128)(2,1)S(1)}, bf16[96,1024]{1,0:T(8,128)(2,1)S(1)}, u32[]{:S(2)}, u32[]{:S(2)}) collective-permute-start(bf16[96,1024]{1,0:T(8,128)(2,1)S(1)} %get-tuple-element.265), channel_id=1, source_target_pairs={{0,4},{4,0},{1,5},{5,1},{2,6},{6,2},{3,7},{7,3},{8,12},{12,8},{9,1... | collective-permute-start | bytes 589832 | tf_op jit(solution)/shard_map/cond/branch_1_fun/ppermute | solution.py:41
  34.8 33.3 %all-to-all-start.3 = ((bf16[8,64,256]{2,1,0:T(8,128)(2,1)}), bf16[8,64,256]{2,1,0:T(8,128)(2,1)S(1)}, u32[]{:S(2)}, u32[]{:S(2)}) async-start(bf16[8,64,256]{2,1,0:T(8,128)(2,1)} %get-tuple-element.262), calls=%async_computation.3 | async-start | bytes 524288 | tf_op jit(solution)/shard_map/cond/branch_1_fun/all_to_all | solution.py:966
  50.9 9.6 %collective-permute-start.15 = (bf16[2,64,1024]{2,1,0:T(8,128)(2,1)}, bf16[2,64,1024]{2,1,0:T(8,128)(2,1)}, u32[]{:S(2)}, u32[]{:S(2)}) collective-permute-start(bf16[2,64,1024]{2,1,0:T(8,128)(2,1)} %pad_maximum_fusion), channel_id=1, source_target_pairs={{0,1},{1,0},{2,3},{3,2},{4,5},{5,4},{6,7},{7,6},{8,9},{9,8},{10,11... | collective-permute-start | bytes 786440 | tf_op jit(solution)/shard_map/cond/branch_1_fun/ppermute | solution.py:41
  53.2 12.2 %collective-permute-start.17 = (bf16[2,64,1024]{2,1,0:T(8,128)(2,1)}, bf16[2,64,1024]{2,1,0:T(8,128)(2,1)}, u32[]{:S(2)}, u32[]{:S(2)}) collective-permute-start(bf16[2,64,1024]{2,1,0:T(8,128)(2,1)} %pad_maximum_fusion.1), channel_id=1, source_target_pairs={{0,1},{1,0},{2,3},{3,2},{4,5},{5,4},{6,7},{7,6},{8,9},{9,8},{10,11... | collective-permute-start | bytes 786440 | tf_op jit(solution)/shard_map/cond/branch_1_fun/ppermute | solution.py:41
  54.4 13.7 %collective-permute-start.19 = (bf16[2,64,1024]{2,1,0:T(8,128)(2,1)}, bf16[2,64,1024]{2,1,0:T(8,128)(2,1)}, u32[]{:S(2)}, u32[]{:S(2)}) collective-permute-start(bf16[2,64,1024]{2,1,0:T(8,128)(2,1)} %pad_maximum_fusion.2), channel_id=1, source_target_pairs={{0,1},{1,0},{2,3},{3,2},{4,5},{5,4},{6,7},{7,6},{8,9},{9,8},{10,11... | collective-permute-start | bytes 786440 | tf_op jit(solution)/shard_map/cond/branch_1_fun/ppermute | solution.py:41
  68.1 1.8 collective-permute-start.20
  69.5 4.3 %collective-permute-start.21 = (bf16[8,32,1024]{2,1,0:T(8,128)(2,1)}, bf16[8,32,1024]{2,1,0:T(8,128)(2,1)}, u32[]{:S(2)}, u32[]{:S(2)}) collective-permute-start(bf16[8,32,1024]{2,1,0:T(8,128)(2,1)} %fusion.1), channel_id=1, source_target_pairs={{0,2},{2,0},{1,3},{3,1},{4,6},{6,4},{5,7},{7,5},{8,10},{10,8},{9,1... | collective-permute-start | bytes 1572872 | tf_op jit(solution)/shard_map/cond/branch_1_fun/ppermute | solution.py:41
  73.8 46.9 %copy-start.11 = (s32[8,128]{1,0:T(8,128)}, s32[8,128]{1,0:T(8,128)S(1)}, u32[]{:S(2)}) copy-start(s32[8,128]{1,0:T(8,128)S(1)} %get-tuple-element.574) | copy-start | bytes 12292
  77.5 1.9 collective-permute-start
  99.4 12.4 %copy-start.28 = (bf16[128,1024]{1,0:T(8,128)(2,1)S(1)}, bf16[128,1024]{1,0:T(8,128)(2,1)}, u32[]{:S(2)}) copy-start(bf16[128,1024]{1,0:T(8,128)(2,1)} %tokens.5) | copy-start | bytes 786436
  99.4 12.4 %copy-start.41 = (f32[1024]{0:T(1024)S(1)}, f32[1024]{0:T(1024)}, u32[]{:S(2)}) copy-start(f32[1024]{0:T(1024)} %param.51) | copy-start | bytes 12292
  102.6 7.4 %collective-permute-start.1 = (bf16[128,1024]{1,0:T(8,128)(2,1)}, bf16[128,1024]{1,0:T(8,128)(2,1)}, u32[]{:S(2)}, u32[]{:S(2)}) collective-permute-start(bf16[128,1024]{1,0:T(8,128)(2,1)} %get-tuple-element.751), channel_id=1, source_target_pairs={{0,1},{1,0},{2,3},{3,2},{4,5},{5,4},{6,7},{7,6},{8,9},{9,8},{10,11... | collective-permute-start | bytes 786440 | tf_op jit(solution)/shard_map/cond/branch_1_fun/ppermute | solution.py:41
  110.1 101.8 %all-gather.10.cloned.1.call-start = ((), (), s32[]{:S(2)}) async-start(), calls=%async_computation.7 | async-start | bytes 1114112 | tf_op jit(solution)/shard_map/all_gather | solution.py:1125
  119.0 14.7 %collective-permute-start.32 = (bf16[288,1024]{1,0:T(8,128)(2,1)}, bf16[288,1024]{1,0:T(8,128)(2,1)}, u32[]{:S(2)}, u32[]{:S(2)}) collective-permute-start(bf16[288,1024]{1,0:T(8,128)(2,1)} %get-tuple-element.590), channel_id=1, source_target_pairs={{0,2},{2,0},{1,3},{3,1},{4,6},{6,4},{5,7},{7,5},{8,10},{10,8},{9,1... | collective-permute-start | bytes 1769480 | tf_op jit(solution)/shard_map/ppermute | solution.py:41
  119.3 38.7 %collective-permute-start.33 = (bf16[288,1024]{1,0:T(8,128)(2,1)}, bf16[288,1024]{1,0:T(8,128)(2,1)}, u32[]{:S(2)}, u32[]{:S(2)}) collective-permute-start(bf16[288,1024]{1,0:T(8,128)(2,1)} %get-tuple-element.601), channel_id=1, source_target_pairs={{0,4},{4,0},{1,5},{5,1},{2,6},{6,2},{3,7},{7,3},{8,12},{12,8},{9,1... | collective-permute-start | bytes 1769480 | tf_op jit(solution)/shard_map/ppermute | solution.py:41
  120.7 8.5 %collective-permute-start.2 = (bf16[128,1024]{1,0:T(8,128)(2,1)}, bf16[128,1024]{1,0:T(8,128)(2,1)S(1)}, u32[]{:S(2)}, u32[]{:S(2)}) collective-permute-start(bf16[128,1024]{1,0:T(8,128)(2,1)} %get-tuple-element.314.own), channel_id=1, source_target_pairs={{0,1},{1,0},{2,3},{3,2},{4,5},{5,4},{6,7},{7,6},{8,9},{9,8},{10,11... | collective-permute-start | bytes 786440 | tf_op jit(solution)/shard_map/cond/branch_1_fun/ppermute | solution.py:41
  133.9 1.9 collective-permute-start.22
  134.0 4.2 %collective-permute-start.23 = (bf16[4,4096]{1,0:T(4,128)(2,1)S(1)}, bf16[4,4096]{1,0:T(4,128)(2,1)S(1)}, u32[]{:S(2)}, u32[]{:S(2)}) collective-permute-start(bf16[4,4096]{1,0:T(4,128)(2,1)S(1)} %get-tuple-element.323), channel_id=1, source_target_pairs={{0,4},{2,6},{4,0},{6,2},{1,5},{3,7},{5,1},{7,3},{8,12},{10,14},{12... | collective-permute-start | bytes 98312 | tf_op jit(solution)/shard_map/cond/branch_1_fun/ppermute | solution.py:37
  134.7 3.7 %collective-permute-start.24 = (bf16[4,4096]{1,0:T(4,128)(2,1)S(1)}, bf16[4,4096]{1,0:T(4,128)(2,1)S(1)}, u32[]{:S(2)}, u32[]{:S(2)}) collective-permute-start(bf16[4,4096]{1,0:T(4,128)(2,1)S(1)} %get-tuple-element.323), channel_id=1, source_target_pairs={{0,6},{2,4},{4,2},{6,0},{1,7},{3,5},{5,3},{7,1},{8,14},{10,12},{12... | collective-permute-start | bytes 98312 | tf_op jit(solution)/shard_map/cond/branch_1_fun/ppermute | solution.py:37
  138.4 9.2 %copy-start.7 = (bf16[4,4096]{1,0:T(4,128)(2,1)}, bf16[4,4096]{1,0:T(4,128)(2,1)S(1)}, u32[]{:S(2)}) copy-start(bf16[4,4096]{1,0:T(4,128)(2,1)S(1)} %add_convert_fusion.t0) | copy-start | bytes 98308 | tf_op jit(solution)/shard_map/cond
  138.4 4.5 %collective-permute-start.25 = (bf16[4,4096]{1,0:T(4,128)(2,1)S(1)}, bf16[4,4096]{1,0:T(4,128)(2,1)S(1)}, u32[]{:S(2)}, u32[]{:S(2)}) collective-permute-start(bf16[4,4096]{1,0:T(4,128)(2,1)S(1)} %add_convert_fusion.t0), channel_id=1, source_target_pairs={{0,8},{8,0},{16,24},{24,16},{1,9},{9,1},{17,25},{25,17},{2,10},{10... | collective-permute-start | bytes 98312 | tf_op jit(solution)/shard_map/cond/branch_1_fun/ppermute | solution.py:33
  139.1 7.8 %collective-permute-start.26 = (bf16[4,4096]{1,0:T(4,128)(2,1)S(1)}, bf16[4,4096]{1,0:T(4,128)(2,1)S(1)}, u32[]{:S(2)}, u32[]{:S(2)}) collective-permute-start(bf16[4,4096]{1,0:T(4,128)(2,1)S(1)} %add_convert_fusion.t0), channel_id=1, source_target_pairs={{0,16},{8,24},{16,0},{24,8},{1,17},{9,25},{17,1},{25,9},{2,18},{10... | collective-permute-start | bytes 98312 | tf_op jit(solution)/shard_map/cond/branch_1_fun/ppermute | solution.py:33
  141.2 6.4 %collective-permute-start.27 = (bf16[4,4096]{1,0:T(4,128)(2,1)S(1)}, bf16[4,4096]{1,0:T(4,128)(2,1)S(1)}, u32[]{:S(2)}, u32[]{:S(2)}) collective-permute-start(bf16[4,4096]{1,0:T(4,128)(2,1)S(1)} %add_convert_fusion.t0), channel_id=1, source_target_pairs={{0,24},{8,16},{16,8},{24,0},{1,25},{9,17},{17,9},{25,1},{2,26},{10... | collective-permute-start | bytes 98312 | tf_op jit(solution)/shard_map/cond/branch_1_fun/ppermute | solution.py:33
  158.1 122.9 %all-gather.12.cloned.1.call-start = ((), (), s32[]{:S(2)}) async-start(), calls=%async_computation.8 | async-start | bytes 1462272 | tf_op jit(solution)/shard_map/all_gather | solution.py:1273
  158.1 15.6 %collective-permute-start.34 = (bf16[256,1024]{1,0:T(8,128)(2,1)}, bf16[256,1024]{1,0:T(8,128)(2,1)S(1)}, u32[]{:S(2)}, u32[]{:S(2)}) collective-permute-start(bf16[256,1024]{1,0:T(8,128)(2,1)} %get-tuple-element.609), channel_id=1, source_target_pairs={{0,4},{4,0},{1,5},{5,1},{2,6},{6,2},{3,7},{7,3},{8,12},{12,8},{9,1... | collective-permute-start | bytes 1572872 | tf_op jit(solution)/shard_map/ppermute | solution.py:41
  159.8 13.9 %collective-permute-start.35 = (bf16[256,1024]{1,0:T(8,128)(2,1)}, bf16[256,1024]{1,0:T(8,128)(2,1)S(1)}, u32[]{:S(2)}, u32[]{:S(2)}) collective-permute-start(bf16[256,1024]{1,0:T(8,128)(2,1)} %get-tuple-element.616), channel_id=1, source_target_pairs={{0,2},{2,0},{1,3},{3,1},{4,6},{6,4},{5,7},{7,5},{8,10},{10,8},{9,1... | collective-permute-start | bytes 1572872 | tf_op jit(solution)/shard_map/ppermute | solution.py:41
  159.8 8.9 %collective-permute-start.3 = (bf16[128,1024]{1,0:T(8,128)(2,1)}, bf16[128,1024]{1,0:T(8,128)(2,1)S(1)}, u32[]{:S(2)}, u32[]{:S(2)}) collective-permute-start(bf16[128,1024]{1,0:T(8,128)(2,1)} %get-tuple-element.340.own), channel_id=1, source_target_pairs={{0,1},{1,0},{2,3},{3,2},{4,5},{5,4},{6,7},{7,6},{8,9},{9,8},{10,11... | collective-permute-start | bytes 786440 | tf_op jit(solution)/shard_map/cond/branch_1_fun/ppermute | solution.py:41
  161.3 1.6 collective-permute-start.4
  173.7 19.9 %copy-start.12 = (s32[8,128]{1,0:T(8,128)S(1)}, s32[8,128]{1,0:T(8,128)}, u32[]{:S(2)}) copy-start(s32[8,128]{1,0:T(8,128)} %copy-done.11) | copy-start | bytes 12292
  173.7 19.9 %copy-start.15 = (s32[8,128]{1,0:T(8,128)S(1)}, s32[8,128]{1,0:T(8,128)}, u32[]{:S(2)}) copy-start(s32[8,128]{1,0:T(8,128)} %copy-done.14) | copy-start | bytes 12292
  173.7 19.9 %copy-start.16 = (f32[4,1,1,256]{3,2,1,0:T(1,128)S(1)}, f32[4,1,1,256]{3,2,1,0:T(1,128)}, u32[]{:S(2)}) copy-start(f32[4,1,1,256]{3,2,1,0:T(1,128)} %get-tuple-element.619) | copy-start | bytes 12292
  173.7 19.9 %copy-start.43 = (s32[4]{0:T(128)S(1)}, s32[4]{0:T(128)}, u32[]{:S(2)}) copy-start(s32[4]{0:T(128)} %param.44) | copy-start | bytes 52
  173.7 9.0 %copy-start.23 = (bf16[256,1024]{1,0:T(8,128)(2,1)}, bf16[256,1024]{1,0:T(8,128)(2,1)S(1)}, u32[]{:S(2)}) copy-start(bf16[256,1024]{1,0:T(8,128)(2,1)S(1)} %get-tuple-element.356.g1) | copy-start | bytes 1572868 | tf_op jit(solution)/shard_map/cond
  173.8 9.0 %collective-permute-start.8 = (bf16[288,1024]{1,0:T(8,128)(2,1)}, bf16[288,1024]{1,0:T(8,128)(2,1)}, u32[]{:S(2)}, u32[]{:S(2)}) collective-permute-start(bf16[288,1024]{1,0:T(8,128)(2,1)} %get-tuple-element.351.f1), channel_id=1, source_target_pairs={{0,2},{2,0},{1,3},{3,1},{4,6},{6,4},{5,7},{7,5},{8,10},{10,8},{9,1... | collective-permute-start | bytes 1769480 | tf_op jit(solution)/shard_map/cond/branch_1_fun/ppermute | solution.py:41
  173.9 8.9 %collective-permute-start.9 = (bf16[256,1024]{1,0:T(8,128)(2,1)S(1)}, bf16[256,1024]{1,0:T(8,128)(2,1)S(1)}, u32[]{:S(2)}, u32[]{:S(2)}) collective-permute-start(bf16[256,1024]{1,0:T(8,128)(2,1)S(1)} %get-tuple-element.356.g1), channel_id=1, source_target_pairs={{0,2},{2,0},{1,3},{3,1},{4,6},{6,4},{5,7},{7,5},{8,10},{10,8},{9,1... | collective-permute-start | bytes 1572872 | tf_op jit(solution)/shard_map/cond/branch_1_fun/ppermute | solution.py:41
  174.3 8.4 %collective-permute-start.5 = (bf16[128,1024]{1,0:T(8,128)(2,1)S(1)}, bf16[128,1024]{1,0:T(8,128)(2,1)}, u32[]{:S(2)}, u32[]{:S(2)}) collective-permute-start(bf16[128,1024]{1,0:T(8,128)(2,1)S(1)} %get-tuple-element.350), channel_id=1, source_target_pairs={{0,4},{4,0},{1,5},{5,1},{2,6},{6,2},{3,7},{7,3},{8,12},{12,8},{9,1... | collective-permute-start | bytes 786440 | tf_op jit(solution)/shard_map/cond/branch_1_fun/ppermute | solution.py:41
  174.8 14.1 %collective-permute-start.6 = (bf16[128,1024]{1,0:T(8,128)(2,1)S(1)}, bf16[128,1024]{1,0:T(8,128)(2,1)}, u32[]{:S(2)}, u32[]{:S(2)}) collective-permute-start(bf16[128,1024]{1,0:T(8,128)(2,1)S(1)} %get-tuple-element.350), channel_id=1, source_target_pairs={{0,2},{2,0},{1,3},{3,1},{4,6},{6,4},{5,7},{7,5},{8,10},{10,8},{9,1... | collective-permute-start | bytes 786440 | tf_op jit(solution)/shard_map/cond/branch_1_fun/ppermute | solution.py:41
  174.8 16.8 %all-to-all-start.1 = ((bf16[8,144,128]{2,1,0:T(8,128)(2,1)}), bf16[8,144,128]{2,1,0:T(8,128)(2,1)}, u32[]{:S(2)}, u32[]{:S(2)}) async-start(bf16[8,144,128]{2,1,0:T(8,128)(2,1)} %get-tuple-element.349), calls=%async_computation.1 | async-start | bytes 589824 | tf_op jit(solution)/shard_map/cond/branch_1_fun/all_to_all | solution.py:1023
  182.7 8.9 %collective-permute-start.7 = (bf16[128,1024]{1,0:T(8,128)(2,1)}, bf16[128,1024]{1,0:T(8,128)(2,1)}, u32[]{:S(2)}, u32[]{:S(2)}) collective-permute-start(bf16[128,1024]{1,0:T(8,128)(2,1)} %collective-permute-done.5), channel_id=1, source_target_pairs={{0,2},{2,0},{1,3},{3,1},{4,6},{6,4},{5,7},{7,5},{8,10},{10,8},{9,1... | collective-permute-start | bytes 786440 | tf_op jit(solution)/shard_map/cond/branch_1_fun/ppermute | solution.py:41
  191.6 17.6 %collective-permute-start.36 = (bf16[2,2,64,1024]{3,2,1,0:T(8,128)(2,1)S(1)}, bf16[2,2,64,1024]{3,2,1,0:T(8,128)(2,1)}, u32[]{:S(2)}, u32[]{:S(2)}) collective-permute-start(bf16[2,2,64,1024]{3,2,1,0:T(8,128)(2,1)S(1)} %get-tuple-element.622), channel_id=1, source_target_pairs={{0,8},{8,0},{16,24},{24,16},{1,9},{9,1},{17,25},{25,17},{2,10},{10... | collective-permute-start | bytes 1572872 | tf_op jit(solution)/shard_map/ppermute | solution.py:33
  192.3 42.7 %collective-permute-start.38 = (bf16[2,2,64,1024]{3,2,1,0:T(8,128)(2,1)S(1)}, bf16[2,2,64,1024]{3,2,1,0:T(8,128)(2,1)}, u32[]{:S(2)}, u32[]{:S(2)}) collective-permute-start(bf16[2,2,64,1024]{3,2,1,0:T(8,128)(2,1)S(1)} %get-tuple-element.640), channel_id=1, source_target_pairs={{0,8},{8,0},{16,24},{24,16},{1,9},{9,1},{17,25},{25,17},{2,10},{10... | collective-permute-start | bytes 1572872 | tf_op jit(solution)/shard_map/ppermute | solution.py:33
  193.9 12.3 %copy-start.21 = (s32[5]{0:T(128)S(1)}, s32[5]{0:T(128)}, u32[]{:S(2)}) copy-start(s32[5]{0:T(128)} %get-tuple-element.362.idx) | copy-start | bytes 64 | tf_op jit(solution)/shard_map/cond
  203.7 1.8 collective-permute-start.10
  211.3 23.7 %collective-permute-start.37 = (bf16[2,64,1024]{2,1,0:T(8,128)(2,1)}, bf16[2,64,1024]{2,1,0:T(8,128)(2,1)}, u32[]{:S(2)}, u32[]{:S(2)}) collective-permute-start(bf16[2,64,1024]{2,1,0:T(8,128)(2,1)} %get-tuple-element.639), channel_id=1, source_target_pairs={{0,16},{8,24},{16,0},{24,8},{1,17},{9,25},{17,1},{25,9},{2,18},{10... | collective-permute-start | bytes 786440 | tf_op jit(solution)/shard_map/ppermute | solution.py:33
  212.0 23.0 %all-to-all-start.2 = ((bf16[8,96,256]{2,1,0:T(8,128)(2,1)}), bf16[8,96,256]{2,1,0:T(8,128)(2,1)}, u32[]{:S(2)}, u32[]{:S(2)}) async-start(bf16[8,96,256]{2,1,0:T(8,128)(2,1)} %get-tuple-element.377), calls=%async_computation.2 | async-start | bytes 786432 | tf_op jit(solution)/shard_map/cond/branch_1_fun/all_to_all | solution.py:1023
  220.4 9.5 %collective-permute-start.11 = (bf16[2,2,64,256]{3,2,1,0:T(8,128)(2,1)}, bf16[2,2,64,256]{3,2,1,0:T(8,128)(2,1)}, u32[]{:S(2)}, u32[]{:S(2)}) collective-permute-start(bf16[2,2,64,256]{3,2,1,0:T(8,128)(2,1)} %get-tuple-element.400), channel_id=1, source_target_pairs={{0,8},{8,0},{16,24},{24,16},{1,9},{9,1},{17,25},{25,17},{2,10},{10... | collective-permute-start | bytes 393224 | tf_op jit(solution)/shard_map/cond/branch_1_fun/ppermute | solution.py:33
  237.2 20.8 %collective-permute-start.39 = (bf16[2,64,1280]{2,1,0:T(8,128)(2,1)}, bf16[2,64,1280]{2,1,0:T(8,128)(2,1)S(1)}, u32[]{:S(2)}, u32[]{:S(2)}) collective-permute-start(bf16[2,64,1280]{2,1,0:T(8,128)(2,1)} %get-tuple-element.660), channel_id=1, source_target_pairs={{0,16},{8,24},{16,0},{24,8},{1,17},{9,25},{17,1},{25,9},{2,18},{10... | collective-permute-start | bytes 983048 | tf_op jit(solution)/shard_map/ppermute | solution.py:33
  238.1 6.4 %collective-permute-start.12 = (bf16[8,64,256]{2,1,0:T(8,128)(2,1)S(1)}, bf16[8,64,256]{2,1,0:T(8,128)(2,1)S(1)}, u32[]{:S(2)}, u32[]{:S(2)}) collective-permute-start(bf16[8,64,256]{2,1,0:T(8,128)(2,1)S(1)} %get-tuple-element.411), channel_id=1, source_target_pairs={{0,2},{2,0},{1,3},{3,1},{4,6},{6,4},{5,7},{7,5},{8,10},{10,8},{9,1... | collective-permute-start | bytes 786440 | tf_op jit(solution)/shard_map/cond/branch_1_fun/ppermute | solution.py:41
  242.9 9.0 %collective-permute-start.13 = (bf16[128,1024]{1,0:T(8,128)(2,1)}, bf16[128,1024]{1,0:T(8,128)(2,1)S(1)}, u32[]{:S(2)}, u32[]{:S(2)}) collective-permute-start(bf16[128,1024]{1,0:T(8,128)(2,1)} %tokens.3.own), channel_id=1, source_target_pairs={{0,1},{1,0},{2,3},{3,2},{4,5},{5,4},{6,7},{7,6},{8,9},{9,8},{10,11... | collective-permute-start | bytes 786440 | tf_op jit(solution)/shard_map/cond/branch_1_fun/ppermute | solution.py:41
  253.7 14.6 %all-to-all-start.4 = ((bf16[8,64,256]{2,1,0:T(8,128)(2,1)}), bf16[8,64,256]{2,1,0:T(8,128)(2,1)S(1)}, u32[]{:S(2)}, u32[]{:S(2)}) async-start(bf16[8,64,256]{2,1,0:T(8,128)(2,1)} %get-tuple-element.668), calls=%async_computation.4 | async-start | bytes 524288 | tf_op jit(solution)/shard_map/all_to_all | solution.py:1299
  261.3 13.4 %collective-permute-start.40 = (bf16[64,2304]{1,0:T(8,128)(2,1)}, bf16[64,2304]{1,0:T(8,128)(2,1)S(1)}, u32[]{:S(2)}, u32[]{:S(2)}) collective-permute-start(bf16[64,2304]{1,0:T(8,128)(2,1)} %get-tuple-element.663), channel_id=1, source_target_pairs={{0,4},{4,0},{1,5},{5,1},{2,6},{6,2},{3,7},{7,3},{8,12},{12,8},{9,1... | collective-permute-start | bytes 884744 | tf_op jit(solution)/shard_map/ppermute | solution.py:41
  (29 other events, 88.6 us)
Sparse Core Ops, SparseCore 0:
  32.0 79.7 all-gather.5
  114.1 45.7 all-gather.7
  162.1 37.8 all-gather.9
  237.3 43.5 all-gather.11
